TPU v7x, 32 devices: a whole 2x2x4 slice. The times are simulated.
32 devices in a mesh: groups: 2 (over y), mp: 8 (over z, x), batch: 2 (over core).
Axes of the slice: x: 2, y: 2, z: 4, core: 2. Of those that a mesh axis runs over, the one named last changes fastest.
Arguments:
- hidden: bfloat16 [64, 8192], P(('groups', 'mp', 'batch')), parts along dimension 0, may hold values from -6 to 6
- attention_norm_gain: bfloat16 [8192], replicated, may hold values from 0.25 to 1.75
- query_key_value_weight: bfloat16 [8192, 10240], P(None, ('mp', 'batch')), may hold values from -0.0625 to 0.0625
- output_weight: bfloat16 [8192, 8192], P(None, 'mp'), may hold values from -0.0625 to 0.0625
- key_cache: bfloat16 [64, 256, 1024], P(('groups', 'mp', 'batch')), parts along dimension 0, may hold values from -180 to 180
- value_cache: bfloat16 [64, 256, 1024], P(('groups', 'mp', 'batch')), parts along dimension 0, may hold values from -6 to 6
- lengths: int32 [64], P(('groups', 'mp', 'batch')), parts along dimension 0, may hold values from 1 to 256
- slots: int32 [64], P(('groups', 'mp', 'batch')), parts along dimension 0, may hold values from 0 to 1
- requests: int32 [32, 2], P(('groups', 'mp', 'batch')), parts along dimension 0, may hold values from 0 to 63, as said below
- adapter_down_matrices: bfloat16 [64, 8192, 64], P(None, 'mp'), may hold values from -0.0625 to 0.0625
- adapter_up_matrices: bfloat16 [64, 64, 8192], P(None, None, 'mp'), may hold values from -0.75 to 0.75
Outputs:
- result: bfloat16 [64, 8192], P(('groups', 'mp', 'batch')), parts along dimension 0
There are 2 independent parts, one for each index of `groups`. A program takes and returns all parts, laid end to end along the dimension named above; an argument that names none is the same for every part. Nothing has to cross between parts.
Inputs may be any that keep to these rules, and one draw needn't show every extreme that they name: `requests`: the 2 entries of one device's list are distinct adapters.
All inputs are finite; a program needn't handle non-finite values.
Results may differ from a plain program's by a relative error of at most 0.012.
The roundings to bfloat16 on the way count: a program that leaves them out, or rounds other values in their place, can miss the bound.
Values may be sent and summed in bfloat16 or wider, within the bound.
No kernel may reach another device: no remote copies, remote signals or barrier semaphores. Data moves between devices by JAX's collectives and lax.ppermute only.
A program may use at most 128 MiB of HBM per device.

v0:
```python
import jax
import jax.numpy as jnp
from jax import lax
from jax.sharding import PartitionSpec as P

HEADS = 64
KV_HEADS = 8
HEAD_DIM = 128
ADAPTER_COUNT = 64


EPS = 1e-05
THETA = 500000.0
ADAPTER_SCALE = 2.0


def rotate(vec, pos):
    width = vec.shape[-1]
    half = width // 2
    freq = THETA ** (-(jnp.arange(half, dtype=jnp.float32) * 2.0) / width)
    angle = pos[..., None, None] * freq
    cosine = jnp.concatenate([jnp.cos(angle), jnp.cos(angle)], -1)
    sine = jnp.concatenate([jnp.sin(angle), jnp.sin(angle)], -1)
    turned = jnp.concatenate([-vec[..., half:], vec[..., :half]], -1)
    return vec * cosine + turned * sine


def apply_up_matrix(
    context_vector, adapter_selector, down_result, output_weight, adapter_up_matrices
):
    base_output = jnp.dot(context_vector, output_weight, preferred_element_type=jnp.float32)
    spread = (adapter_selector[:, :, None] * down_result[:, None, :]).reshape(
        adapter_selector.shape[0], -1
    )
    adapter_table = adapter_up_matrices.reshape(-1, adapter_up_matrices.shape[2])
    adapter_delta = jnp.dot(spread, adapter_table, preferred_element_type=jnp.float32)
    return (base_output + ADAPTER_SCALE * adapter_delta).astype(jnp.bfloat16)


def body(
    hidden,
    attention_norm_gain,
    query_key_value_weight,
    output_weight,
    key_cache,
    value_cache,
    lengths,
    slots,
    requests,
    adapter_down_matrices,
    adapter_up_matrices,
):
    widened = hidden.astype(jnp.float32)
    normed = (
        widened
        * lax.rsqrt(jnp.mean(widened * widened, -1, keepdims=True) + EPS)
        * attention_norm_gain.astype(jnp.float32)
    ).astype(jnp.bfloat16)
    rows = normed.shape[0]
    columns = jnp.dot(
        lax.all_gather(normed, ("mp", "batch"), axis=0, tiled=True),
        query_key_value_weight,
        preferred_element_type=jnp.float32,
    ).astype(jnp.bfloat16)
    mixed = lax.all_to_all(
        lax.all_to_all(columns, "mp", split_axis=0, concat_axis=1, tiled=True),
        "batch",
        split_axis=0,
        concat_axis=1,
        tiled=True,
    )
    width = query_key_value_weight.shape[1]
    qkv = (
        mixed.reshape(rows, lax.axis_size("batch"), lax.axis_size("mp"), width)
        .transpose(0, 2, 1, 3)
        .reshape(rows, -1)
    )
    query_width = HEADS * HEAD_DIM
    kv_width = KV_HEADS * HEAD_DIM
    group = HEADS // KV_HEADS
    scale = HEAD_DIM ** (-0.5)
    pos = lengths.astype(jnp.float32)
    query = rotate(
        qkv[:, :query_width].astype(jnp.float32).reshape(rows, HEADS, HEAD_DIM), pos
    ).astype(jnp.bfloat16)
    fresh_key = rotate(
        qkv[:, query_width : query_width + kv_width]
        .astype(jnp.float32)
        .reshape(rows, KV_HEADS, HEAD_DIM),
        pos,
    ).astype(jnp.bfloat16)
    fresh_value = (
        qkv[:, query_width + kv_width :].astype(jnp.float32).reshape(rows, KV_HEADS, HEAD_DIM)
    )
    grouped = query.reshape(rows, KV_HEADS, group, HEAD_DIM)
    cached = key_cache.reshape(rows, -1, KV_HEADS, HEAD_DIM)
    stored = value_cache.reshape(rows, -1, KV_HEADS, HEAD_DIM)
    scores = (
        jnp.einsum("rgqd,rtgd->rgqt", grouped, cached, preferred_element_type=jnp.float32) * scale
    )
    live = jnp.arange(cached.shape[1])[None, :] < lengths[:, None]
    scores = jnp.where(live[:, None, None, :], scores, -jnp.inf)
    own = (
        jnp.einsum("rgqd,rgd->rgq", grouped, fresh_key, preferred_element_type=jnp.float32) * scale
    )
    top = jnp.maximum(jnp.max(scores, -1), own)
    expo = jnp.exp(scores - top[..., None])
    own_exp = jnp.exp(own - top)
    total = jnp.sum(expo, -1) + own_exp
    probs = (expo / total[..., None]).astype(jnp.bfloat16)
    own_prob = (own_exp / total).astype(jnp.bfloat16)
    context_vector = jnp.einsum(
        "rgqt,rtgd->rgqd", probs, stored, preferred_element_type=jnp.float32
    )
    context_vector = (
        context_vector + own_prob.astype(jnp.float32)[..., None] * fresh_value[:, :, None, :]
    )
    context_vector = context_vector.reshape(rows, query_width).astype(jnp.bfloat16)
    slot_hits = slots[:, None] == jnp.arange(requests.shape[1])[None, :]
    adapter = jnp.sum(jnp.where(slot_hits, requests[0][None, :], 0), 1)
    adapter_selector = (adapter[:, None] == jnp.arange(ADAPTER_COUNT)[None, :]).astype(jnp.bfloat16)
    context_gathered, selector_gathered = (
        lax.all_gather(context_vector, "mp", axis=0, tiled=True),
        lax.all_gather(adapter_selector, "mp", axis=0, tiled=True),
    )
    shared_portion = adapter_down_matrices.shape[1]
    context_slice = lax.dynamic_slice_in_dim(
        context_gathered, lax.axis_index("mp") * shared_portion, shared_portion, 1
    )
    every_adapter = jnp.einsum(
        "gh,thy->gty", context_slice, adapter_down_matrices, preferred_element_type=jnp.float32
    )
    partial_down = jnp.sum(every_adapter * selector_gathered.astype(jnp.float32)[:, :, None], 1)
    down_gathered = lax.psum(partial_down, "mp").astype(jnp.bfloat16)
    projection_result = apply_up_matrix(
        context_gathered, selector_gathered, down_gathered, output_weight, adapter_up_matrices
    )
    returned = lax.all_to_all(projection_result, "mp", split_axis=0, concat_axis=1, tiled=True)
    return (widened + returned.astype(jnp.float32)).astype(jnp.bfloat16)


def solution(mesh):
    in_specs = (
        P(("groups", "mp", "batch"), None),
        P(),
        P(None, ("mp", "batch")),
        P(None, "mp"),
        P(("groups", "mp", "batch"), None, None),
        P(("groups", "mp", "batch"), None, None),
        P(("groups", "mp", "batch")),
        P(("groups", "mp", "batch")),
        P(("groups", "mp", "batch"), None),
        P(None, "mp", None),
        P(None, None, "mp"),
    )
    out_specs = P(("groups", "mp", "batch"), None)
    return jax.shard_map(body, mesh=mesh, in_specs=in_specs, out_specs=out_specs, check_vma=False)
```

profile of v0, /device:TPU:0, one launch (start us, length us, event | category | flops | bytes accessed | tf_op | source)
XLA Modules:
  0.0 142.5 jit_solution(4894443476432670702)
XLA Ops:
  0.0 0.8 convert_element_type.67
  0.8 0.9 fusion.14
  1.8 0.9 fusion.25
  2.6 24.6 %all-gather = bf16[16,2,8192]{2,1,0:T(2,128)(2,1)S(1)} all-gather(bf16[1,2,8192]{2,1,0:T(2,128)(2,1)S(1)} %fusion.25), channel_id=1, replica_groups=mesh['groups'=2,'mp'=8,'batch'=2] {'mp','batch'}, dimensions={0}, use_global_device_ids=true | all-gather | bytes 557056 | tf_op jit(solution)/shard_map/all_gather | solution.py:61
  27.2 0.2 reshape.187
  27.4 5.8 %convolution_convert_fusion = bf16[32,640]{1,0:T(8,128)(2,1)S(1)} fusion(bf16[32,8192]{1,0:T(8,128)(2,1)S(1)} %reshape.187, bf16[8192,640]{1,0:T(8,128)(2,1)} %param.13), kind=kOutput, calls=%fused_computation.8 | convolution fusion | flops 335564800 | bytes 11051008 | tf_op jit(solution)/shard_map/dot_general | solution.py:60
  33.2 0.6 all_to_all.34
  33.8 3.3 %all-to-all-start = ((bf16[8,4,640]{2,1,0:T(4,128)(2,1)}), bf16[8,4,640]{2,1,0:T(4,128)(2,1)S(1)}, u32[]{:S(2)}, u32[]{:S(2)}) async-start(bf16[8,4,640]{2,1,0:T(4,128)(2,1)} %all_to_all.34), calls=%async_computation | async-start | bytes 81920 | tf_op jit(solution)/shard_map/all_to_all | solution.py:66
  37.3 0.2 fusion.33
  37.5 0.1 fusion.34
  37.6 20.8 %all-gather.2 = bf16[8,2,64]{2,1,0:T(2,128)(2,1)S(1)} all-gather(bf16[1,2,64]{2,1,0:T(2,128)(2,1)S(1)} %fusion.34), channel_id=1, replica_groups=mesh['groups'=2,'mp'=8,'batch'=2] {'mp'}, dimensions={0}, use_global_device_ids=true | all-gather | bytes 2304 | tf_op jit(solution)/shard_map/all_gather | solution.py:124
  58.4 0.1 copy.50
  58.4 0.1 copy.49
  58.5 0.1 multiply_cosine_fusion
  58.7 0.1 maximum_bitcast_fusion
  58.8 3.8 %all_to_all.45 = bf16[2,2,5120]{2,1,0:T(2,128)(2,1)S(1)} all-to-all(bf16[2,2,5120]{2,1,0:T(2,128)(2,1)S(1)} %all_to_all.37), channel_id=1, replica_groups=mesh['groups'=2,'mp'=8,'batch'=2] {'batch'}, dimensions={0} | all-to-all | bytes 81920 | tf_op jit(solution)/shard_map/all_to_all | solution.py:65
  62.7 0.1 slice_negate_fusion.1
  62.8 0.1 fusion.20
  62.9 0.1 fusion.31
  63.0 0.1 fusion.19
  63.1 0.1 fusion.28
  63.2 0.5 fusion.36
  63.7 0.2 fusion.13
  63.9 0.3 fusion.4
  64.2 30.8 %all-gather.1 = bf16[8,2,8192]{2,1,0:T(2,128)(2,1)S(1)} all-gather(bf16[1,2,8192]{2,1,0:T(2,128)(2,1)S(1)} %reshape.188), channel_id=1, replica_groups=mesh['groups'=2,'mp'=8,'batch'=2] {'mp'}, dimensions={0}, use_global_device_ids=true | all-gather | bytes 294912 | tf_op jit(solution)/shard_map/all_gather | solution.py:123
  95.0 0.1 reshape.189
  95.1 8.0 %fusion.37 = f32[16,1024]{1,0:T(8,128)S(1)} fusion(bf16[16,8192]{1,0:T(8,128)(2,1)S(1)} %reshape.189, bf16[8192,1024]{1,0:T(8,128)(2,1)} %param.14), kind=kOutput, calls=%fused_computation.71 | convolution fusion | flops 268435456 | bytes 17104896 | tf_op jit(solution)/shard_map/dot_general | solution.py:31
  103.1 6.8 %fusion = f32[16,64]{1,0:T(8,128)S(1)} fusion(bf16[64,1024,64]{1,2,0:T(8,128)(2,1)} %param.20, f32[16,64]{0,1:T(8,128)S(1)} %copy.50, bf16[16,8192]{1,0:T(8,128)(2,1)S(1)} %reshape.189, s32[]{:T(128)S(6)} %select_n.13), kind=kOutput, calls=%fused_computation.1 | convolution fusion | flops 134347776 | bytes 8458244 | tf_op jit(solution)/shard_map/gh,thy->gty/dot_general | solution.py:130
  109.9 17.4 %psum.7 = bf16[16,64]{1,0:T(8,128)(2,1)S(1)} all-reduce(f32[16,64]{1,0:T(8,128)S(1)} %fusion), channel_id=1, replica_groups=mesh['groups'=2,'mp'=8,'batch'=2] {'mp'}, use_global_device_ids=true, to_apply=%region_5.6 | all-reduce | flops 1024 | bytes 6144 | tf_op jit(solution)/shard_map/psum | solution.py:134
  127.3 4.8 %fusion.5 = bf16[16,1024]{1,0:T(8,128)(2,1)S(1)} fusion(f32[16,1024]{1,0:T(8,128)S(1)} %fusion.37, bf16[64,64,1024]{2,1,0:T(8,128)(2,1)} %param.21, bf16[16,64]{1,0:T(8,128)(2,1)S(1)} %psum.7, bf16[16,64]{0,1:T(8,128)(2,1)S(1)} %copy.49), kind=kOutput, calls=%fused_computation.10 | convolution fusion | flops 134332416 | bytes 8491008 | tf_op jit(solution)/shard_map/dot_general | solution.py:36
  132.1 9.8 %all_to_all.46 = bf16[8,2,1024]{2,1,0:T(2,128)(2,1)S(1)} all-to-all(bf16[8,2,1024]{2,1,0:T(2,128)(2,1)S(1)} %all_to_all.40), channel_id=1, replica_groups=mesh['groups'=2,'mp'=8,'batch'=2] {'mp'}, dimensions={0} | all-to-all | bytes 65536 | tf_op jit(solution)/shard_map/all_to_all | solution.py:138
  141.9 0.7 fusion.17
  (31 shorter events, 0.4 us)
Async XLA Ops:
  0.0 63.2 %copy-start = (bf16[2,256,1024]{2,1,0:T(8,128)(2,1)S(1)}, bf16[2,256,1024]{2,1,0:T(8,128)(2,1)}, u32[]{:S(2)}) copy-start(bf16[2,256,1024]{2,1,0:T(8,128)(2,1)} %param.15) | copy-start | bytes 3145732
  0.0 37.2 %copy-start.3 = (s32[2]{0:T(128)S(1)}, s32[2]{0:T(128)}, u32[]{:S(2)}) copy-start(s32[2]{0:T(128)} %param.17) | copy-start | bytes 28
  0.0 37.3 %copy-start.4 = (s32[1,2]{1,0:T(1,128)S(1)}, s32[1,2]{1,0:T(1,128)}, u32[]{:S(2)}) copy-start(s32[1,2]{1,0:T(1,128)} %param.19) | copy-start | bytes 28
  0.0 37.3 %copy-start.5 = (s32[2]{0:T(128)S(1)}, s32[2]{0:T(128)}, u32[]{:S(2)}) copy-start(s32[2]{0:T(128)} %param.18) | copy-start | bytes 28
  27.4 36.5 %copy-start.2 = (bf16[2,256,1024]{2,1,0:T(8,128)(2,1)S(1)}, bf16[2,256,1024]{2,1,0:T(8,128)(2,1)}, u32[]{:S(2)}) copy-start(bf16[2,256,1024]{2,1,0:T(8,128)(2,1)} %param.16) | copy-start | bytes 3145732
  33.8 24.9 %all-to-all-start = ((bf16[8,4,640]{2,1,0:T(4,128)(2,1)}), bf16[8,4,640]{2,1,0:T(4,128)(2,1)S(1)}, u32[]{:S(2)}, u32[]{:S(2)}) async-start(bf16[8,4,640]{2,1,0:T(4,128)(2,1)} %all_to_all.34), calls=%async_computation | async-start | bytes 81920 | tf_op jit(solution)/shard_map/all_to_all | solution.py:66
  109.9 32.0 %copy-start.1 = (bf16[2,8192]{1,0:T(2,128)(2,1)S(1)}, bf16[2,8192]{1,0:T(2,128)(2,1)}, u32[]{:S(2)}) copy-start(bf16[2,8192]{1,0:T(2,128)(2,1)} %param.11) | copy-start | bytes 98308
where the time goes:
time: 143 us
  blocking collectives  107 us (75%)
  matrix products  26.2 us (18%)
  other arithmetic  4.39 us (3%)
  starting transfers between devices  3.34 us (2%)
    all_gather x1, blocking collectives, body(): lax.all_gather(context_vector, 'mp', axis=0, tiled=True)  30.8 us
    all_gather x1, blocking collectives, body(): lax.all_gather(normed, ('mp', 'batch'), axis=0, tiled=True)  24.6 us
    all_gather x1, blocking collectives, body(): lax.all_gather(adapter_selector, 'mp', axis=0, tiled=True)  20.8 us
    psum x1, blocking collectives, body(): down_gathered = lax.psum(partial_down, 'mp').astype(jnp.bfloat16)  17.4 us
    all_to_all x1, blocking collectives, body(): lax.all_to_all(projection_result, 'mp', split_axis=0, concat_axis=1, tile...  9.77 us
    dot_general x1, matrix products, apply_up_matrix(): jnp.dot(context_vector, output_weight, preferred_element_type=jnp.float32)  8.04 us
    dot_general x1, matrix products, body(): jnp.einsum('gh,thy->gty', context_slice, adapter_down_matrices, preferred...  6.76 us
    dot_general x1, matrix products, body(): jnp.dot(lax.all_gather(normed, ('mp', 'batch'), axis=0, tiled=True), quer...  5.76 us
  transfers between devices with their start and end apart: 1, of which 0 were waited for; matrix products, arithmetic and copies ran while one was open for 1% of the time, Pallas kernels for 0%

commit v1 on v0

--- a/solution.py
+++ b/solution.py
@@ -37,7 +37,7 @@
     return (base_output + ADAPTER_SCALE * adapter_delta).astype(jnp.bfloat16)
 
 
-def body(
+def general_body(
     hidden,
     attention_norm_gain,
     query_key_value_weight,
@@ -139,6 +139,140 @@
     return (widened + returned.astype(jnp.float32)).astype(jnp.bfloat16)
 
 
+def fetch(block, axis, shift):
+    size = lax.axis_size(axis)
+    return lax.ppermute(block, axis, [((d + shift) % size, d) for d in range(size)])
+
+
+def gather_ahead(block, axis):
+    return [block] + [fetch(block, axis, k) for k in range(1, lax.axis_size(axis))]
+
+
+def swap_ahead(blocks, axis):
+    size = lax.axis_size(axis)
+    return [blocks[0]] + [fetch(blocks[k], axis, size - k) for k in range(1, size)]
+
+
+def absolute(blocks, axis, ahead):
+    size = lax.axis_size(axis)
+    if not ahead:
+        blocks = [blocks[-k % size] for k in range(size)]
+    twice = jnp.stack(blocks + blocks)
+    return lax.dynamic_slice_in_dim(twice, size - lax.axis_index(axis), size, 0)
+
+
+def fast_body(
+    hidden,
+    attention_norm_gain,
+    query_key_value_weight,
+    output_weight,
+    key_cache,
+    value_cache,
+    lengths,
+    slots,
+    requests,
+    adapter_down_matrices,
+    adapter_up_matrices,
+):
+    widened = hidden.astype(jnp.float32)
+    normed = (
+        widened
+        * lax.rsqrt(jnp.mean(widened * widened, -1, keepdims=True) + EPS)
+        * attention_norm_gain.astype(jnp.float32)
+    ).astype(jnp.bfloat16)
+    rows = normed.shape[0]
+    mp_size, batch_size = lax.axis_size("mp"), lax.axis_size("batch")
+    slot_hits = slots[:, None] == jnp.arange(requests.shape[1])[None, :]
+    adapter = jnp.sum(jnp.where(slot_hits, requests[0][None, :], 0), 1)
+    adapter_gathered = jnp.concatenate(gather_ahead(adapter, "mp"))
+    selector_gathered = (adapter_gathered[:, None] == jnp.arange(ADAPTER_COUNT)[None, :]).astype(
+        jnp.bfloat16
+    )
+    own_core = jnp.concatenate(gather_ahead(normed, "mp"))
+    normed_gathered = jnp.concatenate(gather_ahead(own_core, "batch"))
+    width = query_key_value_weight.shape[1]
+    columns = jnp.dot(
+        normed_gathered, query_key_value_weight, preferred_element_type=jnp.float32
+    ).astype(jnp.bfloat16)
+    columns = columns.reshape(batch_size, mp_size, rows, width)
+    cores = absolute(swap_ahead([columns[e] for e in range(batch_size)], "batch"), "batch", False)
+    mixed = absolute(swap_ahead([cores[:, k] for k in range(mp_size)], "mp"), "mp", False)
+    qkv = mixed.transpose(2, 0, 1, 3).reshape(rows, -1)
+    query_width = HEADS * HEAD_DIM
+    kv_width = KV_HEADS * HEAD_DIM
+    group = HEADS // KV_HEADS
+    scale = HEAD_DIM ** (-0.5)
+    pos = lengths.astype(jnp.float32)
+    query = rotate(
+        qkv[:, :query_width].astype(jnp.float32).reshape(rows, HEADS, HEAD_DIM), pos
+    ).astype(jnp.bfloat16)
+    fresh_key = rotate(
+        qkv[:, query_width : query_width + kv_width]
+        .astype(jnp.float32)
+        .reshape(rows, KV_HEADS, HEAD_DIM),
+        pos,
+    ).astype(jnp.bfloat16)
+    fresh_value = (
+        qkv[:, query_width + kv_width :].astype(jnp.float32).reshape(rows, KV_HEADS, HEAD_DIM)
+    )
+    grouped = query.reshape(rows, KV_HEADS, group, HEAD_DIM)
+    cached = key_cache.reshape(rows, -1, KV_HEADS, HEAD_DIM)
+    stored = value_cache.reshape(rows, -1, KV_HEADS, HEAD_DIM)
+    scores = (
+        jnp.einsum("rgqd,rtgd->rgqt", grouped, cached, preferred_element_type=jnp.float32) * scale
+    )
+    live = jnp.arange(cached.shape[1])[None, :] < lengths[:, None]
+    scores = jnp.where(live[:, None, None, :], scores, -jnp.inf)
+    own = (
+        jnp.einsum("rgqd,rgd->rgq", grouped, fresh_key, preferred_element_type=jnp.float32) * scale
+    )
+    top = jnp.maximum(jnp.max(scores, -1), own)
+    expo = jnp.exp(scores - top[..., None])
+    own_exp = jnp.exp(own - top)
+    total = jnp.sum(expo, -1) + own_exp
+    probs = (expo / total[..., None]).astype(jnp.bfloat16)
+    own_prob = (own_exp / total).astype(jnp.bfloat16)
+    context_vector = jnp.einsum(
+        "rgqt,rtgd->rgqd", probs, stored, preferred_element_type=jnp.float32
+    )
+    context_vector = (
+        context_vector + own_prob.astype(jnp.float32)[..., None] * fresh_value[:, :, None, :]
+    )
+    context_vector = context_vector.reshape(rows, query_width).astype(jnp.bfloat16)
+    context_gathered = jnp.concatenate(gather_ahead(context_vector, "mp"))
+    shared_portion = adapter_down_matrices.shape[1]
+    context_slice = lax.dynamic_slice_in_dim(
+        context_gathered, lax.axis_index("mp") * shared_portion, shared_portion, 1
+    )
+    every_adapter = jnp.einsum(
+        "gh,thy->gty", context_slice, adapter_down_matrices, preferred_element_type=jnp.float32
+    )
+    partial_down = jnp.sum(every_adapter * selector_gathered.astype(jnp.float32)[:, :, None], 1)
+    mine = absolute(list(partial_down.reshape(mp_size, rows, -1)), "mp", True)
+    total = sum(gather_ahead(mine, "mp"))
+    twice = jnp.concatenate([total, total])
+    down_gathered = (
+        lax.dynamic_slice_in_dim(twice, lax.axis_index("mp"), mp_size, 0)
+        .reshape(mp_size * rows, -1)
+        .astype(jnp.bfloat16)
+    )
+    projection_result = apply_up_matrix(
+        context_gathered, selector_gathered, down_gathered, output_weight, adapter_up_matrices
+    )
+    parts = swap_ahead(list(projection_result.reshape(mp_size, rows, -1)), "mp")
+    returned = absolute(parts, "mp", False).transpose(1, 0, 2).reshape(rows, -1)
+    return (widened + returned.astype(jnp.float32)).astype(jnp.bfloat16)
+
+
+MOST_PEERS = 16
+
+
+def body(*arguments):
+    few = lax.axis_size("mp") <= MOST_PEERS
+    whole_heads = arguments[2].shape[1] % HEAD_DIM == 0
+    return (fast_body if few and whole_heads else general_body)(*arguments)
+
+
 def solution(mesh):
     in_specs = (
         P(("groups", "mp", "batch"), None),

time: 143 us -> 123 us (0.86)
  blocking collectives: 107 us -> 0 us
  starting transfers between devices: 3.34 us -> 56.3 us
  waiting for transfers between devices: 0.01 us -> 32.3 us
  other arithmetic: 4.39 us -> 5.9 us
    all_gather x3 -> x0, blocking collectives: 76.1 us -> none  [the longest x1 30.8 us: body(): lax.all_gather(context_vector, 'mp', axis=0, tiled=True)]
    ppermute x0 -> x44, starting transfers between devices: none -> 56.3 us  [fetch(): lax.ppermute(block, axis, [((d + shift) % size, d) for d in range(size)])]
    ppermute x0 -> x44, waiting for transfers between devices: none -> 32.3 us  [fetch(): lax.ppermute(block, axis, [((d + shift) % size, d) for d in range(size)])]
    psum x1 -> x0, blocking collectives: 17.4 us -> none  [body(): down_gathered = lax.psum(partial_down, 'mp').astype(jnp.bfloat16)]
    all_to_all x2 -> x0, blocking collectives: 13.5 us -> none  [the longest x1 9.77 us: body(): lax.all_to_all(projection_result, 'mp', split_axis=0, concat_axis=1, tile...]
    all_to_all x1 -> x0, starting transfers between devices: 3.34 us -> none  [body(): lax.all_to_all(columns, 'mp', split_axis=0, concat_axis=1, tiled=True)]
    convert_element_type x7 -> x10, other arithmetic: 1.67 us -> 3.26 us  [the longest x1 0.86 us: fast_body(): normed = (widened * lax.rsqrt(jnp.mean(widened * widened, -1, keepdims=Tr...]
  transfers between devices with their start and end apart: 1 -> 44, of which waited for: 0 -> 17; matrix products, arithmetic and copies ran while one was open for 1% -> 2% of each run, Pallas kernels for 0% -> 0%
where the time goes in v1:
time: 123 us
  starting transfers between devices  56.3 us (46%)
  waiting for transfers between devices  32.3 us (26%)
  matrix products  26.2 us (21%)
  other arithmetic  5.9 us (5%)
  local copies, waits for them, and re-layouts  2.08 us (2%)
    ppermute x44, starting transfers between devices, fetch(): lax.ppermute(block, axis, [((d + shift) % size, d) for d in range(size)])  56.3 us
    ppermute x44, waiting for transfers between devices, fetch(): lax.ppermute(block, axis, [((d + shift) % size, d) for d in range(size)])  32.3 us
    dot_general x1, matrix products, apply_up_matrix(): jnp.dot(context_vector, output_weight, preferred_element_type=jnp.float32)  8.05 us
    dot_general x1, matrix products, fast_body(): jnp.einsum('gh,thy->gty', context_slice, adapter_down_matrices, preferred...  6.76 us
    dot_general x1, matrix products, fast_body(): jnp.dot(normed_gathered, query_key_value_weight, preferred_element_type=j...  5.75 us
    dot_general x1, matrix products, apply_up_matrix(): jnp.dot(spread, adapter_table, preferred_element_type=jnp.float32)  4.76 us
  transfers between devices with their start and end apart: 44, of which 17 were waited for; matrix products, arithmetic and copies ran while one was open for 2% of the time, Pallas kernels for 0%

profile of v1, /device:TPU:0, one launch (start us, length us, event | category | flops | bytes accessed | tf_op | source)
XLA Modules:
  0.0 123.2 jit_solution(16560882611888504678)
XLA Ops:
  2.6 6.0 %collective-permute-start = (bf16[2,8192]{1,0:T(2,128)(2,1)S(1)}, bf16[2,8192]{1,0:T(2,128)(2,1)S(1)}, u32[]{:S(2)}, u32[]{:S(2)}) collective-permute-start(bf16[2,8192]{1,0:T(2,128)(2,1)S(1)} %fusion.16), channel_id=1, source_target_pairs={{2,0},{4,2},{6,4},{8,6},{10,8},{12,10},{14,12},{0,14},{3,1},{5,3},... | collective-permute-start | bytes 98312 | tf_op jit(solution)/shard_map/ppermute | solution.py:144
  9.1 3.0 %collective-permute-start.3 = (bf16[2,8192]{1,0:T(2,128)(2,1)S(1)}, bf16[2,8192]{1,0:T(2,128)(2,1)S(1)}, u32[]{:S(2)}, u32[]{:S(2)}) collective-permute-start(bf16[2,8192]{1,0:T(2,128)(2,1)S(1)} %fusion.16), channel_id=1, source_target_pairs={{8,0},{10,2},{12,4},{14,6},{0,8},{2,10},{4,12},{6,14},{9,1},{11,3}... | collective-permute-start | bytes 98312 | tf_op jit(solution)/shard_map/ppermute | solution.py:144
  12.1 1.8 %collective-permute-start.5 = (bf16[2,8192]{1,0:T(2,128)(2,1)S(1)}, bf16[2,8192]{1,0:T(2,128)(2,1)S(1)}, u32[]{:S(2)}, u32[]{:S(2)}) collective-permute-start(bf16[2,8192]{1,0:T(2,128)(2,1)S(1)} %fusion.16), channel_id=1, source_target_pairs={{12,0},{14,2},{0,4},{2,6},{4,8},{6,10},{8,12},{10,14},{13,1},{15,3... | collective-permute-start | bytes 98312 | tf_op jit(solution)/shard_map/ppermute | solution.py:144
  15.8 2.3 %collective-permute-done.4 = bf16[2,8192]{1,0:T(2,128)(2,1)S(1)} collective-permute-done((bf16[2,8192]{1,0:T(2,128)(2,1)S(1)}, bf16[2,8192]{1,0:T(2,128)(2,1)S(1)}, u32[]{:S(2)}, u32[]{:S(2)}) %collective-permute-start.4) | collective-permute-done | bytes 32800 | tf_op jit(solution)/shard_map/ppermute | solution.py:144
  23.1 5.8 %convolution_convert_fusion = bf16[32,640]{1,0:T(8,128)(2,1)S(1)} fusion(bf16[32,8192]{1,0:T(8,128)(2,1)S(1)} %concatenate.36, bf16[8192,640]{1,0:T(8,128)(2,1)} %param.13), kind=kOutput, calls=%fused_computation.8 | convolution fusion | flops 335564800 | bytes 11051008 | tf_op jit(solution)/shard_map/dot_general | solution.py:194
  30.6 1.5 %collective-permute-start.10 = (bf16[2,2,640]{2,1,0:T(2,128)(2,1)S(1)}, bf16[2,2,640]{2,1,0:T(2,128)(2,1)S(1)}, u32[]{:S(2)}, u32[]{:S(2)}) collective-permute-start(bf16[2,2,640]{2,1,0:T(2,128)(2,1)S(1)} %get-tuple-element.12), channel_id=1, source_target_pairs={{4,0},{6,2},{8,4},{10,6},{12,8},{14,10},{0,12},{2,14},{5,1},{7,3},... | collective-permute-start | bytes 15368 | tf_op jit(solution)/shard_map/ppermute | solution.py:144
  32.1 1.5 %collective-permute-start.11 = (bf16[2,2,640]{2,1,0:T(2,128)(2,1)S(1)}, bf16[2,2,640]{2,1,0:T(2,128)(2,1)S(1)}, u32[]{:S(2)}, u32[]{:S(2)}) collective-permute-start(bf16[2,2,640]{2,1,0:T(2,128)(2,1)S(1)} %get-tuple-element.11), channel_id=1, source_target_pairs={{6,0},{8,2},{10,4},{12,6},{14,8},{0,10},{2,12},{4,14},{7,1},{9,3},... | collective-permute-start | bytes 15368 | tf_op jit(solution)/shard_map/ppermute | solution.py:144
  33.6 2.4 %collective-permute-start.12 = (bf16[2,2,640]{2,1,0:T(2,128)(2,1)S(1)}, bf16[2,2,640]{2,1,0:T(2,128)(2,1)S(1)}, u32[]{:S(2)}, u32[]{:S(2)}) collective-permute-start(bf16[2,2,640]{2,1,0:T(2,128)(2,1)S(1)} %get-tuple-element.10), channel_id=1, source_target_pairs={{8,0},{10,2},{12,4},{14,6},{0,8},{2,10},{4,12},{6,14},{9,1},{11,3}... | collective-permute-start | bytes 15368 | tf_op jit(solution)/shard_map/ppermute | solution.py:144
  36.0 2.0 %collective-permute-start.14 = (bf16[2,2,640]{2,1,0:T(2,128)(2,1)S(1)}, bf16[2,2,640]{2,1,0:T(2,128)(2,1)S(1)}, u32[]{:S(2)}, u32[]{:S(2)}) collective-permute-start(bf16[2,2,640]{2,1,0:T(2,128)(2,1)S(1)} %get-tuple-element.14), channel_id=1, source_target_pairs={{12,0},{14,2},{0,4},{2,6},{4,8},{6,10},{8,12},{10,14},{13,1},{15,3... | collective-permute-start | bytes 15368 | tf_op jit(solution)/shard_map/ppermute | solution.py:144
  38.0 2.0 %collective-permute-start.15 = (bf16[2,2,640]{2,1,0:T(2,128)(2,1)S(1)}, bf16[2,2,640]{2,1,0:T(2,128)(2,1)S(1)}, u32[]{:S(2)}, u32[]{:S(2)}) collective-permute-start(bf16[2,2,640]{2,1,0:T(2,128)(2,1)S(1)} %get-tuple-element.9), channel_id=1, source_target_pairs={{14,0},{0,2},{2,4},{4,6},{6,8},{8,10},{10,12},{12,14},{15,1},{1,3}... | collective-permute-start | bytes 15368 | tf_op jit(solution)/shard_map/ppermute | solution.py:144
  41.4 3.0 %collective-permute-done.15 = bf16[2,2,640]{2,1,0:T(2,128)(2,1)S(1)} collective-permute-done((bf16[2,2,640]{2,1,0:T(2,128)(2,1)S(1)}, bf16[2,2,640]{2,1,0:T(2,128)(2,1)S(1)}, u32[]{:S(2)}, u32[]{:S(2)}) %collective-permute-start.15) | collective-permute-done | bytes 5152 | tf_op jit(solution)/shard_map/ppermute | solution.py:144
  49.6 2.4 %collective-permute-start.25 = (s32[2]{0:T(128)S(1)}, s32[2]{0:T(128)S(1)}, u32[]{:S(2)}, u32[]{:S(2)}) collective-permute-start(s32[2]{0:T(128)S(1)} %fusion.40), channel_id=1, source_target_pairs={{6,0},{8,2},{10,4},{12,6},{14,8},{0,10},{2,12},{4,14},{7,1},{9,3},... | collective-permute-start | bytes 32 | tf_op jit(solution)/shard_map/ppermute | solution.py:144
  53.4 2.4 %collective-permute-start.27 = (s32[2]{0:T(128)S(1)}, s32[2]{0:T(128)S(1)}, u32[]{:S(2)}, u32[]{:S(2)}) collective-permute-start(s32[2]{0:T(128)S(1)} %fusion.40), channel_id=1, source_target_pairs={{10,0},{12,2},{14,4},{0,6},{2,8},{4,10},{6,12},{8,14},{11,1},{13,3... | collective-permute-start | bytes 32 | tf_op jit(solution)/shard_map/ppermute | solution.py:144
  55.8 1.5 %collective-permute-start.28 = (s32[2]{0:T(128)S(1)}, s32[2]{0:T(128)S(1)}, u32[]{:S(2)}, u32[]{:S(2)}) collective-permute-start(s32[2]{0:T(128)S(1)} %fusion.40), channel_id=1, source_target_pairs={{12,0},{14,2},{0,4},{2,6},{4,8},{6,10},{8,12},{10,14},{13,1},{15,3... | collective-permute-start | bytes 32 | tf_op jit(solution)/shard_map/ppermute | solution.py:144
  57.3 1.5 %collective-permute-start.29 = (s32[2]{0:T(128)S(1)}, s32[2]{0:T(128)S(1)}, u32[]{:S(2)}, u32[]{:S(2)}) collective-permute-start(s32[2]{0:T(128)S(1)} %fusion.40), channel_id=1, source_target_pairs={{14,0},{0,2},{2,4},{4,6},{6,8},{8,10},{10,12},{12,14},{15,1},{1,3}... | collective-permute-start | bytes 32 | tf_op jit(solution)/shard_map/ppermute | solution.py:144
  58.8 2.3 %collective-permute-done.28 = s32[2]{0:T(128)S(1)} collective-permute-done((s32[2]{0:T(128)S(1)}, s32[2]{0:T(128)S(1)}, u32[]{:S(2)}, u32[]{:S(2)}) %collective-permute-start.28) | collective-permute-done | bytes 40 | tf_op jit(solution)/shard_map/ppermute | solution.py:144
  61.1 2.4 %collective-permute-done.29 = s32[2]{0:T(128)S(1)} collective-permute-done((s32[2]{0:T(128)S(1)}, s32[2]{0:T(128)S(1)}, u32[]{:S(2)}, u32[]{:S(2)}) %collective-permute-start.29) | collective-permute-done | bytes 40 | tf_op jit(solution)/shard_map/ppermute | solution.py:144
  64.8 2.4 %collective-permute-start.20 = (bf16[2,8192]{1,0:T(2,128)(2,1)S(1)}, bf16[2,8192]{1,0:T(2,128)(2,1)S(1)}, u32[]{:S(2)}, u32[]{:S(2)}) collective-permute-start(bf16[2,8192]{1,0:T(2,128)(2,1)S(1)} %bitcast.219), channel_id=1, source_target_pairs={{10,0},{12,2},{14,4},{0,6},{2,8},{4,10},{6,12},{8,14},{11,1},{13,3... | collective-permute-start | bytes 98312 | tf_op jit(solution)/shard_map/ppermute | solution.py:144
  68.6 1.9 %collective-permute-done.20 = bf16[2,8192]{1,0:T(2,128)(2,1)S(1)} collective-permute-done((bf16[2,8192]{1,0:T(2,128)(2,1)S(1)}, bf16[2,8192]{1,0:T(2,128)(2,1)S(1)}, u32[]{:S(2)}, u32[]{:S(2)}) %collective-permute-start.20) | collective-permute-done | bytes 32800 | tf_op jit(solution)/shard_map/ppermute | solution.py:144
  70.5 2.4 %collective-permute-done.21 = bf16[2,8192]{1,0:T(2,128)(2,1)S(1)} collective-permute-done((bf16[2,8192]{1,0:T(2,128)(2,1)S(1)}, bf16[2,8192]{1,0:T(2,128)(2,1)S(1)}, u32[]{:S(2)}, u32[]{:S(2)}) %collective-permute-start.21) | collective-permute-done | bytes 32800 | tf_op jit(solution)/shard_map/ppermute | solution.py:144
  72.9 2.3 %collective-permute-done.22 = bf16[2,8192]{1,0:T(2,128)(2,1)S(1)} collective-permute-done((bf16[2,8192]{1,0:T(2,128)(2,1)S(1)}, bf16[2,8192]{1,0:T(2,128)(2,1)S(1)}, u32[]{:S(2)}, u32[]{:S(2)}) %collective-permute-start.22) | collective-permute-done | bytes 32800 | tf_op jit(solution)/shard_map/ppermute | solution.py:144
  75.5 6.8 %fusion = f32[16,64]{1,0:T(8,128)S(1)} fusion(bf16[64,1024,64]{1,2,0:T(8,128)(2,1)} %param.20, f32[16,64]{0,1:T(8,128)S(1)} %get-tuple-element.32, bf16[16,8192]{1,0:T(8,128)(2,1)S(1)} %concatenate.43, s32[]{:T(128)S(6)} %select_n.26), kind=kOutput, calls=%fused_computation.1 | convolution fusion | flops 134347776 | bytes 8458244 | tf_op jit(solution)/shard_map/gh,thy->gty/dot_general | solution.py:247
  83.3 1.9 %collective-permute-start.32 = (f32[8,2,64]{2,1,0:T(2,128)S(1)}, f32[8,2,64]{2,1,0:T(2,128)S(1)}, u32[]{:S(2)}, u32[]{:S(2)}) collective-permute-start(f32[8,2,64]{2,1,0:T(2,128)S(1)} %constant_dynamic-slice_fusion), channel_id=1, source_target_pairs={{6,0},{8,2},{10,4},{12,6},{14,8},{0,10},{2,12},{4,14},{7,1},{9,3},... | collective-permute-start | bytes 12296 | tf_op jit(solution)/shard_map/ppermute | solution.py:144
  85.2 2.4 %collective-permute-start.33 = (f32[8,2,64]{2,1,0:T(2,128)S(1)}, f32[8,2,64]{2,1,0:T(2,128)S(1)}, u32[]{:S(2)}, u32[]{:S(2)}) collective-permute-start(f32[8,2,64]{2,1,0:T(2,128)S(1)} %constant_dynamic-slice_fusion), channel_id=1, source_target_pairs={{8,0},{10,2},{12,4},{14,6},{0,8},{2,10},{4,12},{6,14},{9,1},{11,3}... | collective-permute-start | bytes 12296 | tf_op jit(solution)/shard_map/ppermute | solution.py:144
  90.5 2.6 %collective-permute-done.34 = f32[8,2,64]{2,1,0:T(2,128)S(1)} collective-permute-done((f32[8,2,64]{2,1,0:T(2,128)S(1)}, f32[8,2,64]{2,1,0:T(2,128)S(1)}, u32[]{:S(2)}, u32[]{:S(2)}) %collective-permute-start.34) | collective-permute-done | bytes 4128 | tf_op jit(solution)/shard_map/ppermute | solution.py:144
  93.1 2.3 %collective-permute-done.36 = f32[8,2,64]{2,1,0:T(2,128)S(1)} collective-permute-done((f32[8,2,64]{2,1,0:T(2,128)S(1)}, f32[8,2,64]{2,1,0:T(2,128)S(1)}, u32[]{:S(2)}, u32[]{:S(2)}) %collective-permute-start.36) | collective-permute-done | bytes 4128 | tf_op jit(solution)/shard_map/ppermute | solution.py:144
  95.4 4.8 %fusion.2 = f32[16,1024]{1,0:T(8,128)S(1)} fusion(bf16[64,64,1024]{2,1,0:T(8,128)(2,1)} %param.21, bf16[16,64]{1,0:T(8,128)(2,1)S(1)} %bitcast.223, bf16[16,64]{0,1:T(8,128)(2,1)S(1)} %get-tuple-element.31), kind=kOutput, calls=%fused_computation.5 | convolution fusion | flops 134299648 | bytes 8458240 | tf_op jit(solution)/shard_map/dot_general | solution.py:36
  100.2 8.1 %fusion.4 = bf16[16,1024]{1,0:T(8,128)(2,1)S(1)} fusion(f32[16,1024]{1,0:T(8,128)S(1)} %fusion.2, bf16[16,8192]{1,0:T(8,128)(2,1)S(1)} %concatenate.43, bf16[8192,1024]{1,0:T(8,128)(2,1)} %param.14), kind=kOutput, calls=%fused_computation.10 | convolution fusion | flops 268468224 | bytes 17137664 | tf_op jit(solution)/shard_map/dot_general | solution.py:31
  110.9 2.4 %collective-permute-start.40 = (bf16[2,1024]{1,0:T(2,128)(2,1)S(1)}, bf16[2,1024]{1,0:T(2,128)(2,1)S(1)}, u32[]{:S(2)}, u32[]{:S(2)}) collective-permute-start(bf16[2,1024]{1,0:T(2,128)(2,1)S(1)} %get-tuple-element.21), channel_id=1, source_target_pairs={{8,0},{10,2},{12,4},{14,6},{0,8},{2,10},{4,12},{6,14},{9,1},{11,3}... | collective-permute-start | bytes 12296 | tf_op jit(solution)/shard_map/ppermute | solution.py:144
  113.9 2.1 %collective-permute-start.42 = (bf16[2,1024]{1,0:T(2,128)(2,1)S(1)}, bf16[2,1024]{1,0:T(2,128)(2,1)S(1)}, u32[]{:S(2)}, u32[]{:S(2)}) collective-permute-start(bf16[2,1024]{1,0:T(2,128)(2,1)S(1)} %get-tuple-element.19), channel_id=1, source_target_pairs={{12,0},{14,2},{0,4},{2,6},{4,8},{6,10},{8,12},{10,14},{13,1},{15,3... | collective-permute-start | bytes 12296 | tf_op jit(solution)/shard_map/ppermute | solution.py:144
  117.0 1.8 %collective-permute-done.41 = bf16[2,1024]{1,0:T(2,128)(2,1)S(1)} collective-permute-done((bf16[2,1024]{1,0:T(2,128)(2,1)S(1)}, bf16[2,1024]{1,0:T(2,128)(2,1)S(1)}, u32[]{:S(2)}, u32[]{:S(2)}) %collective-permute-start.41) | collective-permute-done | bytes 4128 | tf_op jit(solution)/shard_map/ppermute | solution.py:144
  119.4 3.0 %collective-permute-done.43 = bf16[2,1024]{1,0:T(2,128)(2,1)S(1)} collective-permute-done((bf16[2,1024]{1,0:T(2,128)(2,1)S(1)}, bf16[2,1024]{1,0:T(2,128)(2,1)S(1)}, u32[]{:S(2)}, u32[]{:S(2)}) %collective-permute-start.43) | collective-permute-done | bytes 4128 | tf_op jit(solution)/shard_map/ppermute | solution.py:144
  (160 shorter events, 32.0 us)
Async XLA Ops:
  2.6 9.5 %collective-permute-start = (bf16[2,8192]{1,0:T(2,128)(2,1)S(1)}, bf16[2,8192]{1,0:T(2,128)(2,1)S(1)}, u32[]{:S(2)}, u32[]{:S(2)}) collective-permute-start(bf16[2,8192]{1,0:T(2,128)(2,1)S(1)} %fusion.16), channel_id=1, source_target_pairs={{2,0},{4,2},{6,4},{8,6},{10,8},{12,10},{14,12},{0,14},{3,1},{5,3},... | collective-permute-start | bytes 98312 | tf_op jit(solution)/shard_map/ppermute | solution.py:144
  9.1 6.7 %collective-permute-start.2 = (bf16[2,8192]{1,0:T(2,128)(2,1)S(1)}, bf16[2,8192]{1,0:T(2,128)(2,1)S(1)}, u32[]{:S(2)}, u32[]{:S(2)}) collective-permute-start(bf16[2,8192]{1,0:T(2,128)(2,1)S(1)} %fusion.16), channel_id=1, source_target_pairs={{6,0},{8,2},{10,4},{12,6},{14,8},{0,10},{2,12},{4,14},{7,1},{9,3},... | collective-permute-start | bytes 98312 | tf_op jit(solution)/shard_map/ppermute | solution.py:144
  9.1 6.7 %collective-permute-start.3 = (bf16[2,8192]{1,0:T(2,128)(2,1)S(1)}, bf16[2,8192]{1,0:T(2,128)(2,1)S(1)}, u32[]{:S(2)}, u32[]{:S(2)}) collective-permute-start(bf16[2,8192]{1,0:T(2,128)(2,1)S(1)} %fusion.16), channel_id=1, source_target_pairs={{8,0},{10,2},{12,4},{14,6},{0,8},{2,10},{4,12},{6,14},{9,1},{11,3}... | collective-permute-start | bytes 98312 | tf_op jit(solution)/shard_map/ppermute | solution.py:144
  12.1 6.0 %collective-permute-start.4 = (bf16[2,8192]{1,0:T(2,128)(2,1)S(1)}, bf16[2,8192]{1,0:T(2,128)(2,1)S(1)}, u32[]{:S(2)}, u32[]{:S(2)}) collective-permute-start(bf16[2,8192]{1,0:T(2,128)(2,1)S(1)} %fusion.16), channel_id=1, source_target_pairs={{10,0},{12,2},{14,4},{0,6},{2,8},{4,10},{6,12},{8,14},{11,1},{13,3... | collective-permute-start | bytes 98312 | tf_op jit(solution)/shard_map/ppermute | solution.py:144
  12.1 7.0 %collective-permute-start.5 = (bf16[2,8192]{1,0:T(2,128)(2,1)S(1)}, bf16[2,8192]{1,0:T(2,128)(2,1)S(1)}, u32[]{:S(2)}, u32[]{:S(2)}) collective-permute-start(bf16[2,8192]{1,0:T(2,128)(2,1)S(1)} %fusion.16), channel_id=1, source_target_pairs={{12,0},{14,2},{0,4},{2,6},{4,8},{6,10},{8,12},{10,14},{13,1},{15,3... | collective-permute-start | bytes 98312 | tf_op jit(solution)/shard_map/ppermute | solution.py:144
  14.0 6.6 %collective-permute-start.6 = (bf16[2,8192]{1,0:T(2,128)(2,1)S(1)}, bf16[2,8192]{1,0:T(2,128)(2,1)S(1)}, u32[]{:S(2)}, u32[]{:S(2)}) collective-permute-start(bf16[2,8192]{1,0:T(2,128)(2,1)S(1)} %fusion.16), channel_id=1, source_target_pairs={{14,0},{0,2},{2,4},{4,6},{6,8},{8,10},{10,12},{12,14},{15,1},{1,3}... | collective-permute-start | bytes 98312 | tf_op jit(solution)/shard_map/ppermute | solution.py:144
  30.3 5.6 %collective-permute-start.9 = (bf16[2,2,640]{2,1,0:T(2,128)(2,1)S(1)}, bf16[2,2,640]{2,1,0:T(2,128)(2,1)S(1)}, u32[]{:S(2)}, u32[]{:S(2)}) collective-permute-start(bf16[2,2,640]{2,1,0:T(2,128)(2,1)S(1)} %get-tuple-element.13), channel_id=1, source_target_pairs={{2,0},{4,2},{6,4},{8,6},{10,8},{12,10},{14,12},{0,14},{3,1},{5,3},... | collective-permute-start | bytes 15368 | tf_op jit(solution)/shard_map/ppermute | solution.py:144
  30.6 7.4 %collective-permute-start.10 = (bf16[2,2,640]{2,1,0:T(2,128)(2,1)S(1)}, bf16[2,2,640]{2,1,0:T(2,128)(2,1)S(1)}, u32[]{:S(2)}, u32[]{:S(2)}) collective-permute-start(bf16[2,2,640]{2,1,0:T(2,128)(2,1)S(1)} %get-tuple-element.12), channel_id=1, source_target_pairs={{4,0},{6,2},{8,4},{10,6},{12,8},{14,10},{0,12},{2,14},{5,1},{7,3},... | collective-permute-start | bytes 15368 | tf_op jit(solution)/shard_map/ppermute | solution.py:144
  32.1 8.0 %collective-permute-start.11 = (bf16[2,2,640]{2,1,0:T(2,128)(2,1)S(1)}, bf16[2,2,640]{2,1,0:T(2,128)(2,1)S(1)}, u32[]{:S(2)}, u32[]{:S(2)}) collective-permute-start(bf16[2,2,640]{2,1,0:T(2,128)(2,1)S(1)} %get-tuple-element.11), channel_id=1, source_target_pairs={{6,0},{8,2},{10,4},{12,6},{14,8},{0,10},{2,12},{4,14},{7,1},{9,3},... | collective-permute-start | bytes 15368 | tf_op jit(solution)/shard_map/ppermute | solution.py:144
  33.6 6.5 %collective-permute-start.12 = (bf16[2,2,640]{2,1,0:T(2,128)(2,1)S(1)}, bf16[2,2,640]{2,1,0:T(2,128)(2,1)S(1)}, u32[]{:S(2)}, u32[]{:S(2)}) collective-permute-start(bf16[2,2,640]{2,1,0:T(2,128)(2,1)S(1)} %get-tuple-element.10), channel_id=1, source_target_pairs={{8,0},{10,2},{12,4},{14,6},{0,8},{2,10},{4,12},{6,14},{9,1},{11,3}... | collective-permute-start | bytes 15368 | tf_op jit(solution)/shard_map/ppermute | solution.py:144
  36.0 5.4 %collective-permute-start.13 = (bf16[2,2,640]{2,1,0:T(2,128)(2,1)S(1)}, bf16[2,2,640]{2,1,0:T(2,128)(2,1)S(1)}, u32[]{:S(2)}, u32[]{:S(2)}) collective-permute-start(bf16[2,2,640]{2,1,0:T(2,128)(2,1)S(1)} %get-tuple-element.15), channel_id=1, source_target_pairs={{10,0},{12,2},{14,4},{0,6},{2,8},{4,10},{6,12},{8,14},{11,1},{13,3... | collective-permute-start | bytes 15368 | tf_op jit(solution)/shard_map/ppermute | solution.py:144
  36.0 5.4 %collective-permute-start.14 = (bf16[2,2,640]{2,1,0:T(2,128)(2,1)S(1)}, bf16[2,2,640]{2,1,0:T(2,128)(2,1)S(1)}, u32[]{:S(2)}, u32[]{:S(2)}) collective-permute-start(bf16[2,2,640]{2,1,0:T(2,128)(2,1)S(1)} %get-tuple-element.14), channel_id=1, source_target_pairs={{12,0},{14,2},{0,4},{2,6},{4,8},{6,10},{8,12},{10,14},{13,1},{15,3... | collective-permute-start | bytes 15368 | tf_op jit(solution)/shard_map/ppermute | solution.py:144
  38.0 6.4 %collective-permute-start.15 = (bf16[2,2,640]{2,1,0:T(2,128)(2,1)S(1)}, bf16[2,2,640]{2,1,0:T(2,128)(2,1)S(1)}, u32[]{:S(2)}, u32[]{:S(2)}) collective-permute-start(bf16[2,2,640]{2,1,0:T(2,128)(2,1)S(1)} %get-tuple-element.9), channel_id=1, source_target_pairs={{14,0},{0,2},{2,4},{4,6},{6,8},{8,10},{10,12},{12,14},{15,1},{1,3}... | collective-permute-start | bytes 15368 | tf_op jit(solution)/shard_map/ppermute | solution.py:144
  46.2 21.0 %collective-permute-start.16 = (bf16[2,8192]{1,0:T(2,128)(2,1)S(1)}, bf16[2,8192]{1,0:T(2,128)(2,1)S(1)}, u32[]{:S(2)}, u32[]{:S(2)}) collective-permute-start(bf16[2,8192]{1,0:T(2,128)(2,1)S(1)} %bitcast.215), channel_id=1, source_target_pairs={{2,0},{4,2},{6,4},{8,6},{10,8},{12,10},{14,12},{0,14},{3,1},{5,3},... | collective-permute-start | bytes 98312 | tf_op jit(solution)/shard_map/ppermute | solution.py:144
  46.8 21.8 %collective-permute-start.17 = (bf16[2,8192]{1,0:T(2,128)(2,1)S(1)}, bf16[2,8192]{1,0:T(2,128)(2,1)S(1)}, u32[]{:S(2)}, u32[]{:S(2)}) collective-permute-start(bf16[2,8192]{1,0:T(2,128)(2,1)S(1)} %bitcast.216), channel_id=1, source_target_pairs={{4,0},{6,2},{8,4},{10,6},{12,8},{14,10},{0,12},{2,14},{5,1},{7,3},... | collective-permute-start | bytes 98312 | tf_op jit(solution)/shard_map/ppermute | solution.py:144
  49.6 6.2 %collective-permute-start.25 = (s32[2]{0:T(128)S(1)}, s32[2]{0:T(128)S(1)}, u32[]{:S(2)}, u32[]{:S(2)}) collective-permute-start(s32[2]{0:T(128)S(1)} %fusion.40), channel_id=1, source_target_pairs={{6,0},{8,2},{10,4},{12,6},{14,8},{0,10},{2,12},{4,14},{7,1},{9,3},... | collective-permute-start | bytes 32 | tf_op jit(solution)/shard_map/ppermute | solution.py:144
  57.3 6.2 %collective-permute-start.29 = (s32[2]{0:T(128)S(1)}, s32[2]{0:T(128)S(1)}, u32[]{:S(2)}, u32[]{:S(2)}) collective-permute-start(s32[2]{0:T(128)S(1)} %fusion.40), channel_id=1, source_target_pairs={{14,0},{0,2},{2,4},{4,6},{6,8},{8,10},{10,12},{12,14},{15,1},{1,3}... | collective-permute-start | bytes 32 | tf_op jit(solution)/shard_map/ppermute | solution.py:144
  64.8 5.7 %collective-permute-start.20 = (bf16[2,8192]{1,0:T(2,128)(2,1)S(1)}, bf16[2,8192]{1,0:T(2,128)(2,1)S(1)}, u32[]{:S(2)}, u32[]{:S(2)}) collective-permute-start(bf16[2,8192]{1,0:T(2,128)(2,1)S(1)} %bitcast.219), channel_id=1, source_target_pairs={{10,0},{12,2},{14,4},{0,6},{2,8},{4,10},{6,12},{8,14},{11,1},{13,3... | collective-permute-start | bytes 98312 | tf_op jit(solution)/shard_map/ppermute | solution.py:144
  67.2 5.7 %collective-permute-start.21 = (bf16[2,8192]{1,0:T(2,128)(2,1)S(1)}, bf16[2,8192]{1,0:T(2,128)(2,1)S(1)}, u32[]{:S(2)}, u32[]{:S(2)}) collective-permute-start(bf16[2,8192]{1,0:T(2,128)(2,1)S(1)} %bitcast.220), channel_id=1, source_target_pairs={{12,0},{14,2},{0,4},{2,6},{4,8},{6,10},{8,12},{10,14},{13,1},{15,3... | collective-permute-start | bytes 98312 | tf_op jit(solution)/shard_map/ppermute | solution.py:144
  68.6 6.6 %collective-permute-start.22 = (bf16[2,8192]{1,0:T(2,128)(2,1)S(1)}, bf16[2,8192]{1,0:T(2,128)(2,1)S(1)}, u32[]{:S(2)}, u32[]{:S(2)}) collective-permute-start(bf16[2,8192]{1,0:T(2,128)(2,1)S(1)} %bitcast.221), channel_id=1, source_target_pairs={{14,0},{0,2},{2,4},{4,6},{6,8},{8,10},{10,12},{12,14},{15,1},{1,3}... | collective-permute-start | bytes 98312 | tf_op jit(solution)/shard_map/ppermute | solution.py:144
  82.7 6.3 %collective-permute-start.31 = (f32[8,2,64]{2,1,0:T(2,128)S(1)}, f32[8,2,64]{2,1,0:T(2,128)S(1)}, u32[]{:S(2)}, u32[]{:S(2)}) collective-permute-start(f32[8,2,64]{2,1,0:T(2,128)S(1)} %constant_dynamic-slice_fusion), channel_id=1, source_target_pairs={{4,0},{6,2},{8,4},{10,6},{12,8},{14,10},{0,12},{2,14},{5,1},{7,3},... | collective-permute-start | bytes 12296 | tf_op jit(solution)/shard_map/ppermute | solution.py:144
  83.3 7.2 %collective-permute-start.32 = (f32[8,2,64]{2,1,0:T(2,128)S(1)}, f32[8,2,64]{2,1,0:T(2,128)S(1)}, u32[]{:S(2)}, u32[]{:S(2)}) collective-permute-start(f32[8,2,64]{2,1,0:T(2,128)S(1)} %constant_dynamic-slice_fusion), channel_id=1, source_target_pairs={{6,0},{8,2},{10,4},{12,6},{14,8},{0,10},{2,12},{4,14},{7,1},{9,3},... | collective-permute-start | bytes 12296 | tf_op jit(solution)/shard_map/ppermute | solution.py:144
  87.6 5.4 %collective-permute-start.34 = (f32[8,2,64]{2,1,0:T(2,128)S(1)}, f32[8,2,64]{2,1,0:T(2,128)S(1)}, u32[]{:S(2)}, u32[]{:S(2)}) collective-permute-start(f32[8,2,64]{2,1,0:T(2,128)S(1)} %constant_dynamic-slice_fusion), channel_id=1, source_target_pairs={{10,0},{12,2},{14,4},{0,6},{2,8},{4,10},{6,12},{8,14},{11,1},{13,3... | collective-permute-start | bytes 12296 | tf_op jit(solution)/shard_map/ppermute | solution.py:144
  87.6 5.5 %collective-permute-start.35 = (f32[8,2,64]{2,1,0:T(2,128)S(1)}, f32[8,2,64]{2,1,0:T(2,128)S(1)}, u32[]{:S(2)}, u32[]{:S(2)}) collective-permute-start(f32[8,2,64]{2,1,0:T(2,128)S(1)} %constant_dynamic-slice_fusion), channel_id=1, source_target_pairs={{12,0},{14,2},{0,4},{2,6},{4,8},{6,10},{8,12},{10,14},{13,1},{15,3... | collective-permute-start | bytes 12296 | tf_op jit(solution)/shard_map/ppermute | solution.py:144
  89.0 6.3 %collective-permute-start.36 = (f32[8,2,64]{2,1,0:T(2,128)S(1)}, f32[8,2,64]{2,1,0:T(2,128)S(1)}, u32[]{:S(2)}, u32[]{:S(2)}) collective-permute-start(f32[8,2,64]{2,1,0:T(2,128)S(1)} %constant_dynamic-slice_fusion), channel_id=1, source_target_pairs={{14,0},{0,2},{2,4},{4,6},{6,8},{8,10},{10,12},{12,14},{15,1},{1,3}... | collective-permute-start | bytes 12296 | tf_op jit(solution)/shard_map/ppermute | solution.py:144
  108.3 5.6 %collective-permute-start.37 = (bf16[2,1024]{1,0:T(2,128)(2,1)S(1)}, bf16[2,1024]{1,0:T(2,128)(2,1)S(1)}, u32[]{:S(2)}, u32[]{:S(2)}) collective-permute-start(bf16[2,1024]{1,0:T(2,128)(2,1)S(1)} %get-tuple-element.24), channel_id=1, source_target_pairs={{2,0},{4,2},{6,4},{8,6},{10,8},{12,10},{14,12},{0,14},{3,1},{5,3},... | collective-permute-start | bytes 12296 | tf_op jit(solution)/shard_map/ppermute | solution.py:144
  109.5 6.5 %collective-permute-start.38 = (bf16[2,1024]{1,0:T(2,128)(2,1)S(1)}, bf16[2,1024]{1,0:T(2,128)(2,1)S(1)}, u32[]{:S(2)}, u32[]{:S(2)}) collective-permute-start(bf16[2,1024]{1,0:T(2,128)(2,1)S(1)} %get-tuple-element.23), channel_id=1, source_target_pairs={{4,0},{6,2},{8,4},{10,6},{12,8},{14,10},{0,12},{2,14},{5,1},{7,3},... | collective-permute-start | bytes 12296 | tf_op jit(solution)/shard_map/ppermute | solution.py:144
  110.9 6.0 %collective-permute-start.39 = (bf16[2,1024]{1,0:T(2,128)(2,1)S(1)}, bf16[2,1024]{1,0:T(2,128)(2,1)S(1)}, u32[]{:S(2)}, u32[]{:S(2)}) collective-permute-start(bf16[2,1024]{1,0:T(2,128)(2,1)S(1)} %get-tuple-element.22), channel_id=1, source_target_pairs={{6,0},{8,2},{10,4},{12,6},{14,8},{0,10},{2,12},{4,14},{7,1},{9,3},... | collective-permute-start | bytes 12296 | tf_op jit(solution)/shard_map/ppermute | solution.py:144
  110.9 6.0 %collective-permute-start.40 = (bf16[2,1024]{1,0:T(2,128)(2,1)S(1)}, bf16[2,1024]{1,0:T(2,128)(2,1)S(1)}, u32[]{:S(2)}, u32[]{:S(2)}) collective-permute-start(bf16[2,1024]{1,0:T(2,128)(2,1)S(1)} %get-tuple-element.21), channel_id=1, source_target_pairs={{8,0},{10,2},{12,4},{14,6},{0,8},{2,10},{4,12},{6,14},{9,1},{11,3}... | collective-permute-start | bytes 12296 | tf_op jit(solution)/shard_map/ppermute | solution.py:144
  113.4 5.4 %collective-permute-start.41 = (bf16[2,1024]{1,0:T(2,128)(2,1)S(1)}, bf16[2,1024]{1,0:T(2,128)(2,1)S(1)}, u32[]{:S(2)}, u32[]{:S(2)}) collective-permute-start(bf16[2,1024]{1,0:T(2,128)(2,1)S(1)} %get-tuple-element.20), channel_id=1, source_target_pairs={{10,0},{12,2},{14,4},{0,6},{2,8},{4,10},{6,12},{8,14},{11,1},{13,3... | collective-permute-start | bytes 12296 | tf_op jit(solution)/shard_map/ppermute | solution.py:144
  113.9 5.4 %collective-permute-start.42 = (bf16[2,1024]{1,0:T(2,128)(2,1)S(1)}, bf16[2,1024]{1,0:T(2,128)(2,1)S(1)}, u32[]{:S(2)}, u32[]{:S(2)}) collective-permute-start(bf16[2,1024]{1,0:T(2,128)(2,1)S(1)} %get-tuple-element.19), channel_id=1, source_target_pairs={{12,0},{14,2},{0,4},{2,6},{4,8},{6,10},{8,12},{10,14},{13,1},{15,3... | collective-permute-start | bytes 12296 | tf_op jit(solution)/shard_map/ppermute | solution.py:144
  116.0 6.4 %collective-permute-start.43 = (bf16[2,1024]{1,0:T(2,128)(2,1)S(1)}, bf16[2,1024]{1,0:T(2,128)(2,1)S(1)}, u32[]{:S(2)}, u32[]{:S(2)}) collective-permute-start(bf16[2,1024]{1,0:T(2,128)(2,1)S(1)} %get-tuple-element.18), channel_id=1, source_target_pairs={{14,0},{0,2},{2,4},{4,6},{6,8},{8,10},{10,12},{12,14},{15,1},{1,3}... | collective-permute-start | bytes 12296 | tf_op jit(solution)/shard_map/ppermute | solution.py:144
  (17 other events, 192.4 us)

commit v2 on v1

--- a/solution.py
+++ b/solution.py
@@ -139,26 +139,52 @@
     return (widened + returned.astype(jnp.float32)).astype(jnp.bfloat16)
 
 
-def fetch(block, axis, shift):
+def trade(block, axis, bit):
+    return lax.ppermute(block, axis, [(d ^ bit, d) for d in range(lax.axis_size(axis))])
+
+
+def bits_of(axis):
     size = lax.axis_size(axis)
-    return lax.ppermute(block, axis, [((d + shift) % size, d) for d in range(size)])
-
-
-def gather_ahead(block, axis):
-    return [block] + [fetch(block, axis, k) for k in range(1, lax.axis_size(axis))]
-
-
-def swap_ahead(blocks, axis):
-    size = lax.axis_size(axis)
-    return [blocks[0]] + [fetch(blocks[k], axis, size - k) for k in range(1, size)]
-
-
-def absolute(blocks, axis, ahead):
-    size = lax.axis_size(axis)
-    if not ahead:
-        blocks = [blocks[-k % size] for k in range(size)]
-    twice = jnp.stack(blocks + blocks)
-    return lax.dynamic_slice_in_dim(twice, size - lax.axis_index(axis), size, 0)
+    return [1 << b for b in reversed(range(size.bit_length() - 1))]
+
+
+def gather_near(block, axis):
+    held = block[None]
+    for bit in reversed(bits_of(axis)):
+        held = jnp.concatenate([held, trade(held, axis, bit)])
+    return held
+
+
+def gather_far(block, axis):
+    held = block[None]
+    for bit in bits_of(axis):
+        held = jnp.stack([held, trade(held, axis, bit)], 1)
+        held = held.reshape(-1, *block.shape)
+    return held
+
+
+def exchange(blocks, axis):
+    size, shape = lax.axis_size(axis), blocks.shape[1:]
+    for bit in bits_of(axis):
+        split = blocks.reshape(size // (2 * bit), 2, bit, *shape)
+        got = trade(split[:, 1], axis, bit)
+        blocks = jnp.stack([split[:, 0], got], 1).reshape(size, *shape)
+    return blocks
+
+
+def absolute(blocks, axis):
+    size, shape = lax.axis_size(axis), blocks.shape[1:]
+    index = lax.axis_index(axis)
+    for bit in bits_of(axis):
+        split = blocks.reshape(size // (2 * bit), 2, bit, *shape)
+        blocks = jnp.where((index & bit) > 0, split[:, ::-1], split).reshape(size, *shape)
+    return blocks
+
+
+def sum_all(block, axis):
+    for bit in bits_of(axis):
+        block = block + trade(block, axis, bit)
+    return block
 
 
 def fast_body(
@@ -184,19 +210,19 @@
     mp_size, batch_size = lax.axis_size("mp"), lax.axis_size("batch")
     slot_hits = slots[:, None] == jnp.arange(requests.shape[1])[None, :]
     adapter = jnp.sum(jnp.where(slot_hits, requests[0][None, :], 0), 1)
-    adapter_gathered = jnp.concatenate(gather_ahead(adapter, "mp"))
+    adapter_gathered = gather_far(adapter, "mp").reshape(-1)
     selector_gathered = (adapter_gathered[:, None] == jnp.arange(ADAPTER_COUNT)[None, :]).astype(
         jnp.bfloat16
     )
-    own_core = jnp.concatenate(gather_ahead(normed, "mp"))
-    normed_gathered = jnp.concatenate(gather_ahead(own_core, "batch"))
+    own_core = gather_far(normed, "mp")
+    normed_gathered = gather_near(own_core, "batch").reshape(-1, normed.shape[1])
     width = query_key_value_weight.shape[1]
     columns = jnp.dot(
         normed_gathered, query_key_value_weight, preferred_element_type=jnp.float32
     ).astype(jnp.bfloat16)
     columns = columns.reshape(batch_size, mp_size, rows, width)
-    cores = absolute(swap_ahead([columns[e] for e in range(batch_size)], "batch"), "batch", False)
-    mixed = absolute(swap_ahead([cores[:, k] for k in range(mp_size)], "mp"), "mp", False)
+    cores = absolute(exchange(columns, "batch"), "batch")
+    mixed = absolute(exchange(cores.transpose(1, 0, 2, 3), "mp"), "mp")
     qkv = mixed.transpose(2, 0, 1, 3).reshape(rows, -1)
     query_width = HEADS * HEAD_DIM
     kv_width = KV_HEADS * HEAD_DIM
@@ -239,7 +265,7 @@
         context_vector + own_prob.astype(jnp.float32)[..., None] * fresh_value[:, :, None, :]
     )
     context_vector = context_vector.reshape(rows, query_width).astype(jnp.bfloat16)
-    context_gathered = jnp.concatenate(gather_ahead(context_vector, "mp"))
+    context_gathered = gather_far(context_vector, "mp").reshape(-1, query_width)
     shared_portion = adapter_down_matrices.shape[1]
     context_slice = lax.dynamic_slice_in_dim(
         context_gathered, lax.axis_index("mp") * shared_portion, shared_portion, 1
@@ -248,29 +274,22 @@
         "gh,thy->gty", context_slice, adapter_down_matrices, preferred_element_type=jnp.float32
     )
     partial_down = jnp.sum(every_adapter * selector_gathered.astype(jnp.float32)[:, :, None], 1)
-    mine = absolute(list(partial_down.reshape(mp_size, rows, -1)), "mp", True)
-    total = sum(gather_ahead(mine, "mp"))
-    twice = jnp.concatenate([total, total])
-    down_gathered = (
-        lax.dynamic_slice_in_dim(twice, lax.axis_index("mp"), mp_size, 0)
-        .reshape(mp_size * rows, -1)
-        .astype(jnp.bfloat16)
-    )
+    mine = absolute(partial_down.reshape(mp_size, rows, -1), "mp")
+    total = absolute(sum_all(mine, "mp"), "mp")
+    down_gathered = total.reshape(mp_size * rows, -1).astype(jnp.bfloat16)
     projection_result = apply_up_matrix(
         context_gathered, selector_gathered, down_gathered, output_weight, adapter_up_matrices
     )
-    parts = swap_ahead(list(projection_result.reshape(mp_size, rows, -1)), "mp")
-    returned = absolute(parts, "mp", False).transpose(1, 0, 2).reshape(rows, -1)
+    parts = exchange(projection_result.reshape(mp_size, rows, -1), "mp")
+    returned = absolute(parts, "mp").transpose(1, 0, 2).reshape(rows, -1)
     return (widened + returned.astype(jnp.float32)).astype(jnp.bfloat16)
 
 
-MOST_PEERS = 16
-
-
 def body(*arguments):
-    few = lax.axis_size("mp") <= MOST_PEERS
+    size = lax.axis_size("mp")
+    small = size <= 16 and size & (size - 1) == 0 and lax.axis_size("batch") == 2
     whole_heads = arguments[2].shape[1] % HEAD_DIM == 0
-    return (fast_body if few and whole_heads else general_body)(*arguments)
+    return (fast_body if small and whole_heads else general_body)(*arguments)
 
 
 def solution(mesh):

time: 123 us -> 103 us (0.84)
  starting transfers between devices: 56.3 us -> 28.1 us
  waiting for transfers between devices: 32.3 us -> 38.7 us
  other arithmetic: 5.9 us -> 9.25 us
  matrix products: 26.2 us -> 23.6 us
    ppermute x44 -> x20, starting transfers between devices: 56.3 us -> 28.1 us  [trade(): lax.ppermute(block, axis, [(d ^ bit, d) for d in range(lax.axis_size(axis...]
    ppermute x44 -> x20, waiting for transfers between devices: 32.3 us -> 38.7 us  [trade(): lax.ppermute(block, axis, [(d ^ bit, d) for d in range(lax.axis_size(axis...]
    dot_general x1, matrix products: 4.76 us -> 1.38 us  [apply_up_matrix(): jnp.dot(spread, adapter_table, preferred_element_type=jnp.float32)]
    another operation x1 -> x15, other arithmetic: 0.18 us -> 2.46 us  [the longest x10 2.19 us: gather_far(): held = jnp.stack([held, trade(held, axis, bit)], 1)]
    concatenate x4 -> x0, local copies, waits for them, and re-layouts: 1.32 us -> none  [the longest x1 0.47 us: fast_body(): normed_gathered = jnp.concatenate(gather_ahead(own_core, 'batch'))]
  transfers between devices with their start and end apart: 44 -> 20, of which waited for: 17 -> 15; matrix products, arithmetic and copies ran while one was open for 2% -> 20% of each run, Pallas kernels for 0% -> 0%
where the time goes in v2:
time: 103 us; the launch traced here: 102 us
  waiting for transfers between devices  38.7 us (38%)
  starting transfers between devices  28.1 us (27%)
  matrix products  23.6 us (23%)
  other arithmetic  9.25 us (9%)
  local copies, waits for them, and re-layouts  2.12 us (2%)
    ppermute x20, waiting for transfers between devices, trade(): lax.ppermute(block, axis, [(d ^ bit, d) for d in range(lax.axis_size(axis...  38.7 us
    ppermute x20, starting transfers between devices, trade(): lax.ppermute(block, axis, [(d ^ bit, d) for d in range(lax.axis_size(axis...  28.1 us
    dot_general x1, matrix products, apply_up_matrix(): jnp.dot(context_vector, output_weight, preferred_element_type=jnp.float32)  8.75 us
    dot_general x1, matrix products, fast_body(): jnp.einsum('gh,thy->gty', context_slice, adapter_down_matrices, preferred...  6.76 us
    dot_general x1, matrix products, fast_body(): jnp.dot(normed_gathered, query_key_value_weight, preferred_element_type=j...  5.76 us
    another operation x10, other arithmetic, gather_far(): held = jnp.stack([held, trade(held, axis, bit)], 1)  2.19 us
  transfers between devices with their start and end apart: 20, of which 15 were waited for; matrix products, arithmetic and copies ran while one was open for 20% of the time, Pallas kernels for 0%

profile of v2, /device:TPU:0, one launch (start us, length us, event | category | flops | bytes accessed | tf_op | source)
XLA Modules:
  0.0 102.3 jit_solution(2724816203226268826)
XLA Ops:
  0.8 0.9 fusion.14
  1.8 0.9 fusion.64
  2.6 4.1 %collective-permute-start = (bf16[1,2,8192]{2,1,0:T(2,128)(2,1)S(1)}, bf16[1,2,8192]{2,1,0:T(2,128)(2,1)S(1)}, u32[]{:S(2)}, u32[]{:S(2)}) collective-permute-start(bf16[1,2,8192]{2,1,0:T(2,128)(2,1)S(1)} %fusion.64), channel_id=1, source_target_pairs={{8,0},{10,2},{12,4},{14,6},{0,8},{2,10},{4,12},{6,14},{9,1},{11,3}... | collective-permute-start | bytes 98312 | tf_op jit(solution)/shard_map/ppermute | solution.py:143
  7.6 1.4 %collective-permute-done = bf16[1,2,8192]{2,1,0:T(2,128)(2,1)S(1)} collective-permute-done((bf16[1,2,8192]{2,1,0:T(2,128)(2,1)S(1)}, bf16[1,2,8192]{2,1,0:T(2,128)(2,1)S(1)}, u32[]{:S(2)}, u32[]{:S(2)}) %collective-permute-start) | collective-permute-done | bytes 32800 | tf_op jit(solution)/shard_map/ppermute | solution.py:143
  9.1 1.6 %collective-permute-start.1 = (bf16[2,2,8192]{2,1,0:T(2,128)(2,1)S(1)}, bf16[2,2,8192]{2,1,0:T(2,128)(2,1)S(1)}, u32[]{:S(2)}, u32[]{:S(2)}) collective-permute-start(bf16[2,2,8192]{2,1,0:T(2,128)(2,1)S(1)} %get-tuple-element.10), channel_id=1, source_target_pairs={{4,0},{6,2},{0,4},{2,6},{12,8},{14,10},{8,12},{10,14},{5,1},{7,3},... | collective-permute-start | bytes 196616 | tf_op jit(solution)/shard_map/ppermute | solution.py:143
  10.7 2.7 %collective-permute-done.1 = bf16[2,2,8192]{2,1,0:T(2,128)(2,1)S(1)} collective-permute-done((bf16[2,2,8192]{2,1,0:T(2,128)(2,1)S(1)}, bf16[2,2,8192]{2,1,0:T(2,128)(2,1)S(1)}, u32[]{:S(2)}, u32[]{:S(2)}) %collective-permute-start.1) | collective-permute-done | bytes 65568 | tf_op jit(solution)/shard_map/ppermute | solution.py:143
  13.7 1.8 %collective-permute-start.2 = (bf16[4,2,8192]{2,1,0:T(2,128)(2,1)S(1)}, bf16[4,2,8192]{2,1,0:T(2,128)(2,1)S(1)}, u32[]{:S(2)}, u32[]{:S(2)}) collective-permute-start(bf16[4,2,8192]{2,1,0:T(2,128)(2,1)S(1)} %bitcast.184), channel_id=1, source_target_pairs={{2,0},{0,2},{6,4},{4,6},{10,8},{8,10},{14,12},{12,14},{3,1},{1,3},... | collective-permute-start | bytes 393224 | tf_op jit(solution)/shard_map/ppermute | solution.py:143
  15.5 3.3 %collective-permute-done.2 = bf16[4,2,8192]{2,1,0:T(2,128)(2,1)S(1)} collective-permute-done((bf16[4,2,8192]{2,1,0:T(2,128)(2,1)S(1)}, bf16[4,2,8192]{2,1,0:T(2,128)(2,1)S(1)}, u32[]{:S(2)}, u32[]{:S(2)}) %collective-permute-start.2) | collective-permute-done | bytes 131104 | tf_op jit(solution)/shard_map/ppermute | solution.py:143
  20.2 2.6 %collective-permute-start.11 = (s32[1,2]{1,0:T(1,128)S(1)}, s32[1,2]{1,0:T(1,128)S(1)}, u32[]{:S(2)}, u32[]{:S(2)}) collective-permute-start(s32[1,2]{1,0:T(1,128)S(1)} %bitcast.229), channel_id=1, source_target_pairs={{8,0},{10,2},{12,4},{14,6},{0,8},{2,10},{4,12},{6,14},{9,1},{11,3}... | collective-permute-start | bytes 32 | tf_op jit(solution)/shard_map/ppermute | solution.py:143
  24.5 5.8 %convolution_convert_fusion = bf16[32,640]{1,0:T(8,128)(2,1)S(1)} fusion(bf16[32,8192]{1,0:T(8,128)(2,1)S(1)} %reshape.278, bf16[8192,640]{1,0:T(8,128)(2,1)} %param.13), kind=kOutput, calls=%fused_computation.8 | convolution fusion | flops 335564800 | bytes 11051008 | tf_op jit(solution)/shard_map/dot_general | solution.py:220
  32.3 4.3 %collective-permute-done.5 = bf16[1,4,2,2,640]{4,3,2,1,0:T(2,128)(2,1)S(1)} collective-permute-done((bf16[1,4,2,2,640]{4,3,2,1,0:T(2,128)(2,1)S(1)}, bf16[1,4,2,2,640]{4,3,2,1,0:T(2,128)(2,1)S(1)}, u32[]{:S(2)}, u32[]{:S(2)}) %collective-permute-start.5) | collective-permute-done | bytes 20512 | tf_op jit(solution)/shard_map/ppermute | solution.py:143
  36.6 1.9 %collective-permute-start.6 = (bf16[2,2,2,2,640]{4,3,2,1,0:T(2,128)(2,1)S(1)}, bf16[2,2,2,2,640]{4,3,2,1,0:T(2,128)(2,1)S(1)}, u32[]{:S(2)}, u32[]{:S(2)}) collective-permute-start(bf16[2,2,2,2,640]{4,3,2,1,0:T(2,128)(2,1)S(1)} %get-tuple-element.16), channel_id=1, source_target_pairs={{4,0},{6,2},{0,4},{2,6},{12,8},{14,10},{8,12},{10,14},{5,1},{7,3},... | collective-permute-start | bytes 61448 | tf_op jit(solution)/shard_map/ppermute | solution.py:143
  38.5 1.9 %collective-permute-done.6 = bf16[2,2,2,2,640]{4,3,2,1,0:T(2,128)(2,1)S(1)} collective-permute-done((bf16[2,2,2,2,640]{4,3,2,1,0:T(2,128)(2,1)S(1)}, bf16[2,2,2,2,640]{4,3,2,1,0:T(2,128)(2,1)S(1)}, u32[]{:S(2)}, u32[]{:S(2)}) %collective-permute-start.6) | collective-permute-done | bytes 20512 | tf_op jit(solution)/shard_map/ppermute | solution.py:143
  40.6 1.6 %collective-permute-start.7 = (bf16[4,1,2,2,640]{4,3,2,0,1:T(2,128)(2,1)S(1)}, bf16[4,1,2,2,640]{4,3,2,0,1:T(2,128)(2,1)S(1)}, u32[]{:S(2)}, u32[]{:S(2)}) collective-permute-start(bf16[4,1,2,2,640]{4,3,2,0,1:T(2,128)(2,1)S(1)} %get-tuple-element.14), channel_id=1, source_target_pairs={{2,0},{0,2},{6,4},{4,6},{10,8},{8,10},{14,12},{12,14},{3,1},{1,3},... | collective-permute-start | bytes 61448 | tf_op jit(solution)/shard_map/ppermute | solution.py:143
  42.1 1.9 %collective-permute-start.12 = (s32[2,2]{1,0:T(2,128)S(1)}, s32[2,2]{1,0:T(2,128)S(1)}, u32[]{:S(2)}, u32[]{:S(2)}) collective-permute-start(s32[2,2]{1,0:T(2,128)S(1)} %get-tuple-element.30), channel_id=1, source_target_pairs={{4,0},{6,2},{0,4},{2,6},{12,8},{14,10},{8,12},{10,14},{5,1},{7,3},... | collective-permute-start | bytes 56 | tf_op jit(solution)/shard_map/ppermute | solution.py:143
  47.0 1.8 %collective-permute-start.13 = (s32[4,2]{0,1:T(2,128)S(1)}, s32[4,2]{0,1:T(2,128)S(1)}, u32[]{:S(2)}, u32[]{:S(2)}) collective-permute-start(s32[4,2]{0,1:T(2,128)S(1)} %reshape.292), channel_id=1, source_target_pairs={{2,0},{0,2},{6,4},{4,6},{10,8},{8,10},{14,12},{12,14},{3,1},{1,3},... | collective-permute-start | bytes 104 | tf_op jit(solution)/shard_map/ppermute | solution.py:143
  48.8 2.4 %collective-permute-done.8 = bf16[1,2,8192]{2,1,0:T(2,128)(2,1)S(1)} collective-permute-done((bf16[1,2,8192]{2,1,0:T(2,128)(2,1)S(1)}, bf16[1,2,8192]{2,1,0:T(2,128)(2,1)S(1)}, u32[]{:S(2)}, u32[]{:S(2)}) %collective-permute-start.8) | collective-permute-done | bytes 32800 | tf_op jit(solution)/shard_map/ppermute | solution.py:143
  51.3 1.9 %collective-permute-start.9 = (bf16[2,2,8192]{2,1,0:T(2,128)(2,1)S(1)}, bf16[2,2,8192]{2,1,0:T(2,128)(2,1)S(1)}, u32[]{:S(2)}, u32[]{:S(2)}) collective-permute-start(bf16[2,2,8192]{2,1,0:T(2,128)(2,1)S(1)} %get-tuple-element.6), channel_id=1, source_target_pairs={{4,0},{6,2},{0,4},{2,6},{12,8},{14,10},{8,12},{10,14},{5,1},{7,3},... | collective-permute-start | bytes 196616 | tf_op jit(solution)/shard_map/ppermute | solution.py:143
  53.3 2.3 %collective-permute-done.9 = bf16[2,2,8192]{2,1,0:T(2,128)(2,1)S(1)} collective-permute-done((bf16[2,2,8192]{2,1,0:T(2,128)(2,1)S(1)}, bf16[2,2,8192]{2,1,0:T(2,128)(2,1)S(1)}, u32[]{:S(2)}, u32[]{:S(2)}) %collective-permute-start.9) | collective-permute-done | bytes 65568 | tf_op jit(solution)/shard_map/ppermute | solution.py:143
  55.8 1.6 %collective-permute-start.10 = (bf16[4,2,8192]{2,1,0:T(2,128)(2,1)S(1)}, bf16[4,2,8192]{2,1,0:T(2,128)(2,1)S(1)}, u32[]{:S(2)}, u32[]{:S(2)}) collective-permute-start(bf16[4,2,8192]{2,1,0:T(2,128)(2,1)S(1)} %bitcast.182), channel_id=1, source_target_pairs={{2,0},{0,2},{6,4},{4,6},{10,8},{8,10},{14,12},{12,14},{3,1},{1,3},... | collective-permute-start | bytes 393224 | tf_op jit(solution)/shard_map/ppermute | solution.py:143
  57.4 3.5 %collective-permute-done.10 = bf16[4,2,8192]{2,1,0:T(2,128)(2,1)S(1)} collective-permute-done((bf16[4,2,8192]{2,1,0:T(2,128)(2,1)S(1)}, bf16[4,2,8192]{2,1,0:T(2,128)(2,1)S(1)}, u32[]{:S(2)}, u32[]{:S(2)}) %collective-permute-start.10) | collective-permute-done | bytes 131104 | tf_op jit(solution)/shard_map/ppermute | solution.py:143
  61.5 6.8 %fusion = f32[16,64]{1,0:T(8,128)S(1)} fusion(bf16[64,1024,64]{1,2,0:T(8,128)(2,1)} %param.20, f32[16,64]{0,1:T(8,128)S(1)} %get-tuple-element.34, bf16[16,8192]{1,0:T(8,128)(2,1)S(1)} %reshape_reshape.56, s32[]{:T(128)S(6)} %select_n.119), kind=kOutput, calls=%fused_computation.1 | convolution fusion | flops 134347776 | bytes 8458244 | tf_op jit(solution)/shard_map/gh,thy->gty/dot_general | solution.py:273
  68.7 4.2 %collective-permute-done.14 = f32[8,2,64]{2,1,0:T(2,128)S(1)} collective-permute-done((f32[8,2,64]{2,1,0:T(2,128)S(1)}, f32[8,2,64]{2,1,0:T(2,128)S(1)}, u32[]{:S(2)}, u32[]{:S(2)}) %collective-permute-start.14) | collective-permute-done | bytes 4128 | tf_op jit(solution)/shard_map/ppermute | solution.py:143
  72.9 1.8 %collective-permute-start.15 = (f32[8,2,64]{2,1,0:T(2,128)S(1)}, f32[8,2,64]{2,1,0:T(2,128)S(1)}, u32[]{:S(2)}, u32[]{:S(2)}) collective-permute-start(f32[8,2,64]{2,1,0:T(2,128)S(1)} %bitcast_add_fusion), channel_id=1, source_target_pairs={{4,0},{6,2},{0,4},{2,6},{12,8},{14,10},{8,12},{10,14},{5,1},{7,3},... | collective-permute-start | bytes 12296 | tf_op jit(solution)/shard_map/ppermute | solution.py:143
  74.7 1.9 %collective-permute-done.15 = f32[8,2,64]{2,1,0:T(2,128)S(1)} collective-permute-done((f32[8,2,64]{2,1,0:T(2,128)S(1)}, f32[8,2,64]{2,1,0:T(2,128)S(1)}, u32[]{:S(2)}, u32[]{:S(2)}) %collective-permute-start.15) | collective-permute-done | bytes 4128 | tf_op jit(solution)/shard_map/ppermute | solution.py:143
  76.6 1.6 %collective-permute-start.16 = (f32[8,2,64]{2,1,0:T(2,128)S(1)}, f32[8,2,64]{2,1,0:T(2,128)S(1)}, u32[]{:S(2)}, u32[]{:S(2)}) collective-permute-start(f32[8,2,64]{2,1,0:T(2,128)S(1)} %add.46), channel_id=1, source_target_pairs={{2,0},{0,2},{6,4},{4,6},{10,8},{8,10},{14,12},{12,14},{3,1},{1,3},... | collective-permute-start | bytes 12296 | tf_op jit(solution)/shard_map/ppermute | solution.py:143
  78.2 8.8 %fusion.54 = f32[16,1024]{1,0:T(8,128)S(1)} fusion(bf16[16,8192]{1,0:T(8,128)(2,1)S(1)} %reshape_reshape.56, bf16[8192,1024]{1,0:T(8,128)(2,1)} %param.14), kind=kOutput, calls=%fused_computation.130 | convolution fusion | flops 268435456 | bytes 17104896 | tf_op jit(solution)/shard_map/dot_general | solution.py:31
  87.0 1.4 %fusion.5 = bf16[16,1024]{1,0:T(8,128)(2,1)S(1)} fusion(f32[16,1024]{1,0:T(8,128)S(1)} %fusion.54, bf16[64,64,1024]{2,1,0:T(8,128)(2,1)S(1)} %bitcast.178, bf16[16,64]{1,0:T(8,128)(2,1)S(1)} %bitcast.207, bf16[16,64]{0,1:T(8,128)(2,1)S(1)} %get-tuple-element.33), kind=kOutput, calls=%fused_computation.10 | convolution fusion | flops 134332416 | bytes 8491008 | tf_op jit(solution)/shard_map/dot_general | solution.py:36
  89.0 4.1 %collective-permute-done.17 = bf16[1,4,2,1024]{3,2,1,0:T(2,128)(2,1)S(1)} collective-permute-done((bf16[1,4,2,1024]{3,2,1,0:T(2,128)(2,1)S(1)}, bf16[1,4,2,1024]{3,2,1,0:T(2,128)(2,1)S(1)}, u32[]{:S(2)}, u32[]{:S(2)}) %collective-permute-start.17) | collective-permute-done | bytes 16416 | tf_op jit(solution)/shard_map/ppermute | solution.py:143
  93.2 1.9 %collective-permute-start.18 = (bf16[2,2,2,1024]{3,2,1,0:T(2,128)(2,1)S(1)}, bf16[2,2,2,1024]{3,2,1,0:T(2,128)(2,1)S(1)}, u32[]{:S(2)}, u32[]{:S(2)}) collective-permute-start(bf16[2,2,2,1024]{3,2,1,0:T(2,128)(2,1)S(1)} %get-tuple-element.22), channel_id=1, source_target_pairs={{4,0},{6,2},{0,4},{2,6},{12,8},{14,10},{8,12},{10,14},{5,1},{7,3},... | collective-permute-start | bytes 49160 | tf_op jit(solution)/shard_map/ppermute | solution.py:143
  95.1 2.0 %collective-permute-done.18 = bf16[2,2,2,1024]{3,2,1,0:T(2,128)(2,1)S(1)} collective-permute-done((bf16[2,2,2,1024]{3,2,1,0:T(2,128)(2,1)S(1)}, bf16[2,2,2,1024]{3,2,1,0:T(2,128)(2,1)S(1)}, u32[]{:S(2)}, u32[]{:S(2)}) %collective-permute-start.18) | collective-permute-done | bytes 16416 | tf_op jit(solution)/shard_map/ppermute | solution.py:143
  97.3 3.6 %collective-permute-done.19 = bf16[4,1,2,1024]{3,2,0,1:T(2,128)(2,1)S(1)} collective-permute-done((bf16[4,1,2,1024]{3,2,0,1:T(2,128)(2,1)S(1)}, bf16[4,1,2,1024]{3,2,0,1:T(2,128)(2,1)S(1)}, u32[]{:S(2)}, u32[]{:S(2)}) %collective-permute-start.19) | collective-permute-done | bytes 16416 | tf_op jit(solution)/shard_map/ppermute | solution.py:143
  (114 shorter events, 14.1 us)
Async XLA Ops:
  0.0 45.3 %copy-start = (bf16[2,256,1024]{2,1,0:T(8,128)(2,1)S(1)}, bf16[2,256,1024]{2,1,0:T(8,128)(2,1)}, u32[]{:S(2)}) copy-start(bf16[2,256,1024]{2,1,0:T(8,128)(2,1)} %param.15) | copy-start | bytes 3145732
  2.6 6.3 %collective-permute-start = (bf16[1,2,8192]{2,1,0:T(2,128)(2,1)S(1)}, bf16[1,2,8192]{2,1,0:T(2,128)(2,1)S(1)}, u32[]{:S(2)}, u32[]{:S(2)}) collective-permute-start(bf16[1,2,8192]{2,1,0:T(2,128)(2,1)S(1)} %fusion.64), channel_id=1, source_target_pairs={{8,0},{10,2},{12,4},{14,6},{0,8},{2,10},{4,12},{6,14},{9,1},{11,3}... | collective-permute-start | bytes 98312 | tf_op jit(solution)/shard_map/ppermute | solution.py:143
  9.1 4.3 %collective-permute-start.1 = (bf16[2,2,8192]{2,1,0:T(2,128)(2,1)S(1)}, bf16[2,2,8192]{2,1,0:T(2,128)(2,1)S(1)}, u32[]{:S(2)}, u32[]{:S(2)}) collective-permute-start(bf16[2,2,8192]{2,1,0:T(2,128)(2,1)S(1)} %get-tuple-element.10), channel_id=1, source_target_pairs={{4,0},{6,2},{0,4},{2,6},{12,8},{14,10},{8,12},{10,14},{5,1},{7,3},... | collective-permute-start | bytes 196616 | tf_op jit(solution)/shard_map/ppermute | solution.py:143
  13.7 5.0 %collective-permute-start.2 = (bf16[4,2,8192]{2,1,0:T(2,128)(2,1)S(1)}, bf16[4,2,8192]{2,1,0:T(2,128)(2,1)S(1)}, u32[]{:S(2)}, u32[]{:S(2)}) collective-permute-start(bf16[4,2,8192]{2,1,0:T(2,128)(2,1)S(1)} %bitcast.184), channel_id=1, source_target_pairs={{2,0},{0,2},{6,4},{4,6},{10,8},{8,10},{14,12},{12,14},{3,1},{1,3},... | collective-permute-start | bytes 393224 | tf_op jit(solution)/shard_map/ppermute | solution.py:143
  19.3 4.3 %collective-permute-start.3 = (bf16[1,8,2,8192]{3,2,1,0:T(2,128)(2,1)S(1)}, bf16[1,8,2,8192]{3,2,1,0:T(2,128)(2,1)S(1)}, u32[]{:S(2)}, u32[]{:S(2)}) collective-permute-start(bf16[1,8,2,8192]{3,2,1,0:T(2,128)(2,1)S(1)} %bitcast.179), channel_id=1, source_target_pairs={{1,0},{0,1},{3,2},{2,3},{5,4},{4,5},{7,6},{6,7},{9,8},{8,9},{11,10... | collective-permute-start | bytes 786440 | tf_op jit(solution)/shard_map/ppermute | solution.py:143
  20.2 21.9 %collective-permute-start.11 = (s32[1,2]{1,0:T(1,128)S(1)}, s32[1,2]{1,0:T(1,128)S(1)}, u32[]{:S(2)}, u32[]{:S(2)}) collective-permute-start(s32[1,2]{1,0:T(1,128)S(1)} %bitcast.229), channel_id=1, source_target_pairs={{8,0},{10,2},{12,4},{14,6},{0,8},{2,10},{4,12},{6,14},{9,1},{11,3}... | collective-permute-start | bytes 32 | tf_op jit(solution)/shard_map/ppermute | solution.py:143
  23.6 8.6 %copy-start.3 = (s32[2]{0:T(128)S(1)}, s32[2]{0:T(128)}, u32[]{:S(2)}) copy-start(s32[2]{0:T(128)} %param.17) | copy-start | bytes 28
  24.5 21.4 %copy-start.2 = (bf16[2,256,1024]{2,1,0:T(8,128)(2,1)S(1)}, bf16[2,256,1024]{2,1,0:T(8,128)(2,1)}, u32[]{:S(2)}) copy-start(bf16[2,256,1024]{2,1,0:T(8,128)(2,1)} %param.16) | copy-start | bytes 3145732
  30.4 1.3 %collective-permute-start.4 = (bf16[1,1,8,2,640]{4,3,2,1,0:T(2,128)(2,1)S(1)}, bf16[1,1,8,2,640]{4,3,2,1,0:T(2,128)(2,1)S(1)}, u32[]{:S(2)}, u32[]{:S(2)}) collective-permute-start(bf16[1,1,8,2,640]{4,3,2,1,0:T(2,128)(2,1)S(1)} %slice_bitcast_fusion.3), channel_id=1, source_target_pairs={{1,0},{0,1},{3,2},{2,3},{5,4},{4,5},{7,6},{6,7},{9,8},{8,9},{11,10... | collective-permute-start | bytes 61448 | tf_op jit(solution)/shard_map/ppermute | solution.py:143
  31.8 4.7 %collective-permute-start.5 = (bf16[1,4,2,2,640]{4,3,2,1,0:T(2,128)(2,1)S(1)}, bf16[1,4,2,2,640]{4,3,2,1,0:T(2,128)(2,1)S(1)}, u32[]{:S(2)}, u32[]{:S(2)}) collective-permute-start(bf16[1,4,2,2,640]{4,3,2,1,0:T(2,128)(2,1)S(1)} %bitcast.220), channel_id=1, source_target_pairs={{8,0},{10,2},{12,4},{14,6},{0,8},{2,10},{4,12},{6,14},{9,1},{11,3}... | collective-permute-start | bytes 61448 | tf_op jit(solution)/shard_map/ppermute | solution.py:143
  36.6 3.8 %collective-permute-start.6 = (bf16[2,2,2,2,640]{4,3,2,1,0:T(2,128)(2,1)S(1)}, bf16[2,2,2,2,640]{4,3,2,1,0:T(2,128)(2,1)S(1)}, u32[]{:S(2)}, u32[]{:S(2)}) collective-permute-start(bf16[2,2,2,2,640]{4,3,2,1,0:T(2,128)(2,1)S(1)} %get-tuple-element.16), channel_id=1, source_target_pairs={{4,0},{6,2},{0,4},{2,6},{12,8},{14,10},{8,12},{10,14},{5,1},{7,3},... | collective-permute-start | bytes 61448 | tf_op jit(solution)/shard_map/ppermute | solution.py:143
  40.6 3.8 %collective-permute-start.7 = (bf16[4,1,2,2,640]{4,3,2,0,1:T(2,128)(2,1)S(1)}, bf16[4,1,2,2,640]{4,3,2,0,1:T(2,128)(2,1)S(1)}, u32[]{:S(2)}, u32[]{:S(2)}) collective-permute-start(bf16[4,1,2,2,640]{4,3,2,0,1:T(2,128)(2,1)S(1)} %get-tuple-element.14), channel_id=1, source_target_pairs={{2,0},{0,2},{6,4},{4,6},{10,8},{8,10},{14,12},{12,14},{3,1},{1,3},... | collective-permute-start | bytes 61448 | tf_op jit(solution)/shard_map/ppermute | solution.py:143
  42.1 4.6 %collective-permute-start.12 = (s32[2,2]{1,0:T(2,128)S(1)}, s32[2,2]{1,0:T(2,128)S(1)}, u32[]{:S(2)}, u32[]{:S(2)}) collective-permute-start(s32[2,2]{1,0:T(2,128)S(1)} %get-tuple-element.30), channel_id=1, source_target_pairs={{4,0},{6,2},{0,4},{2,6},{12,8},{14,10},{8,12},{10,14},{5,1},{7,3},... | collective-permute-start | bytes 56 | tf_op jit(solution)/shard_map/ppermute | solution.py:143
  46.3 4.9 %collective-permute-start.8 = (bf16[1,2,8192]{2,1,0:T(2,128)(2,1)S(1)}, bf16[1,2,8192]{2,1,0:T(2,128)(2,1)S(1)}, u32[]{:S(2)}, u32[]{:S(2)}) collective-permute-start(bf16[1,2,8192]{2,1,0:T(2,128)(2,1)S(1)} %convert_element_type.117), channel_id=1, source_target_pairs={{8,0},{10,2},{12,4},{14,6},{0,8},{2,10},{4,12},{6,14},{9,1},{11,3}... | collective-permute-start | bytes 98312 | tf_op jit(solution)/shard_map/ppermute | solution.py:143
  47.0 6.2 %collective-permute-start.13 = (s32[4,2]{0,1:T(2,128)S(1)}, s32[4,2]{0,1:T(2,128)S(1)}, u32[]{:S(2)}, u32[]{:S(2)}) collective-permute-start(s32[4,2]{0,1:T(2,128)S(1)} %reshape.292), channel_id=1, source_target_pairs={{2,0},{0,2},{6,4},{4,6},{10,8},{8,10},{14,12},{12,14},{3,1},{1,3},... | collective-permute-start | bytes 104 | tf_op jit(solution)/shard_map/ppermute | solution.py:143
  51.3 4.3 %collective-permute-start.9 = (bf16[2,2,8192]{2,1,0:T(2,128)(2,1)S(1)}, bf16[2,2,8192]{2,1,0:T(2,128)(2,1)S(1)}, u32[]{:S(2)}, u32[]{:S(2)}) collective-permute-start(bf16[2,2,8192]{2,1,0:T(2,128)(2,1)S(1)} %get-tuple-element.6), channel_id=1, source_target_pairs={{4,0},{6,2},{0,4},{2,6},{12,8},{14,10},{8,12},{10,14},{5,1},{7,3},... | collective-permute-start | bytes 196616 | tf_op jit(solution)/shard_map/ppermute | solution.py:143
  55.8 5.0 %collective-permute-start.10 = (bf16[4,2,8192]{2,1,0:T(2,128)(2,1)S(1)}, bf16[4,2,8192]{2,1,0:T(2,128)(2,1)S(1)}, u32[]{:S(2)}, u32[]{:S(2)}) collective-permute-start(bf16[4,2,8192]{2,1,0:T(2,128)(2,1)S(1)} %bitcast.182), channel_id=1, source_target_pairs={{2,0},{0,2},{6,4},{4,6},{10,8},{8,10},{14,12},{12,14},{3,1},{1,3},... | collective-permute-start | bytes 393224 | tf_op jit(solution)/shard_map/ppermute | solution.py:143
  68.3 4.6 %collective-permute-start.14 = (f32[8,2,64]{2,1,0:T(2,128)S(1)}, f32[8,2,64]{2,1,0:T(2,128)S(1)}, u32[]{:S(2)}, u32[]{:S(2)}) collective-permute-start(f32[8,2,64]{2,1,0:T(2,128)S(1)} %bitcast.211), channel_id=1, source_target_pairs={{8,0},{10,2},{12,4},{14,6},{0,8},{2,10},{4,12},{6,14},{9,1},{11,3}... | collective-permute-start | bytes 12296 | tf_op jit(solution)/shard_map/ppermute | solution.py:143
  72.9 3.7 %collective-permute-start.15 = (f32[8,2,64]{2,1,0:T(2,128)S(1)}, f32[8,2,64]{2,1,0:T(2,128)S(1)}, u32[]{:S(2)}, u32[]{:S(2)}) collective-permute-start(f32[8,2,64]{2,1,0:T(2,128)S(1)} %bitcast_add_fusion), channel_id=1, source_target_pairs={{4,0},{6,2},{0,4},{2,6},{12,8},{14,10},{8,12},{10,14},{5,1},{7,3},... | collective-permute-start | bytes 12296 | tf_op jit(solution)/shard_map/ppermute | solution.py:143
  76.6 10.4 %slice-start = ((s8[8388608]{0:T(1024)(128)(4,1)}), s8[4194304]{0:T(1024)(128)(4,1)S(1)}, s32[]{:S(2)}) async-start(s8[8388608]{0:T(1024)(128)(4,1)} %bitcast.177), calls=%async_computation | async-start | bytes 8388608
  76.6 10.4 %slice-start.1 = ((s8[8388608]{0:T(1024)(128)(4,1)}), s8[4194304]{0:T(1024)(128)(4,1)S(1)}, s32[]{:S(2)}) async-start(s8[8388608]{0:T(1024)(128)(4,1)} %bitcast.177), calls=%async_computation.1 | async-start | bytes 8388608
  76.6 10.3 %collective-permute-start.16 = (f32[8,2,64]{2,1,0:T(2,128)S(1)}, f32[8,2,64]{2,1,0:T(2,128)S(1)}, u32[]{:S(2)}, u32[]{:S(2)}) collective-permute-start(f32[8,2,64]{2,1,0:T(2,128)S(1)} %add.46), channel_id=1, source_target_pairs={{2,0},{0,2},{6,4},{4,6},{10,8},{8,10},{14,12},{12,14},{3,1},{1,3},... | collective-permute-start | bytes 12296 | tf_op jit(solution)/shard_map/ppermute | solution.py:143
  86.9 14.7 %copy-start.1 = (bf16[2,8192]{1,0:T(2,128)(2,1)S(1)}, bf16[2,8192]{1,0:T(2,128)(2,1)}, u32[]{:S(2)}) copy-start(bf16[2,8192]{1,0:T(2,128)(2,1)} %param.11) | copy-start | bytes 98308
  88.5 4.7 %collective-permute-start.17 = (bf16[1,4,2,1024]{3,2,1,0:T(2,128)(2,1)S(1)}, bf16[1,4,2,1024]{3,2,1,0:T(2,128)(2,1)S(1)}, u32[]{:S(2)}, u32[]{:S(2)}) collective-permute-start(bf16[1,4,2,1024]{3,2,1,0:T(2,128)(2,1)S(1)} %get-tuple-element.24), channel_id=1, source_target_pairs={{8,0},{10,2},{12,4},{14,6},{0,8},{2,10},{4,12},{6,14},{9,1},{11,3}... | collective-permute-start | bytes 49160 | tf_op jit(solution)/shard_map/ppermute | solution.py:143
  93.2 3.8 %collective-permute-start.18 = (bf16[2,2,2,1024]{3,2,1,0:T(2,128)(2,1)S(1)}, bf16[2,2,2,1024]{3,2,1,0:T(2,128)(2,1)S(1)}, u32[]{:S(2)}, u32[]{:S(2)}) collective-permute-start(bf16[2,2,2,1024]{3,2,1,0:T(2,128)(2,1)S(1)} %get-tuple-element.22), channel_id=1, source_target_pairs={{4,0},{6,2},{0,4},{2,6},{12,8},{14,10},{8,12},{10,14},{5,1},{7,3},... | collective-permute-start | bytes 49160 | tf_op jit(solution)/shard_map/ppermute | solution.py:143
  97.1 3.8 %collective-permute-start.19 = (bf16[4,1,2,1024]{3,2,0,1:T(2,128)(2,1)S(1)}, bf16[4,1,2,1024]{3,2,0,1:T(2,128)(2,1)S(1)}, u32[]{:S(2)}, u32[]{:S(2)}) collective-permute-start(bf16[4,1,2,1024]{3,2,0,1:T(2,128)(2,1)S(1)} %get-tuple-element.20), channel_id=1, source_target_pairs={{2,0},{0,2},{6,4},{4,6},{10,8},{8,10},{14,12},{12,14},{3,1},{1,3},... | collective-permute-start | bytes 49160 | tf_op jit(solution)/shard_map/ppermute | solution.py:143

commit v3 on v0

--- a/solution.py
+++ b/solution.py
@@ -1,6 +1,8 @@
 import jax
 import jax.numpy as jnp
 from jax import lax
+from jax.experimental import pallas as pl
+from jax.experimental.pallas import tpu as pltpu
 from jax.sharding import PartitionSpec as P
 
 HEADS = 64
@@ -37,7 +39,7 @@
     return (base_output + ADAPTER_SCALE * adapter_delta).astype(jnp.bfloat16)
 
 
-def body(
+def general_body(
     hidden,
     attention_norm_gain,
     query_key_value_weight,
@@ -139,6 +141,322 @@
     return (widened + returned.astype(jnp.float32)).astype(jnp.bfloat16)
 
 
+MIB = 1 << 20
+LANES = 128
+VMEM = pl.BlockSpec(memory_space=pltpu.VMEM)
+SMEM = pl.BlockSpec(memory_space=pltpu.SMEM)
+ANY = pl.BlockSpec(memory_space=pl.ANY)
+
+
+def call(kernel, name, out_shape, in_specs, moved, limit=2 * MIB, flops=0, **options):
+    return pl.pallas_call(
+        kernel,
+        out_shape=out_shape,
+        in_specs=in_specs,
+        out_specs=jax.tree.map(lambda _: VMEM, out_shape),
+        compiler_params=pltpu.CompilerParams(vmem_limit_bytes=limit),
+        cost_estimate=pl.CostEstimate(flops=flops, bytes_accessed=moved, transcendentals=0),
+        name=name,
+        **options,
+    )
+
+
+def norm_rows(hidden, gain, slots, requests, copies):
+    rows, width = hidden.shape
+
+    def kernel(hidden_ref, gain_ref, slots_ref, requests_ref, out_ref):
+        wide = hidden_ref[...].astype(jnp.float32)
+        inverse = lax.rsqrt(jnp.mean(wide * wide, -1, keepdims=True) + EPS)
+        for k in range(width // LANES):
+            part = pl.ds(k * LANES, LANES)
+            normed = hidden_ref[:, part].astype(jnp.float32) * inverse
+            normed = normed * gain_ref[k : k + 1, :].astype(jnp.float32)
+            normed = normed.astype(jnp.bfloat16)
+            for c in range(copies):
+                out_ref[c, :, part] = normed
+        row = lax.broadcasted_iota(jnp.int32, (rows, LANES), 0)
+        adapter = jnp.zeros((rows, LANES), jnp.float32)
+        for r in range(rows):
+            chosen = requests_ref[0, slots_ref[r]].astype(jnp.float32)
+            adapter = jnp.where(row == r, chosen, adapter)
+        for c in range(copies):
+            out_ref[c, :, pl.ds(width, LANES)] = adapter.astype(jnp.bfloat16)
+
+    return call(
+        kernel,
+        "norm_rows",
+        jax.ShapeDtypeStruct((copies, rows, width + LANES), jnp.bfloat16),
+        [VMEM, VMEM, SMEM, SMEM],
+        hidden.size * 2 * (copies + 1),
+    )(hidden, gain.reshape(-1, LANES), slots, requests)
+
+
+def hold(weight, after, *passed):
+    def kernel(weight_ref, after_ref, *refs):
+        del weight_ref, after_ref
+        for source, target in zip(refs[: len(passed)], refs[len(passed) + 1 :]):
+            target[...] = source[...]
+
+    outs = call(
+        kernel,
+        "hold_weight",
+        (pltpu.VMEM(weight.shape, weight.dtype),)
+        + tuple(jax.ShapeDtypeStruct(p.shape, p.dtype) for p in passed),
+        [VMEM, ANY] + [VMEM] * len(passed),
+        weight.size * 2,
+        limit=MIB,
+        input_output_aliases={0: 0},
+    )(weight, after, *passed)
+    return outs if passed else outs[0]
+
+
+def multiply(rows, weight, out_type, name, chunk=1024):
+    count, depth = rows.shape[0], weight.shape[0]
+
+    def kernel(rows_ref, weight_ref, out_ref):
+        total = jnp.zeros((count, weight.shape[1]), jnp.float32)
+        for k in range(depth // chunk):
+            part = pl.ds(k * chunk, chunk)
+            total = total + jnp.dot(
+                rows_ref[:, part], weight_ref[part, :], preferred_element_type=jnp.float32
+            )
+        out_ref[...] = total.astype(out_type)
+
+    return call(
+        kernel,
+        name,
+        jax.ShapeDtypeStruct((count, weight.shape[1]), out_type),
+        [VMEM, VMEM],
+        weight.size,
+        flops=2 * count * weight.size,
+    )(rows, weight)
+
+
+def pick_adapters(adapter, down, up, after):
+    count, rank = adapter.shape[0], up.shape[1]
+    down_shape, up_shape = (count,) + down.shape[1:], (count,) + up.shape[1:]
+
+    def kernel(adapter_ref, down_ref, up_ref, after_ref, down_out, up_out, sems):
+        del after_ref
+        copies = []
+        for r in range(count):
+            chosen = adapter_ref[r]
+            copies.append(
+                pltpu.make_async_copy(down_ref.at[chosen], down_out.at[r], sems.at[0, r])
+            )
+            copies.append(pltpu.make_async_copy(up_ref.at[chosen], up_out.at[r], sems.at[1, r]))
+        for copy in copies:
+            copy.start()
+        for copy in copies:
+            copy.wait()
+
+    return call(
+        kernel,
+        "pick_adapters",
+        (pltpu.VMEM(down_shape, down.dtype), pltpu.VMEM(up_shape, up.dtype)),
+        [SMEM, ANY, ANY, ANY],
+        2 * count * rank * (down.shape[2] + up.shape[2]),
+        limit=36 * MIB,
+        scratch_shapes=[pltpu.SemaphoreType.DMA((2, count))],
+    )(adapter, down, up, after)
+
+
+def down_partials(rows, place, down, copies):
+    count, rank, depth = down.shape
+
+    def kernel(place_ref, rows_ref, down_ref, out_ref):
+        start = pl.multiple_of(place_ref[0] * depth, depth)
+        every = lax.dot_general(
+            rows_ref[:, pl.ds(start, depth)],
+            down_ref[...].reshape(count * rank, depth),
+            (((1,), (1,)), ((), ())),
+            preferred_element_type=jnp.float32,
+        )
+        row = lax.broadcasted_iota(jnp.int32, (count, LANES), 0)
+        lane = lax.broadcasted_iota(jnp.int32, (count, LANES), 1)
+        total = jnp.zeros((count, LANES), jnp.float32)
+        for s in range(count * rank // LANES):
+            mine = row == (lane + s * LANES) // rank
+            total = total + jnp.where(mine, every[:, s * LANES : (s + 1) * LANES], 0.0)
+        for c in range(copies):
+            out_ref[c] = total
+
+    return call(
+        kernel,
+        "down_partials",
+        jax.ShapeDtypeStruct((copies, count, LANES), jnp.float32),
+        [SMEM, VMEM, VMEM],
+        down.size * 2,
+        limit=4 * MIB,
+        flops=2 * count * down.size,
+    )(place, rows, down)
+
+
+def add_up(base, partials, up):
+    count, rank, width = up.shape
+
+    def kernel(base_ref, partials_ref, up_ref, out_ref):
+        total = partials_ref[0]
+        for c in range(1, partials.shape[0]):
+            total = total + partials_ref[c]
+        down = total.astype(jnp.bfloat16).astype(jnp.float32)
+        row = lax.broadcasted_iota(jnp.int32, (count, LANES), 0)
+        lane = lax.broadcasted_iota(jnp.int32, (count, LANES), 1)
+        spread = jnp.concatenate(
+            [
+                jnp.where(row == (lane + s * LANES) // rank, down, 0.0)
+                for s in range(count * rank // LANES)
+            ],
+            1,
+        ).astype(jnp.bfloat16)
+        delta = jnp.dot(
+            spread, up_ref[...].reshape(count * rank, width), preferred_element_type=jnp.float32
+        )
+        out_ref[...] = (base_ref[...] + ADAPTER_SCALE * delta).astype(jnp.bfloat16)
+
+    return call(
+        kernel,
+        "add_up",
+        jax.ShapeDtypeStruct((count, width), jnp.bfloat16),
+        [VMEM, VMEM, VMEM],
+        up.size * 2,
+        limit=4 * MIB,
+        flops=2 * count * up.size,
+    )(base, partials, up)
+
+
+def add_rows(hidden, parts):
+    width = parts.shape[2]
+
+    def kernel(hidden_ref, parts_ref, out_ref):
+        for k in range(parts.shape[0]):
+            part = pl.ds(k * width, width)
+            total = hidden_ref[:, part].astype(jnp.float32) + parts_ref[k].astype(jnp.float32)
+            out_ref[:, part] = total.astype(jnp.bfloat16)
+
+    return call(
+        kernel,
+        "add_rows",
+        jax.ShapeDtypeStruct(hidden.shape, hidden.dtype),
+        [VMEM, VMEM],
+        hidden.size * 6,
+    )(hidden, parts)
+
+
+def swap_cores(block):
+    return lax.ppermute(block, "batch", [(0, 1), (1, 0)])
+
+
+def exchange(blocks):
+    return lax.all_to_all(blocks, "mp", split_axis=0, concat_axis=0, tiled=True)
+
+
+def attend(qkv, cosine, sine, key_cache, value_cache, lengths):
+    rows = qkv.shape[0]
+    query_width = HEADS * HEAD_DIM
+    kv_width = KV_HEADS * HEAD_DIM
+    group = HEADS // KV_HEADS
+    scale = HEAD_DIM ** (-0.5)
+
+    def turn(part):
+        vec = part.astype(jnp.float32).reshape(rows, -1, HEAD_DIM)
+        half = HEAD_DIM // 2
+        turned = jnp.concatenate([-vec[..., half:], vec[..., :half]], -1)
+        return (vec * cosine[:, None] + turned * sine[:, None]).astype(jnp.bfloat16)
+
+    query = turn(qkv[:, :query_width])
+    fresh_key = turn(qkv[:, query_width : query_width + kv_width])
+    fresh_value = (
+        qkv[:, query_width + kv_width :].astype(jnp.float32).reshape(rows, KV_HEADS, HEAD_DIM)
+    )
+    grouped = query.reshape(rows, KV_HEADS, group, HEAD_DIM)
+    cached = key_cache.reshape(rows, -1, KV_HEADS, HEAD_DIM)
+    stored = value_cache.reshape(rows, -1, KV_HEADS, HEAD_DIM)
+    scores = (
+        jnp.einsum("rgqd,rtgd->rgqt", grouped, cached, preferred_element_type=jnp.float32) * scale
+    )
+    live = jnp.arange(cached.shape[1])[None, :] < lengths[:, None]
+    scores = jnp.where(live[:, None, None, :], scores, -jnp.inf)
+    own = (
+        jnp.einsum("rgqd,rgd->rgq", grouped, fresh_key, preferred_element_type=jnp.float32) * scale
+    )
+    top = jnp.maximum(jnp.max(scores, -1), own)
+    expo = jnp.exp(scores - top[..., None])
+    own_exp = jnp.exp(own - top)
+    total = jnp.sum(expo, -1) + own_exp
+    probs = (expo / total[..., None]).astype(jnp.bfloat16)
+    own_prob = (own_exp / total).astype(jnp.bfloat16)
+    context_vector = jnp.einsum(
+        "rgqt,rtgd->rgqd", probs, stored, preferred_element_type=jnp.float32
+    )
+    context_vector = (
+        context_vector + own_prob.astype(jnp.float32)[..., None] * fresh_value[:, :, None, :]
+    )
+    return context_vector.reshape(rows, query_width).astype(jnp.bfloat16)
+
+
+def angles(lengths):
+    half = HEAD_DIM // 2
+    freq = THETA ** (-(jnp.arange(half, dtype=jnp.float32) * 2.0) / HEAD_DIM)
+    angle = lengths.astype(jnp.float32)[:, None] * freq
+    cosine, sine = jnp.cos(angle), jnp.sin(angle)
+    return jnp.concatenate([cosine, cosine], -1), jnp.concatenate([sine, sine], -1)
+
+
+def fast_body(
+    hidden,
+    attention_norm_gain,
+    query_key_value_weight,
+    output_weight,
+    key_cache,
+    value_cache,
+    lengths,
+    slots,
+    requests,
+    adapter_down_matrices,
+    adapter_up_matrices,
+):
+    rows, features = hidden.shape
+    mp_size = lax.axis_size("mp")
+    width = query_key_value_weight.shape[1]
+    cosine, sine = angles(lengths)
+
+    sent = norm_rows(hidden, attention_norm_gain, slots, requests, mp_size)
+    near = exchange(sent)
+    far = swap_cores(near)
+    held_weight = hold(query_key_value_weight, sent)
+    adapter = near[:, :, features].reshape(-1).astype(jnp.int32)
+    normed = jnp.concatenate([near, far]).reshape(-1, features + LANES)
+    columns = multiply(normed, held_weight, jnp.bfloat16, "project_qkv")
+
+    split = columns.reshape(2, mp_size, rows, width)
+    mixed = jnp.stack([split[0], swap_cores(split[1])], 1)
+    mixed = exchange(mixed)
+    held_weight, cosine, sine = hold(output_weight, columns, cosine, sine)
+    mixed = jnp.where(lax.axis_index("batch") == 0, mixed, mixed[:, ::-1])
+    qkv = mixed.transpose(2, 0, 1, 3).reshape(rows, -1)
+
+    context = attend(qkv, cosine, sine, key_cache, value_cache, lengths)
+    picked_down, picked_up = pick_adapters(
+        adapter, adapter_down_matrices.swapaxes(1, 2), adapter_up_matrices, context
+    )
+    copies = jnp.broadcast_to(context[None], (mp_size, *context.shape))
+    gathered = exchange(copies).reshape(-1, context.shape[1])
+
+    place = lax.axis_index("mp").astype(jnp.int32).reshape(1)
+    partials = exchange(down_partials(gathered, place, picked_down, mp_size))
+    base = multiply(gathered, held_weight, jnp.float32, "project_out")
+    projected = add_up(base, partials, picked_up)
+    returned = exchange(projected.reshape(mp_size, rows, -1))
+    return add_rows(hidden, returned)
+
+
+def body(*arguments):
+    small = lax.axis_size("mp") <= 16 and lax.axis_size("batch") == 2
+    whole_heads = arguments[2].shape[1] % HEAD_DIM == 0
+    return (fast_body if small and whole_heads else general_body)(*arguments)
+
+
 def solution(mesh):
     in_specs = (
         P(("groups", "mp", "batch"), None),

time: 143 us -> 121 us (0.85)
  blocking collectives: 107 us -> 29.3 us
  local copies, waits for them, and re-layouts: 1.33 us -> 59.4 us
  matrix products: 26.2 us -> 0.9 us
  starting transfers between devices: 3.34 us -> 15.8 us
  Pallas kernels: 0 us -> 11.8 us
  other arithmetic: 4.39 us -> 1.78 us
    all_gather x3 -> x0, blocking collectives: 76.1 us -> none  [the longest x1 30.8 us: body(): lax.all_gather(context_vector, 'mp', axis=0, tiled=True)]
    unnamed x17 -> x38, local copies, waits for them, and re-layouts: 0.45 us -> 56.5 us
    dot_general x7 -> x3, matrix products: 26.2 us -> 0.9 us  [the longest x1 0.46 us: attend(): jnp.einsum('rgqd,rtgd->rgqt', grouped, cached, preferred_element_type=jnp...]
    psum x1 -> x0, blocking collectives: 17.4 us -> none  [body(): down_gathered = lax.psum(partial_down, 'mp').astype(jnp.bfloat16)]
    all_to_all x2, blocking collectives: 13.5 us -> 29.3 us  [exchange(): return lax.all_to_all(blocks, 'mp', split_axis=0, concat_axis=0, tiled=True)]
    all_to_all x1 -> x3, starting transfers between devices: 3.34 us -> 15.3 us  [exchange(): return lax.all_to_all(blocks, 'mp', split_axis=0, concat_axis=0, tiled=True)]
    pallas_call x0 -> x9, Pallas kernels: none -> 11.8 us  [the longest x1 4.53 us: pick_adapters(): call(kernel, 'pick_adapters', (pltpu.VMEM(down_shape, down.dtype), pltpu....]
  transfers between devices with their start and end apart: 1 -> 5, of which waited for: 0 -> 1; matrix products, arithmetic and copies ran while one was open for 1% -> 0% of each run, Pallas kernels for 0% -> 6%
where the time goes in v3:
time: 121 us; the launch traced here: 120 us
  local copies, waits for them, and re-layouts  59.4 us (49%)
  blocking collectives  29.3 us (24%)
  starting transfers between devices  15.8 us (13%)
  Pallas kernels  11.8 us (10%)
  other arithmetic  1.78 us (1%)
    unnamed x38, local copies, waits for them, and re-layouts  56.5 us
    all_to_all x2, blocking collectives, exchange(): return lax.all_to_all(blocks, 'mp', split_axis=0, concat_axis=0, tiled=True)  29.3 us
    all_to_all x3, starting transfers between devices, exchange(): return lax.all_to_all(blocks, 'mp', split_axis=0, concat_axis=0, tiled=True)  15.3 us
    pallas_call x1, Pallas kernels, pick_adapters(): call(kernel, 'pick_adapters', (pltpu.VMEM(down_shape, down.dtype), pltpu....  4.53 us
    pallas_call x2, Pallas kernels, multiply(): call(kernel, name, jax.ShapeDtypeStruct((count, weight.shape[1]), out_typ...  4.13 us
  transfers between devices with their start and end apart: 5, of which 1 were waited for; matrix products, arithmetic and copies ran while one was open for 0% of the time, Pallas kernels for 6%

profile of v3, /device:TPU:0, one launch (start us, length us, event | category | flops | bytes accessed | tf_op | source)
XLA Modules:
  0.0 120.1 jit_solution(9952388390942639609)
XLA Ops:
  0.0 9.0 %copy.64.weight_ref = bf16[8192,640]{1,0:T(8,128)(2,1)} copy(bf16[8192,640]{1,0:T(8,128)(2,1)} %param.13) | data formatting | bytes 20971520
  9.0 15.2 %copy.65.weight_ref = bf16[8192,1024]{1,0:T(8,128)(2,1)} copy(bf16[8192,1024]{1,0:T(8,128)(2,1)} %param.14) | data formatting | bytes 33554432
  24.2 0.8 norm_rows.1.after_ref
  25.0 16.9 %all_to_all.25 = bf16[8,2,8320]{2,1,0:T(2,128)(2,1)S(1)} all-to-all(bf16[8,2,8320]{2,1,0:T(2,128)(2,1)S(1)} %norm_rows.1.after_ref), channel_id=1, replica_groups=mesh['groups'=2,'mp'=8,'batch'=2] {'mp'}, dimensions={0} | all-to-all | bytes 532480 | tf_op jit(solution)/shard_map/all_to_all | solution.py:351
  42.0 4.0 %copy-done.5 = bf16[8192,640]{1,0:T(8,128)(2,1)} copy-done((bf16[8192,640]{1,0:T(8,128)(2,1)}, bf16[8192,640]{1,0:T(8,128)(2,1)S(1)}, u32[]{:S(2)}) %copy-start.5) | copy-done | bytes 10485784
  46.1 0.7 pad_maximum_fusion
  47.0 4.0 %copy-done.6 = bf16[8192,640]{1,0:T(8,128)(2,1)S(1)} copy-done((bf16[8192,640]{1,0:T(8,128)(2,1)S(1)}, bf16[8192,640]{1,0:T(8,128)(2,1)}, u32[]{:S(2)}) %copy-start.6) | copy-done | bytes 10485784
  51.0 1.9 %project_qkv.1.after_ref = bf16[32,640]{1,0:T(8,128)(2,1)S(1)} custom-call(bf16[32,8320]{1,0:T(8,128)(2,1)S(1)} %reshape.85.rows_ref, bf16[8192,640]{1,0:T(8,128)(2,1)S(1)} %copy-done.6), custom_call_target="tpu_custom_call" | custom-call | flops 335544320 | bytes 5242880 | tf_op jit(solution)/shard_map/project_qkv/pallas_call | solution.py:225
  52.9 0.6 collective-permute-start.1
  53.6 0.7 collective-permute-done.1
  54.3 0.6 copy.27
  55.0 3.3 %all-to-all-start.1 = ((bf16[8,2,2,640]{3,2,1,0:T(2,128)(2,1)}), bf16[8,2,2,640]{3,2,1,0:T(2,128)(2,1)S(1)}, u32[]{:S(2)}, u32[]{:S(2)}) async-start(bf16[8,2,2,640]{3,2,1,0:T(2,128)(2,1)} %copy.27), calls=%async_computation.1 | async-start | bytes 81920 | tf_op jit(solution)/shard_map/all_to_all | solution.py:351
  58.4 5.8 %copy-done.1 = bf16[8192,1024]{1,0:T(8,128)(2,1)S(1)} copy-done((bf16[8192,1024]{1,0:T(8,128)(2,1)S(1)}, bf16[8192,1024]{1,0:T(8,128)(2,1)}, u32[]{:S(2)}) %copy-start.1) | copy-done | bytes 16777240
  64.2 5.7 %copy-done.2 = bf16[8192,1024]{1,0:T(8,128)(2,1)} copy-done((bf16[8192,1024]{1,0:T(8,128)(2,1)}, bf16[8192,1024]{1,0:T(8,128)(2,1)S(1)}, u32[]{:S(2)}) %copy-start.2) | copy-done | bytes 16777240
  70.5 0.5 fusion.21
  71.2 0.3 fusion.2
  71.5 0.8 broadcast_in_dim.12
  72.4 5.9 %all-to-all-start.2 = ((bf16[8,2,8192]{2,1,0:T(2,128)(2,1)}), bf16[8,2,8192]{2,1,0:T(2,128)(2,1)}, u32[]{:S(2)}, u32[]{:S(2)}) async-start(bf16[8,2,8192]{2,1,0:T(2,128)(2,1)} %broadcast_in_dim.12), calls=%async_computation.2 | async-start | bytes 524288 | tf_op jit(solution)/shard_map/all_to_all | solution.py:351
  78.3 0.2 convert_reduce_fusion
  78.6 3.4 %copy-done.7 = bf16[64,1024,64]{1,2,0:T(8,128)(2,1)S(1)} copy-done((bf16[64,1024,64]{1,2,0:T(8,128)(2,1)S(1)}, bf16[64,1024,64]{1,2,0:T(8,128)(2,1)}, u32[]{:S(2)}) %copy-start.7) | copy-done | bytes 8388632
  82.0 4.5 %pick_adapters.1 = (bf16[16,64,1024]{2,1,0:T(8,128)(2,1)S(1)}, bf16[16,64,1024]{2,1,0:T(8,128)(2,1)S(1)}) custom-call(s32[16]{0:T(128)S(1)} %reshape.99.adapter_ref, bf16[64,64,1024]{2,1,0:T(8,128)(2,1)S(1)} %bitcast.62, bf16[64,64,1024]{2,1,0:T(8,128)(2,1)} %up_ref.1, bf16[2,8192]{1,0:T(2,128)(2,1)S(1)} %bitcast.64), custom_call_target="tpu_custom_call" | custom-call | bytes 4194304 | tf_op jit(solution)/shard_map/pick_adapters/pallas_call | solution.py:253
  86.5 1.3 %copy-done.8 = bf16[16,64,1024]{2,1,0:T(8,128)(2,1)} copy-done((bf16[16,64,1024]{2,1,0:T(8,128)(2,1)}, bf16[16,64,1024]{2,1,0:T(8,128)(2,1)S(1)}, u32[]{:S(2)}) %copy-start.8) | copy-done | bytes 2097176
  87.9 1.0 reshape.93.rows_ref
  88.9 1.6 %copy-done.9 = bf16[16,64,1024]{2,1,0:T(8,128)(2,1)S(1)} copy-done((bf16[16,64,1024]{2,1,0:T(8,128)(2,1)S(1)}, bf16[16,64,1024]{2,1,0:T(8,128)(2,1)}, u32[]{:S(2)}) %copy-start.9) | copy-done | bytes 2097176
  90.5 1.3 %down_partials.1 = f32[8,16,128]{2,1,0:T(8,128)} custom-call(s32[1]{0:T(128)} %bitcast.10.place_ref, bf16[16,8192]{1,0:T(8,128)(2,1)S(1)} %reshape.93.rows_ref, bf16[16,64,1024]{2,1,0:T(8,128)(2,1)S(1)} %copy-done.9), custom_call_target="tpu_custom_call" | custom-call | flops 33554432 | bytes 2097152 | tf_op jit(solution)/shard_map/down_partials/pallas_call | solution.py:284
  91.8 6.0 %all-to-all-start.3 = ((f32[8,16,128]{2,1,0:T(8,128)}), f32[8,16,128]{2,1,0:T(8,128)S(1)}, u32[]{:S(2)}, u32[]{:S(2)}) async-start(f32[8,16,128]{2,1,0:T(8,128)} %down_partials.1), calls=%async_computation.3 | async-start | bytes 131072 | tf_op jit(solution)/shard_map/all_to_all | solution.py:351
  97.8 5.8 %copy-done.3 = bf16[8192,1024]{1,0:T(8,128)(2,1)S(1)} copy-done((bf16[8192,1024]{1,0:T(8,128)(2,1)S(1)}, bf16[8192,1024]{1,0:T(8,128)(2,1)}, u32[]{:S(2)}) %copy-start.3) | copy-done | bytes 16777240
  103.6 2.3 %project_out.1.base_ref = f32[16,1024]{1,0:T(8,128)S(1)} custom-call(bf16[16,8192]{1,0:T(8,128)(2,1)S(1)} %reshape.93.rows_ref, bf16[8192,1024]{1,0:T(8,128)(2,1)S(1)} %copy-done.3), custom_call_target="tpu_custom_call" | custom-call | flops 268435456 | bytes 8388608 | tf_op jit(solution)/shard_map/project_out/pallas_call | solution.py:225
  105.8 0.4 add_up.1
  106.3 12.5 %all_to_all.26.parts_ref = bf16[8,2,1024]{2,1,0:T(2,128)(2,1)S(1)} all-to-all(bf16[8,2,1024]{2,1,0:T(2,128)(2,1)S(1)} %reshape.95), channel_id=1, replica_groups=mesh['groups'=2,'mp'=8,'batch'=2] {'mp'}, dimensions={0} | all-to-all | bytes 65536 | tf_op jit(solution)/shard_map/all_to_all | solution.py:351
  118.7 0.8 copy-done.11
  119.5 0.7 add_rows.1
  (60 shorter events, 1.5 us)
Async XLA Ops:
  0.0 70.5 %copy-start = (bf16[2,256,1024]{2,1,0:T(8,128)(2,1)S(1)}, bf16[2,256,1024]{2,1,0:T(8,128)(2,1)}, u32[]{:S(2)}) copy-start(bf16[2,256,1024]{2,1,0:T(8,128)(2,1)} %param.15) | copy-start | bytes 3145732
  9.0 15.2 %copy-start.10 = (bf16[2,8192]{1,0:T(2,128)(2,1)S(1)}, bf16[2,8192]{1,0:T(2,128)(2,1)}, u32[]{:S(2)}) copy-start(bf16[2,8192]{1,0:T(2,128)(2,1)} %hidden_ref.3) | copy-start | bytes 98308
  9.0 15.2 %copy-start.12 = (bf16[8192]{0:T(1024)(128)(2,1)S(1)}, bf16[8192]{0:T(1024)(128)(2,1)}, u32[]{:S(2)}) copy-start(bf16[8192]{0:T(1024)(128)(2,1)} %param.12) | copy-start | bytes 49156
  9.0 15.2 %copy-start.13 = (s32[2]{0:T(128)S(1)}, s32[2]{0:T(128)}, u32[]{:S(2)}) copy-start(s32[2]{0:T(128)} %slots_ref.1) | copy-start | bytes 28
  9.0 15.2 %copy-start.14 = (s32[1,2]{1,0:T(1,128)S(1)}, s32[1,2]{1,0:T(1,128)}, u32[]{:S(2)}) copy-start(s32[1,2]{1,0:T(1,128)} %requests_ref.1) | copy-start | bytes 28
  9.0 32.9 %copy-start.16 = (s32[2]{0:T(128)S(1)}, s32[2]{0:T(128)}, u32[]{:S(2)}) copy-start(s32[2]{0:T(128)} %param.17) | copy-start | bytes 28
  9.0 32.9 %copy-start.4 = (bf16[8192,640]{1,0:T(8,128)(2,1)S(1)}, bf16[8192,640]{1,0:T(8,128)(2,1)}, u32[]{:S(2)}) copy-start(bf16[8192,640]{1,0:T(8,128)(2,1)} %copy.64.weight_ref) | copy-start | bytes 31457284
  41.9 4.2 %collective-permute-start = (bf16[8,2,8320]{2,1,0:T(2,128)(2,1)S(1)}, bf16[8,2,8320]{2,1,0:T(2,128)(2,1)S(1)}, u32[]{:S(2)}, u32[]{:S(2)}) collective-permute-start(bf16[8,2,8320]{2,1,0:T(2,128)(2,1)S(1)} %all_to_all.25), channel_id=1, source_target_pairs={{0,1},{1,0},{2,3},{3,2},{4,5},{5,4},{6,7},{7,6},{8,9},{9,8},{10,11... | collective-permute-start | bytes 798728 | tf_op jit(solution)/shard_map/ppermute | solution.py:347
  42.0 4.0 %copy-start.5 = (bf16[8192,640]{1,0:T(8,128)(2,1)}, bf16[8192,640]{1,0:T(8,128)(2,1)S(1)}, u32[]{:S(2)}) copy-start(bf16[8192,640]{1,0:T(8,128)(2,1)S(1)} %hold_weight.2.weight_ref) | copy-start | bytes 31457284
  47.0 4.0 %copy-start.6 = (bf16[8192,640]{1,0:T(8,128)(2,1)S(1)}, bf16[8192,640]{1,0:T(8,128)(2,1)}, u32[]{:S(2)}) copy-start(bf16[8192,640]{1,0:T(8,128)(2,1)} %copy-done.5) | copy-start | bytes 31457284
  51.0 20.2 %copy-start.15 = (bf16[2,256,1024]{2,1,0:T(8,128)(2,1)S(1)}, bf16[2,256,1024]{2,1,0:T(8,128)(2,1)}, u32[]{:S(2)}) copy-start(bf16[2,256,1024]{2,1,0:T(8,128)(2,1)} %param.16) | copy-start | bytes 3145732
  52.9 1.4 %collective-permute-start.1 = (bf16[8,2,640]{2,0,1:T(8,128)(2,1)S(1)}, bf16[8,2,640]{2,0,1:T(8,128)(2,1)S(1)}, u32[]{:S(2)}, u32[]{:S(2)}) collective-permute-start(bf16[8,2,640]{2,0,1:T(8,128)(2,1)S(1)} %copy.25), channel_id=1, source_target_pairs={{0,1},{1,0},{2,3},{3,2},{4,5},{5,4},{6,7},{7,6},{8,9},{9,8},{10,11... | collective-permute-start | bytes 61448 | tf_op jit(solution)/shard_map/ppermute | solution.py:347
  55.0 14.9 %all-to-all-start.1 = ((bf16[8,2,2,640]{3,2,1,0:T(2,128)(2,1)}), bf16[8,2,2,640]{3,2,1,0:T(2,128)(2,1)S(1)}, u32[]{:S(2)}, u32[]{:S(2)}) async-start(bf16[8,2,2,640]{3,2,1,0:T(2,128)(2,1)} %copy.27), calls=%async_computation.1 | async-start | bytes 81920 | tf_op jit(solution)/shard_map/all_to_all | solution.py:351
  58.4 5.8 %copy-start.1 = (bf16[8192,1024]{1,0:T(8,128)(2,1)S(1)}, bf16[8192,1024]{1,0:T(8,128)(2,1)}, u32[]{:S(2)}) copy-start(bf16[8192,1024]{1,0:T(8,128)(2,1)} %copy.65.weight_ref) | copy-start | bytes 50331652
  64.2 5.7 %copy-start.2 = (bf16[8192,1024]{1,0:T(8,128)(2,1)}, bf16[8192,1024]{1,0:T(8,128)(2,1)S(1)}, u32[]{:S(2)}) copy-start(bf16[8192,1024]{1,0:T(8,128)(2,1)S(1)} %get-tuple-element.12.weight_ref) | copy-start | bytes 50331652
  72.4 15.5 %all-to-all-start.2 = ((bf16[8,2,8192]{2,1,0:T(2,128)(2,1)}), bf16[8,2,8192]{2,1,0:T(2,128)(2,1)}, u32[]{:S(2)}, u32[]{:S(2)}) async-start(bf16[8,2,8192]{2,1,0:T(2,128)(2,1)} %broadcast_in_dim.12), calls=%async_computation.2 | async-start | bytes 524288 | tf_op jit(solution)/shard_map/all_to_all | solution.py:351
  78.6 3.4 %copy-start.7 = (bf16[64,1024,64]{1,2,0:T(8,128)(2,1)S(1)}, bf16[64,1024,64]{1,2,0:T(8,128)(2,1)}, u32[]{:S(2)}) copy-start(bf16[64,1024,64]{1,2,0:T(8,128)(2,1)} %param.20) | copy-start | bytes 25165828
  86.5 1.3 %copy-start.8 = (bf16[16,64,1024]{2,1,0:T(8,128)(2,1)}, bf16[16,64,1024]{2,1,0:T(8,128)(2,1)S(1)}, u32[]{:S(2)}) copy-start(bf16[16,64,1024]{2,1,0:T(8,128)(2,1)S(1)} %get-tuple-element.13.down_ref) | copy-start | bytes 6291460
  88.9 1.6 %copy-start.9 = (bf16[16,64,1024]{2,1,0:T(8,128)(2,1)S(1)}, bf16[16,64,1024]{2,1,0:T(8,128)(2,1)}, u32[]{:S(2)}) copy-start(bf16[16,64,1024]{2,1,0:T(8,128)(2,1)} %copy-done.8) | copy-start | bytes 6291460
  91.8 14.0 %all-to-all-start.3 = ((f32[8,16,128]{2,1,0:T(8,128)}), f32[8,16,128]{2,1,0:T(8,128)S(1)}, u32[]{:S(2)}, u32[]{:S(2)}) async-start(f32[8,16,128]{2,1,0:T(8,128)} %down_partials.1), calls=%async_computation.3 | async-start | bytes 131072 | tf_op jit(solution)/shard_map/all_to_all | solution.py:351
  97.8 5.8 %copy-start.3 = (bf16[8192,1024]{1,0:T(8,128)(2,1)S(1)}, bf16[8192,1024]{1,0:T(8,128)(2,1)}, u32[]{:S(2)}) copy-start(bf16[8192,1024]{1,0:T(8,128)(2,1)} %copy-done.2) | copy-start | bytes 50331652
  118.7 0.8 copy-start.11

commit v4 on v3

--- a/solution.py
+++ b/solution.py
@@ -143,6 +143,8 @@
 
 MIB = 1 << 20
 LANES = 128
+BATCH = 4
+STREAM = 53 * MIB
 VMEM = pl.BlockSpec(memory_space=pltpu.VMEM)
 SMEM = pl.BlockSpec(memory_space=pltpu.SMEM)
 ANY = pl.BlockSpec(memory_space=pl.ANY)
@@ -161,10 +163,10 @@
     )
 
 
-def norm_rows(hidden, gain, slots, requests, copies):
+def norm_rows(hidden, gain, slots, requests, lengths, copies):
     rows, width = hidden.shape
 
-    def kernel(hidden_ref, gain_ref, slots_ref, requests_ref, out_ref):
+    def kernel(hidden_ref, gain_ref, slots_ref, requests_ref, lengths_ref, out_ref, pos_ref):
         wide = hidden_ref[...].astype(jnp.float32)
         inverse = lax.rsqrt(jnp.mean(wide * wide, -1, keepdims=True) + EPS)
         for k in range(width // LANES):
@@ -181,103 +183,146 @@
             adapter = jnp.where(row == r, chosen, adapter)
         for c in range(copies):
             out_ref[c, :, pl.ds(width, LANES)] = adapter.astype(jnp.bfloat16)
+        position = jnp.zeros((rows, LANES), jnp.float32)
+        for r in range(rows):
+            position = jnp.where(row == r, lengths_ref[r].astype(jnp.float32), position)
+        pos_ref[...] = position
 
     return call(
         kernel,
         "norm_rows",
-        jax.ShapeDtypeStruct((copies, rows, width + LANES), jnp.bfloat16),
-        [VMEM, VMEM, SMEM, SMEM],
+        (
+            jax.ShapeDtypeStruct((copies, rows, width + LANES), jnp.bfloat16),
+            jax.ShapeDtypeStruct((rows, LANES), jnp.float32),
+        ),
+        [VMEM, VMEM, SMEM, SMEM, SMEM],
         hidden.size * 2 * (copies + 1),
-    )(hidden, gain.reshape(-1, LANES), slots, requests)
-
-
-def hold(weight, after, *passed):
-    def kernel(weight_ref, after_ref, *refs):
-        del weight_ref, after_ref
-        for source, target in zip(refs[: len(passed)], refs[len(passed) + 1 :]):
-            target[...] = source[...]
-
-    outs = call(
-        kernel,
-        "hold_weight",
-        (pltpu.VMEM(weight.shape, weight.dtype),)
-        + tuple(jax.ShapeDtypeStruct(p.shape, p.dtype) for p in passed),
-        [VMEM, ANY] + [VMEM] * len(passed),
+    )(hidden, gain.reshape(-1, LANES), slots, requests, lengths)
+
+
+def stream(weight_ref, held_ref, sems, parts):
+    depth = held_ref.shape[0] // parts
+    copies = []
+    for k in range(parts):
+        rows = pl.ds(k * depth, depth)
+        copies.append(
+            pltpu.make_async_copy(weight_ref.at[rows], held_ref.at[rows], sems.at[k])
+        )
+        copies[-1].start()
+
+    def part(k):
+        copies[k].wait()
+        return held_ref[pl.ds(k * depth, depth)]
+
+    return part
+
+
+def project_qkv(near, far, weight, core, parts=16):
+    groups, rows, _ = near.shape
+    depth, width = weight.shape
+    count, step = 2 * groups * rows, weight.shape[0] // parts
+
+    def kernel(core_ref, near_ref, far_ref, weight_ref, out_ref, rows_ref, held_ref, sems):
+        part = stream(weight_ref, held_ref, sems, parts)
+        for e, source in enumerate((near_ref, far_ref)):
+            for j in range(groups):
+                place = pl.ds((e * groups + j) * rows, rows)
+                rows_ref[place] = source[j, :, pl.ds(0, depth)]
+        total = jnp.zeros((count, width), jnp.float32)
+        for k in range(parts):
+            total = total + jnp.dot(
+                rows_ref[:, pl.ds(k * step, step)], part(k), preferred_element_type=jnp.float32
+            )
+        for e in range(2):
+            for j in range(groups):
+                place = (e * groups + j) * rows
+                out_ref[2 * j + (core_ref[0] ^ e)] = total[place : place + rows].astype(
+                    jnp.bfloat16
+                )
+
+    return call(
+        kernel,
+        "project_qkv",
+        jax.ShapeDtypeStruct((2 * groups, rows, width), jnp.bfloat16),
+        [SMEM, VMEM, VMEM, ANY],
         weight.size * 2,
-        limit=MIB,
-        input_output_aliases={0: 0},
-    )(weight, after, *passed)
-    return outs if passed else outs[0]
-
-
-def multiply(rows, weight, out_type, name, chunk=1024):
-    count, depth = rows.shape[0], weight.shape[0]
-
-    def kernel(rows_ref, weight_ref, out_ref):
-        total = jnp.zeros((count, weight.shape[1]), jnp.float32)
-        for k in range(depth // chunk):
-            part = pl.ds(k * chunk, chunk)
+        limit=STREAM,
+        flops=2 * count * weight.size,
+        scratch_shapes=[
+            pltpu.VMEM((count, depth), jnp.bfloat16),
+            pltpu.VMEM(weight.shape, weight.dtype),
+            pltpu.SemaphoreType.DMA((parts,)),
+        ],
+    )(core, near, far, weight)
+
+
+def project_out(rows, weight, parts=16):
+    count, step = rows.shape[0], weight.shape[0] // parts
+
+    def kernel(rows_ref, weight_ref, out_ref, held_ref, sems):
+        part = stream(weight_ref, held_ref, sems, parts)
+        total = jnp.zeros(out_ref.shape, jnp.float32)
+        for k in range(parts):
             total = total + jnp.dot(
-                rows_ref[:, part], weight_ref[part, :], preferred_element_type=jnp.float32
+                rows_ref[:, pl.ds(k * step, step)], part(k), preferred_element_type=jnp.float32
             )
-        out_ref[...] = total.astype(out_type)
-
-    return call(
-        kernel,
-        name,
-        jax.ShapeDtypeStruct((count, weight.shape[1]), out_type),
-        [VMEM, VMEM],
-        weight.size,
+        out_ref[...] = total
+
+    return call(
+        kernel,
+        "project_out",
+        jax.ShapeDtypeStruct((count, weight.shape[1]), jnp.float32),
+        [VMEM, ANY],
+        weight.size * 2,
+        limit=STREAM,
         flops=2 * count * weight.size,
+        scratch_shapes=[
+            pltpu.VMEM(weight.shape, weight.dtype),
+            pltpu.SemaphoreType.DMA((parts,)),
+        ],
     )(rows, weight)
 
 
-def pick_adapters(adapter, down, up, after):
-    count, rank = adapter.shape[0], up.shape[1]
-    down_shape, up_shape = (count,) + down.shape[1:], (count,) + up.shape[1:]
-
-    def kernel(adapter_ref, down_ref, up_ref, after_ref, down_out, up_out, sems):
-        del after_ref
-        copies = []
-        for r in range(count):
-            chosen = adapter_ref[r]
-            copies.append(
-                pltpu.make_async_copy(down_ref.at[chosen], down_out.at[r], sems.at[0, r])
+def pick(adapter_ref, store_ref, held_ref, sems):
+    count, rank = adapter_ref.shape[0], store_ref.shape[1]
+    copies = []
+    for r in range(count):
+        copies.append(
+            pltpu.make_async_copy(
+                store_ref.at[adapter_ref[r]], held_ref.at[pl.ds(r * rank, rank)], sems.at[r]
             )
-            copies.append(pltpu.make_async_copy(up_ref.at[chosen], up_out.at[r], sems.at[1, r]))
-        for copy in copies:
-            copy.start()
-        for copy in copies:
+        )
+        copies[-1].start()
+
+    def batch(k):
+        for copy in copies[k * BATCH : (k + 1) * BATCH]:
             copy.wait()
-
-    return call(
-        kernel,
-        "pick_adapters",
-        (pltpu.VMEM(down_shape, down.dtype), pltpu.VMEM(up_shape, up.dtype)),
-        [SMEM, ANY, ANY, ANY],
-        2 * count * rank * (down.shape[2] + up.shape[2]),
-        limit=36 * MIB,
-        scratch_shapes=[pltpu.SemaphoreType.DMA((2, count))],
-    )(adapter, down, up, after)
-
-
-def down_partials(rows, place, down, copies):
-    count, rank, depth = down.shape
-
-    def kernel(place_ref, rows_ref, down_ref, out_ref):
-        start = pl.multiple_of(place_ref[0] * depth, depth)
-        every = lax.dot_general(
-            rows_ref[:, pl.ds(start, depth)],
-            down_ref[...].reshape(count * rank, depth),
-            (((1,), (1,)), ((), ())),
-            preferred_element_type=jnp.float32,
-        )
+        return held_ref[pl.ds(k * BATCH * rank, BATCH * rank)]
+
+    return batch
+
+
+def down_partials(rows, place, adapter, store, copies):
+    count = adapter.shape[0]
+    rank, depth = store.shape[1:]
+
+    def kernel(place_ref, adapter_ref, rows_ref, store_ref, out_ref, held_ref, sems):
+        batch = pick(adapter_ref, store_ref, held_ref, sems)
+        slices = rows_ref[:, pl.ds(pl.multiple_of(place_ref[0] * depth, depth), depth)]
         row = lax.broadcasted_iota(jnp.int32, (count, LANES), 0)
         lane = lax.broadcasted_iota(jnp.int32, (count, LANES), 1)
         total = jnp.zeros((count, LANES), jnp.float32)
-        for s in range(count * rank // LANES):
-            mine = row == (lane + s * LANES) // rank
-            total = total + jnp.where(mine, every[:, s * LANES : (s + 1) * LANES], 0.0)
+        for k in range(count // BATCH):
+            every = lax.dot_general(
+                slices,
+                batch(k),
+                (((1,), (1,)), ((), ())),
+                preferred_element_type=jnp.float32,
+            )
+            for s in range(BATCH * rank // LANES):
+                first = k * BATCH * rank + s * LANES
+                mine = row == (lane + first) // rank
+                total = total + jnp.where(mine, every[:, s * LANES : (s + 1) * LANES], 0.0)
         for c in range(copies):
             out_ref[c] = total
 
@@ -285,44 +330,66 @@
         kernel,
         "down_partials",
         jax.ShapeDtypeStruct((copies, count, LANES), jnp.float32),
-        [SMEM, VMEM, VMEM],
-        down.size * 2,
-        limit=4 * MIB,
-        flops=2 * count * down.size,
-    )(place, rows, down)
-
-
-def add_up(base, partials, up):
-    count, rank, width = up.shape
-
-    def kernel(base_ref, partials_ref, up_ref, out_ref):
+        [SMEM, SMEM, VMEM, ANY],
+        2 * count * rank * depth,
+        limit=STREAM,
+        flops=2 * count * count * rank * depth,
+        scratch_shapes=[
+            pltpu.VMEM((count * rank, depth), store.dtype),
+            pltpu.SemaphoreType.DMA((count,)),
+        ],
+    )(place, adapter, rows, store)
+
+
+def add_up(base, partials, adapter, store):
+    count = adapter.shape[0]
+    rank, width = store.shape[1:]
+
+    def kernel(adapter_ref, base_ref, partials_ref, store_ref, out_ref, held_ref, sems):
+        batch = pick(adapter_ref, store_ref, held_ref, sems)
         total = partials_ref[0]
         for c in range(1, partials.shape[0]):
             total = total + partials_ref[c]
         down = total.astype(jnp.bfloat16).astype(jnp.float32)
         row = lax.broadcasted_iota(jnp.int32, (count, LANES), 0)
         lane = lax.broadcasted_iota(jnp.int32, (count, LANES), 1)
-        spread = jnp.concatenate(
-            [
-                jnp.where(row == (lane + s * LANES) // rank, down, 0.0)
-                for s in range(count * rank // LANES)
-            ],
-            1,
-        ).astype(jnp.bfloat16)
-        delta = jnp.dot(
-            spread, up_ref[...].reshape(count * rank, width), preferred_element_type=jnp.float32
-        )
+        delta = jnp.zeros((count, width), jnp.float32)
+        for k in range(count // BATCH):
+            spread = []
+            for s in range(BATCH * rank // LANES):
+                first = k * BATCH * rank + s * LANES
+                spread.append(jnp.where(row == (lane + first) // rank, down, 0.0))
+            spread = jnp.concatenate(spread, 1).astype(jnp.bfloat16)
+            delta = delta + jnp.dot(spread, batch(k), preferred_element_type=jnp.float32)
         out_ref[...] = (base_ref[...] + ADAPTER_SCALE * delta).astype(jnp.bfloat16)
 
     return call(
         kernel,
         "add_up",
         jax.ShapeDtypeStruct((count, width), jnp.bfloat16),
-        [VMEM, VMEM, VMEM],
-        up.size * 2,
-        limit=4 * MIB,
-        flops=2 * count * up.size,
-    )(base, partials, up)
+        [SMEM, VMEM, VMEM, ANY],
+        2 * count * rank * width,
+        limit=STREAM,
+        flops=2 * count * count * rank * width,
+        scratch_shapes=[
+            pltpu.VMEM((count * rank, width), store.dtype),
+            pltpu.SemaphoreType.DMA((count,)),
+        ],
+    )(adapter, base, partials, store)
+
+
+def widen(hidden, after):
+    def kernel(hidden_ref, after_ref, out_ref):
+        del after_ref
+        out_ref[...] = hidden_ref[...].astype(jnp.float32)
+
+    return call(
+        kernel,
+        "widen",
+        jax.ShapeDtypeStruct(hidden.shape, jnp.float32),
+        [VMEM, ANY],
+        hidden.size * 64,
+    )(hidden, after)
 
 
 def add_rows(hidden, parts):
@@ -331,13 +398,13 @@
     def kernel(hidden_ref, parts_ref, out_ref):
         for k in range(parts.shape[0]):
             part = pl.ds(k * width, width)
-            total = hidden_ref[:, part].astype(jnp.float32) + parts_ref[k].astype(jnp.float32)
+            total = hidden_ref[:, part] + parts_ref[k].astype(jnp.float32)
             out_ref[:, part] = total.astype(jnp.bfloat16)
 
     return call(
         kernel,
         "add_rows",
-        jax.ShapeDtypeStruct(hidden.shape, hidden.dtype),
+        jax.ShapeDtypeStruct(hidden.shape, parts.dtype),
         [VMEM, VMEM],
         hidden.size * 6,
     )(hidden, parts)
@@ -347,8 +414,8 @@
     return lax.ppermute(block, "batch", [(0, 1), (1, 0)])
 
 
-def exchange(blocks):
-    return lax.all_to_all(blocks, "mp", split_axis=0, concat_axis=0, tiled=True)
+def exchange(blocks, axes="mp"):
+    return lax.all_to_all(blocks, axes, split_axis=0, concat_axis=0, tiled=True)
 
 
 def attend(qkv, cosine, sine, key_cache, value_cache, lengths):
@@ -395,10 +462,10 @@
     return context_vector.reshape(rows, query_width).astype(jnp.bfloat16)
 
 
-def angles(lengths):
+def angles(positions):
     half = HEAD_DIM // 2
     freq = THETA ** (-(jnp.arange(half, dtype=jnp.float32) * 2.0) / HEAD_DIM)
-    angle = lengths.astype(jnp.float32)[:, None] * freq
+    angle = positions[:, :half] * freq
     cosine, sine = jnp.cos(angle), jnp.sin(angle)
     return jnp.concatenate([cosine, cosine], -1), jnp.concatenate([sine, sine], -1)
 
@@ -418,37 +485,31 @@
 ):
     rows, features = hidden.shape
     mp_size = lax.axis_size("mp")
-    width = query_key_value_weight.shape[1]
-    cosine, sine = angles(lengths)
-
-    sent = norm_rows(hidden, attention_norm_gain, slots, requests, mp_size)
+    core = lax.axis_index("batch").astype(jnp.int32).reshape(1)
+    place = lax.axis_index("mp").astype(jnp.int32).reshape(1)
+
+    sent, positions = norm_rows(
+        hidden, attention_norm_gain, slots, requests, lengths, mp_size
+    )
+    cosine, sine = angles(positions)
     near = exchange(sent)
-    far = swap_cores(near)
-    held_weight = hold(query_key_value_weight, sent)
     adapter = near[:, :, features].reshape(-1).astype(jnp.int32)
-    normed = jnp.concatenate([near, far]).reshape(-1, features + LANES)
-    columns = multiply(normed, held_weight, jnp.bfloat16, "project_qkv")
-
-    split = columns.reshape(2, mp_size, rows, width)
-    mixed = jnp.stack([split[0], swap_cores(split[1])], 1)
-    mixed = exchange(mixed)
-    held_weight, cosine, sine = hold(output_weight, columns, cosine, sine)
-    mixed = jnp.where(lax.axis_index("batch") == 0, mixed, mixed[:, ::-1])
-    qkv = mixed.transpose(2, 0, 1, 3).reshape(rows, -1)
+    mixed = exchange(
+        project_qkv(near, swap_cores(near), query_key_value_weight, core), ("mp", "batch")
+    )
+    qkv = mixed.transpose(1, 0, 2).reshape(rows, -1)
 
     context = attend(qkv, cosine, sine, key_cache, value_cache, lengths)
-    picked_down, picked_up = pick_adapters(
-        adapter, adapter_down_matrices.swapaxes(1, 2), adapter_up_matrices, context
-    )
     copies = jnp.broadcast_to(context[None], (mp_size, *context.shape))
     gathered = exchange(copies).reshape(-1, context.shape[1])
 
-    place = lax.axis_index("mp").astype(jnp.int32).reshape(1)
-    partials = exchange(down_partials(gathered, place, picked_down, mp_size))
-    base = multiply(gathered, held_weight, jnp.float32, "project_out")
-    projected = add_up(base, partials, picked_up)
+    partials = exchange(
+        down_partials(gathered, place, adapter, adapter_down_matrices.swapaxes(1, 2), mp_size)
+    )
+    base = project_out(gathered, output_weight)
+    projected = add_up(base, partials, adapter, adapter_up_matrices)
     returned = exchange(projected.reshape(mp_size, rows, -1))
-    return add_rows(hidden, returned)
+    return add_rows(widen(hidden, projected), returned)
 
 
 def body(*arguments):

time: 121 us -> 84.8 us (0.70)
  local copies, waits for them, and re-layouts: 59.4 us -> 5.23 us
  waiting for transfers between devices: 0.75 us -> 32.4 us
  blocking collectives: 29.3 us -> 0 us
  Pallas kernels: 11.8 us -> 20.5 us
  starting transfers between devices: 15.8 us -> 23.2 us
    unnamed x38 -> x18, local copies, waits for them, and re-layouts: 56.5 us -> 3.59 us
    all_to_all x3 -> x5, waiting for transfers between devices: 0.01 us -> 30.9 us  [exchange(): return lax.all_to_all(blocks, axes, split_axis=0, concat_axis=0, tiled=True)]
    all_to_all x2 -> x0, blocking collectives: 29.3 us -> none  [exchange(): return lax.all_to_all(blocks, 'mp', split_axis=0, concat_axis=0, tiled=True)]
    all_to_all x3 -> x5, starting transfers between devices: 15.3 us -> 23.2 us  [exchange(): return lax.all_to_all(blocks, axes, split_axis=0, concat_axis=0, tiled=True)]
    pallas_call x7 -> x5, Pallas kernels: 10.2 us -> 14 us  [the longest x1 6.19 us: project_out(): call(kernel, 'project_out', jax.ShapeDtypeStruct((count, weight.shape[1])...]
    pallas_call x1, Pallas kernels: 1.28 us -> 3.98 us  [down_partials(): call(kernel, 'down_partials', jax.ShapeDtypeStruct((copies, count, LANES)...]
    pallas_call x1, Pallas kernels: 0.4 us -> 2.5 us  [add_up(): call(kernel, 'add_up', jax.ShapeDtypeStruct((count, width), jnp.bfloat16)...]
  transfers between devices with their start and end apart: 5 -> 6, of which waited for: 1 -> 6; matrix products, arithmetic and copies ran while one was open for 0% -> 1% of each run, Pallas kernels for 6% -> 7%
where the time goes in v4:
time: 84.8 us; the launch traced here: 84.1 us
  waiting for transfers between devices  32.4 us (38%)
  starting transfers between devices  23.2 us (27%)
  Pallas kernels  20.5 us (24%)
  local copies, waits for them, and re-layouts  5.23 us (6%)
  other arithmetic  1.63 us (2%)
  matrix products  0.9 us (1%)
    all_to_all x5, waiting for transfers between devices, exchange(): return lax.all_to_all(blocks, axes, split_axis=0, concat_axis=0, tiled=True)  30.9 us
    all_to_all x5, starting transfers between devices, exchange(): return lax.all_to_all(blocks, axes, split_axis=0, concat_axis=0, tiled=True)  23.2 us
    pallas_call x1, Pallas kernels, project_out(): call(kernel, 'project_out', jax.ShapeDtypeStruct((count, weight.shape[1])...  6.19 us
    pallas_call x1, Pallas kernels, project_qkv(): call(kernel, 'project_qkv', jax.ShapeDtypeStruct((2 * groups, rows, width...  5.63 us
    pallas_call x1, Pallas kernels, down_partials(): call(kernel, 'down_partials', jax.ShapeDtypeStruct((copies, count, LANES)...  3.98 us
    unnamed x18, local copies, waits for them, and re-layouts  3.59 us
    pallas_call x1, Pallas kernels, add_up(): call(kernel, 'add_up', jax.ShapeDtypeStruct((count, width), jnp.bfloat16)...  2.5 us
  transfers between devices with their start and end apart: 6, of which 6 were waited for; matrix products, arithmetic and copies ran while one was open for 1% of the time, Pallas kernels for 7%

profile of v4, /device:TPU:0, one launch (start us, length us, event | category | flops | bytes accessed | tf_op | source)
XLA Modules:
  0.0 84.1 jit_solution(15409766321236656066)
XLA Ops:
  0.0 0.8 %copy-done.1 = bf16[2,8192]{1,0:T(2,128)(2,1)S(1)} copy-done((bf16[2,8192]{1,0:T(2,128)(2,1)S(1)}, bf16[2,8192]{1,0:T(2,128)(2,1)}, u32[]{:S(2)}) %copy-start.1) | copy-done | bytes 32792
  0.9 0.7 copy-done.3
  1.6 0.7 copy-done.4
  2.2 0.7 copy-done.5
  2.9 0.7 copy-done.6
  3.5 1.5 %norm_rows.1 = (bf16[8,2,8320]{2,1,0:T(2,128)(2,1)}, f32[2,128]{1,0:T(2,128)S(1)}) custom-call(bf16[2,8192]{1,0:T(2,128)(2,1)S(1)} %copy-done.1, bf16[64,128]{1,0:T(8,128)(2,1)S(1)} %bitcast.62, s32[2]{0:T(128)S(1)} %copy-done.4, s32[1,2]{1,0:T(1,128)S(1)} %copy-done.5, s32[2]{0:T(128)S(1)} %copy-done.6), custom_call_target="tpu_custom_call" | custom-call | bytes 294912 | tf_op jit(solution)/shard_map/norm_rows/pallas_call | solution.py:191
  5.1 7.3 %all-to-all-start = ((bf16[8,2,8320]{2,1,0:T(2,128)(2,1)}), bf16[8,2,8320]{2,1,0:T(2,128)(2,1)S(1)}, u32[]{:S(2)}, u32[]{:S(2)}) async-start(bf16[8,2,8320]{2,1,0:T(2,128)(2,1)} %get-tuple-element.7), calls=%async_computation | async-start | bytes 532480 | tf_op jit(solution)/shard_map/all_to_all | solution.py:418
  12.3 0.7 iota_compare_fusion
  13.1 8.3 %all-to-all-done.near_ref = bf16[8,2,8320]{2,1,0:T(2,128)(2,1)S(1)} async-done(((bf16[8,2,8320]{2,1,0:T(2,128)(2,1)}), bf16[8,2,8320]{2,1,0:T(2,128)(2,1)S(1)}, u32[]{:S(2)}, u32[]{:S(2)}) %all-to-all-start) | async-done | bytes 266272 | tf_op jit(solution)/shard_map/all_to_all | solution.py:418
  21.4 1.5 %collective-permute-done.far_ref = bf16[8,2,8320]{2,1,0:T(2,128)(2,1)S(1)} collective-permute-done((bf16[8,2,8320]{2,1,0:T(2,128)(2,1)S(1)}, bf16[8,2,8320]{2,1,0:T(2,128)(2,1)S(1)}, u32[]{:S(2)}, u32[]{:S(2)}) %collective-permute-start) | collective-permute-done | bytes 266272 | tf_op jit(solution)/shard_map/ppermute | solution.py:414
  22.9 5.6 %project_qkv.1 = bf16[16,2,640]{2,1,0:T(2,128)(2,1)} custom-call(s32[1]{0:T(128)} %bitcast.1.core_ref, bf16[8,2,8320]{2,1,0:T(2,128)(2,1)S(1)} %all-to-all-done.near_ref, bf16[8,2,8320]{2,1,0:T(2,128)(2,1)S(1)} %collective-permute-done.far_ref, bf16[8192,640]{1,0:T(8,128)(2,1)} %weight_ref.2), custom_call_target="tpu_custom_call" | custom-call | flops 335544320 | bytes 10485760 | tf_op jit(solution)/shard_map/project_qkv/pallas_call | solution.py:243
  28.5 3.7 %all-to-all-start.1 = ((bf16[16,2,640]{2,1,0:T(2,128)(2,1)}), bf16[16,2,640]{2,1,0:T(2,128)(2,1)S(1)}, u32[]{:S(2)}, u32[]{:S(2)}) async-start(bf16[16,2,640]{2,1,0:T(2,128)(2,1)} %project_qkv.1), calls=%async_computation.1 | async-start | bytes 81920 | tf_op jit(solution)/shard_map/all_to_all | solution.py:418
  32.3 6.6 %all-to-all-done.1 = bf16[16,2,640]{2,1,0:T(2,128)(2,1)S(1)} async-done(((bf16[16,2,640]{2,1,0:T(2,128)(2,1)}), bf16[16,2,640]{2,1,0:T(2,128)(2,1)S(1)}, u32[]{:S(2)}, u32[]{:S(2)}) %all-to-all-start.1) | async-done | bytes 40992 | tf_op jit(solution)/shard_map/all_to_all | solution.py:418
  39.2 0.1 fusion.9
  39.3 0.1 fusion.15
  39.5 0.5 fusion.22
  39.9 0.2 fusion.7
  40.2 0.3 fusion.2
  40.5 0.8 broadcast_in_dim.16
  41.4 3.4 %all-to-all-start.2 = ((bf16[8,2,8192]{2,1,0:T(2,128)(2,1)}), bf16[8,2,8192]{2,1,0:T(2,128)(2,1)S(1)}, u32[]{:S(2)}, u32[]{:S(2)}) async-start(bf16[8,2,8192]{2,1,0:T(2,128)(2,1)} %broadcast_in_dim.16), calls=%async_computation.2 | async-start | bytes 524288 | tf_op jit(solution)/shard_map/all_to_all | solution.py:418
  44.8 0.2 convert_reduce_fusion
  45.1 8.7 %all-to-all-done.2 = bf16[8,2,8192]{2,1,0:T(2,128)(2,1)S(1)} async-done(((bf16[8,2,8192]{2,1,0:T(2,128)(2,1)}), bf16[8,2,8192]{2,1,0:T(2,128)(2,1)S(1)}, u32[]{:S(2)}, u32[]{:S(2)}) %all-to-all-start.2) | async-done | bytes 262176 | tf_op jit(solution)/shard_map/all_to_all | solution.py:418
  53.7 0.1 reshape.87.rows_ref
  53.8 4.0 %down_partials.1 = f32[8,16,128]{2,1,0:T(8,128)} custom-call(s32[1]{0:T(128)} %bitcast.10.place_ref, s32[16]{0:T(128)S(1)} %reshape.90.adapter_ref, bf16[16,8192]{1,0:T(8,128)(2,1)S(1)} %reshape.87.rows_ref, bf16[64,64,1024]{2,1,0:T(8,128)(2,1)} %bitcast.63), custom_call_target="tpu_custom_call" | custom-call | flops 33554432 | bytes 2097152 | tf_op jit(solution)/shard_map/down_partials/pallas_call | solution.py:329
  57.8 3.6 %all-to-all-start.3 = ((f32[8,16,128]{2,1,0:T(8,128)}), f32[8,16,128]{2,1,0:T(8,128)S(1)}, u32[]{:S(2)}, u32[]{:S(2)}) async-start(f32[8,16,128]{2,1,0:T(8,128)} %down_partials.1), calls=%async_computation.3 | async-start | bytes 131072 | tf_op jit(solution)/shard_map/all_to_all | solution.py:418
  61.4 6.2 %project_out.1.base_ref = f32[16,1024]{1,0:T(8,128)S(1)} custom-call(bf16[16,8192]{1,0:T(8,128)(2,1)S(1)} %reshape.87.rows_ref, bf16[8192,1024]{1,0:T(8,128)(2,1)} %weight_ref.3), custom_call_target="tpu_custom_call" | custom-call | flops 268435456 | bytes 16777216 | tf_op jit(solution)/shard_map/project_out/pallas_call | solution.py:271
  67.6 0.7 all-to-all-done.3.partials_ref
  68.3 2.5 %add_up.1.after_ref = bf16[16,1024]{1,0:T(8,128)(2,1)S(1)} custom-call(s32[16]{0:T(128)S(1)} %reshape.90.adapter_ref, f32[16,1024]{1,0:T(8,128)S(1)} %project_out.1.base_ref, f32[8,16,128]{2,1,0:T(8,128)S(1)} %all-to-all-done.3.partials_ref, bf16[64,64,1024]{2,1,0:T(8,128)(2,1)} %store_ref.1), custom_call_target="tpu_custom_call" | custom-call | flops 33554432 | bytes 2097152 | tf_op jit(solution)/shard_map/add_up/pallas_call | solution.py:366
  70.8 0.6 reshape.89
  71.4 5.3 %all-to-all-start.4 = ((bf16[8,2,1024]{2,1,0:T(2,128)(2,1)}), bf16[8,2,1024]{2,1,0:T(2,128)(2,1)S(1)}, u32[]{:S(2)}, u32[]{:S(2)}) async-start(bf16[8,2,1024]{2,1,0:T(2,128)(2,1)} %reshape.89), calls=%async_computation.4 | async-start | bytes 65536 | tf_op jit(solution)/shard_map/all_to_all | solution.py:418
  76.8 6.7 %all-to-all-done.4.parts_ref = bf16[8,2,1024]{2,1,0:T(2,128)(2,1)S(1)} async-done(((bf16[8,2,1024]{2,1,0:T(2,128)(2,1)}), bf16[8,2,1024]{2,1,0:T(2,128)(2,1)S(1)}, u32[]{:S(2)}, u32[]{:S(2)}) %all-to-all-start.4) | async-done | bytes 32800 | tf_op jit(solution)/shard_map/all_to_all | solution.py:418
  83.4 0.7 add_rows.1
  (27 shorter events, 0.6 us)
Async XLA Ops:
  0.0 39.5 %copy-start = (bf16[2,256,1024]{2,1,0:T(8,128)(2,1)S(1)}, bf16[2,256,1024]{2,1,0:T(8,128)(2,1)}, u32[]{:S(2)}) copy-start(bf16[2,256,1024]{2,1,0:T(8,128)(2,1)} %param.15) | copy-start | bytes 3145732
  0.0 0.8 %copy-start.1 = (bf16[2,8192]{1,0:T(2,128)(2,1)S(1)}, bf16[2,8192]{1,0:T(2,128)(2,1)}, u32[]{:S(2)}) copy-start(bf16[2,8192]{1,0:T(2,128)(2,1)} %hidden_ref.3) | copy-start | bytes 98308
  0.9 0.7 copy-start.3
  1.6 0.7 copy-start.4
  2.2 0.7 copy-start.5
  2.9 0.7 copy-start.6
  3.5 36.6 %copy-start.7 = (bf16[2,256,1024]{2,1,0:T(8,128)(2,1)S(1)}, bf16[2,256,1024]{2,1,0:T(8,128)(2,1)}, u32[]{:S(2)}) copy-start(bf16[2,256,1024]{2,1,0:T(8,128)(2,1)} %param.16) | copy-start | bytes 3145732
  5.1 16.3 %all-to-all-start = ((bf16[8,2,8320]{2,1,0:T(2,128)(2,1)}), bf16[8,2,8320]{2,1,0:T(2,128)(2,1)S(1)}, u32[]{:S(2)}, u32[]{:S(2)}) async-start(bf16[8,2,8320]{2,1,0:T(2,128)(2,1)} %get-tuple-element.7), calls=%async_computation | async-start | bytes 532480 | tf_op jit(solution)/shard_map/all_to_all | solution.py:418
  21.3 1.5 %collective-permute-start = (bf16[8,2,8320]{2,1,0:T(2,128)(2,1)S(1)}, bf16[8,2,8320]{2,1,0:T(2,128)(2,1)S(1)}, u32[]{:S(2)}, u32[]{:S(2)}) collective-permute-start(bf16[8,2,8320]{2,1,0:T(2,128)(2,1)S(1)} %all-to-all-done.near_ref), channel_id=1, source_target_pairs={{0,1},{1,0},{2,3},{3,2},{4,5},{5,4},{6,7},{7,6},{8,9},{9,8},{10,11... | collective-permute-start | bytes 798728 | tf_op jit(solution)/shard_map/ppermute | solution.py:414
  28.5 10.4 %all-to-all-start.1 = ((bf16[16,2,640]{2,1,0:T(2,128)(2,1)}), bf16[16,2,640]{2,1,0:T(2,128)(2,1)S(1)}, u32[]{:S(2)}, u32[]{:S(2)}) async-start(bf16[16,2,640]{2,1,0:T(2,128)(2,1)} %project_qkv.1), calls=%async_computation.1 | async-start | bytes 81920 | tf_op jit(solution)/shard_map/all_to_all | solution.py:418
  41.4 12.4 %all-to-all-start.2 = ((bf16[8,2,8192]{2,1,0:T(2,128)(2,1)}), bf16[8,2,8192]{2,1,0:T(2,128)(2,1)S(1)}, u32[]{:S(2)}, u32[]{:S(2)}) async-start(bf16[8,2,8192]{2,1,0:T(2,128)(2,1)} %broadcast_in_dim.16), calls=%async_computation.2 | async-start | bytes 524288 | tf_op jit(solution)/shard_map/all_to_all | solution.py:418
  57.8 10.5 %all-to-all-start.3 = ((f32[8,16,128]{2,1,0:T(8,128)}), f32[8,16,128]{2,1,0:T(8,128)S(1)}, u32[]{:S(2)}, u32[]{:S(2)}) async-start(f32[8,16,128]{2,1,0:T(8,128)} %down_partials.1), calls=%async_computation.3 | async-start | bytes 131072 | tf_op jit(solution)/shard_map/all_to_all | solution.py:418
  61.4 15.4 %copy-start.2 = (bf16[2,8192]{1,0:T(2,128)(2,1)S(1)}, bf16[2,8192]{1,0:T(2,128)(2,1)}, u32[]{:S(2)}) copy-start(bf16[2,8192]{1,0:T(2,128)(2,1)} %hidden_ref.3) | copy-start | bytes 98308
  71.4 12.0 %all-to-all-start.4 = ((bf16[8,2,1024]{2,1,0:T(2,128)(2,1)}), bf16[8,2,1024]{2,1,0:T(2,128)(2,1)S(1)}, u32[]{:S(2)}, u32[]{:S(2)}) async-start(bf16[8,2,1024]{2,1,0:T(2,128)(2,1)} %reshape.89), calls=%async_computation.4 | async-start | bytes 65536 | tf_op jit(solution)/shard_map/all_to_all | solution.py:418

commit v5 on v4

--- a/solution.py
+++ b/solution.py
@@ -144,7 +144,6 @@
 MIB = 1 << 20
 LANES = 128
 BATCH = 4
-STREAM = 53 * MIB
 VMEM = pl.BlockSpec(memory_space=pltpu.VMEM)
 SMEM = pl.BlockSpec(memory_space=pltpu.SMEM)
 ANY = pl.BlockSpec(memory_space=pl.ANY)
@@ -163,10 +162,10 @@
     )
 
 
-def norm_rows(hidden, gain, slots, requests, lengths, copies):
+def norm_rows(hidden, gain, copies):
     rows, width = hidden.shape
 
-    def kernel(hidden_ref, gain_ref, slots_ref, requests_ref, lengths_ref, out_ref, pos_ref):
+    def kernel(hidden_ref, gain_ref, out_ref):
         wide = hidden_ref[...].astype(jnp.float32)
         inverse = lax.rsqrt(jnp.mean(wide * wide, -1, keepdims=True) + EPS)
         for k in range(width // LANES):
@@ -176,95 +175,61 @@
             normed = normed.astype(jnp.bfloat16)
             for c in range(copies):
                 out_ref[c, :, part] = normed
-        row = lax.broadcasted_iota(jnp.int32, (rows, LANES), 0)
-        adapter = jnp.zeros((rows, LANES), jnp.float32)
-        for r in range(rows):
-            chosen = requests_ref[0, slots_ref[r]].astype(jnp.float32)
-            adapter = jnp.where(row == r, chosen, adapter)
-        for c in range(copies):
-            out_ref[c, :, pl.ds(width, LANES)] = adapter.astype(jnp.bfloat16)
-        position = jnp.zeros((rows, LANES), jnp.float32)
-        for r in range(rows):
-            position = jnp.where(row == r, lengths_ref[r].astype(jnp.float32), position)
-        pos_ref[...] = position
 
     return call(
         kernel,
         "norm_rows",
-        (
-            jax.ShapeDtypeStruct((copies, rows, width + LANES), jnp.bfloat16),
-            jax.ShapeDtypeStruct((rows, LANES), jnp.float32),
-        ),
-        [VMEM, VMEM, SMEM, SMEM, SMEM],
+        jax.ShapeDtypeStruct((copies, rows, width), jnp.bfloat16),
+        [VMEM, VMEM],
         hidden.size * 2 * (copies + 1),
-    )(hidden, gain.reshape(-1, LANES), slots, requests, lengths)
-
-
-def stream(weight_ref, held_ref, sems, parts):
-    depth = held_ref.shape[0] // parts
-    copies = []
-    for k in range(parts):
-        rows = pl.ds(k * depth, depth)
-        copies.append(
-            pltpu.make_async_copy(weight_ref.at[rows], held_ref.at[rows], sems.at[k])
-        )
-        copies[-1].start()
-
-    def part(k):
-        copies[k].wait()
-        return held_ref[pl.ds(k * depth, depth)]
-
-    return part
-
-
-def project_qkv(near, far, weight, core, parts=16):
+    )(hidden, gain.reshape(-1, LANES))
+
+
+def project_qkv(near, far, weight, adapter, chunk=1024):
     groups, rows, _ = near.shape
     depth, width = weight.shape
-    count, step = 2 * groups * rows, weight.shape[0] // parts
-
-    def kernel(core_ref, near_ref, far_ref, weight_ref, out_ref, rows_ref, held_ref, sems):
-        part = stream(weight_ref, held_ref, sems, parts)
+    count = 2 * groups * rows
+
+    def kernel(near_ref, far_ref, weight_ref, adapter_ref, out_ref, rows_ref):
         for e, source in enumerate((near_ref, far_ref)):
             for j in range(groups):
-                place = pl.ds((e * groups + j) * rows, rows)
-                rows_ref[place] = source[j, :, pl.ds(0, depth)]
+                rows_ref[pl.ds((e * groups + j) * rows, rows)] = source[j]
         total = jnp.zeros((count, width), jnp.float32)
-        for k in range(parts):
+        for k in range(depth // chunk):
+            part = pl.ds(k * chunk, chunk)
             total = total + jnp.dot(
-                rows_ref[:, pl.ds(k * step, step)], part(k), preferred_element_type=jnp.float32
+                rows_ref[:, part], weight_ref[part, :], preferred_element_type=jnp.float32
             )
+        core = lax.axis_index("batch")
         for e in range(2):
             for j in range(groups):
                 place = (e * groups + j) * rows
-                out_ref[2 * j + (core_ref[0] ^ e)] = total[place : place + rows].astype(
+                device = 2 * j + (core ^ e)
+                out_ref[device, :, pl.ds(0, width)] = total[place : place + rows].astype(
                     jnp.bfloat16
                 )
+                out_ref[device, :, pl.ds(width, LANES)] = adapter_ref[...]
 
     return call(
         kernel,
         "project_qkv",
-        jax.ShapeDtypeStruct((2 * groups, rows, width), jnp.bfloat16),
-        [SMEM, VMEM, VMEM, ANY],
+        jax.ShapeDtypeStruct((2 * groups, rows, width + LANES), jnp.bfloat16),
+        [VMEM, VMEM, VMEM, VMEM],
         weight.size * 2,
-        limit=STREAM,
         flops=2 * count * weight.size,
-        scratch_shapes=[
-            pltpu.VMEM((count, depth), jnp.bfloat16),
-            pltpu.VMEM(weight.shape, weight.dtype),
-            pltpu.SemaphoreType.DMA((parts,)),
-        ],
-    )(core, near, far, weight)
-
-
-def project_out(rows, weight, parts=16):
-    count, step = rows.shape[0], weight.shape[0] // parts
-
-    def kernel(rows_ref, weight_ref, out_ref, held_ref, sems):
-        part = stream(weight_ref, held_ref, sems, parts)
+        scratch_shapes=[pltpu.VMEM((count, depth), jnp.bfloat16)],
+    )(near, far, weight, adapter)
+
+
+def project_out(rows, weight, chunk=1024):
+    count, depth = rows.shape
+
+    def kernel(rows_ref, weight_ref, out_ref):
         total = jnp.zeros(out_ref.shape, jnp.float32)
-        for k in range(parts):
+        for k in range(depth // chunk):
+            part = pl.ds(k * chunk, chunk)
             total = total + jnp.dot(
-                rows_ref[:, pl.ds(k * step, step)], part(k), preferred_element_type=jnp.float32
+                rows_ref[:, part], weight_ref[part, :], preferred_element_type=jnp.float32
             )
         out_ref[...] = total
 
@@ -272,50 +237,32 @@
         kernel,
         "project_out",
         jax.ShapeDtypeStruct((count, weight.shape[1]), jnp.float32),
-        [VMEM, ANY],
+        [VMEM, VMEM],
         weight.size * 2,
-        limit=STREAM,
         flops=2 * count * weight.size,
-        scratch_shapes=[
-            pltpu.VMEM(weight.shape, weight.dtype),
-            pltpu.SemaphoreType.DMA((parts,)),
-        ],
     )(rows, weight)
 
 
-def pick(adapter_ref, store_ref, held_ref, sems):
-    count, rank = adapter_ref.shape[0], store_ref.shape[1]
-    copies = []
-    for r in range(count):
-        copies.append(
-            pltpu.make_async_copy(
-                store_ref.at[adapter_ref[r]], held_ref.at[pl.ds(r * rank, rank)], sems.at[r]
-            )
-        )
-        copies[-1].start()
-
-    def batch(k):
-        for copy in copies[k * BATCH : (k + 1) * BATCH]:
-            copy.wait()
-        return held_ref[pl.ds(k * BATCH * rank, BATCH * rank)]
-
-    return batch
-
-
-def down_partials(rows, place, adapter, store, copies):
+def batch_of(store_ref, adapter_ref, k):
+    return jnp.concatenate(
+        [store_ref[adapter_ref[r]] for r in range(k * BATCH, (k + 1) * BATCH)]
+    )
+
+
+def down_partials(rows, adapter, store, copies):
     count = adapter.shape[0]
     rank, depth = store.shape[1:]
 
-    def kernel(place_ref, adapter_ref, rows_ref, store_ref, out_ref, held_ref, sems):
-        batch = pick(adapter_ref, store_ref, held_ref, sems)
-        slices = rows_ref[:, pl.ds(pl.multiple_of(place_ref[0] * depth, depth), depth)]
+    def kernel(adapter_ref, rows_ref, store_ref, out_ref):
+        start = pl.multiple_of(lax.axis_index("mp") * depth, depth)
+        slices = rows_ref[:, pl.ds(start, depth)]
         row = lax.broadcasted_iota(jnp.int32, (count, LANES), 0)
         lane = lax.broadcasted_iota(jnp.int32, (count, LANES), 1)
         total = jnp.zeros((count, LANES), jnp.float32)
         for k in range(count // BATCH):
             every = lax.dot_general(
                 slices,
-                batch(k),
+                batch_of(store_ref, adapter_ref, k),
                 (((1,), (1,)), ((), ())),
                 preferred_element_type=jnp.float32,
             )
@@ -330,25 +277,21 @@
         kernel,
         "down_partials",
         jax.ShapeDtypeStruct((copies, count, LANES), jnp.float32),
-        [SMEM, SMEM, VMEM, ANY],
+        [SMEM, VMEM, VMEM],
         2 * count * rank * depth,
-        limit=STREAM,
+        limit=4 * MIB,
         flops=2 * count * count * rank * depth,
-        scratch_shapes=[
-            pltpu.VMEM((count * rank, depth), store.dtype),
-            pltpu.SemaphoreType.DMA((count,)),
-        ],
-    )(place, adapter, rows, store)
+    )(adapter, rows, store)
 
 
 def add_up(base, partials, adapter, store):
     count = adapter.shape[0]
     rank, width = store.shape[1:]
-
-    def kernel(adapter_ref, base_ref, partials_ref, store_ref, out_ref, held_ref, sems):
-        batch = pick(adapter_ref, store_ref, held_ref, sems)
+    groups = partials.shape[0]
+
+    def kernel(adapter_ref, base_ref, partials_ref, store_ref, out_ref):
         total = partials_ref[0]
-        for c in range(1, partials.shape[0]):
+        for c in range(1, groups):
             total = total + partials_ref[c]
         down = total.astype(jnp.bfloat16).astype(jnp.float32)
         row = lax.broadcasted_iota(jnp.int32, (count, LANES), 0)
@@ -360,21 +303,21 @@
                 first = k * BATCH * rank + s * LANES
                 spread.append(jnp.where(row == (lane + first) // rank, down, 0.0))
             spread = jnp.concatenate(spread, 1).astype(jnp.bfloat16)
-            delta = delta + jnp.dot(spread, batch(k), preferred_element_type=jnp.float32)
-        out_ref[...] = (base_ref[...] + ADAPTER_SCALE * delta).astype(jnp.bfloat16)
+            delta = delta + jnp.dot(
+                spread, batch_of(store_ref, adapter_ref, k), preferred_element_type=jnp.float32
+            )
+        result = (base_ref[...] + ADAPTER_SCALE * delta).astype(jnp.bfloat16)
+        for j in range(groups):
+            out_ref[j] = result[j * count // groups : (j + 1) * count // groups]
 
     return call(
         kernel,
         "add_up",
-        jax.ShapeDtypeStruct((count, width), jnp.bfloat16),
-        [SMEM, VMEM, VMEM, ANY],
+        jax.ShapeDtypeStruct((groups, count // groups, width), jnp.bfloat16),
+        [SMEM, VMEM, VMEM, VMEM],
         2 * count * rank * width,
-        limit=STREAM,
+        limit=4 * MIB,
         flops=2 * count * count * rank * width,
-        scratch_shapes=[
-            pltpu.VMEM((count * rank, width), store.dtype),
-            pltpu.SemaphoreType.DMA((count,)),
-        ],
     )(adapter, base, partials, store)
 
 
@@ -462,10 +405,10 @@
     return context_vector.reshape(rows, query_width).astype(jnp.bfloat16)
 
 
-def angles(positions):
+def angles(lengths):
     half = HEAD_DIM // 2
     freq = THETA ** (-(jnp.arange(half, dtype=jnp.float32) * 2.0) / HEAD_DIM)
-    angle = positions[:, :half] * freq
+    angle = lengths.astype(jnp.float32)[:, None] * freq
     cosine, sine = jnp.cos(angle), jnp.sin(angle)
     return jnp.concatenate([cosine, cosine], -1), jnp.concatenate([sine, sine], -1)
 
@@ -483,32 +426,33 @@
     adapter_down_matrices,
     adapter_up_matrices,
 ):
-    rows, features = hidden.shape
+    rows = hidden.shape[0]
     mp_size = lax.axis_size("mp")
-    core = lax.axis_index("batch").astype(jnp.int32).reshape(1)
-    place = lax.axis_index("mp").astype(jnp.int32).reshape(1)
-
-    sent, positions = norm_rows(
-        hidden, attention_norm_gain, slots, requests, lengths, mp_size
-    )
-    cosine, sine = angles(positions)
-    near = exchange(sent)
-    adapter = near[:, :, features].reshape(-1).astype(jnp.int32)
-    mixed = exchange(
-        project_qkv(near, swap_cores(near), query_key_value_weight, core), ("mp", "batch")
-    )
-    qkv = mixed.transpose(1, 0, 2).reshape(rows, -1)
+    width = query_key_value_weight.shape[1]
+
+    slot_hits = slots[:, None] == jnp.arange(requests.shape[1])[None, :]
+    adapter = jnp.sum(jnp.where(slot_hits, requests[0][None, :], 0), 1)
+    adapter = jnp.broadcast_to(adapter[:, None], (rows, LANES)).astype(jnp.bfloat16)
+    cosine, sine = angles(lengths)
+
+    near = exchange(norm_rows(hidden, attention_norm_gain, mp_size))
+    columns = project_qkv(near, swap_cores(near), query_key_value_weight, adapter)
+    mixed = exchange(columns, ("mp", "batch"))
+    adapter = mixed.reshape(mp_size, -1, rows, width + LANES)[:, :, :, width]
+    adapter = lax.dynamic_index_in_dim(adapter, lax.axis_index("batch"), 1, keepdims=False)
+    adapter = adapter.reshape(-1).astype(jnp.int32)
+    qkv = mixed[:, :, :width].transpose(1, 0, 2).reshape(rows, -1)
 
     context = attend(qkv, cosine, sine, key_cache, value_cache, lengths)
     copies = jnp.broadcast_to(context[None], (mp_size, *context.shape))
     gathered = exchange(copies).reshape(-1, context.shape[1])
 
     partials = exchange(
-        down_partials(gathered, place, adapter, adapter_down_matrices.swapaxes(1, 2), mp_size)
+        down_partials(gathered, adapter, adapter_down_matrices.swapaxes(1, 2), mp_size)
     )
     base = project_out(gathered, output_weight)
     projected = add_up(base, partials, adapter, adapter_up_matrices)
-    returned = exchange(projected.reshape(mp_size, rows, -1))
+    returned = exchange(projected)
     return add_rows(widen(hidden, projected), returned)
 
 

time: 84.8 us -> 88.1 us (1.039)
  local copies, waits for them, and re-layouts: 5.23 us -> 19.4 us
  Pallas kernels: 20.5 us -> 9.83 us
  waiting for transfers between devices: 32.4 us -> 30.1 us
  other arithmetic: 1.63 us -> 3.02 us
    unnamed x18 -> x21, local copies, waits for them, and re-layouts: 3.59 us -> 18.3 us
    pallas_call x1, Pallas kernels: 6.19 us -> 2.26 us  [project_out(): call(kernel, 'project_out', jax.ShapeDtypeStruct((count, weight.shape[1])...]
    pallas_call x1, Pallas kernels: 5.63 us -> 2.53 us  [project_qkv(): call(kernel, 'project_qkv', jax.ShapeDtypeStruct((2 * groups, rows, width...]
    pallas_call x1, Pallas kernels: 3.98 us -> 1.84 us  [down_partials(): call(kernel, 'down_partials', jax.ShapeDtypeStruct((copies, count, LANES)...]
    all_to_all x5, waiting for transfers between devices: 30.9 us -> 29.3 us  [exchange(): return lax.all_to_all(blocks, axes, split_axis=0, concat_axis=0, tiled=True)]
    pallas_call x2, Pallas kernels: 4.05 us -> 2.54 us  [the longest x1 1.55 us: add_up(): call(kernel, 'add_up', jax.ShapeDtypeStruct((groups, count // groups, wid...]
  transfers between devices with their start and end apart: 6 -> 6, of which waited for: 6 -> 5; matrix products, arithmetic and copies ran while one was open for 1% -> 3% of each run, Pallas kernels for 7% -> 3%
where the time goes in v5:
time: 88.1 us; the launch traced here: 87.3 us
  waiting for transfers between devices  30.1 us (34%)
  starting transfers between devices  23.9 us (27%)
  local copies, waits for them, and re-layouts  19.4 us (22%)
  Pallas kernels  9.83 us (11%)
  other arithmetic  3.02 us (3%)
  matrix products  0.9 us (1%)
    all_to_all x5, waiting for transfers between devices, exchange(): return lax.all_to_all(blocks, axes, split_axis=0, concat_axis=0, tiled=True)  29.3 us
    all_to_all x5, starting transfers between devices, exchange(): return lax.all_to_all(blocks, axes, split_axis=0, concat_axis=0, tiled=True)  23.9 us
    unnamed x21, local copies, waits for them, and re-layouts  18.3 us
    pallas_call x1, Pallas kernels, project_qkv(): call(kernel, 'project_qkv', jax.ShapeDtypeStruct((2 * groups, rows, width...  2.53 us
    pallas_call x1, Pallas kernels, project_out(): call(kernel, 'project_out', jax.ShapeDtypeStruct((count, weight.shape[1])...  2.26 us
    pallas_call x1, Pallas kernels, down_partials(): call(kernel, 'down_partials', jax.ShapeDtypeStruct((copies, count, LANES)...  1.84 us
  transfers between devices with their start and end apart: 6, of which 5 were waited for; matrix products, arithmetic and copies ran while one was open for 3% of the time, Pallas kernels for 3%

profile of v5, /device:TPU:0, one launch (start us, length us, event | category | flops | bytes accessed | tf_op | source)
XLA Modules:
  0.0 87.3 jit_solution(328896738269219756)
XLA Ops:
  0.0 0.8 copy-done.5
  0.9 0.7 copy-done.7
  1.6 1.0 %norm_rows.1 = bf16[8,2,8192]{2,1,0:T(2,128)(2,1)} custom-call(bf16[2,8192]{1,0:T(2,128)(2,1)S(1)} %copy-done.5, bf16[64,128]{1,0:T(8,128)(2,1)S(1)} %bitcast.67), custom_call_target="tpu_custom_call" | custom-call | bytes 294912 | tf_op jit(solution)/shard_map/norm_rows/pallas_call | solution.py:179
  2.6 7.3 %all-to-all-start = ((bf16[8,2,8192]{2,1,0:T(2,128)(2,1)}), bf16[8,2,8192]{2,1,0:T(2,128)(2,1)S(1)}, u32[]{:S(2)}, u32[]{:S(2)}) async-start(bf16[8,2,8192]{2,1,0:T(2,128)(2,1)} %norm_rows.1), calls=%async_computation | async-start | bytes 524288 | tf_op jit(solution)/shard_map/all_to_all | solution.py:361
  9.8 0.9 fusion.20
  10.7 0.7 iota_compare_fusion
  11.4 7.3 %all-to-all-done.near_ref = bf16[8,2,8192]{2,1,0:T(2,128)(2,1)S(1)} async-done(((bf16[8,2,8192]{2,1,0:T(2,128)(2,1)}), bf16[8,2,8192]{2,1,0:T(2,128)(2,1)S(1)}, u32[]{:S(2)}, u32[]{:S(2)}) %all-to-all-start) | async-done | bytes 262176 | tf_op jit(solution)/shard_map/all_to_all | solution.py:361
  18.7 0.7 convert_element_type.46
  19.4 0.1 multiply_cosine_fusion
  19.5 0.7 collective-permute-done.far_ref
  20.3 4.0 %copy-done.2 = bf16[8192,640]{1,0:T(8,128)(2,1)S(1)} copy-done((bf16[8192,640]{1,0:T(8,128)(2,1)S(1)}, bf16[8192,640]{1,0:T(8,128)(2,1)}, u32[]{:S(2)}) %copy-start.2) | copy-done | bytes 10485784
  24.3 2.5 %project_qkv.1 = bf16[16,2,768]{2,1,0:T(2,128)(2,1)} custom-call(bf16[8,2,8192]{2,1,0:T(2,128)(2,1)S(1)} %all-to-all-done.near_ref, bf16[8,2,8192]{2,1,0:T(2,128)(2,1)S(1)} %collective-permute-done.far_ref, bf16[8192,640]{1,0:T(8,128)(2,1)S(1)} %copy-done.2, bf16[2,128]{1,0:T(2,128)(2,1)S(1)} %broadcast_in_dim.33.adapter_ref), custom_call_target="tpu_custom_call" | custom-call | flops 335544320 | bytes 10485760 | tf_op jit(solution)/shard_map/project_qkv/pallas_call | solution.py:213
  26.8 3.7 %all-to-all-start.1 = ((bf16[16,2,768]{2,1,0:T(2,128)(2,1)}), bf16[16,2,768]{2,1,0:T(2,128)(2,1)S(1)}, u32[]{:S(2)}, u32[]{:S(2)}) async-start(bf16[16,2,768]{2,1,0:T(2,128)(2,1)} %project_qkv.1), calls=%async_computation.1 | async-start | bytes 98304 | tf_op jit(solution)/shard_map/all_to_all | solution.py:361
  30.6 6.7 %all-to-all-done.1 = bf16[16,2,768]{2,1,0:T(2,128)(2,1)S(1)} async-done(((bf16[16,2,768]{2,1,0:T(2,128)(2,1)}), bf16[16,2,768]{2,1,0:T(2,128)(2,1)S(1)}, u32[]{:S(2)}, u32[]{:S(2)}) %all-to-all-start.1) | async-done | bytes 49184 | tf_op jit(solution)/shard_map/all_to_all | solution.py:361
  37.8 0.1 fusion.15
  37.9 0.5 fusion.21
  38.4 0.2 fusion.7
  38.6 0.3 fusion.2
  39.0 0.8 broadcast_in_dim.36
  39.8 3.4 %all-to-all-start.2 = ((bf16[8,2,8192]{2,1,0:T(2,128)(2,1)}), bf16[8,2,8192]{2,1,0:T(2,128)(2,1)S(1)}, u32[]{:S(2)}, u32[]{:S(2)}) async-start(bf16[8,2,8192]{2,1,0:T(2,128)(2,1)} %broadcast_in_dim.36), calls=%async_computation.2 | async-start | bytes 524288 | tf_op jit(solution)/shard_map/all_to_all | solution.py:361
  43.3 0.1 copy.24
  43.5 8.6 %all-to-all-done.2 = bf16[8,2,8192]{2,1,0:T(2,128)(2,1)S(1)} async-done(((bf16[8,2,8192]{2,1,0:T(2,128)(2,1)}), bf16[8,2,8192]{2,1,0:T(2,128)(2,1)S(1)}, u32[]{:S(2)}, u32[]{:S(2)}) %all-to-all-start.2) | async-done | bytes 262176 | tf_op jit(solution)/shard_map/all_to_all | solution.py:361
  52.2 3.4 %copy-done.3 = bf16[64,1024,64]{1,2,0:T(8,128)(2,1)S(1)} copy-done((bf16[64,1024,64]{1,2,0:T(8,128)(2,1)S(1)}, bf16[64,1024,64]{1,2,0:T(8,128)(2,1)}, u32[]{:S(2)}) %copy-start.3) | copy-done | bytes 8388632
  55.6 1.8 %down_partials.1 = f32[8,16,128]{2,1,0:T(8,128)} custom-call(s32[16]{0:T(128)S(1)} %reshape.89.adapter_ref, bf16[16,8192]{1,0:T(8,128)(2,1)S(1)} %reshape.88.rows_ref, bf16[64,64,1024]{2,1,0:T(8,128)(2,1)S(1)} %bitcast.66), custom_call_target="tpu_custom_call" | custom-call | flops 33554432 | bytes 2097152 | tf_op jit(solution)/shard_map/down_partials/pallas_call | solution.py:276
  57.5 3.6 %all-to-all-start.3 = ((f32[8,16,128]{2,1,0:T(8,128)}), f32[8,16,128]{2,1,0:T(8,128)S(1)}, u32[]{:S(2)}, u32[]{:S(2)}) async-start(f32[8,16,128]{2,1,0:T(8,128)} %down_partials.1), calls=%async_computation.3 | async-start | bytes 131072 | tf_op jit(solution)/shard_map/all_to_all | solution.py:361
  61.0 5.8 %copy-done.1 = bf16[8192,1024]{1,0:T(8,128)(2,1)S(1)} copy-done((bf16[8192,1024]{1,0:T(8,128)(2,1)S(1)}, bf16[8192,1024]{1,0:T(8,128)(2,1)}, u32[]{:S(2)}) %copy-start.1) | copy-done | bytes 16777240
  66.8 2.3 %project_out.1.base_ref = f32[16,1024]{1,0:T(8,128)S(1)} custom-call(bf16[16,8192]{1,0:T(8,128)(2,1)S(1)} %reshape.88.rows_ref, bf16[8192,1024]{1,0:T(8,128)(2,1)S(1)} %copy-done.1), custom_call_target="tpu_custom_call" | custom-call | flops 268435456 | bytes 16777216 | tf_op jit(solution)/shard_map/project_out/pallas_call | solution.py:236
  69.0 3.4 %copy-done.4 = bf16[64,64,1024]{2,1,0:T(8,128)(2,1)S(1)} copy-done((bf16[64,64,1024]{2,1,0:T(8,128)(2,1)S(1)}, bf16[64,64,1024]{2,1,0:T(8,128)(2,1)}, u32[]{:S(2)}) %copy-start.4) | copy-done | bytes 8388632
  72.4 1.6 %add_up.1.after_ref = bf16[8,2,1024]{2,1,0:T(2,128)(2,1)} custom-call(s32[16]{0:T(128)S(1)} %reshape.89.adapter_ref, f32[16,1024]{1,0:T(8,128)S(1)} %project_out.1.base_ref, f32[8,16,128]{2,1,0:T(8,128)S(1)} %all-to-all-done.3.partials_ref, bf16[64,64,1024]{2,1,0:T(8,128)(2,1)S(1)} %copy-done.4), custom_call_target="tpu_custom_call" | custom-call | flops 33554432 | bytes 2097152 | tf_op jit(solution)/shard_map/add_up/pallas_call | solution.py:313
  74.0 6.0 %all-to-all-start.4 = ((bf16[8,2,1024]{2,1,0:T(2,128)(2,1)}), bf16[8,2,1024]{2,1,0:T(2,128)(2,1)S(1)}, u32[]{:S(2)}, u32[]{:S(2)}) async-start(bf16[8,2,1024]{2,1,0:T(2,128)(2,1)} %add_up.1.after_ref), calls=%async_computation.4 | async-start | bytes 65536 | tf_op jit(solution)/shard_map/all_to_all | solution.py:361
  80.0 6.7 %all-to-all-done.4.parts_ref = bf16[8,2,1024]{2,1,0:T(2,128)(2,1)S(1)} async-done(((bf16[8,2,1024]{2,1,0:T(2,128)(2,1)}), bf16[8,2,1024]{2,1,0:T(2,128)(2,1)S(1)}, u32[]{:S(2)}, u32[]{:S(2)}) %all-to-all-start.4) | async-done | bytes 32800 | tf_op jit(solution)/shard_map/all_to_all | solution.py:361
  86.7 0.7 add_rows.1
  (36 shorter events, 0.9 us)
Async XLA Ops:
  0.0 37.9 %copy-start = (bf16[2,256,1024]{2,1,0:T(8,128)(2,1)S(1)}, bf16[2,256,1024]{2,1,0:T(8,128)(2,1)}, u32[]{:S(2)}) copy-start(bf16[2,256,1024]{2,1,0:T(8,128)(2,1)} %param.15) | copy-start | bytes 3145732
  0.0 0.8 copy-start.5
  0.9 0.7 copy-start.7
  2.6 16.2 %all-to-all-start = ((bf16[8,2,8192]{2,1,0:T(2,128)(2,1)}), bf16[8,2,8192]{2,1,0:T(2,128)(2,1)S(1)}, u32[]{:S(2)}, u32[]{:S(2)}) async-start(bf16[8,2,8192]{2,1,0:T(2,128)(2,1)} %norm_rows.1), calls=%async_computation | async-start | bytes 524288 | tf_op jit(solution)/shard_map/all_to_all | solution.py:361
  18.7 1.5 %collective-permute-start = (bf16[8,2,8192]{2,1,0:T(2,128)(2,1)S(1)}, bf16[8,2,8192]{2,1,0:T(2,128)(2,1)S(1)}, u32[]{:S(2)}, u32[]{:S(2)}) collective-permute-start(bf16[8,2,8192]{2,1,0:T(2,128)(2,1)S(1)} %all-to-all-done.near_ref), channel_id=1, source_target_pairs={{0,1},{1,0},{2,3},{3,2},{4,5},{5,4},{6,7},{7,6},{8,9},{9,8},{10,11... | collective-permute-start | bytes 786440 | tf_op jit(solution)/shard_map/ppermute | solution.py:357
  20.3 4.0 %copy-start.2 = (bf16[8192,640]{1,0:T(8,128)(2,1)S(1)}, bf16[8192,640]{1,0:T(8,128)(2,1)}, u32[]{:S(2)}) copy-start(bf16[8192,640]{1,0:T(8,128)(2,1)} %weight_ref.2) | copy-start | bytes 31457284
  24.3 14.3 %copy-start.8 = (bf16[2,256,1024]{2,1,0:T(8,128)(2,1)S(1)}, bf16[2,256,1024]{2,1,0:T(8,128)(2,1)}, u32[]{:S(2)}) copy-start(bf16[2,256,1024]{2,1,0:T(8,128)(2,1)} %param.16) | copy-start | bytes 3145732
  26.8 10.5 %all-to-all-start.1 = ((bf16[16,2,768]{2,1,0:T(2,128)(2,1)}), bf16[16,2,768]{2,1,0:T(2,128)(2,1)S(1)}, u32[]{:S(2)}, u32[]{:S(2)}) async-start(bf16[16,2,768]{2,1,0:T(2,128)(2,1)} %project_qkv.1), calls=%async_computation.1 | async-start | bytes 98304 | tf_op jit(solution)/shard_map/all_to_all | solution.py:361
  39.8 12.3 %all-to-all-start.2 = ((bf16[8,2,8192]{2,1,0:T(2,128)(2,1)}), bf16[8,2,8192]{2,1,0:T(2,128)(2,1)S(1)}, u32[]{:S(2)}, u32[]{:S(2)}) async-start(bf16[8,2,8192]{2,1,0:T(2,128)(2,1)} %broadcast_in_dim.36), calls=%async_computation.2 | async-start | bytes 524288 | tf_op jit(solution)/shard_map/all_to_all | solution.py:361
  52.2 3.4 %copy-start.3 = (bf16[64,1024,64]{1,2,0:T(8,128)(2,1)S(1)}, bf16[64,1024,64]{1,2,0:T(8,128)(2,1)}, u32[]{:S(2)}) copy-start(bf16[64,1024,64]{1,2,0:T(8,128)(2,1)} %param.20) | copy-start | bytes 25165828
  57.5 11.6 %all-to-all-start.3 = ((f32[8,16,128]{2,1,0:T(8,128)}), f32[8,16,128]{2,1,0:T(8,128)S(1)}, u32[]{:S(2)}, u32[]{:S(2)}) async-start(f32[8,16,128]{2,1,0:T(8,128)} %down_partials.1), calls=%async_computation.3 | async-start | bytes 131072 | tf_op jit(solution)/shard_map/all_to_all | solution.py:361
  61.0 5.8 %copy-start.1 = (bf16[8192,1024]{1,0:T(8,128)(2,1)S(1)}, bf16[8192,1024]{1,0:T(8,128)(2,1)}, u32[]{:S(2)}) copy-start(bf16[8192,1024]{1,0:T(8,128)(2,1)} %weight_ref.3) | copy-start | bytes 50331652
  66.8 13.2 %copy-start.6 = (bf16[2,8192]{1,0:T(2,128)(2,1)S(1)}, bf16[2,8192]{1,0:T(2,128)(2,1)}, u32[]{:S(2)}) copy-start(bf16[2,8192]{1,0:T(2,128)(2,1)} %hidden_ref.3) | copy-start | bytes 98308
  69.0 3.4 %copy-start.4 = (bf16[64,64,1024]{2,1,0:T(8,128)(2,1)S(1)}, bf16[64,64,1024]{2,1,0:T(8,128)(2,1)}, u32[]{:S(2)}) copy-start(bf16[64,64,1024]{2,1,0:T(8,128)(2,1)} %store_ref.1) | copy-start | bytes 25165828
  74.0 12.7 %all-to-all-start.4 = ((bf16[8,2,1024]{2,1,0:T(2,128)(2,1)}), bf16[8,2,1024]{2,1,0:T(2,128)(2,1)S(1)}, u32[]{:S(2)}, u32[]{:S(2)}) async-start(bf16[8,2,1024]{2,1,0:T(2,128)(2,1)} %add_up.1.after_ref), calls=%async_computation.4 | async-start | bytes 65536 | tf_op jit(solution)/shard_map/all_to_all | solution.py:361

commit v6 on v5

--- a/solution.py
+++ b/solution.py
@@ -144,6 +144,7 @@
 MIB = 1 << 20
 LANES = 128
 BATCH = 4
+STREAM = 53 * MIB
 VMEM = pl.BlockSpec(memory_space=pltpu.VMEM)
 SMEM = pl.BlockSpec(memory_space=pltpu.SMEM)
 ANY = pl.BlockSpec(memory_space=pl.ANY)
@@ -208,7 +209,9 @@
                 out_ref[device, :, pl.ds(0, width)] = total[place : place + rows].astype(
                     jnp.bfloat16
                 )
-                out_ref[device, :, pl.ds(width, LANES)] = adapter_ref[...]
+                out_ref[device, :, pl.ds(width, LANES)] = (
+                    adapter_ref[...] if e == 0 else jnp.zeros_like(adapter_ref)
+                )
 
     return call(
         kernel,
@@ -221,15 +224,35 @@
     )(near, far, weight, adapter)
 
 
-def project_out(rows, weight, chunk=1024):
-    count, depth = rows.shape
-
-    def kernel(rows_ref, weight_ref, out_ref):
+def stream(weight_ref, held_ref, sems, parts):
+    depth = held_ref.shape[0] // parts
+    copies = []
+    for k in range(parts):
+        rows = pl.ds(k * depth, depth)
+        copies.append(
+            pltpu.make_async_copy(weight_ref.at[rows], held_ref.at[rows], sems.at[k])
+        )
+        copies[-1].start()
+
+    def part(k):
+        copies[k].wait()
+        return held_ref[pl.ds(k * depth, depth)]
+
+    return part
+
+
+def project_out(gathered, weight, parts=16):
+    groups, rows, depth = gathered.shape
+    count, step = groups * rows, depth // parts
+
+    def kernel(gathered_ref, weight_ref, out_ref, rows_ref, held_ref, sems):
+        part = stream(weight_ref, held_ref, sems, parts)
+        for j in range(groups):
+            rows_ref[pl.ds(j * rows, rows)] = gathered_ref[j]
         total = jnp.zeros(out_ref.shape, jnp.float32)
-        for k in range(depth // chunk):
-            part = pl.ds(k * chunk, chunk)
+        for k in range(parts):
             total = total + jnp.dot(
-                rows_ref[:, part], weight_ref[part, :], preferred_element_type=jnp.float32
+                rows_ref[:, pl.ds(k * step, step)], part(k), preferred_element_type=jnp.float32
             )
         out_ref[...] = total
 
@@ -237,32 +260,35 @@
         kernel,
         "project_out",
         jax.ShapeDtypeStruct((count, weight.shape[1]), jnp.float32),
-        [VMEM, VMEM],
+        [VMEM, ANY],
         weight.size * 2,
+        limit=STREAM,
         flops=2 * count * weight.size,
-    )(rows, weight)
-
-
-def batch_of(store_ref, adapter_ref, k):
-    return jnp.concatenate(
-        [store_ref[adapter_ref[r]] for r in range(k * BATCH, (k + 1) * BATCH)]
-    )
-
-
-def down_partials(rows, adapter, store, copies):
-    count = adapter.shape[0]
+        scratch_shapes=[
+            pltpu.VMEM((count, depth), gathered.dtype),
+            pltpu.VMEM(weight.shape, weight.dtype),
+            pltpu.SemaphoreType.DMA((parts,)),
+        ],
+    )(gathered, weight)
+
+
+def down_partials(gathered, adapter, store):
+    groups, rows, _ = gathered.shape
+    count = groups * rows
     rank, depth = store.shape[1:]
 
-    def kernel(adapter_ref, rows_ref, store_ref, out_ref):
+    def kernel(adapter_ref, gathered_ref, store_ref, out_ref, rows_ref):
         start = pl.multiple_of(lax.axis_index("mp") * depth, depth)
-        slices = rows_ref[:, pl.ds(start, depth)]
+        for j in range(groups):
+            rows_ref[pl.ds(j * rows, rows)] = gathered_ref[j, :, pl.ds(start, depth)]
         row = lax.broadcasted_iota(jnp.int32, (count, LANES), 0)
         lane = lax.broadcasted_iota(jnp.int32, (count, LANES), 1)
         total = jnp.zeros((count, LANES), jnp.float32)
         for k in range(count // BATCH):
+            chosen = [adapter_ref[r // rows, r % rows] for r in range(k * BATCH, (k + 1) * BATCH)]
             every = lax.dot_general(
-                slices,
-                batch_of(store_ref, adapter_ref, k),
+                rows_ref[...],
+                jnp.concatenate([store_ref[c] for c in chosen]),
                 (((1,), (1,)), ((), ())),
                 preferred_element_type=jnp.float32,
             )
@@ -270,26 +296,48 @@
                 first = k * BATCH * rank + s * LANES
                 mine = row == (lane + first) // rank
                 total = total + jnp.where(mine, every[:, s * LANES : (s + 1) * LANES], 0.0)
-        for c in range(copies):
+        for c in range(groups):
             out_ref[c] = total
 
     return call(
         kernel,
         "down_partials",
-        jax.ShapeDtypeStruct((copies, count, LANES), jnp.float32),
+        jax.ShapeDtypeStruct((groups, count, LANES), jnp.float32),
         [SMEM, VMEM, VMEM],
         2 * count * rank * depth,
         limit=4 * MIB,
         flops=2 * count * count * rank * depth,
-    )(adapter, rows, store)
+        scratch_shapes=[pltpu.VMEM((count, depth), gathered.dtype)],
+    )(adapter, gathered, store)
+
+
+def pick(adapter_ref, store_ref, held_ref, sems):
+    groups, rows = adapter_ref.shape
+    count, rank = groups * rows, store_ref.shape[1]
+    copies = []
+    for r in range(count):
+        copies.append(
+            pltpu.make_async_copy(
+                store_ref.at[adapter_ref[r // rows, r % rows]], held_ref.at[pl.ds(r * rank, rank)], sems.at[r]
+            )
+        )
+        copies[-1].start()
+
+    def batch(k):
+        for copy in copies[k * BATCH : (k + 1) * BATCH]:
+            copy.wait()
+        return held_ref[pl.ds(k * BATCH * rank, BATCH * rank)]
+
+    return batch
 
 
 def add_up(base, partials, adapter, store):
-    count = adapter.shape[0]
+    count = adapter.size
     rank, width = store.shape[1:]
     groups = partials.shape[0]
 
-    def kernel(adapter_ref, base_ref, partials_ref, store_ref, out_ref):
+    def kernel(adapter_ref, base_ref, partials_ref, store_ref, out_ref, held_ref, sems):
+        batch = pick(adapter_ref, store_ref, held_ref, sems)
         total = partials_ref[0]
         for c in range(1, groups):
             total = total + partials_ref[c]
@@ -304,7 +352,7 @@
                 spread.append(jnp.where(row == (lane + first) // rank, down, 0.0))
             spread = jnp.concatenate(spread, 1).astype(jnp.bfloat16)
             delta = delta + jnp.dot(
-                spread, batch_of(store_ref, adapter_ref, k), preferred_element_type=jnp.float32
+                spread, batch(k), preferred_element_type=jnp.float32
             )
         result = (base_ref[...] + ADAPTER_SCALE * delta).astype(jnp.bfloat16)
         for j in range(groups):
@@ -314,25 +362,15 @@
         kernel,
         "add_up",
         jax.ShapeDtypeStruct((groups, count // groups, width), jnp.bfloat16),
-        [SMEM, VMEM, VMEM, VMEM],
+        [SMEM, VMEM, VMEM, ANY],
         2 * count * rank * width,
-        limit=4 * MIB,
+        limit=STREAM,
         flops=2 * count * count * rank * width,
+        scratch_shapes=[
+            pltpu.VMEM((count * rank, width), store.dtype),
+            pltpu.SemaphoreType.DMA((count,)),
+        ],
     )(adapter, base, partials, store)
-
-
-def widen(hidden, after):
-    def kernel(hidden_ref, after_ref, out_ref):
-        del after_ref
-        out_ref[...] = hidden_ref[...].astype(jnp.float32)
-
-    return call(
-        kernel,
-        "widen",
-        jax.ShapeDtypeStruct(hidden.shape, jnp.float32),
-        [VMEM, ANY],
-        hidden.size * 64,
-    )(hidden, after)
 
 
 def add_rows(hidden, parts):
@@ -341,7 +379,7 @@
     def kernel(hidden_ref, parts_ref, out_ref):
         for k in range(parts.shape[0]):
             part = pl.ds(k * width, width)
-            total = hidden_ref[:, part] + parts_ref[k].astype(jnp.float32)
+            total = hidden_ref[:, part].astype(jnp.float32) + parts_ref[k].astype(jnp.float32)
             out_ref[:, part] = total.astype(jnp.bfloat16)
 
     return call(
@@ -361,7 +399,7 @@
     return lax.all_to_all(blocks, axes, split_axis=0, concat_axis=0, tiled=True)
 
 
-def attend(qkv, cosine, sine, key_cache, value_cache, lengths):
+def attend(qkv, cosine, sine, key_cache, value_cache, live):
     rows = qkv.shape[0]
     query_width = HEADS * HEAD_DIM
     kv_width = KV_HEADS * HEAD_DIM
@@ -385,7 +423,6 @@
     scores = (
         jnp.einsum("rgqd,rtgd->rgqt", grouped, cached, preferred_element_type=jnp.float32) * scale
     )
-    live = jnp.arange(cached.shape[1])[None, :] < lengths[:, None]
     scores = jnp.where(live[:, None, None, :], scores, -jnp.inf)
     own = (
         jnp.einsum("rgqd,rgd->rgq", grouped, fresh_key, preferred_element_type=jnp.float32) * scale
@@ -430,30 +467,33 @@
     mp_size = lax.axis_size("mp")
     width = query_key_value_weight.shape[1]
 
+    near = exchange(norm_rows(hidden, attention_norm_gain, mp_size))
+    far = swap_cores(near)
+
+    near, lengths, slots, requests = lax.optimization_barrier((near, lengths, slots, requests))
     slot_hits = slots[:, None] == jnp.arange(requests.shape[1])[None, :]
     adapter = jnp.sum(jnp.where(slot_hits, requests[0][None, :], 0), 1)
     adapter = jnp.broadcast_to(adapter[:, None], (rows, LANES)).astype(jnp.bfloat16)
     cosine, sine = angles(lengths)
-
-    near = exchange(norm_rows(hidden, attention_norm_gain, mp_size))
-    columns = project_qkv(near, swap_cores(near), query_key_value_weight, adapter)
+    live = jnp.arange(key_cache.shape[1])[None, :] < lengths[:, None]
+    far, cosine, sine, live = lax.optimization_barrier((far, cosine, sine, live))
+
+    columns = project_qkv(near, far, query_key_value_weight, adapter)
     mixed = exchange(columns, ("mp", "batch"))
     adapter = mixed.reshape(mp_size, -1, rows, width + LANES)[:, :, :, width]
-    adapter = lax.dynamic_index_in_dim(adapter, lax.axis_index("batch"), 1, keepdims=False)
-    adapter = adapter.reshape(-1).astype(jnp.int32)
+    adapter = jnp.sum(adapter.astype(jnp.float32), 1).astype(jnp.int32)
     qkv = mixed[:, :, :width].transpose(1, 0, 2).reshape(rows, -1)
 
-    context = attend(qkv, cosine, sine, key_cache, value_cache, lengths)
-    copies = jnp.broadcast_to(context[None], (mp_size, *context.shape))
-    gathered = exchange(copies).reshape(-1, context.shape[1])
+    context = attend(qkv, cosine, sine, key_cache, value_cache, live)
+    context, adapter = lax.optimization_barrier((context, adapter))
+    gathered = exchange(jnp.broadcast_to(context[None], (mp_size, *context.shape)))
 
     partials = exchange(
-        down_partials(gathered, adapter, adapter_down_matrices.swapaxes(1, 2), mp_size)
+        down_partials(gathered, adapter, adapter_down_matrices.swapaxes(1, 2))
     )
     base = project_out(gathered, output_weight)
     projected = add_up(base, partials, adapter, adapter_up_matrices)
-    returned = exchange(projected)
-    return add_rows(widen(hidden, projected), returned)
+    return add_rows(hidden, exchange(projected))
 
 
 def body(*arguments):

time: 88.1 us -> 79.5 us (0.902)
  blocking collectives: 0 us -> 33.6 us
  waiting for transfers between devices: 30.1 us -> 10.3 us
  local copies, waits for them, and re-layouts: 19.4 us -> 5.85 us
  starting transfers between devices: 23.9 us -> 10.9 us
  Pallas kernels: 9.83 us -> 14.2 us
    all_to_all x0 -> x3, blocking collectives: none -> 33.6 us  [exchange(): return lax.all_to_all(blocks, axes, split_axis=0, concat_axis=0, tiled=True)]
    all_to_all x5 -> x2, waiting for transfers between devices: 29.3 us -> 9.61 us  [exchange(): return lax.all_to_all(blocks, axes, split_axis=0, concat_axis=0, tiled=True)]
    all_to_all x5 -> x2, starting transfers between devices: 23.9 us -> 10.8 us  [exchange(): return lax.all_to_all(blocks, axes, split_axis=0, concat_axis=0, tiled=True)]
    unnamed x21 -> x18, local copies, waits for them, and re-layouts: 18.3 us -> 5.61 us
    pallas_call x1, Pallas kernels: 2.26 us -> 6.19 us  [project_out(): call(kernel, 'project_out', jax.ShapeDtypeStruct((count, weight.shape[1])...]
    pallas_call x1, Pallas kernels: 1.55 us -> 2.53 us  [add_up(): call(kernel, 'add_up', jax.ShapeDtypeStruct((groups, count // groups, wid...]
    pallas_call x2 -> x1, Pallas kernels: 1.84 us -> 1.89 us  [down_partials(): call(kernel, 'down_partials', jax.ShapeDtypeStruct((groups, count, LANES)...]
  transfers between devices with their start and end apart: 6 -> 3, of which waited for: 5 -> 3; matrix products, arithmetic and copies ran while one was open for 3% -> 1% of each run, Pallas kernels for 3% -> 8%
where the time goes in v6:
time: 79.5 us; the launch traced here: 79 us
  blocking collectives  33.6 us (42%)
  Pallas kernels  14.2 us (18%)
  starting transfers between devices  10.9 us (14%)
  waiting for transfers between devices  10.3 us (13%)
  local copies, waits for them, and re-layouts  5.85 us (7%)
  other arithmetic  3.11 us (4%)
  matrix products  0.9 us (1%)
    all_to_all x3, blocking collectives, exchange(): return lax.all_to_all(blocks, axes, split_axis=0, concat_axis=0, tiled=True)  33.6 us
    all_to_all x2, starting transfers between devices, exchange(): return lax.all_to_all(blocks, axes, split_axis=0, concat_axis=0, tiled=True)  10.8 us
    all_to_all x2, waiting for transfers between devices, exchange(): return lax.all_to_all(blocks, axes, split_axis=0, concat_axis=0, tiled=True)  9.61 us
    pallas_call x1, Pallas kernels, project_out(): call(kernel, 'project_out', jax.ShapeDtypeStruct((count, weight.shape[1])...  6.19 us
    unnamed x18, local copies, waits for them, and re-layouts  5.61 us
    pallas_call x1, Pallas kernels, add_up(): call(kernel, 'add_up', jax.ShapeDtypeStruct((groups, count // groups, wid...  2.53 us
    pallas_call x1, Pallas kernels, project_qkv(): call(kernel, 'project_qkv', jax.ShapeDtypeStruct((2 * groups, rows, width...  1.92 us
    pallas_call x1, Pallas kernels, down_partials(): call(kernel, 'down_partials', jax.ShapeDtypeStruct((groups, count, LANES)...  1.89 us
  transfers between devices with their start and end apart: 3, of which 3 were waited for; matrix products, arithmetic and copies ran while one was open for 1% of the time, Pallas kernels for 8%

profile of v6, /device:TPU:0, one launch (start us, length us, event | category | flops | bytes accessed | tf_op | source)
XLA Modules:
  0.0 79.0 jit_solution(11066569662630470774)
XLA Ops:
  0.0 0.8 %copy-done.3 = bf16[2,8192]{1,0:T(2,128)(2,1)S(1)} copy-done((bf16[2,8192]{1,0:T(2,128)(2,1)S(1)}, bf16[2,8192]{1,0:T(2,128)(2,1)}, u32[]{:S(2)}) %copy-start.3) | copy-done | bytes 32792
  0.9 0.7 copy-done.5
  1.6 1.0 %norm_rows.1 = bf16[8,2,8192]{2,1,0:T(2,128)(2,1)} custom-call(bf16[2,8192]{1,0:T(2,128)(2,1)S(1)} %copy-done.3, bf16[64,128]{1,0:T(8,128)(2,1)S(1)} %bitcast.65), custom_call_target="tpu_custom_call" | custom-call | bytes 294912 | tf_op jit(solution)/shard_map/norm_rows/pallas_call | solution.py:180
  2.6 7.3 %all-to-all-start = ((bf16[8,2,8192]{2,1,0:T(2,128)(2,1)}), bf16[8,2,8192]{2,1,0:T(2,128)(2,1)S(1)}, u32[]{:S(2)}, u32[]{:S(2)}) async-start(bf16[8,2,8192]{2,1,0:T(2,128)(2,1)} %norm_rows.1), calls=%async_computation | async-start | bytes 524288 | tf_op jit(solution)/shard_map/all_to_all | solution.py:399
  9.8 8.9 %all-to-all-done.near_ref = bf16[8,2,8192]{2,1,0:T(2,128)(2,1)S(1)} async-done(((bf16[8,2,8192]{2,1,0:T(2,128)(2,1)}), bf16[8,2,8192]{2,1,0:T(2,128)(2,1)S(1)}, u32[]{:S(2)}, u32[]{:S(2)}) %all-to-all-start) | async-done | bytes 262176 | tf_op jit(solution)/shard_map/all_to_all | solution.py:399
  18.7 0.7 convert_element_type.40
  19.4 0.9 %fusion.21 = s32[2]{0:T(128)S(1)} fusion(s32[2]{0:T(128)} %bitcast.75, s32[2]{0:T(128)} %param.18), kind=kLoop, calls=%fused_computation.47 | loop fusion | flops 10 | bytes 24 | tf_op jit(solution)/shard_map/reduce_sum | solution.py:475
  20.2 0.1 multiply_sine_fusion
  20.4 0.1 pad_maximum_fusion
  20.5 0.7 iota_compare_fusion
  21.2 0.7 collective-permute-done.far_ref
  22.0 4.0 %copy-done.1 = bf16[8192,640]{1,0:T(8,128)(2,1)S(1)} copy-done((bf16[8192,640]{1,0:T(8,128)(2,1)S(1)}, bf16[8192,640]{1,0:T(8,128)(2,1)}, u32[]{:S(2)}) %copy-start.1) | copy-done | bytes 10485784
  26.0 1.9 %project_qkv.1 = bf16[16,2,768]{2,1,0:T(2,128)(2,1)S(1)} custom-call(bf16[8,2,8192]{2,1,0:T(2,128)(2,1)S(1)} %all-to-all-done.near_ref, bf16[8,2,8192]{2,1,0:T(2,128)(2,1)S(1)} %collective-permute-done.far_ref, bf16[8192,640]{1,0:T(8,128)(2,1)S(1)} %copy-done.1, bf16[2,128]{1,0:T(2,128)(2,1)S(1)} %broadcast_in_dim.34.adapter_ref), custom_call_target="tpu_custom_call" | custom-call | flops 335544320 | bytes 10485760 | tf_op jit(solution)/shard_map/project_qkv/pallas_call | solution.py:216
  27.9 10.4 %all_to_all.25 = bf16[16,2,768]{2,1,0:T(2,128)(2,1)S(1)} all-to-all(bf16[16,2,768]{2,1,0:T(2,128)(2,1)S(1)} %project_qkv.1), channel_id=1, replica_groups=mesh['groups'=2,'mp'=8,'batch'=2] {'mp','batch'}, dimensions={0} | all-to-all | bytes 98304 | tf_op jit(solution)/shard_map/all_to_all | solution.py:399
  38.4 0.1 convert_reduce_fusion
  38.5 0.1 slice_negate_fusion.1
  38.6 0.1 fusion.9
  38.7 0.1 fusion.19
  38.8 0.1 fusion.8
  38.9 0.1 fusion.16
  39.0 0.5 select_reduce_fusion
  39.5 0.2 fusion.6
  39.7 0.3 fusion.1
  40.1 0.1 broadcast_in_dim.36
  40.2 11.4 %all_to_all.26.gathered_ref = bf16[8,2,8192]{2,1,0:T(2,128)(2,1)S(1)} all-to-all(bf16[8,2,8192]{2,1,0:T(2,128)(2,1)S(1)} %broadcast_in_dim.36), channel_id=1, replica_groups=mesh['groups'=2,'mp'=8,'batch'=2] {'mp'}, dimensions={0} | all-to-all | bytes 524288 | tf_op jit(solution)/shard_map/all_to_all | solution.py:399
  51.6 1.9 %down_partials.1 = f32[8,16,128]{2,1,0:T(8,128)} custom-call(s32[8,2]{1,0:T(8,128)S(1)} %convert_element_type.51.adapter_ref, bf16[8,2,8192]{2,1,0:T(2,128)(2,1)S(1)} %all_to_all.26.gathered_ref, bf16[64,64,1024]{2,1,0:T(8,128)(2,1)S(1)} %bitcast.64), custom_call_target="tpu_custom_call" | custom-call | flops 33554432 | bytes 2097152 | tf_op jit(solution)/shard_map/down_partials/pallas_call | solution.py:302
  53.5 3.6 %all-to-all-start.3 = ((f32[8,16,128]{2,1,0:T(8,128)}), f32[8,16,128]{2,1,0:T(8,128)S(1)}, u32[]{:S(2)}, u32[]{:S(2)}) async-start(f32[8,16,128]{2,1,0:T(8,128)} %down_partials.1), calls=%async_computation.3 | async-start | bytes 131072 | tf_op jit(solution)/shard_map/all_to_all | solution.py:399
  57.1 6.2 %project_out.1.base_ref = f32[16,1024]{1,0:T(8,128)S(1)} custom-call(bf16[8,2,8192]{2,1,0:T(2,128)(2,1)S(1)} %all_to_all.26.gathered_ref, bf16[8192,1024]{1,0:T(8,128)(2,1)} %weight_ref.3), custom_call_target="tpu_custom_call" | custom-call | flops 268435456 | bytes 16777216 | tf_op jit(solution)/shard_map/project_out/pallas_call | solution.py:259
  63.3 0.7 all-to-all-done.3.partials_ref
  64.0 2.5 %add_up.1 = bf16[8,2,1024]{2,1,0:T(2,128)(2,1)S(1)} custom-call(s32[8,2]{1,0:T(8,128)S(1)} %convert_element_type.51.adapter_ref, f32[16,1024]{1,0:T(8,128)S(1)} %project_out.1.base_ref, f32[8,16,128]{2,1,0:T(8,128)S(1)} %all-to-all-done.3.partials_ref, bf16[64,64,1024]{2,1,0:T(8,128)(2,1)} %store_ref.1), custom_call_target="tpu_custom_call" | custom-call | flops 33554432 | bytes 2097152 | tf_op jit(solution)/shard_map/add_up/pallas_call | solution.py:361
  66.5 11.8 %all_to_all.27.parts_ref = bf16[8,2,1024]{2,1,0:T(2,128)(2,1)S(1)} all-to-all(bf16[8,2,1024]{2,1,0:T(2,128)(2,1)S(1)} %add_up.1), channel_id=1, replica_groups=mesh['groups'=2,'mp'=8,'batch'=2] {'mp'}, dimensions={0} | all-to-all | bytes 65536 | tf_op jit(solution)/shard_map/all_to_all | solution.py:399
  78.3 0.7 add_rows.1
  (25 shorter events, 0.3 us)
Async XLA Ops:
  0.0 39.0 %copy-start = (bf16[2,256,1024]{2,1,0:T(8,128)(2,1)S(1)}, bf16[2,256,1024]{2,1,0:T(8,128)(2,1)}, u32[]{:S(2)}) copy-start(bf16[2,256,1024]{2,1,0:T(8,128)(2,1)} %param.15) | copy-start | bytes 3145732
  0.0 0.8 %copy-start.3 = (bf16[2,8192]{1,0:T(2,128)(2,1)S(1)}, bf16[2,8192]{1,0:T(2,128)(2,1)}, u32[]{:S(2)}) copy-start(bf16[2,8192]{1,0:T(2,128)(2,1)} %hidden_ref.3) | copy-start | bytes 98308
  0.9 0.7 copy-start.5
  2.6 16.2 %all-to-all-start = ((bf16[8,2,8192]{2,1,0:T(2,128)(2,1)}), bf16[8,2,8192]{2,1,0:T(2,128)(2,1)S(1)}, u32[]{:S(2)}, u32[]{:S(2)}) async-start(bf16[8,2,8192]{2,1,0:T(2,128)(2,1)} %norm_rows.1), calls=%async_computation | async-start | bytes 524288 | tf_op jit(solution)/shard_map/all_to_all | solution.py:399
  20.4 1.6 %collective-permute-start = (bf16[8,2,8192]{2,1,0:T(2,128)(2,1)S(1)}, bf16[8,2,8192]{2,1,0:T(2,128)(2,1)S(1)}, u32[]{:S(2)}, u32[]{:S(2)}) collective-permute-start(bf16[8,2,8192]{2,1,0:T(2,128)(2,1)S(1)} %all-to-all-done.near_ref), channel_id=1, source_target_pairs={{0,1},{1,0},{2,3},{3,2},{4,5},{5,4},{6,7},{7,6},{8,9},{9,8},{10,11... | collective-permute-start | bytes 786440 | tf_op jit(solution)/shard_map/ppermute | solution.py:395
  22.0 4.0 %copy-start.1 = (bf16[8192,640]{1,0:T(8,128)(2,1)S(1)}, bf16[8192,640]{1,0:T(8,128)(2,1)}, u32[]{:S(2)}) copy-start(bf16[8192,640]{1,0:T(8,128)(2,1)} %weight_ref.2) | copy-start | bytes 31457284
  26.0 13.7 %copy-start.6 = (bf16[2,256,1024]{2,1,0:T(8,128)(2,1)S(1)}, bf16[2,256,1024]{2,1,0:T(8,128)(2,1)}, u32[]{:S(2)}) copy-start(bf16[2,256,1024]{2,1,0:T(8,128)(2,1)} %param.16) | copy-start | bytes 3145732
  26.0 25.6 %copy-start.2 = (bf16[64,1024,64]{1,2,0:T(8,128)(2,1)S(1)}, bf16[64,1024,64]{1,2,0:T(8,128)(2,1)}, u32[]{:S(2)}) copy-start(bf16[64,1024,64]{1,2,0:T(8,128)(2,1)} %param.20) | copy-start | bytes 25165828
  53.5 10.5 %all-to-all-start.3 = ((f32[8,16,128]{2,1,0:T(8,128)}), f32[8,16,128]{2,1,0:T(8,128)S(1)}, u32[]{:S(2)}, u32[]{:S(2)}) async-start(f32[8,16,128]{2,1,0:T(8,128)} %down_partials.1), calls=%async_computation.3 | async-start | bytes 131072 | tf_op jit(solution)/shard_map/all_to_all | solution.py:399
  57.1 21.2 %copy-start.4 = (bf16[2,8192]{1,0:T(2,128)(2,1)S(1)}, bf16[2,8192]{1,0:T(2,128)(2,1)}, u32[]{:S(2)}) copy-start(bf16[2,8192]{1,0:T(2,128)(2,1)} %hidden_ref.3) | copy-start | bytes 98308

commit v7 on v6

--- a/solution.py
+++ b/solution.py
@@ -163,10 +163,30 @@
     )
 
 
-def norm_rows(hidden, gain, copies):
+def both_halves(frequency):
+    def kernel(frequency_ref, out_ref):
+        out_ref[...] = jnp.concatenate([frequency_ref[...], frequency_ref[...]], 1)
+
+    return call(
+        kernel,
+        "both_halves",
+        jax.ShapeDtypeStruct((1, 2 * frequency.shape[1]), frequency.dtype),
+        [VMEM],
+        16 * MIB,
+    )(frequency)
+
+
+def norm_rows(hidden, gain, frequency, lengths, slots, requests, copies):
     rows, width = hidden.shape
-
-    def kernel(hidden_ref, gain_ref, out_ref):
+    numbers = (lengths, slots, requests)
+
+    def kernel(hidden_ref, gain_ref, frequency_ref, *refs):
+        sources, (out_ref, angle_ref, adapter_ref) = refs[:3], refs[3:6]
+        held, sems = refs[6:9], refs[9]
+        fetches = []
+        for k in range(3):
+            fetches.append(pltpu.make_async_copy(sources[k], held[k], sems.at[k]))
+            fetches[-1].start()
         wide = hidden_ref[...].astype(jnp.float32)
         inverse = lax.rsqrt(jnp.mean(wide * wide, -1, keepdims=True) + EPS)
         for k in range(width // LANES):
@@ -176,14 +196,33 @@
             normed = normed.astype(jnp.bfloat16)
             for c in range(copies):
                 out_ref[c, :, part] = normed
+        for fetch in fetches:
+            fetch.wait()
+        lengths_ref, slots_ref, requests_ref = held
+        row = lax.broadcasted_iota(jnp.int32, (rows, LANES), 0)
+        position = jnp.zeros((rows, LANES), jnp.float32)
+        adapter = jnp.zeros((rows, LANES), jnp.float32)
+        for r in range(rows):
+            chosen = requests_ref[0, slots_ref[r]]
+            position = jnp.where(row == r, lengths_ref[r].astype(jnp.float32), position)
+            adapter = jnp.where(row == r, chosen.astype(jnp.float32), adapter)
+        angle_ref[0] = position
+        angle_ref[1] = position * frequency_ref[...]
+        adapter_ref[...] = adapter.astype(jnp.bfloat16)
 
     return call(
         kernel,
         "norm_rows",
-        jax.ShapeDtypeStruct((copies, rows, width), jnp.bfloat16),
-        [VMEM, VMEM],
-        hidden.size * 2 * (copies + 1),
-    )(hidden, gain.reshape(-1, LANES))
+        (
+            jax.ShapeDtypeStruct((copies, rows, width), jnp.bfloat16),
+            jax.ShapeDtypeStruct((2, rows, LANES), jnp.float32),
+            jax.ShapeDtypeStruct((rows, LANES), jnp.bfloat16),
+        ),
+        [VMEM] * 3 + [ANY] * 3,
+        32 * MIB,
+        scratch_shapes=[pltpu.SMEM(n.shape, n.dtype) for n in numbers]
+        + [pltpu.SemaphoreType.DMA((3,))],
+    )(hidden, gain.reshape(-1, LANES), frequency, *numbers)
 
 
 def project_qkv(near, far, weight, adapter, chunk=1024):
@@ -442,14 +481,6 @@
     return context_vector.reshape(rows, query_width).astype(jnp.bfloat16)
 
 
-def angles(lengths):
-    half = HEAD_DIM // 2
-    freq = THETA ** (-(jnp.arange(half, dtype=jnp.float32) * 2.0) / HEAD_DIM)
-    angle = lengths.astype(jnp.float32)[:, None] * freq
-    cosine, sine = jnp.cos(angle), jnp.sin(angle)
-    return jnp.concatenate([cosine, cosine], -1), jnp.concatenate([sine, sine], -1)
-
-
 def fast_body(
     hidden,
     attention_norm_gain,
@@ -467,15 +498,18 @@
     mp_size = lax.axis_size("mp")
     width = query_key_value_weight.shape[1]
 
-    near = exchange(norm_rows(hidden, attention_norm_gain, mp_size))
+    half = HEAD_DIM // 2
+    frequency = THETA ** (-(jnp.arange(half, dtype=jnp.float32) * 2.0) / HEAD_DIM)
+    frequency = both_halves(frequency[None])
+    sent, angle, adapter = norm_rows(
+        hidden, attention_norm_gain, frequency, lengths, slots, requests, mp_size
+    )
+    near = exchange(sent)
     far = swap_cores(near)
 
-    near, lengths, slots, requests = lax.optimization_barrier((near, lengths, slots, requests))
-    slot_hits = slots[:, None] == jnp.arange(requests.shape[1])[None, :]
-    adapter = jnp.sum(jnp.where(slot_hits, requests[0][None, :], 0), 1)
-    adapter = jnp.broadcast_to(adapter[:, None], (rows, LANES)).astype(jnp.bfloat16)
-    cosine, sine = angles(lengths)
-    live = jnp.arange(key_cache.shape[1])[None, :] < lengths[:, None]
+    near, angle, adapter = lax.optimization_barrier((near, angle, adapter))
+    cosine, sine = jnp.cos(angle[1]), jnp.sin(angle[1])
+    live = jnp.arange(key_cache.shape[1])[None, :] < angle[0, :, :1]
     far, cosine, sine, live = lax.optimization_barrier((far, cosine, sine, live))
 
     columns = project_qkv(near, far, query_key_value_weight, adapter)

time: 79.5 us -> 80.3 us (1.010)
  other arithmetic: 3.11 us -> 0.76 us
  local copies, waits for them, and re-layouts: 5.85 us -> 7.89 us
    unnamed x18 -> x22, local copies, waits for them, and re-layouts: 5.61 us -> 7.56 us
    reduce_sum x1 -> x0, other arithmetic: 0.85 us -> none  [fast_body(): adapter = jnp.sum(jnp.where(slot_hits, requests[0][None, :], 0), 1)]
  transfers between devices with their start and end apart: 3 -> 3, of which waited for: 3 -> 3; matrix products, arithmetic and copies ran while one was open for 1% -> 0% of each run, Pallas kernels for 8% -> 8%
where the time goes in v7:
time: 80.3 us; the launch traced here: 79.8 us
  blocking collectives  33.6 us (42%)
  Pallas kernels  14.6 us (18%)
  waiting for transfers between devices  11 us (14%)
  starting transfers between devices  10.9 us (14%)
  local copies, waits for them, and re-layouts  7.89 us (10%)
  matrix products  0.9 us (1%)
    all_to_all x3, blocking collectives, exchange(): return lax.all_to_all(blocks, axes, split_axis=0, concat_axis=0, tiled=True)  33.6 us
    all_to_all x2, starting transfers between devices, exchange(): return lax.all_to_all(blocks, axes, split_axis=0, concat_axis=0, tiled=True)  10.8 us
    all_to_all x2, waiting for transfers between devices, exchange(): return lax.all_to_all(blocks, axes, split_axis=0, concat_axis=0, tiled=True)  9.61 us
    unnamed x22, local copies, waits for them, and re-layouts  7.56 us
    pallas_call x1, Pallas kernels, project_out(): call(kernel, 'project_out', jax.ShapeDtypeStruct((count, weight.shape[1])...  6.19 us
    pallas_call x1, Pallas kernels, add_up(): call(kernel, 'add_up', jax.ShapeDtypeStruct((groups, count // groups, wid...  2.53 us
    pallas_call x1, Pallas kernels, project_qkv(): call(kernel, 'project_qkv', jax.ShapeDtypeStruct((2 * groups, rows, width...  1.94 us
    pallas_call x1, Pallas kernels, down_partials(): call(kernel, 'down_partials', jax.ShapeDtypeStruct((groups, count, LANES)...  1.89 us
  transfers between devices with their start and end apart: 3, of which 3 were waited for; matrix products, arithmetic and copies ran while one was open for 0% of the time, Pallas kernels for 8%

profile of v7, /device:TPU:0, one launch (start us, length us, event | category | flops | bytes accessed | tf_op | source)
XLA Modules:
  0.0 79.8 jit_solution(9411929337940266732)
XLA Ops:
  0.1 0.8 %copy-done.3 = bf16[2,8192]{1,0:T(2,128)(2,1)S(1)} copy-done((bf16[2,8192]{1,0:T(2,128)(2,1)S(1)}, bf16[2,8192]{1,0:T(2,128)(2,1)}, u32[]{:S(2)}) %copy-start.3) | copy-done | bytes 32792
  0.9 0.7 copy-done.5
  1.6 0.7 copy-done.6
  2.3 0.7 copy-done.7
  3.0 0.7 copy-done.8
  3.6 1.3 %norm_rows.1 = (bf16[8,2,8192]{2,1,0:T(2,128)(2,1)}, f32[2,2,128]{2,1,0:T(2,128)S(1)}, bf16[2,128]{1,0:T(2,128)(2,1)S(1)}) custom-call(bf16[2,8192]{1,0:T(2,128)(2,1)S(1)} %copy-done.3, bf16[64,128]{1,0:T(8,128)(2,1)S(1)} %bitcast.66, f32[1,128]{1,0:T(1,128)S(1)} %both_halves.1.frequency_ref, s32[2]{0:T(128)S(1)} %copy-done.6, s32[2]{0:T(128)S(1)} %copy-done.7, ...), custom_call_target="tpu_custom_call" | custom-call | bytes 33554432 | tf_op jit(solution)/shard_map/norm_rows/pallas_call | solution.py:213
  4.9 7.3 %all-to-all-start = ((bf16[8,2,8192]{2,1,0:T(2,128)(2,1)}), bf16[8,2,8192]{2,1,0:T(2,128)(2,1)S(1)}, u32[]{:S(2)}, u32[]{:S(2)}) async-start(bf16[8,2,8192]{2,1,0:T(2,128)(2,1)} %get-tuple-element.17), calls=%async_computation | async-start | bytes 524288 | tf_op jit(solution)/shard_map/all_to_all | solution.py:438
  12.2 8.9 %all-to-all-done.near_ref = bf16[8,2,8192]{2,1,0:T(2,128)(2,1)S(1)} async-done(((bf16[8,2,8192]{2,1,0:T(2,128)(2,1)}), bf16[8,2,8192]{2,1,0:T(2,128)(2,1)S(1)}, u32[]{:S(2)}, u32[]{:S(2)}) %all-to-all-start) | async-done | bytes 262176 | tf_op jit(solution)/shard_map/all_to_all | solution.py:438
  21.1 0.1 slice_reduce_fusion
  21.3 0.1 broadcast_compare_fusion
  21.4 1.4 %collective-permute-done.far_ref = bf16[8,2,8192]{2,1,0:T(2,128)(2,1)S(1)} collective-permute-done((bf16[8,2,8192]{2,1,0:T(2,128)(2,1)S(1)}, bf16[8,2,8192]{2,1,0:T(2,128)(2,1)S(1)}, u32[]{:S(2)}, u32[]{:S(2)}) %collective-permute-start) | collective-permute-done | bytes 262176 | tf_op jit(solution)/shard_map/ppermute | solution.py:434
  22.8 4.0 %copy-done.1 = bf16[8192,640]{1,0:T(8,128)(2,1)S(1)} copy-done((bf16[8192,640]{1,0:T(8,128)(2,1)S(1)}, bf16[8192,640]{1,0:T(8,128)(2,1)}, u32[]{:S(2)}) %copy-start.1) | copy-done | bytes 10485784
  26.8 1.9 %project_qkv.1 = bf16[16,2,768]{2,1,0:T(2,128)(2,1)S(1)} custom-call(bf16[8,2,8192]{2,1,0:T(2,128)(2,1)S(1)} %all-to-all-done.near_ref, bf16[8,2,8192]{2,1,0:T(2,128)(2,1)S(1)} %collective-permute-done.far_ref, bf16[8192,640]{1,0:T(8,128)(2,1)S(1)} %copy-done.1, bf16[2,128]{1,0:T(2,128)(2,1)S(1)} %get-tuple-element.24.adapter_ref), custom_call_target="tpu_custom_call" | custom-call | flops 335544320 | bytes 10485760 | tf_op jit(solution)/shard_map/project_qkv/pallas_call | solution.py:255
  28.7 10.4 %all_to_all.25 = bf16[16,2,768]{2,1,0:T(2,128)(2,1)S(1)} all-to-all(bf16[16,2,768]{2,1,0:T(2,128)(2,1)S(1)} %project_qkv.1), channel_id=1, replica_groups=mesh['groups'=2,'mp'=8,'batch'=2] {'mp','batch'}, dimensions={0} | all-to-all | bytes 98304 | tf_op jit(solution)/shard_map/all_to_all | solution.py:438
  39.2 0.1 convert_reduce_fusion
  39.3 0.1 slice_negate_fusion.1
  39.4 0.1 fusion.9
  39.5 0.1 fusion.19
  39.6 0.1 fusion.8
  39.7 0.1 fusion.16
  39.8 0.5 select_reduce_fusion
  40.3 0.2 fusion.6
  40.5 0.3 fusion.1
  40.9 0.1 broadcast_in_dim.16
  41.0 11.4 %all_to_all.26.gathered_ref = bf16[8,2,8192]{2,1,0:T(2,128)(2,1)S(1)} all-to-all(bf16[8,2,8192]{2,1,0:T(2,128)(2,1)S(1)} %broadcast_in_dim.16), channel_id=1, replica_groups=mesh['groups'=2,'mp'=8,'batch'=2] {'mp'}, dimensions={0} | all-to-all | bytes 524288 | tf_op jit(solution)/shard_map/all_to_all | solution.py:438
  52.4 1.9 %down_partials.1 = f32[8,16,128]{2,1,0:T(8,128)} custom-call(s32[8,2]{1,0:T(8,128)S(1)} %convert_element_type.52.adapter_ref, bf16[8,2,8192]{2,1,0:T(2,128)(2,1)S(1)} %all_to_all.26.gathered_ref, bf16[64,64,1024]{2,1,0:T(8,128)(2,1)S(1)} %bitcast.65), custom_call_target="tpu_custom_call" | custom-call | flops 33554432 | bytes 2097152 | tf_op jit(solution)/shard_map/down_partials/pallas_call | solution.py:341
  54.3 3.6 %all-to-all-start.3 = ((f32[8,16,128]{2,1,0:T(8,128)}), f32[8,16,128]{2,1,0:T(8,128)S(1)}, u32[]{:S(2)}, u32[]{:S(2)}) async-start(f32[8,16,128]{2,1,0:T(8,128)} %down_partials.1), calls=%async_computation.3 | async-start | bytes 131072 | tf_op jit(solution)/shard_map/all_to_all | solution.py:438
  57.9 6.2 %project_out.1.base_ref = f32[16,1024]{1,0:T(8,128)S(1)} custom-call(bf16[8,2,8192]{2,1,0:T(2,128)(2,1)S(1)} %all_to_all.26.gathered_ref, bf16[8192,1024]{1,0:T(8,128)(2,1)} %weight_ref.3), custom_call_target="tpu_custom_call" | custom-call | flops 268435456 | bytes 16777216 | tf_op jit(solution)/shard_map/project_out/pallas_call | solution.py:298
  64.1 0.7 all-to-all-done.3.partials_ref
  64.8 2.5 %add_up.1 = bf16[8,2,1024]{2,1,0:T(2,128)(2,1)S(1)} custom-call(s32[8,2]{1,0:T(8,128)S(1)} %convert_element_type.52.adapter_ref, f32[16,1024]{1,0:T(8,128)S(1)} %project_out.1.base_ref, f32[8,16,128]{2,1,0:T(8,128)S(1)} %all-to-all-done.3.partials_ref, bf16[64,64,1024]{2,1,0:T(8,128)(2,1)} %store_ref.1), custom_call_target="tpu_custom_call" | custom-call | flops 33554432 | bytes 2097152 | tf_op jit(solution)/shard_map/add_up/pallas_call | solution.py:400
  67.3 11.8 %all_to_all.27.parts_ref = bf16[8,2,1024]{2,1,0:T(2,128)(2,1)S(1)} all-to-all(bf16[8,2,1024]{2,1,0:T(2,128)(2,1)S(1)} %add_up.1), channel_id=1, replica_groups=mesh['groups'=2,'mp'=8,'batch'=2] {'mp'}, dimensions={0} | all-to-all | bytes 65536 | tf_op jit(solution)/shard_map/all_to_all | solution.py:438
  79.1 0.7 add_rows.1
  (28 shorter events, 0.4 us)
Async XLA Ops:
  0.0 39.8 %copy-start = (bf16[2,256,1024]{2,1,0:T(8,128)(2,1)S(1)}, bf16[2,256,1024]{2,1,0:T(8,128)(2,1)}, u32[]{:S(2)}) copy-start(bf16[2,256,1024]{2,1,0:T(8,128)(2,1)} %param.15) | copy-start | bytes 3145732
  0.1 0.8 %copy-start.3 = (bf16[2,8192]{1,0:T(2,128)(2,1)S(1)}, bf16[2,8192]{1,0:T(2,128)(2,1)}, u32[]{:S(2)}) copy-start(bf16[2,8192]{1,0:T(2,128)(2,1)} %hidden_ref.3) | copy-start | bytes 98308
  0.9 0.7 copy-start.5
  1.6 0.7 copy-start.6
  2.3 0.7 copy-start.7
  3.0 0.7 copy-start.8
  4.9 16.2 %all-to-all-start = ((bf16[8,2,8192]{2,1,0:T(2,128)(2,1)}), bf16[8,2,8192]{2,1,0:T(2,128)(2,1)S(1)}, u32[]{:S(2)}, u32[]{:S(2)}) async-start(bf16[8,2,8192]{2,1,0:T(2,128)(2,1)} %get-tuple-element.17), calls=%async_computation | async-start | bytes 524288 | tf_op jit(solution)/shard_map/all_to_all | solution.py:438
  21.2 1.6 %collective-permute-start = (bf16[8,2,8192]{2,1,0:T(2,128)(2,1)S(1)}, bf16[8,2,8192]{2,1,0:T(2,128)(2,1)S(1)}, u32[]{:S(2)}, u32[]{:S(2)}) collective-permute-start(bf16[8,2,8192]{2,1,0:T(2,128)(2,1)S(1)} %all-to-all-done.near_ref), channel_id=1, source_target_pairs={{0,1},{1,0},{2,3},{3,2},{4,5},{5,4},{6,7},{7,6},{8,9},{9,8},{10,11... | collective-permute-start | bytes 786440 | tf_op jit(solution)/shard_map/ppermute | solution.py:434
  22.8 4.0 %copy-start.1 = (bf16[8192,640]{1,0:T(8,128)(2,1)S(1)}, bf16[8192,640]{1,0:T(8,128)(2,1)}, u32[]{:S(2)}) copy-start(bf16[8192,640]{1,0:T(8,128)(2,1)} %weight_ref.2) | copy-start | bytes 31457284
  26.8 13.7 %copy-start.9 = (bf16[2,256,1024]{2,1,0:T(8,128)(2,1)S(1)}, bf16[2,256,1024]{2,1,0:T(8,128)(2,1)}, u32[]{:S(2)}) copy-start(bf16[2,256,1024]{2,1,0:T(8,128)(2,1)} %param.16) | copy-start | bytes 3145732
  26.8 25.6 %copy-start.2 = (bf16[64,1024,64]{1,2,0:T(8,128)(2,1)S(1)}, bf16[64,1024,64]{1,2,0:T(8,128)(2,1)}, u32[]{:S(2)}) copy-start(bf16[64,1024,64]{1,2,0:T(8,128)(2,1)} %param.20) | copy-start | bytes 25165828
  54.3 10.5 %all-to-all-start.3 = ((f32[8,16,128]{2,1,0:T(8,128)}), f32[8,16,128]{2,1,0:T(8,128)S(1)}, u32[]{:S(2)}, u32[]{:S(2)}) async-start(f32[8,16,128]{2,1,0:T(8,128)} %down_partials.1), calls=%async_computation.3 | async-start | bytes 131072 | tf_op jit(solution)/shard_map/all_to_all | solution.py:438
  57.9 21.2 %copy-start.4 = (bf16[2,8192]{1,0:T(2,128)(2,1)S(1)}, bf16[2,8192]{1,0:T(2,128)(2,1)}, u32[]{:S(2)}) copy-start(bf16[2,8192]{1,0:T(2,128)(2,1)} %hidden_ref.3) | copy-start | bytes 98308

commit v8 on v6

--- a/solution.py
+++ b/solution.py
@@ -1,3 +1,5 @@
+import math
+
 import jax
 import jax.numpy as jnp
 from jax import lax
@@ -169,13 +171,9 @@
     def kernel(hidden_ref, gain_ref, out_ref):
         wide = hidden_ref[...].astype(jnp.float32)
         inverse = lax.rsqrt(jnp.mean(wide * wide, -1, keepdims=True) + EPS)
-        for k in range(width // LANES):
-            part = pl.ds(k * LANES, LANES)
-            normed = hidden_ref[:, part].astype(jnp.float32) * inverse
-            normed = normed * gain_ref[k : k + 1, :].astype(jnp.float32)
-            normed = normed.astype(jnp.bfloat16)
-            for c in range(copies):
-                out_ref[c, :, part] = normed
+        normed = (wide * inverse * gain_ref[...].astype(jnp.float32)).astype(jnp.bfloat16)
+        for c in range(copies):
+            out_ref[c] = normed
 
     return call(
         kernel,
@@ -183,18 +181,34 @@
         jax.ShapeDtypeStruct((copies, rows, width), jnp.bfloat16),
         [VMEM, VMEM],
         hidden.size * 2 * (copies + 1),
-    )(hidden, gain.reshape(-1, LANES))
-
-
-def project_qkv(near, far, weight, adapter, chunk=1024):
+    )(hidden, gain[None])
+
+
+def project_qkv(near, far, weight, lengths, slots, requests, chunk=1024):
     groups, rows, _ = near.shape
     depth, width = weight.shape
     count = 2 * groups * rows
 
-    def kernel(near_ref, far_ref, weight_ref, adapter_ref, out_ref, rows_ref):
+    def kernel(
+        lengths_ref, slots_ref, requests_ref, near_ref, far_ref, weight_ref, out_ref, turn_ref,
+        rows_ref,
+    ):
         for e, source in enumerate((near_ref, far_ref)):
             for j in range(groups):
                 rows_ref[pl.ds((e * groups + j) * rows, rows)] = source[j]
+        row = lax.broadcasted_iota(jnp.int32, (rows, LANES), 0)
+        lane = lax.broadcasted_iota(jnp.int32, (rows, LANES), 1)
+        position = jnp.zeros((rows, LANES), jnp.float32)
+        adapter = jnp.zeros((rows, LANES), jnp.float32)
+        for r in range(rows):
+            chosen = requests_ref[0, slots_ref[r]]
+            position = jnp.where(row == r, lengths_ref[r].astype(jnp.float32), position)
+            adapter = jnp.where(row == r, chosen.astype(jnp.float32), adapter)
+        exponent = (lane % (HEAD_DIM // 2)).astype(jnp.float32) * (2.0 / HEAD_DIM)
+        angle = position * jnp.exp(exponent * -math.log(THETA))
+        turn_ref[0] = jnp.cos(angle)
+        turn_ref[1] = jnp.sin(angle)
+        turn_ref[2] = position
         total = jnp.zeros((count, width), jnp.float32)
         for k in range(depth // chunk):
             part = pl.ds(k * chunk, chunk)
@@ -210,18 +224,21 @@
                     jnp.bfloat16
                 )
                 out_ref[device, :, pl.ds(width, LANES)] = (
-                    adapter_ref[...] if e == 0 else jnp.zeros_like(adapter_ref)
-                )
+                    adapter if e == 0 else jnp.zeros_like(adapter)
+                ).astype(jnp.bfloat16)
 
     return call(
         kernel,
         "project_qkv",
-        jax.ShapeDtypeStruct((2 * groups, rows, width + LANES), jnp.bfloat16),
-        [VMEM, VMEM, VMEM, VMEM],
+        (
+            jax.ShapeDtypeStruct((2 * groups, rows, width + LANES), jnp.bfloat16),
+            jax.ShapeDtypeStruct((3, rows, LANES), jnp.float32),
+        ),
+        [SMEM] * 3 + [VMEM] * 3,
         weight.size * 2,
         flops=2 * count * weight.size,
         scratch_shapes=[pltpu.VMEM((count, depth), jnp.bfloat16)],
-    )(near, far, weight, adapter)
+    )(lengths, slots, requests, near, far, weight)
 
 
 def stream(weight_ref, held_ref, sems, parts):
@@ -442,14 +459,6 @@
     return context_vector.reshape(rows, query_width).astype(jnp.bfloat16)
 
 
-def angles(lengths):
-    half = HEAD_DIM // 2
-    freq = THETA ** (-(jnp.arange(half, dtype=jnp.float32) * 2.0) / HEAD_DIM)
-    angle = lengths.astype(jnp.float32)[:, None] * freq
-    cosine, sine = jnp.cos(angle), jnp.sin(angle)
-    return jnp.concatenate([cosine, cosine], -1), jnp.concatenate([sine, sine], -1)
-
-
 def fast_body(
     hidden,
     attention_norm_gain,
@@ -468,23 +477,17 @@
     width = query_key_value_weight.shape[1]
 
     near = exchange(norm_rows(hidden, attention_norm_gain, mp_size))
-    far = swap_cores(near)
-
-    near, lengths, slots, requests = lax.optimization_barrier((near, lengths, slots, requests))
-    slot_hits = slots[:, None] == jnp.arange(requests.shape[1])[None, :]
-    adapter = jnp.sum(jnp.where(slot_hits, requests[0][None, :], 0), 1)
-    adapter = jnp.broadcast_to(adapter[:, None], (rows, LANES)).astype(jnp.bfloat16)
-    cosine, sine = angles(lengths)
-    live = jnp.arange(key_cache.shape[1])[None, :] < lengths[:, None]
-    far, cosine, sine, live = lax.optimization_barrier((far, cosine, sine, live))
-
-    columns = project_qkv(near, far, query_key_value_weight, adapter)
+    columns, turn = project_qkv(
+        near, swap_cores(near), query_key_value_weight, lengths, slots, requests
+    )
     mixed = exchange(columns, ("mp", "batch"))
+    mixed, turn = lax.optimization_barrier((mixed, turn))
+    live = jnp.arange(key_cache.shape[1])[None, :] < turn[2, :, :1].astype(jnp.int32)
     adapter = mixed.reshape(mp_size, -1, rows, width + LANES)[:, :, :, width]
     adapter = jnp.sum(adapter.astype(jnp.float32), 1).astype(jnp.int32)
     qkv = mixed[:, :, :width].transpose(1, 0, 2).reshape(rows, -1)
 
-    context = attend(qkv, cosine, sine, key_cache, value_cache, live)
+    context = attend(qkv, turn[0], turn[1], key_cache, value_cache, live)
     context, adapter = lax.optimization_barrier((context, adapter))
     gathered = exchange(jnp.broadcast_to(context[None], (mp_size, *context.shape)))
 

time: 79.5 us -> 79.4 us (level)
  blocking collectives: 33.6 us -> 49.5 us
  waiting for transfers between devices: 10.3 us -> 2.23 us
  starting transfers between devices: 10.9 us -> 3.57 us
  other arithmetic: 3.11 us -> 0.85 us
  local copies, waits for them, and re-layouts: 5.85 us -> 7.76 us
    all_to_all x3 -> x4, blocking collectives: 33.6 us -> 49.5 us  [exchange(): return lax.all_to_all(blocks, axes, split_axis=0, concat_axis=0, tiled=True)]
    all_to_all x2 -> x1, waiting for transfers between devices: 9.61 us -> 0.7 us  [exchange(): return lax.all_to_all(blocks, axes, split_axis=0, concat_axis=0, tiled=True)]
    all_to_all x2 -> x1, starting transfers between devices: 10.8 us -> 3.57 us  [exchange(): return lax.all_to_all(blocks, axes, split_axis=0, concat_axis=0, tiled=True)]
    unnamed x18 -> x20, local copies, waits for them, and re-layouts: 5.61 us -> 6.76 us
    reduce_sum x1 -> x0, other arithmetic: 0.85 us -> none  [fast_body(): adapter = jnp.sum(jnp.where(slot_hits, requests[0][None, :], 0), 1)]
    ppermute x1, waiting for transfers between devices: 0.71 us -> 1.53 us  [swap_cores(): return lax.ppermute(block, 'batch', [(0, 1), (1, 0)])]
    pallas_call x1, Pallas kernels: 0.99 us -> 0.19 us  [norm_rows(): call(kernel, 'norm_rows', jax.ShapeDtypeStruct((copies, rows, width), jnp...]
  transfers between devices with their start and end apart: 3 -> 2, of which waited for: 3 -> 2; matrix products, arithmetic and copies ran while one was open for 1% -> 0% of each run, Pallas kernels for 8% -> 8%
where the time goes in v8:
time: 79.4 us; the launch traced here: 79 us
  blocking collectives  49.5 us (62%)
  Pallas kernels  14 us (18%)
  local copies, waits for them, and re-layouts  7.76 us (10%)
  starting transfers between devices  3.57 us (4%)
  waiting for transfers between devices  2.23 us (3%)
  matrix products  0.9 us (1%)
  other arithmetic  0.85 us (1%)
    all_to_all x4, blocking collectives, exchange(): return lax.all_to_all(blocks, axes, split_axis=0, concat_axis=0, tiled=True)  49.5 us
    unnamed x20, local copies, waits for them, and re-layouts  6.76 us
    pallas_call x1, Pallas kernels, project_out(): call(kernel, 'project_out', jax.ShapeDtypeStruct((count, weight.shape[1])...  6.19 us
    all_to_all x1, starting transfers between devices, exchange(): return lax.all_to_all(blocks, axes, split_axis=0, concat_axis=0, tiled=True)  3.57 us
    pallas_call x1, Pallas kernels, add_up(): call(kernel, 'add_up', jax.ShapeDtypeStruct((groups, count // groups, wid...  2.53 us
    pallas_call x1, Pallas kernels, project_qkv(): call(kernel, 'project_qkv', (jax.ShapeDtypeStruct((2 * groups, rows, widt...  2.49 us
    pallas_call x1, Pallas kernels, down_partials(): call(kernel, 'down_partials', jax.ShapeDtypeStruct((groups, count, LANES)...  1.91 us
  transfers between devices with their start and end apart: 2, of which 2 were waited for; matrix products, arithmetic and copies ran while one was open for 0% of the time, Pallas kernels for 8%

profile of v8, /device:TPU:0, one launch (start us, length us, event | category | flops | bytes accessed | tf_op | source)
XLA Modules:
  0.0 79.0 jit_solution(193905643210294449)
XLA Ops:
  0.0 0.8 %broadcast_in_dim.16.gain_ref = bf16[1,8192]{1,0:T(2,128)(2,1)S(1)} reshape(bf16[8192]{0:T(1024)(128)(2,1)} %param.12) | data formatting | bytes 32768 | tf_op jit(solution)/shard_map/broadcast_in_dim | solution.py:184
  0.8 0.0 copy-start.3
  0.8 0.7 copy-done.3
  1.6 0.2 norm_rows.1
  1.8 16.0 %all_to_all.25.near_ref = bf16[8,2,8192]{2,1,0:T(2,128)(2,1)S(1)} all-to-all(bf16[8,2,8192]{2,1,0:T(2,128)(2,1)S(1)} %norm_rows.1), channel_id=1, replica_groups=mesh['groups'=2,'mp'=8,'batch'=2] {'mp'}, dimensions={0} | all-to-all | bytes 524288 | tf_op jit(solution)/shard_map/all_to_all | solution.py:416
  17.8 1.5 %collective-permute-done.far_ref = bf16[8,2,8192]{2,1,0:T(2,128)(2,1)S(1)} collective-permute-done((bf16[8,2,8192]{2,1,0:T(2,128)(2,1)S(1)}, bf16[8,2,8192]{2,1,0:T(2,128)(2,1)S(1)}, u32[]{:S(2)}, u32[]{:S(2)}) %collective-permute-start) | collective-permute-done | bytes 262176 | tf_op jit(solution)/shard_map/ppermute | solution.py:412
  19.3 4.0 %copy-done.1 = bf16[8192,640]{1,0:T(8,128)(2,1)S(1)} copy-done((bf16[8192,640]{1,0:T(8,128)(2,1)S(1)}, bf16[8192,640]{1,0:T(8,128)(2,1)}, u32[]{:S(2)}) %copy-start.1) | copy-done | bytes 10485784
  23.3 0.7 copy-done.5
  23.9 0.7 copy-done.6
  24.6 0.7 copy-done.7
  25.2 2.5 %project_qkv.1 = (bf16[16,2,768]{2,1,0:T(2,128)(2,1)S(1)}, f32[3,2,128]{2,1,0:T(2,128)S(1)}) custom-call(s32[2]{0:T(128)S(1)} %copy-done.5, s32[2]{0:T(128)S(1)} %copy-done.6, s32[1,2]{1,0:T(1,128)S(1)} %copy-done.7, bf16[8,2,8192]{2,1,0:T(2,128)(2,1)S(1)} %all_to_all.25.near_ref, bf16[8,2,8192]{2,1,0:T(2,128)(2,1)S(1)} %collective-permute-done.far_ref, ...), custom_call_target="tpu_custom_call" | custom-call | flops 335544320 | bytes 10485760 | tf_op jit(solution)/shard_map/project_qkv/pallas_call | solution.py:230
  27.7 10.4 %all_to_all.26 = bf16[16,2,768]{2,1,0:T(2,128)(2,1)S(1)} all-to-all(bf16[16,2,768]{2,1,0:T(2,128)(2,1)S(1)} %get-tuple-element.11), channel_id=1, replica_groups=mesh['groups'=2,'mp'=8,'batch'=2] {'mp','batch'}, dimensions={0} | all-to-all | bytes 98304 | tf_op jit(solution)/shard_map/all_to_all | solution.py:416
  38.1 0.1 convert_reduce_fusion.1
  38.3 0.1 iota_compare_fusion
  38.4 0.1 convert_reduce_fusion
  38.5 0.1 slice_negate_fusion.1
  38.6 0.1 fusion.10
  38.7 0.1 fusion.18
  38.8 0.1 fusion.9
  38.9 0.1 fusion.15
  39.0 0.5 fusion.20
  39.5 0.2 fusion.7
  39.7 0.3 fusion.2
  40.1 0.1 broadcast_in_dim.29
  40.2 11.4 %all_to_all.27.gathered_ref = bf16[8,2,8192]{2,1,0:T(2,128)(2,1)S(1)} all-to-all(bf16[8,2,8192]{2,1,0:T(2,128)(2,1)S(1)} %broadcast_in_dim.29), channel_id=1, replica_groups=mesh['groups'=2,'mp'=8,'batch'=2] {'mp'}, dimensions={0} | all-to-all | bytes 524288 | tf_op jit(solution)/shard_map/all_to_all | solution.py:416
  51.6 1.9 %down_partials.1 = f32[8,16,128]{2,1,0:T(8,128)} custom-call(s32[8,2]{1,0:T(8,128)S(1)} %convert_element_type.56.adapter_ref, bf16[8,2,8192]{2,1,0:T(2,128)(2,1)S(1)} %all_to_all.27.gathered_ref, bf16[64,64,1024]{2,1,0:T(8,128)(2,1)S(1)} %bitcast.64), custom_call_target="tpu_custom_call" | custom-call | flops 33554432 | bytes 2097152 | tf_op jit(solution)/shard_map/down_partials/pallas_call | solution.py:319
  53.5 3.6 %all-to-all-start.3 = ((f32[8,16,128]{2,1,0:T(8,128)}), f32[8,16,128]{2,1,0:T(8,128)S(1)}, u32[]{:S(2)}, u32[]{:S(2)}) async-start(f32[8,16,128]{2,1,0:T(8,128)} %down_partials.1), calls=%async_computation.3 | async-start | bytes 131072 | tf_op jit(solution)/shard_map/all_to_all | solution.py:416
  57.1 6.2 %project_out.1.base_ref = f32[16,1024]{1,0:T(8,128)S(1)} custom-call(bf16[8,2,8192]{2,1,0:T(2,128)(2,1)S(1)} %all_to_all.27.gathered_ref, bf16[8192,1024]{1,0:T(8,128)(2,1)} %weight_ref.3), custom_call_target="tpu_custom_call" | custom-call | flops 268435456 | bytes 16777216 | tf_op jit(solution)/shard_map/project_out/pallas_call | solution.py:276
  63.3 0.7 all-to-all-done.3.partials_ref
  64.0 2.5 %add_up.1 = bf16[8,2,1024]{2,1,0:T(2,128)(2,1)S(1)} custom-call(s32[8,2]{1,0:T(8,128)S(1)} %convert_element_type.56.adapter_ref, f32[16,1024]{1,0:T(8,128)S(1)} %project_out.1.base_ref, f32[8,16,128]{2,1,0:T(8,128)S(1)} %all-to-all-done.3.partials_ref, bf16[64,64,1024]{2,1,0:T(8,128)(2,1)} %store_ref.1), custom_call_target="tpu_custom_call" | custom-call | flops 33554432 | bytes 2097152 | tf_op jit(solution)/shard_map/add_up/pallas_call | solution.py:378
  66.5 11.8 %all_to_all.28.parts_ref = bf16[8,2,1024]{2,1,0:T(2,128)(2,1)S(1)} all-to-all(bf16[8,2,1024]{2,1,0:T(2,128)(2,1)S(1)} %add_up.1), channel_id=1, replica_groups=mesh['groups'=2,'mp'=8,'batch'=2] {'mp'}, dimensions={0} | all-to-all | bytes 65536 | tf_op jit(solution)/shard_map/all_to_all | solution.py:416
  78.3 0.7 add_rows.1
  (23 shorter events, 0.2 us)
Async XLA Ops:
  0.0 39.0 %copy-start = (bf16[2,256,1024]{2,1,0:T(8,128)(2,1)S(1)}, bf16[2,256,1024]{2,1,0:T(8,128)(2,1)}, u32[]{:S(2)}) copy-start(bf16[2,256,1024]{2,1,0:T(8,128)(2,1)} %param.15) | copy-start | bytes 3145732
  0.8 0.8 copy-start.3
  17.8 1.5 %collective-permute-start = (bf16[8,2,8192]{2,1,0:T(2,128)(2,1)S(1)}, bf16[8,2,8192]{2,1,0:T(2,128)(2,1)S(1)}, u32[]{:S(2)}, u32[]{:S(2)}) collective-permute-start(bf16[8,2,8192]{2,1,0:T(2,128)(2,1)S(1)} %all_to_all.25.near_ref), channel_id=1, source_target_pairs={{0,1},{1,0},{2,3},{3,2},{4,5},{5,4},{6,7},{7,6},{8,9},{9,8},{10,11... | collective-permute-start | bytes 786440 | tf_op jit(solution)/shard_map/ppermute | solution.py:412
  19.3 4.0 %copy-start.1 = (bf16[8192,640]{1,0:T(8,128)(2,1)S(1)}, bf16[8192,640]{1,0:T(8,128)(2,1)}, u32[]{:S(2)}) copy-start(bf16[8192,640]{1,0:T(8,128)(2,1)} %weight_ref.2) | copy-start | bytes 31457284
  23.3 0.7 copy-start.5
  23.9 0.7 copy-start.6
  24.6 0.7 copy-start.7
  25.2 14.5 %copy-start.8 = (bf16[2,256,1024]{2,1,0:T(8,128)(2,1)S(1)}, bf16[2,256,1024]{2,1,0:T(8,128)(2,1)}, u32[]{:S(2)}) copy-start(bf16[2,256,1024]{2,1,0:T(8,128)(2,1)} %param.16) | copy-start | bytes 3145732
  25.2 26.4 %copy-start.2 = (bf16[64,1024,64]{1,2,0:T(8,128)(2,1)S(1)}, bf16[64,1024,64]{1,2,0:T(8,128)(2,1)}, u32[]{:S(2)}) copy-start(bf16[64,1024,64]{1,2,0:T(8,128)(2,1)} %param.20) | copy-start | bytes 25165828
  53.5 10.5 %all-to-all-start.3 = ((f32[8,16,128]{2,1,0:T(8,128)}), f32[8,16,128]{2,1,0:T(8,128)S(1)}, u32[]{:S(2)}, u32[]{:S(2)}) async-start(f32[8,16,128]{2,1,0:T(8,128)} %down_partials.1), calls=%async_computation.3 | async-start | bytes 131072 | tf_op jit(solution)/shard_map/all_to_all | solution.py:416
  57.1 21.2 %copy-start.4 = (bf16[2,8192]{1,0:T(2,128)(2,1)S(1)}, bf16[2,8192]{1,0:T(2,128)(2,1)}, u32[]{:S(2)}) copy-start(bf16[2,8192]{1,0:T(2,128)(2,1)} %hidden_ref.3) | copy-start | bytes 98308

commit v9 on v8

--- a/solution.py
+++ b/solution.py
@@ -146,6 +146,7 @@
 MIB = 1 << 20
 LANES = 128
 BATCH = 4
+LONG = 10**10
 STREAM = 53 * MIB
 VMEM = pl.BlockSpec(memory_space=pltpu.VMEM)
 SMEM = pl.BlockSpec(memory_space=pltpu.SMEM)
@@ -165,10 +166,27 @@
     )
 
 
-def norm_rows(hidden, gain, copies):
+def frequencies():
+    def kernel(out_ref):
+        lane = lax.broadcasted_iota(jnp.int32, (1, HEAD_DIM), 1)
+        exponent = (lane % (HEAD_DIM // 2)).astype(jnp.float32) * (2.0 / HEAD_DIM)
+        out_ref[...] = jnp.exp(exponent * -math.log(THETA))
+
+    return call(
+        kernel,
+        "frequencies",
+        jax.ShapeDtypeStruct((1, HEAD_DIM), jnp.float32),
+        [],
+        0,
+        flops=LONG // 8,
+    )()
+
+
+def norm_rows(hidden, gain, after, copies):
     rows, width = hidden.shape
 
-    def kernel(hidden_ref, gain_ref, out_ref):
+    def kernel(hidden_ref, gain_ref, after_ref, out_ref):
+        del after_ref
         wide = hidden_ref[...].astype(jnp.float32)
         inverse = lax.rsqrt(jnp.mean(wide * wide, -1, keepdims=True) + EPS)
         normed = (wide * inverse * gain_ref[...].astype(jnp.float32)).astype(jnp.bfloat16)
@@ -179,66 +197,88 @@
         kernel,
         "norm_rows",
         jax.ShapeDtypeStruct((copies, rows, width), jnp.bfloat16),
-        [VMEM, VMEM],
+        [VMEM, VMEM, ANY],
         hidden.size * 2 * (copies + 1),
-    )(hidden, gain[None])
-
-
-def project_qkv(near, far, weight, lengths, slots, requests, chunk=1024):
-    groups, rows, _ = near.shape
+        flops=LONG,
+    )(hidden, gain[None], after)
+
+
+def turns(near, frequency, lengths, slots, requests, context):
+    groups, rows, depth = near.shape
+
+    def kernel(
+        lengths_ref, slots_ref, requests_ref, near_ref, frequency_ref, lined_ref, cosine_ref,
+        sine_ref, mask_ref, adapter_ref,
+    ):
+        for j in range(groups):
+            lined_ref[pl.ds(j * rows, rows)] = near_ref[j]
+        row = lax.broadcasted_iota(jnp.int32, (rows, LANES), 0)
+        length = jnp.zeros((rows, LANES), jnp.int32)
+        adapter = jnp.zeros((rows, LANES), jnp.int32)
+        for r in range(rows):
+            length = jnp.where(row == r, lengths_ref[r], length)
+            adapter = jnp.where(row == r, requests_ref[0, slots_ref[r]], adapter)
+        angle = length.astype(jnp.float32) * frequency_ref[...]
+        cosine_ref[...] = jnp.cos(angle)
+        sine_ref[...] = jnp.sin(angle)
+        lane = lax.broadcasted_iota(jnp.int32, (rows, LANES), 1)
+        for t in range(0, context, LANES):
+            mask_ref[:, pl.ds(t, LANES)] = jnp.where(lane + t < length, 0.0, -jnp.inf)
+        adapter_ref[...] = adapter.astype(jnp.float32).astype(jnp.bfloat16)
+
+    return call(
+        kernel,
+        "turns",
+        (
+            jax.ShapeDtypeStruct((groups * rows, depth), near.dtype),
+            jax.ShapeDtypeStruct((rows, HEAD_DIM), jnp.float32),
+            jax.ShapeDtypeStruct((rows, HEAD_DIM), jnp.float32),
+            jax.ShapeDtypeStruct((rows, context), jnp.float32),
+            jax.ShapeDtypeStruct((rows, LANES), jnp.bfloat16),
+        ),
+        [SMEM] * 3 + [VMEM] * 2,
+        near.size * 4,
+    )(lengths, slots, requests, near, frequency)
+
+
+def project_qkv(lined, far, weight, adapter, chunk=1024):
+    groups, rows, _ = far.shape
     depth, width = weight.shape
-    count = 2 * groups * rows
-
-    def kernel(
-        lengths_ref, slots_ref, requests_ref, near_ref, far_ref, weight_ref, out_ref, turn_ref,
-        rows_ref,
-    ):
-        for e, source in enumerate((near_ref, far_ref)):
-            for j in range(groups):
-                rows_ref[pl.ds((e * groups + j) * rows, rows)] = source[j]
-        row = lax.broadcasted_iota(jnp.int32, (rows, LANES), 0)
-        lane = lax.broadcasted_iota(jnp.int32, (rows, LANES), 1)
-        position = jnp.zeros((rows, LANES), jnp.float32)
-        adapter = jnp.zeros((rows, LANES), jnp.float32)
-        for r in range(rows):
-            chosen = requests_ref[0, slots_ref[r]]
-            position = jnp.where(row == r, lengths_ref[r].astype(jnp.float32), position)
-            adapter = jnp.where(row == r, chosen.astype(jnp.float32), adapter)
-        exponent = (lane % (HEAD_DIM // 2)).astype(jnp.float32) * (2.0 / HEAD_DIM)
-        angle = position * jnp.exp(exponent * -math.log(THETA))
-        turn_ref[0] = jnp.cos(angle)
-        turn_ref[1] = jnp.sin(angle)
-        turn_ref[2] = position
-        total = jnp.zeros((count, width), jnp.float32)
+    half = groups * rows
+
+    def kernel(lined_ref, far_ref, weight_ref, adapter_ref, out_ref, far_lined_ref):
+        for j in range(groups):
+            far_lined_ref[pl.ds(j * rows, rows)] = far_ref[j]
+        total = jnp.zeros((2 * half, width), jnp.float32)
         for k in range(depth // chunk):
             part = pl.ds(k * chunk, chunk)
             total = total + jnp.dot(
-                rows_ref[:, part], weight_ref[part, :], preferred_element_type=jnp.float32
+                jnp.concatenate([lined_ref[:, part], far_lined_ref[:, part]]),
+                weight_ref[part, :],
+                preferred_element_type=jnp.float32,
             )
         core = lax.axis_index("batch")
+        adapter = adapter_ref[...]
         for e in range(2):
             for j in range(groups):
-                place = (e * groups + j) * rows
+                place = e * half + j * rows
                 device = 2 * j + (core ^ e)
                 out_ref[device, :, pl.ds(0, width)] = total[place : place + rows].astype(
                     jnp.bfloat16
                 )
                 out_ref[device, :, pl.ds(width, LANES)] = (
                     adapter if e == 0 else jnp.zeros_like(adapter)
-                ).astype(jnp.bfloat16)
+                )
 
     return call(
         kernel,
         "project_qkv",
-        (
-            jax.ShapeDtypeStruct((2 * groups, rows, width + LANES), jnp.bfloat16),
-            jax.ShapeDtypeStruct((3, rows, LANES), jnp.float32),
-        ),
-        [SMEM] * 3 + [VMEM] * 3,
+        jax.ShapeDtypeStruct((2 * groups, rows, width + LANES), jnp.bfloat16),
+        [VMEM] * 4,
         weight.size * 2,
-        flops=2 * count * weight.size,
-        scratch_shapes=[pltpu.VMEM((count, depth), jnp.bfloat16)],
-    )(lengths, slots, requests, near, far, weight)
+        flops=LONG,
+        scratch_shapes=[pltpu.VMEM((half, depth), jnp.bfloat16)],
+    )(lined, far, weight, adapter)
 
 
 def stream(weight_ref, held_ref, sems, parts):
@@ -416,7 +456,7 @@
     return lax.all_to_all(blocks, axes, split_axis=0, concat_axis=0, tiled=True)
 
 
-def attend(qkv, cosine, sine, key_cache, value_cache, live):
+def attend(qkv, cosine, sine, key_cache, value_cache, mask):
     rows = qkv.shape[0]
     query_width = HEADS * HEAD_DIM
     kv_width = KV_HEADS * HEAD_DIM
@@ -440,7 +480,7 @@
     scores = (
         jnp.einsum("rgqd,rtgd->rgqt", grouped, cached, preferred_element_type=jnp.float32) * scale
     )
-    scores = jnp.where(live[:, None, None, :], scores, -jnp.inf)
+    scores = scores + mask[:, None, None, :]
     own = (
         jnp.einsum("rgqd,rgd->rgq", grouped, fresh_key, preferred_element_type=jnp.float32) * scale
     )
@@ -476,18 +516,18 @@
     mp_size = lax.axis_size("mp")
     width = query_key_value_weight.shape[1]
 
-    near = exchange(norm_rows(hidden, attention_norm_gain, mp_size))
-    columns, turn = project_qkv(
-        near, swap_cores(near), query_key_value_weight, lengths, slots, requests
-    )
+    frequency = frequencies()
+    near = exchange(norm_rows(hidden, attention_norm_gain, frequency, mp_size))
+    lined, cosine, sine, mask, adapter = turns(
+        near, frequency, lengths, slots, requests, key_cache.shape[1]
+    )
+    columns = project_qkv(lined, swap_cores(near), query_key_value_weight, adapter)
     mixed = exchange(columns, ("mp", "batch"))
-    mixed, turn = lax.optimization_barrier((mixed, turn))
-    live = jnp.arange(key_cache.shape[1])[None, :] < turn[2, :, :1].astype(jnp.int32)
     adapter = mixed.reshape(mp_size, -1, rows, width + LANES)[:, :, :, width]
     adapter = jnp.sum(adapter.astype(jnp.float32), 1).astype(jnp.int32)
     qkv = mixed[:, :, :width].transpose(1, 0, 2).reshape(rows, -1)
 
-    context = attend(qkv, turn[0], turn[1], key_cache, value_cache, live)
+    context = attend(qkv, cosine, sine, key_cache, value_cache, mask)
     context, adapter = lax.optimization_barrier((context, adapter))
     gathered = exchange(jnp.broadcast_to(context[None], (mp_size, *context.shape)))
 

time: 79.4 us -> 73.2 us (0.922)
  local copies, waits for them, and re-layouts: 7.76 us -> 1.84 us
    unnamed x20 -> x22, local copies, waits for them, and re-layouts: 6.76 us -> 0.84 us
    pallas_call x1 -> x3, Pallas kernels: 2.49 us -> 2.64 us  [the longest x1 1.91 us: project_qkv(): call(kernel, 'project_qkv', jax.ShapeDtypeStruct((2 * groups, rows, width...]
  transfers between devices with their start and end apart: 2 -> 2, of which waited for: 2 -> 2; matrix products, arithmetic and copies ran while one was open for 0% -> 0% of each run, Pallas kernels for 8% -> 9%
where the time goes in v9:
time: 73.2 us; the launch traced here: 72.8 us
  blocking collectives  49.9 us (68%)
  Pallas kernels  14.2 us (19%)
  starting transfers between devices  3.57 us (5%)
  local copies, waits for them, and re-layouts  1.84 us (3%)
  waiting for transfers between devices  1.49 us (2%)
  matrix products  0.9 us (1%)
    all_to_all x4, blocking collectives, exchange(): return lax.all_to_all(blocks, axes, split_axis=0, concat_axis=0, tiled=True)  49.9 us
    pallas_call x1, Pallas kernels, project_out(): call(kernel, 'project_out', jax.ShapeDtypeStruct((count, weight.shape[1])...  6.19 us
    all_to_all x1, starting transfers between devices, exchange(): return lax.all_to_all(blocks, axes, split_axis=0, concat_axis=0, tiled=True)  3.57 us
    pallas_call x1, Pallas kernels, add_up(): call(kernel, 'add_up', jax.ShapeDtypeStruct((groups, count // groups, wid...  2.64 us
    pallas_call x1, Pallas kernels, project_qkv(): call(kernel, 'project_qkv', jax.ShapeDtypeStruct((2 * groups, rows, width...  1.91 us
    pallas_call x1, Pallas kernels, down_partials(): call(kernel, 'down_partials', jax.ShapeDtypeStruct((groups, count, LANES)...  1.9 us
  transfers between devices with their start and end apart: 2, of which 2 were waited for; matrix products, arithmetic and copies ran while one was open for 0% of the time, Pallas kernels for 9%

profile of v9, /device:TPU:0, one launch (start us, length us, event | category | flops | bytes accessed | tf_op | source)
XLA Modules:
  0.0 72.8 jit_solution(9104014601225125943)
XLA Ops:
  0.0 0.0 copy-start
  0.0 0.8 %broadcast_in_dim.4.gain_ref = bf16[1,8192]{1,0:T(2,128)(2,1)S(1)} reshape(bf16[8192]{0:T(1024)(128)(2,1)} %param.12) | data formatting | bytes 32768 | tf_op jit(solution)/shard_map/broadcast_in_dim | solution.py:203
  0.8 0.0 copy-start.1
  0.9 0.7 %copy-done.1 = bf16[2,8192]{1,0:T(2,128)(2,1)S(1)} copy-done((bf16[2,8192]{1,0:T(2,128)(2,1)S(1)}, bf16[2,8192]{1,0:T(2,128)(2,1)}, u32[]{:S(2)}) %copy-start.1) | copy-done | bytes 32792
  1.6 0.2 norm_rows.1
  1.8 16.2 %all_to_all.25.near_ref = bf16[8,2,8192]{2,1,0:T(2,128)(2,1)S(1)} all-to-all(bf16[8,2,8192]{2,1,0:T(2,128)(2,1)S(1)} %norm_rows.1), channel_id=1, replica_groups=mesh['groups'=2,'mp'=8,'batch'=2] {'mp'}, dimensions={0} | all-to-all | bytes 524288 | tf_op jit(solution)/shard_map/all_to_all | solution.py:456
  18.0 0.0 collective-permute-start
  18.1 0.0 copy-done.3
  18.1 0.0 copy-done.4
  18.1 0.7 turns.1
  18.8 0.8 %collective-permute-done.far_ref = bf16[8,2,8192]{2,1,0:T(2,128)(2,1)S(1)} collective-permute-done((bf16[8,2,8192]{2,1,0:T(2,128)(2,1)S(1)}, bf16[8,2,8192]{2,1,0:T(2,128)(2,1)S(1)}, u32[]{:S(2)}, u32[]{:S(2)}) %collective-permute-start) | collective-permute-done | bytes 262176 | tf_op jit(solution)/shard_map/ppermute | solution.py:452
  19.6 1.9 %project_qkv.1 = bf16[16,2,768]{2,1,0:T(2,128)(2,1)S(1)} custom-call(bf16[16,8192]{1,0:T(8,128)(2,1)S(1)} %get-tuple-element.12.lined_ref, bf16[8,2,8192]{2,1,0:T(2,128)(2,1)S(1)} %collective-permute-done.far_ref, bf16[8192,640]{1,0:T(8,128)(2,1)S(1)} %copy-done.6, bf16[2,128]{1,0:T(2,128)(2,1)S(1)} %get-tuple-element.13.adapter_ref), custom_call_target="tpu_custom_call" | custom-call | flops 10000000000 | bytes 10485760 | tf_op jit(solution)/shard_map/project_qkv/pallas_call | solution.py:273
  21.5 10.5 %all_to_all.26 = bf16[16,2,768]{2,1,0:T(2,128)(2,1)S(1)} all-to-all(bf16[16,2,768]{2,1,0:T(2,128)(2,1)S(1)} %project_qkv.1), channel_id=1, replica_groups=mesh['groups'=2,'mp'=8,'batch'=2] {'mp','batch'}, dimensions={0} | all-to-all | bytes 98304 | tf_op jit(solution)/shard_map/all_to_all | solution.py:456
  32.1 0.1 convert_reduce_fusion
  32.2 0.1 slice_negate_fusion.1
  32.3 0.1 fusion.10
  32.4 0.1 fusion.18
  32.5 0.1 fusion.9
  32.6 0.1 fusion.15
  32.7 0.5 fusion.20
  33.2 0.2 fusion.7
  33.4 0.0 copy-done.7
  33.4 0.3 fusion.2
  33.8 0.1 broadcast_in_dim.5
  33.9 11.4 %all_to_all.27.gathered_ref = bf16[8,2,8192]{2,1,0:T(2,128)(2,1)S(1)} all-to-all(bf16[8,2,8192]{2,1,0:T(2,128)(2,1)S(1)} %broadcast_in_dim.5), channel_id=1, replica_groups=mesh['groups'=2,'mp'=8,'batch'=2] {'mp'}, dimensions={0} | all-to-all | bytes 524288 | tf_op jit(solution)/shard_map/all_to_all | solution.py:456
  45.3 1.9 %down_partials.1 = f32[8,16,128]{2,1,0:T(8,128)} custom-call(s32[8,2]{1,0:T(8,128)S(1)} %convert_element_type.43.adapter_ref, bf16[8,2,8192]{2,1,0:T(2,128)(2,1)S(1)} %all_to_all.27.gathered_ref, bf16[64,64,1024]{2,1,0:T(8,128)(2,1)S(1)} %bitcast.62), custom_call_target="tpu_custom_call" | custom-call | flops 33554432 | bytes 2097152 | tf_op jit(solution)/shard_map/down_partials/pallas_call | solution.py:359
  47.2 3.6 %all-to-all-start.3 = ((f32[8,16,128]{2,1,0:T(8,128)}), f32[8,16,128]{2,1,0:T(8,128)S(1)}, u32[]{:S(2)}, u32[]{:S(2)}) async-start(f32[8,16,128]{2,1,0:T(8,128)} %down_partials.1), calls=%async_computation.3 | async-start | bytes 131072 | tf_op jit(solution)/shard_map/all_to_all | solution.py:456
  50.8 6.2 %project_out.1.base_ref = f32[16,1024]{1,0:T(8,128)S(1)} custom-call(bf16[8,2,8192]{2,1,0:T(2,128)(2,1)S(1)} %all_to_all.27.gathered_ref, bf16[8192,1024]{1,0:T(8,128)(2,1)} %weight_ref.3), custom_call_target="tpu_custom_call" | custom-call | flops 268435456 | bytes 16777216 | tf_op jit(solution)/shard_map/project_out/pallas_call | solution.py:316
  57.0 0.7 all-to-all-done.3.partials_ref
  57.7 2.6 %add_up.1 = bf16[8,2,1024]{2,1,0:T(2,128)(2,1)S(1)} custom-call(s32[8,2]{1,0:T(8,128)S(1)} %convert_element_type.43.adapter_ref, f32[16,1024]{1,0:T(8,128)S(1)} %project_out.1.base_ref, f32[8,16,128]{2,1,0:T(8,128)S(1)} %all-to-all-done.3.partials_ref, bf16[64,64,1024]{2,1,0:T(8,128)(2,1)} %store_ref.1), custom_call_target="tpu_custom_call" | custom-call | flops 33554432 | bytes 2097152 | tf_op jit(solution)/shard_map/add_up/pallas_call | solution.py:418
  60.4 11.8 %all_to_all.28.parts_ref = bf16[8,2,1024]{2,1,0:T(2,128)(2,1)S(1)} all-to-all(bf16[8,2,1024]{2,1,0:T(2,128)(2,1)S(1)} %add_up.1), channel_id=1, replica_groups=mesh['groups'=2,'mp'=8,'batch'=2] {'mp'}, dimensions={0} | all-to-all | bytes 65536 | tf_op jit(solution)/shard_map/all_to_all | solution.py:456
  72.1 0.7 add_rows.1
  (25 shorter events, 0.2 us)
Async XLA Ops:
  0.0 32.7 %copy-start = (bf16[2,256,1024]{2,1,0:T(8,128)(2,1)S(1)}, bf16[2,256,1024]{2,1,0:T(8,128)(2,1)}, u32[]{:S(2)}) copy-start(bf16[2,256,1024]{2,1,0:T(8,128)(2,1)} %param.15) | copy-start | bytes 3145732
  0.8 0.8 %copy-start.1 = (bf16[2,8192]{1,0:T(2,128)(2,1)S(1)}, bf16[2,8192]{1,0:T(2,128)(2,1)}, u32[]{:S(2)}) copy-start(bf16[2,8192]{1,0:T(2,128)(2,1)} %hidden_ref.3) | copy-start | bytes 98308
  1.6 16.4 %copy-start.3 = (s32[2]{0:T(128)S(1)}, s32[2]{0:T(128)}, u32[]{:S(2)}) copy-start(s32[2]{0:T(128)} %lengths_ref.1) | copy-start | bytes 28
  1.6 16.4 %copy-start.4 = (s32[2]{0:T(128)S(1)}, s32[2]{0:T(128)}, u32[]{:S(2)}) copy-start(s32[2]{0:T(128)} %slots_ref.1) | copy-start | bytes 28
  1.6 16.5 %copy-start.5 = (s32[1,2]{1,0:T(1,128)S(1)}, s32[1,2]{1,0:T(1,128)}, u32[]{:S(2)}) copy-start(s32[1,2]{1,0:T(1,128)} %requests_ref.1) | copy-start | bytes 28
  1.6 18.0 %copy-start.6 = (bf16[8192,640]{1,0:T(8,128)(2,1)S(1)}, bf16[8192,640]{1,0:T(8,128)(2,1)}, u32[]{:S(2)}) copy-start(bf16[8192,640]{1,0:T(8,128)(2,1)} %weight_ref.2) | copy-start | bytes 31457284
  18.0 1.5 %collective-permute-start = (bf16[8,2,8192]{2,1,0:T(2,128)(2,1)S(1)}, bf16[8,2,8192]{2,1,0:T(2,128)(2,1)S(1)}, u32[]{:S(2)}, u32[]{:S(2)}) collective-permute-start(bf16[8,2,8192]{2,1,0:T(2,128)(2,1)S(1)} %all_to_all.25.near_ref), channel_id=1, source_target_pairs={{0,1},{1,0},{2,3},{3,2},{4,5},{5,4},{6,7},{7,6},{8,9},{9,8},{10,11... | collective-permute-start | bytes 786440 | tf_op jit(solution)/shard_map/ppermute | solution.py:452
  19.6 25.7 %slice-start = ((s8[8388608]{0:T(1024)(128)(4,1)}), s8[4194304]{0:T(1024)(128)(4,1)S(1)}, s32[]{:S(2)}) async-start(s8[8388608]{0:T(1024)(128)(4,1)} %bitcast.60), calls=%async_computation.5 | async-start | bytes 8388608
  19.6 13.8 %copy-start.7 = (bf16[2,256,1024]{2,1,0:T(8,128)(2,1)S(1)}, bf16[2,256,1024]{2,1,0:T(8,128)(2,1)}, u32[]{:S(2)}) copy-start(bf16[2,256,1024]{2,1,0:T(8,128)(2,1)} %param.16) | copy-start | bytes 3145732
  19.6 25.7 %slice-start.1 = ((s8[8388608]{0:T(1024)(128)(4,1)}), s8[4194304]{0:T(1024)(128)(4,1)S(1)}, s32[]{:S(2)}) async-start(s8[8388608]{0:T(1024)(128)(4,1)} %bitcast.60), calls=%async_computation.6 | async-start | bytes 8388608
  47.2 10.5 %all-to-all-start.3 = ((f32[8,16,128]{2,1,0:T(8,128)}), f32[8,16,128]{2,1,0:T(8,128)S(1)}, u32[]{:S(2)}, u32[]{:S(2)}) async-start(f32[8,16,128]{2,1,0:T(8,128)} %down_partials.1), calls=%async_computation.3 | async-start | bytes 131072 | tf_op jit(solution)/shard_map/all_to_all | solution.py:456
  50.8 21.3 %copy-start.2 = (bf16[2,8192]{1,0:T(2,128)(2,1)S(1)}, bf16[2,8192]{1,0:T(2,128)(2,1)}, u32[]{:S(2)}) copy-start(bf16[2,8192]{1,0:T(2,128)(2,1)} %hidden_ref.3) | copy-start | bytes 98308

commit v10 on v9

--- a/solution.py
+++ b/solution.py
@@ -166,20 +166,21 @@
     )
 
 
-def frequencies():
+def exponents():
     def kernel(out_ref):
         lane = lax.broadcasted_iota(jnp.int32, (1, HEAD_DIM), 1)
-        exponent = (lane % (HEAD_DIM // 2)).astype(jnp.float32) * (2.0 / HEAD_DIM)
-        out_ref[...] = jnp.exp(exponent * -math.log(THETA))
-
-    return call(
-        kernel,
-        "frequencies",
-        jax.ShapeDtypeStruct((1, HEAD_DIM), jnp.float32),
-        [],
-        0,
-        flops=LONG // 8,
-    )()
+        out_ref[...] = (lane % (HEAD_DIM // 2)).astype(jnp.float32) * (-2.0 / HEAD_DIM)
+
+    shape = jax.ShapeDtypeStruct((1, HEAD_DIM), jnp.float32)
+    return call(kernel, "exponents", shape, [], 0, flops=LONG // 8)()
+
+
+def frequencies(exponent):
+    def kernel(exponent_ref, out_ref):
+        out_ref[...] = jnp.exp(exponent_ref[...] * math.log(THETA))
+
+    shape = jax.ShapeDtypeStruct(exponent.shape, jnp.float32)
+    return call(kernel, "frequencies", shape, [VMEM], 0, flops=LONG // 8)(exponent)
 
 
 def norm_rows(hidden, gain, after, copies):
@@ -298,12 +299,22 @@
     return part
 
 
-def project_out(gathered, weight, parts=16):
+def project_out(gathered, weight, adapter, store, parts=16):
     groups, rows, depth = gathered.shape
     count, step = groups * rows, depth // parts
-
-    def kernel(gathered_ref, weight_ref, out_ref, rows_ref, held_ref, sems):
+    rank, width = store.shape[1:]
+
+    def kernel(
+        adapter_ref, gathered_ref, weight_ref, store_ref, out_ref, up_ref, rows_ref, held_ref, sems,
+        up_sems,
+    ):
         part = stream(weight_ref, held_ref, sems, parts)
+        picks = []
+        for r in range(count):
+            chosen = adapter_ref[r // rows, r % rows]
+            target = up_ref.at[pl.ds(r * rank, rank)]
+            picks.append(pltpu.make_async_copy(store_ref.at[chosen], target, up_sems.at[r]))
+            picks[-1].start()
         for j in range(groups):
             rows_ref[pl.ds(j * rows, rows)] = gathered_ref[j]
         total = jnp.zeros(out_ref.shape, jnp.float32)
@@ -312,21 +323,27 @@
                 rows_ref[:, pl.ds(k * step, step)], part(k), preferred_element_type=jnp.float32
             )
         out_ref[...] = total
+        for pick in picks:
+            pick.wait()
 
     return call(
         kernel,
         "project_out",
-        jax.ShapeDtypeStruct((count, weight.shape[1]), jnp.float32),
-        [VMEM, ANY],
-        weight.size * 2,
+        (
+            jax.ShapeDtypeStruct((count, weight.shape[1]), jnp.float32),
+            pltpu.VMEM((count * rank, width), store.dtype),
+        ),
+        [SMEM, VMEM, ANY, ANY],
+        weight.size * 2 + count * rank * width * 2,
         limit=STREAM,
         flops=2 * count * weight.size,
         scratch_shapes=[
             pltpu.VMEM((count, depth), gathered.dtype),
             pltpu.VMEM(weight.shape, weight.dtype),
             pltpu.SemaphoreType.DMA((parts,)),
+            pltpu.SemaphoreType.DMA((count,)),
         ],
-    )(gathered, weight)
+    )(adapter, gathered, weight, store)
 
 
 def down_partials(gathered, adapter, store):
@@ -368,49 +385,23 @@
     )(adapter, gathered, store)
 
 
-def pick(adapter_ref, store_ref, held_ref, sems):
-    groups, rows = adapter_ref.shape
-    count, rank = groups * rows, store_ref.shape[1]
-    copies = []
-    for r in range(count):
-        copies.append(
-            pltpu.make_async_copy(
-                store_ref.at[adapter_ref[r // rows, r % rows]], held_ref.at[pl.ds(r * rank, rank)], sems.at[r]
-            )
-        )
-        copies[-1].start()
-
-    def batch(k):
-        for copy in copies[k * BATCH : (k + 1) * BATCH]:
-            copy.wait()
-        return held_ref[pl.ds(k * BATCH * rank, BATCH * rank)]
-
-    return batch
-
-
-def add_up(base, partials, adapter, store):
-    count = adapter.size
-    rank, width = store.shape[1:]
-    groups = partials.shape[0]
-
-    def kernel(adapter_ref, base_ref, partials_ref, store_ref, out_ref, held_ref, sems):
-        batch = pick(adapter_ref, store_ref, held_ref, sems)
+def add_up(base, partials, up):
+    groups, count, _ = partials.shape
+    depth, width = up.shape
+    rank = depth // count
+
+    def kernel(base_ref, partials_ref, up_ref, out_ref):
         total = partials_ref[0]
         for c in range(1, groups):
             total = total + partials_ref[c]
         down = total.astype(jnp.bfloat16).astype(jnp.float32)
         row = lax.broadcasted_iota(jnp.int32, (count, LANES), 0)
         lane = lax.broadcasted_iota(jnp.int32, (count, LANES), 1)
-        delta = jnp.zeros((count, width), jnp.float32)
-        for k in range(count // BATCH):
-            spread = []
-            for s in range(BATCH * rank // LANES):
-                first = k * BATCH * rank + s * LANES
-                spread.append(jnp.where(row == (lane + first) // rank, down, 0.0))
-            spread = jnp.concatenate(spread, 1).astype(jnp.bfloat16)
-            delta = delta + jnp.dot(
-                spread, batch(k), preferred_element_type=jnp.float32
-            )
+        spread = []
+        for s in range(0, depth, LANES):
+            spread.append(jnp.where(row == (lane + s) // rank, down, 0.0))
+        spread = jnp.concatenate(spread, 1).astype(jnp.bfloat16)
+        delta = jnp.dot(spread, up_ref[...], preferred_element_type=jnp.float32)
         result = (base_ref[...] + ADAPTER_SCALE * delta).astype(jnp.bfloat16)
         for j in range(groups):
             out_ref[j] = result[j * count // groups : (j + 1) * count // groups]
@@ -419,15 +410,11 @@
         kernel,
         "add_up",
         jax.ShapeDtypeStruct((groups, count // groups, width), jnp.bfloat16),
-        [SMEM, VMEM, VMEM, ANY],
-        2 * count * rank * width,
-        limit=STREAM,
-        flops=2 * count * count * rank * width,
-        scratch_shapes=[
-            pltpu.VMEM((count * rank, width), store.dtype),
-            pltpu.SemaphoreType.DMA((count,)),
-        ],
-    )(adapter, base, partials, store)
+        [VMEM] * 3,
+        up.size * 2,
+        limit=4 * MIB,
+        flops=2 * count * up.size,
+    )(base, partials, up)
 
 
 def add_rows(hidden, parts):
@@ -516,7 +503,7 @@
     mp_size = lax.axis_size("mp")
     width = query_key_value_weight.shape[1]
 
-    frequency = frequencies()
+    frequency = frequencies(exponents())
     near = exchange(norm_rows(hidden, attention_norm_gain, frequency, mp_size))
     lined, cosine, sine, mask, adapter = turns(
         near, frequency, lengths, slots, requests, key_cache.shape[1]
@@ -534,8 +521,8 @@
     partials = exchange(
         down_partials(gathered, adapter, adapter_down_matrices.swapaxes(1, 2))
     )
-    base = project_out(gathered, output_weight)
-    projected = add_up(base, partials, adapter, adapter_up_matrices)
+    base, up = project_out(gathered, output_weight, adapter, adapter_up_matrices)
+    projected = add_up(base, partials, up)
     return add_rows(hidden, exchange(projected))
 
 

time: 73.2 us -> 73.4 us (level)
    pallas_call x2 -> x3, Pallas kernels: 6.2 us -> 8.51 us  [the longest x1 8.5 us: project_out(): call(kernel, 'project_out', (jax.ShapeDtypeStruct((count, weight.shape[1]...]
    pallas_call x1, Pallas kernels: 2.64 us -> 0.39 us  [add_up(): call(kernel, 'add_up', jax.ShapeDtypeStruct((groups, count // groups, wid...]
    unnamed x22 -> x32, local copies, waits for them, and re-layouts: 0.84 us -> 1.75 us
    broadcast_in_dim x1, local copies, waits for them, and re-layouts: 0.83 us -> 0.02 us  [norm_rows(): gain[None]]
  transfers between devices with their start and end apart: 2 -> 2, of which waited for: 2 -> 1; matrix products, arithmetic and copies ran while one was open for 0% -> 0% of each run, Pallas kernels for 9% -> 13%
where the time goes in v10:
time: 73.4 us; the launch traced here: 73 us
  blocking collectives  50.6 us (69%)
  Pallas kernels  14.3 us (19%)
  starting transfers between devices  3.57 us (5%)
  local copies, waits for them, and re-layouts  1.94 us (3%)
  matrix products  0.9 us (1%)
  waiting for transfers between devices  0.8 us (1%)
    all_to_all x4, blocking collectives, exchange(): return lax.all_to_all(blocks, axes, split_axis=0, concat_axis=0, tiled=True)  50.6 us
    pallas_call x1, Pallas kernels, project_out(): call(kernel, 'project_out', (jax.ShapeDtypeStruct((count, weight.shape[1]...  8.5 us
    all_to_all x1, starting transfers between devices, exchange(): return lax.all_to_all(blocks, axes, split_axis=0, concat_axis=0, tiled=True)  3.57 us
    pallas_call x1, Pallas kernels, project_qkv(): call(kernel, 'project_qkv', jax.ShapeDtypeStruct((2 * groups, rows, width...  1.92 us
    pallas_call x1, Pallas kernels, down_partials(): call(kernel, 'down_partials', jax.ShapeDtypeStruct((groups, count, LANES)...  1.9 us
    unnamed x32, local copies, waits for them, and re-layouts  1.75 us
  transfers between devices with their start and end apart: 2, of which 1 were waited for; matrix products, arithmetic and copies ran while one was open for 0% of the time, Pallas kernels for 13%

profile of v10, /device:TPU:0, one launch (start us, length us, event | category | flops | bytes accessed | tf_op | source)
XLA Modules:
  0.0 73.0 jit_solution(4951512972460935372)
XLA Ops:
  0.0 0.0 slice-start.2
  0.0 0.8 %copy-done.8 = bf16[8192]{0:T(1024)(128)(2,1)S(1)} copy-done((bf16[8192]{0:T(1024)(128)(2,1)S(1)}, bf16[8192]{0:T(1024)(128)(2,1)}, u32[]{:S(2)}) %copy-start.8) | copy-done | bytes 16408
  0.8 0.0 copy-done.4
  0.9 0.0 slice-start.3
  0.9 0.0 slice-start.4
  0.9 0.2 norm_rows.1
  1.1 16.2 %all_to_all.25.near_ref = bf16[8,2,8192]{2,1,0:T(2,128)(2,1)S(1)} all-to-all(bf16[8,2,8192]{2,1,0:T(2,128)(2,1)S(1)} %norm_rows.1), channel_id=1, replica_groups=mesh['groups'=2,'mp'=8,'batch'=2] {'mp'}, dimensions={0} | all-to-all | bytes 524288 | tf_op jit(solution)/shard_map/all_to_all | solution.py:443
  17.3 0.0 collective-permute-start
  17.4 0.7 turns.1
  18.1 0.8 %collective-permute-done.far_ref = bf16[8,2,8192]{2,1,0:T(2,128)(2,1)S(1)} collective-permute-done((bf16[8,2,8192]{2,1,0:T(2,128)(2,1)S(1)}, bf16[8,2,8192]{2,1,0:T(2,128)(2,1)S(1)}, u32[]{:S(2)}, u32[]{:S(2)}) %collective-permute-start) | collective-permute-done | bytes 262176 | tf_op jit(solution)/shard_map/ppermute | solution.py:439
  18.9 0.0 copy-start.9
  18.9 1.9 %project_qkv.1 = bf16[16,2,768]{2,1,0:T(2,128)(2,1)S(1)} custom-call(bf16[16,8192]{1,0:T(8,128)(2,1)S(1)} %get-tuple-element.14.lined_ref, bf16[8,2,8192]{2,1,0:T(2,128)(2,1)S(1)} %collective-permute-done.far_ref, bf16[8192,640]{1,0:T(8,128)(2,1)S(1)} %bitcast.64, bf16[2,128]{1,0:T(2,128)(2,1)S(1)} %get-tuple-element.15.adapter_ref), custom_call_target="tpu_custom_call" | custom-call | flops 10000000000 | bytes 10485760 | tf_op jit(solution)/shard_map/project_qkv/pallas_call | solution.py:274
  20.8 10.5 %all_to_all.26 = bf16[16,2,768]{2,1,0:T(2,128)(2,1)S(1)} all-to-all(bf16[16,2,768]{2,1,0:T(2,128)(2,1)S(1)} %project_qkv.1), channel_id=1, replica_groups=mesh['groups'=2,'mp'=8,'batch'=2] {'mp','batch'}, dimensions={0} | all-to-all | bytes 98304 | tf_op jit(solution)/shard_map/all_to_all | solution.py:443
  31.5 0.1 slice_negate_fusion.1
  31.5 0.1 fusion.10
  31.6 0.1 fusion.18
  31.7 0.1 fusion.9
  31.8 0.1 fusion.15
  31.9 0.5 fusion.20
  32.4 0.2 fusion.7
  32.6 0.3 fusion.2
  33.0 0.1 convert_reduce_fusion
  33.1 0.0 copy-start.3
  33.1 0.1 broadcast_in_dim.5
  33.3 11.4 %all_to_all.27.gathered_ref = bf16[8,2,8192]{2,1,0:T(2,128)(2,1)S(1)} all-to-all(bf16[8,2,8192]{2,1,0:T(2,128)(2,1)S(1)} %broadcast_in_dim.5), channel_id=1, replica_groups=mesh['groups'=2,'mp'=8,'batch'=2] {'mp'}, dimensions={0} | all-to-all | bytes 524288 | tf_op jit(solution)/shard_map/all_to_all | solution.py:443
  44.7 1.9 %down_partials.1 = f32[8,16,128]{2,1,0:T(8,128)} custom-call(s32[8,2]{1,0:T(8,128)S(1)} %convert_element_type.43.adapter_ref, bf16[8,2,8192]{2,1,0:T(2,128)(2,1)S(1)} %all_to_all.27.gathered_ref, bf16[64,64,1024]{2,1,0:T(8,128)(2,1)S(1)} %bitcast.62), custom_call_target="tpu_custom_call" | custom-call | flops 33554432 | bytes 2097152 | tf_op jit(solution)/shard_map/down_partials/pallas_call | solution.py:376
  46.6 3.6 %all-to-all-start.3 = ((f32[8,16,128]{2,1,0:T(8,128)}), f32[8,16,128]{2,1,0:T(8,128)S(1)}, u32[]{:S(2)}, u32[]{:S(2)}) async-start(f32[8,16,128]{2,1,0:T(8,128)} %down_partials.1), calls=%async_computation.3 | async-start | bytes 131072 | tf_op jit(solution)/shard_map/all_to_all | solution.py:443
  50.2 8.5 %project_out.1 = (f32[16,1024]{1,0:T(8,128)}, bf16[1024,1024]{1,0:T(8,128)(2,1)S(1)}) custom-call(s32[8,2]{1,0:T(8,128)} %copy-done.3, bf16[8,2,8192]{2,1,0:T(2,128)(2,1)} %copy-done.1, bf16[8192,1024]{1,0:T(8,128)(2,1)} %weight_ref.3, bf16[64,64,1024]{2,1,0:T(8,128)(2,1)} %store_ref.1), custom_call_target="tpu_custom_call" | custom-call | flops 268435456 | bytes 18874368 | tf_op jit(solution)/shard_map/project_out/pallas_call | solution.py:329
  58.7 0.8 %copy-done.2 = f32[16,1024]{1,0:T(8,128)S(1)} copy-done((f32[16,1024]{1,0:T(8,128)S(1)}, f32[16,1024]{1,0:T(8,128)}, u32[]{:S(2)}) %copy-start.2) | copy-done | bytes 65560
  59.5 0.4 add_up.1
  59.9 12.5 %all_to_all.28.parts_ref = bf16[8,2,1024]{2,1,0:T(2,128)(2,1)S(1)} all-to-all(bf16[8,2,1024]{2,1,0:T(2,128)(2,1)S(1)} %add_up.1), channel_id=1, replica_groups=mesh['groups'=2,'mp'=8,'batch'=2] {'mp'}, dimensions={0} | all-to-all | bytes 65536 | tf_op jit(solution)/shard_map/all_to_all | solution.py:443
  72.4 0.7 add_rows.1
  (37 shorter events, 0.2 us)
Async XLA Ops:
  0.0 31.9 %copy-start = (bf16[2,256,1024]{2,1,0:T(8,128)(2,1)S(1)}, bf16[2,256,1024]{2,1,0:T(8,128)(2,1)}, u32[]{:S(2)}) copy-start(bf16[2,256,1024]{2,1,0:T(8,128)(2,1)} %param.15) | copy-start | bytes 3145732
  0.0 0.8 %copy-start.8 = (bf16[8192]{0:T(1024)(128)(2,1)S(1)}, bf16[8192]{0:T(1024)(128)(2,1)}, u32[]{:S(2)}) copy-start(bf16[8192]{0:T(1024)(128)(2,1)} %param.12) | copy-start | bytes 49156
  0.0 0.9 %copy-start.4 = (bf16[2,8192]{1,0:T(2,128)(2,1)S(1)}, bf16[2,8192]{1,0:T(2,128)(2,1)}, u32[]{:S(2)}) copy-start(bf16[2,8192]{1,0:T(2,128)(2,1)} %hidden_ref.3) | copy-start | bytes 98308
  0.0 18.9 %slice-start.2 = ((s8[10485760]{0:T(1024)(128)(4,1)}), s8[4194304]{0:T(1024)(128)(4,1)S(1)}, s32[]{:S(2)}) async-start(s8[10485760]{0:T(1024)(128)(4,1)} %bitcast.63), calls=%async_computation.7 | async-start | bytes 8388608
  0.9 16.5 %copy-start.5 = (s32[2]{0:T(128)S(1)}, s32[2]{0:T(128)}, u32[]{:S(2)}) copy-start(s32[2]{0:T(128)} %lengths_ref.1) | copy-start | bytes 28
  0.9 16.5 %copy-start.6 = (s32[2]{0:T(128)S(1)}, s32[2]{0:T(128)}, u32[]{:S(2)}) copy-start(s32[2]{0:T(128)} %slots_ref.1) | copy-start | bytes 28
  0.9 16.5 %copy-start.7 = (s32[1,2]{1,0:T(1,128)S(1)}, s32[1,2]{1,0:T(1,128)}, u32[]{:S(2)}) copy-start(s32[1,2]{1,0:T(1,128)} %requests_ref.1) | copy-start | bytes 28
  0.9 18.0 %slice-start.3 = ((s8[10485760]{0:T(1024)(128)(4,1)}), s8[4194304]{0:T(1024)(128)(4,1)S(1)}, s32[]{:S(2)}) async-start(s8[10485760]{0:T(1024)(128)(4,1)} %bitcast.63), calls=%async_computation.8 | async-start | bytes 8388608
  0.9 18.0 %slice-start.4 = ((s8[10485760]{0:T(1024)(128)(4,1)}), s8[2097152]{0:T(1024)(128)(4,1)S(1)}, s32[]{:S(2)}) async-start(s8[10485760]{0:T(1024)(128)(4,1)} %bitcast.63), calls=%async_computation.9 | async-start | bytes 4194304
  17.3 1.5 %collective-permute-start = (bf16[8,2,8192]{2,1,0:T(2,128)(2,1)S(1)}, bf16[8,2,8192]{2,1,0:T(2,128)(2,1)S(1)}, u32[]{:S(2)}, u32[]{:S(2)}) collective-permute-start(bf16[8,2,8192]{2,1,0:T(2,128)(2,1)S(1)} %all_to_all.25.near_ref), channel_id=1, source_target_pairs={{0,1},{1,0},{2,3},{3,2},{4,5},{5,4},{6,7},{7,6},{8,9},{9,8},{10,11... | collective-permute-start | bytes 786440 | tf_op jit(solution)/shard_map/ppermute | solution.py:439
  18.9 25.8 %slice-start = ((s8[8388608]{0:T(1024)(128)(4,1)}), s8[4194304]{0:T(1024)(128)(4,1)S(1)}, s32[]{:S(2)}) async-start(s8[8388608]{0:T(1024)(128)(4,1)} %bitcast.60), calls=%async_computation.5 | async-start | bytes 8388608
  18.9 13.7 %copy-start.9 = (bf16[2,256,1024]{2,1,0:T(8,128)(2,1)S(1)}, bf16[2,256,1024]{2,1,0:T(8,128)(2,1)}, u32[]{:S(2)}) copy-start(bf16[2,256,1024]{2,1,0:T(8,128)(2,1)} %param.16) | copy-start | bytes 3145732
  18.9 25.8 %slice-start.1 = ((s8[8388608]{0:T(1024)(128)(4,1)}), s8[4194304]{0:T(1024)(128)(4,1)S(1)}, s32[]{:S(2)}) async-start(s8[8388608]{0:T(1024)(128)(4,1)} %bitcast.60), calls=%async_computation.6 | async-start | bytes 8388608
  33.1 17.0 %copy-start.3 = (s32[8,2]{1,0:T(8,128)}, s32[8,2]{1,0:T(8,128)S(1)}, u32[]{:S(2)}) copy-start(s32[8,2]{1,0:T(8,128)S(1)} %convert_element_type.43.adapter_ref) | copy-start | bytes 196
  44.7 5.5 %copy-start.1 = (bf16[8,2,8192]{2,1,0:T(2,128)(2,1)}, bf16[8,2,8192]{2,1,0:T(2,128)(2,1)S(1)}, u32[]{:S(2)}) copy-start(bf16[8,2,8192]{2,1,0:T(2,128)(2,1)S(1)} %all_to_all.27.gathered_ref) | copy-start | bytes 786436
  46.6 12.1 %all-to-all-start.3 = ((f32[8,16,128]{2,1,0:T(8,128)}), f32[8,16,128]{2,1,0:T(8,128)S(1)}, u32[]{:S(2)}, u32[]{:S(2)}) async-start(f32[8,16,128]{2,1,0:T(8,128)} %down_partials.1), calls=%async_computation.3 | async-start | bytes 131072 | tf_op jit(solution)/shard_map/all_to_all | solution.py:443
  58.7 0.8 %copy-start.2 = (f32[16,1024]{1,0:T(8,128)S(1)}, f32[16,1024]{1,0:T(8,128)}, u32[]{:S(2)}) copy-start(f32[16,1024]{1,0:T(8,128)} %get-tuple-element.21.base_ref) | copy-start | bytes 196612

commit v11 on v10

--- a/solution.py
+++ b/solution.py
@@ -305,18 +305,24 @@
     rank, width = store.shape[1:]
 
     def kernel(
-        adapter_ref, gathered_ref, weight_ref, store_ref, out_ref, up_ref, rows_ref, held_ref, sems,
-        up_sems,
+        adapter_ref, gathered_ref, weight_ref, store_ref, out_ref, up_ref, ids_ref, near_ref,
+        rows_ref, held_ref, sems, up_sems, other_sems,
     ):
+        ids = pltpu.make_async_copy(adapter_ref, ids_ref, other_sems.at[0])
+        near = pltpu.make_async_copy(gathered_ref, near_ref, other_sems.at[1])
+        ids.start()
+        near.start()
         part = stream(weight_ref, held_ref, sems, parts)
+        ids.wait()
         picks = []
         for r in range(count):
-            chosen = adapter_ref[r // rows, r % rows]
+            chosen = ids_ref[r // rows, r % rows]
             target = up_ref.at[pl.ds(r * rank, rank)]
             picks.append(pltpu.make_async_copy(store_ref.at[chosen], target, up_sems.at[r]))
             picks[-1].start()
+        near.wait()
         for j in range(groups):
-            rows_ref[pl.ds(j * rows, rows)] = gathered_ref[j]
+            rows_ref[pl.ds(j * rows, rows)] = near_ref[j]
         total = jnp.zeros(out_ref.shape, jnp.float32)
         for k in range(parts):
             total = total + jnp.dot(
@@ -330,18 +336,21 @@
         kernel,
         "project_out",
         (
-            jax.ShapeDtypeStruct((count, weight.shape[1]), jnp.float32),
+            pltpu.VMEM((count, weight.shape[1]), jnp.float32),
             pltpu.VMEM((count * rank, width), store.dtype),
         ),
-        [SMEM, VMEM, ANY, ANY],
+        [ANY] * 4,
         weight.size * 2 + count * rank * width * 2,
         limit=STREAM,
         flops=2 * count * weight.size,
         scratch_shapes=[
+            pltpu.SMEM(adapter.shape, adapter.dtype),
+            pltpu.VMEM(gathered.shape, gathered.dtype),
             pltpu.VMEM((count, depth), gathered.dtype),
             pltpu.VMEM(weight.shape, weight.dtype),
             pltpu.SemaphoreType.DMA((parts,)),
             pltpu.SemaphoreType.DMA((count,)),
+            pltpu.SemaphoreType.DMA((2,)),
         ],
     )(adapter, gathered, weight, store)
 
@@ -353,35 +362,36 @@
 
     def kernel(adapter_ref, gathered_ref, store_ref, out_ref, rows_ref):
         start = pl.multiple_of(lax.axis_index("mp") * depth, depth)
+        rows_ref[...] = jnp.zeros_like(rows_ref)
         for j in range(groups):
             rows_ref[pl.ds(j * rows, rows)] = gathered_ref[j, :, pl.ds(start, depth)]
-        row = lax.broadcasted_iota(jnp.int32, (count, LANES), 0)
-        lane = lax.broadcasted_iota(jnp.int32, (count, LANES), 1)
-        total = jnp.zeros((count, LANES), jnp.float32)
-        for k in range(count // BATCH):
-            chosen = [adapter_ref[r // rows, r % rows] for r in range(k * BATCH, (k + 1) * BATCH)]
+        lane = lax.broadcasted_iota(jnp.int32, (rank, LANES), 1)
+        total = jnp.zeros((rank, LANES), jnp.float32)
+        for k in range(0, count, BATCH):
+            chosen = [adapter_ref[r // rows, r % rows] for r in range(k, k + BATCH)]
             every = lax.dot_general(
+                jnp.concatenate([store_ref[c] for c in chosen]),
                 rows_ref[...],
-                jnp.concatenate([store_ref[c] for c in chosen]),
                 (((1,), (1,)), ((), ())),
                 preferred_element_type=jnp.float32,
             )
-            for s in range(BATCH * rank // LANES):
-                first = k * BATCH * rank + s * LANES
-                mine = row == (lane + first) // rank
-                total = total + jnp.where(mine, every[:, s * LANES : (s + 1) * LANES], 0.0)
+            for i in range(BATCH):
+                mine = every[i * rank : (i + 1) * rank]
+                total = total + jnp.where(lane == k + i, mine, 0.0)
+        turned = total.T[:count]
+        turned = jnp.concatenate([turned, turned], 1)
         for c in range(groups):
-            out_ref[c] = total
+            out_ref[c] = turned
 
     return call(
         kernel,
         "down_partials",
-        jax.ShapeDtypeStruct((groups, count, LANES), jnp.float32),
+        jax.ShapeDtypeStruct((groups, count, 2 * rank), jnp.float32),
         [SMEM, VMEM, VMEM],
         2 * count * rank * depth,
         limit=4 * MIB,
         flops=2 * count * count * rank * depth,
-        scratch_shapes=[pltpu.VMEM((count, depth), gathered.dtype)],
+        scratch_shapes=[pltpu.VMEM((LANES, depth), gathered.dtype)],
     )(adapter, gathered, store)
 
 

time: 73.4 us -> 73.4 us (level)
  transfers between devices with their start and end apart: 2 -> 2, of which waited for: 1 -> 1; matrix products, arithmetic and copies ran while one was open for 0% -> 0% of each run, Pallas kernels for 13% -> 12%
where the time goes in v11:
time: 73.4 us; the launch traced here: 73 us
  blocking collectives  50.6 us (69%)
  Pallas kernels  14.4 us (20%)
  starting transfers between devices  3.58 us (5%)
  local copies, waits for them, and re-layouts  1.87 us (3%)
  matrix products  0.9 us (1%)
  waiting for transfers between devices  0.8 us (1%)
    all_to_all x4, blocking collectives, exchange(): return lax.all_to_all(blocks, axes, split_axis=0, concat_axis=0, tiled=True)  50.6 us
    pallas_call x1, Pallas kernels, project_out(): call(kernel, 'project_out', (pltpu.VMEM((count, weight.shape[1]), jnp.flo...  8.39 us
    all_to_all x1, starting transfers between devices, exchange(): return lax.all_to_all(blocks, axes, split_axis=0, concat_axis=0, tiled=True)  3.57 us
    pallas_call x1, Pallas kernels, down_partials(): call(kernel, 'down_partials', jax.ShapeDtypeStruct((groups, count, 2 * ra...  2.09 us
    pallas_call x1, Pallas kernels, project_qkv(): call(kernel, 'project_qkv', jax.ShapeDtypeStruct((2 * groups, rows, width...  1.92 us
    unnamed x32, local copies, waits for them, and re-layouts  1.67 us
  transfers between devices with their start and end apart: 2, of which 1 were waited for; matrix products, arithmetic and copies ran while one was open for 0% of the time, Pallas kernels for 12%

profile of v11, /device:TPU:0, one launch (start us, length us, event | category | flops | bytes accessed | tf_op | source)
XLA Modules:
  0.0 73.0 jit_solution(16492774858395247471)
XLA Ops:
  0.0 0.0 slice-start.2
  0.0 0.8 %copy-done.8 = bf16[8192]{0:T(1024)(128)(2,1)S(1)} copy-done((bf16[8192]{0:T(1024)(128)(2,1)S(1)}, bf16[8192]{0:T(1024)(128)(2,1)}, u32[]{:S(2)}) %copy-start.8) | copy-done | bytes 16408
  0.8 0.0 copy-done.3
  0.9 0.0 slice-start.3
  0.9 0.0 slice-start.4
  0.9 0.2 norm_rows.1
  1.1 16.2 %all_to_all.25.near_ref = bf16[8,2,8192]{2,1,0:T(2,128)(2,1)S(1)} all-to-all(bf16[8,2,8192]{2,1,0:T(2,128)(2,1)S(1)} %norm_rows.1), channel_id=1, replica_groups=mesh['groups'=2,'mp'=8,'batch'=2] {'mp'}, dimensions={0} | all-to-all | bytes 524288 | tf_op jit(solution)/shard_map/all_to_all | solution.py:453
  17.3 0.0 collective-permute-start
  17.4 0.7 turns.1
  18.1 0.8 %collective-permute-done.far_ref = bf16[8,2,8192]{2,1,0:T(2,128)(2,1)S(1)} collective-permute-done((bf16[8,2,8192]{2,1,0:T(2,128)(2,1)S(1)}, bf16[8,2,8192]{2,1,0:T(2,128)(2,1)S(1)}, u32[]{:S(2)}, u32[]{:S(2)}) %collective-permute-start) | collective-permute-done | bytes 262176 | tf_op jit(solution)/shard_map/ppermute | solution.py:449
  18.9 0.0 copy-start.9
  18.9 1.9 %project_qkv.1 = bf16[16,2,768]{2,1,0:T(2,128)(2,1)S(1)} custom-call(bf16[16,8192]{1,0:T(8,128)(2,1)S(1)} %get-tuple-element.14.lined_ref, bf16[8,2,8192]{2,1,0:T(2,128)(2,1)S(1)} %collective-permute-done.far_ref, bf16[8192,640]{1,0:T(8,128)(2,1)S(1)} %bitcast.64, bf16[2,128]{1,0:T(2,128)(2,1)S(1)} %get-tuple-element.15.adapter_ref), custom_call_target="tpu_custom_call" | custom-call | flops 10000000000 | bytes 10485760 | tf_op jit(solution)/shard_map/project_qkv/pallas_call | solution.py:274
  20.8 10.5 %all_to_all.26 = bf16[16,2,768]{2,1,0:T(2,128)(2,1)S(1)} all-to-all(bf16[16,2,768]{2,1,0:T(2,128)(2,1)S(1)} %project_qkv.1), channel_id=1, replica_groups=mesh['groups'=2,'mp'=8,'batch'=2] {'mp','batch'}, dimensions={0} | all-to-all | bytes 98304 | tf_op jit(solution)/shard_map/all_to_all | solution.py:453
  31.5 0.1 slice_negate_fusion.1
  31.5 0.1 fusion.10
  31.6 0.1 fusion.18
  31.7 0.1 fusion.9
  31.8 0.1 fusion.15
  31.9 0.5 fusion.20
  32.4 0.2 fusion.7
  32.6 0.3 fusion.2
  33.0 0.1 convert_reduce_fusion
  33.1 0.0 copy-start.2
  33.1 0.1 broadcast_in_dim.5
  33.3 11.4 %all_to_all.27.gathered_ref = bf16[8,2,8192]{2,1,0:T(2,128)(2,1)S(1)} all-to-all(bf16[8,2,8192]{2,1,0:T(2,128)(2,1)S(1)} %broadcast_in_dim.5), channel_id=1, replica_groups=mesh['groups'=2,'mp'=8,'batch'=2] {'mp'}, dimensions={0} | all-to-all | bytes 524288 | tf_op jit(solution)/shard_map/all_to_all | solution.py:453
  44.7 2.1 %down_partials.1 = f32[8,16,128]{2,1,0:T(8,128)} custom-call(s32[8,2]{1,0:T(8,128)S(1)} %convert_element_type.43.adapter_ref, bf16[8,2,8192]{2,1,0:T(2,128)(2,1)S(1)} %all_to_all.27.gathered_ref, bf16[64,64,1024]{2,1,0:T(8,128)(2,1)S(1)} %bitcast.62), custom_call_target="tpu_custom_call" | custom-call | flops 33554432 | bytes 2097152 | tf_op jit(solution)/shard_map/down_partials/pallas_call | solution.py:386
  46.7 3.6 %all-to-all-start.3 = ((f32[8,16,128]{2,1,0:T(8,128)}), f32[8,16,128]{2,1,0:T(8,128)S(1)}, u32[]{:S(2)}, u32[]{:S(2)}) async-start(f32[8,16,128]{2,1,0:T(8,128)} %down_partials.1), calls=%async_computation.3 | async-start | bytes 131072 | tf_op jit(solution)/shard_map/all_to_all | solution.py:453
  50.3 8.4 %project_out.1 = (f32[16,1024]{1,0:T(8,128)S(1)}, bf16[1024,1024]{1,0:T(8,128)(2,1)S(1)}) custom-call(s32[8,2]{1,0:T(8,128)} %copy-done.2, bf16[8,2,8192]{2,1,0:T(2,128)(2,1)} %copy-done.1, bf16[8192,1024]{1,0:T(8,128)(2,1)} %weight_ref.3, bf16[64,64,1024]{2,1,0:T(8,128)(2,1)} %store_ref.1), custom_call_target="tpu_custom_call" | custom-call | flops 268435456 | bytes 18874368 | tf_op jit(solution)/shard_map/project_out/pallas_call | solution.py:335
  58.7 0.4 add_up.1
  59.1 12.5 %all_to_all.28.parts_ref = bf16[8,2,1024]{2,1,0:T(2,128)(2,1)S(1)} all-to-all(bf16[8,2,1024]{2,1,0:T(2,128)(2,1)S(1)} %add_up.1), channel_id=1, replica_groups=mesh['groups'=2,'mp'=8,'batch'=2] {'mp'}, dimensions={0} | all-to-all | bytes 65536 | tf_op jit(solution)/shard_map/all_to_all | solution.py:453
  71.6 0.8 %copy-done.4 = bf16[2,8192]{1,0:T(2,128)(2,1)S(1)} copy-done((bf16[2,8192]{1,0:T(2,128)(2,1)S(1)}, bf16[2,8192]{1,0:T(2,128)(2,1)}, u32[]{:S(2)}) %copy-start.4) | copy-done | bytes 32792
  72.4 0.7 add_rows.1
  (37 shorter events, 0.2 us)
Async XLA Ops:
  0.0 31.9 %copy-start = (bf16[2,256,1024]{2,1,0:T(8,128)(2,1)S(1)}, bf16[2,256,1024]{2,1,0:T(8,128)(2,1)}, u32[]{:S(2)}) copy-start(bf16[2,256,1024]{2,1,0:T(8,128)(2,1)} %param.15) | copy-start | bytes 3145732
  0.0 0.8 %copy-start.8 = (bf16[8192]{0:T(1024)(128)(2,1)S(1)}, bf16[8192]{0:T(1024)(128)(2,1)}, u32[]{:S(2)}) copy-start(bf16[8192]{0:T(1024)(128)(2,1)} %param.12) | copy-start | bytes 49156
  0.0 0.9 %copy-start.3 = (bf16[2,8192]{1,0:T(2,128)(2,1)S(1)}, bf16[2,8192]{1,0:T(2,128)(2,1)}, u32[]{:S(2)}) copy-start(bf16[2,8192]{1,0:T(2,128)(2,1)} %hidden_ref.3) | copy-start | bytes 98308
  0.0 18.9 %slice-start.2 = ((s8[10485760]{0:T(1024)(128)(4,1)}), s8[4194304]{0:T(1024)(128)(4,1)S(1)}, s32[]{:S(2)}) async-start(s8[10485760]{0:T(1024)(128)(4,1)} %bitcast.63), calls=%async_computation.7 | async-start | bytes 8388608
  0.9 16.5 %copy-start.5 = (s32[2]{0:T(128)S(1)}, s32[2]{0:T(128)}, u32[]{:S(2)}) copy-start(s32[2]{0:T(128)} %lengths_ref.1) | copy-start | bytes 28
  0.9 16.5 %copy-start.6 = (s32[2]{0:T(128)S(1)}, s32[2]{0:T(128)}, u32[]{:S(2)}) copy-start(s32[2]{0:T(128)} %slots_ref.1) | copy-start | bytes 28
  0.9 16.5 %copy-start.7 = (s32[1,2]{1,0:T(1,128)S(1)}, s32[1,2]{1,0:T(1,128)}, u32[]{:S(2)}) copy-start(s32[1,2]{1,0:T(1,128)} %requests_ref.1) | copy-start | bytes 28
  0.9 18.0 %slice-start.3 = ((s8[10485760]{0:T(1024)(128)(4,1)}), s8[4194304]{0:T(1024)(128)(4,1)S(1)}, s32[]{:S(2)}) async-start(s8[10485760]{0:T(1024)(128)(4,1)} %bitcast.63), calls=%async_computation.8 | async-start | bytes 8388608
  0.9 18.0 %slice-start.4 = ((s8[10485760]{0:T(1024)(128)(4,1)}), s8[2097152]{0:T(1024)(128)(4,1)S(1)}, s32[]{:S(2)}) async-start(s8[10485760]{0:T(1024)(128)(4,1)} %bitcast.63), calls=%async_computation.9 | async-start | bytes 4194304
  17.3 1.5 %collective-permute-start = (bf16[8,2,8192]{2,1,0:T(2,128)(2,1)S(1)}, bf16[8,2,8192]{2,1,0:T(2,128)(2,1)S(1)}, u32[]{:S(2)}, u32[]{:S(2)}) collective-permute-start(bf16[8,2,8192]{2,1,0:T(2,128)(2,1)S(1)} %all_to_all.25.near_ref), channel_id=1, source_target_pairs={{0,1},{1,0},{2,3},{3,2},{4,5},{5,4},{6,7},{7,6},{8,9},{9,8},{10,11... | collective-permute-start | bytes 786440 | tf_op jit(solution)/shard_map/ppermute | solution.py:449
  18.9 25.8 %slice-start = ((s8[8388608]{0:T(1024)(128)(4,1)}), s8[4194304]{0:T(1024)(128)(4,1)S(1)}, s32[]{:S(2)}) async-start(s8[8388608]{0:T(1024)(128)(4,1)} %bitcast.60), calls=%async_computation.5 | async-start | bytes 8388608
  18.9 13.7 %copy-start.9 = (bf16[2,256,1024]{2,1,0:T(8,128)(2,1)S(1)}, bf16[2,256,1024]{2,1,0:T(8,128)(2,1)}, u32[]{:S(2)}) copy-start(bf16[2,256,1024]{2,1,0:T(8,128)(2,1)} %param.16) | copy-start | bytes 3145732
  18.9 25.8 %slice-start.1 = ((s8[8388608]{0:T(1024)(128)(4,1)}), s8[4194304]{0:T(1024)(128)(4,1)S(1)}, s32[]{:S(2)}) async-start(s8[8388608]{0:T(1024)(128)(4,1)} %bitcast.60), calls=%async_computation.6 | async-start | bytes 8388608
  33.1 17.2 %copy-start.2 = (s32[8,2]{1,0:T(8,128)}, s32[8,2]{1,0:T(8,128)S(1)}, u32[]{:S(2)}) copy-start(s32[8,2]{1,0:T(8,128)S(1)} %convert_element_type.43.adapter_ref) | copy-start | bytes 196
  44.7 5.7 %copy-start.1 = (bf16[8,2,8192]{2,1,0:T(2,128)(2,1)}, bf16[8,2,8192]{2,1,0:T(2,128)(2,1)S(1)}, u32[]{:S(2)}) copy-start(bf16[8,2,8192]{2,1,0:T(2,128)(2,1)S(1)} %all_to_all.27.gathered_ref) | copy-start | bytes 786436
  46.7 12.0 %all-to-all-start.3 = ((f32[8,16,128]{2,1,0:T(8,128)}), f32[8,16,128]{2,1,0:T(8,128)S(1)}, u32[]{:S(2)}, u32[]{:S(2)}) async-start(f32[8,16,128]{2,1,0:T(8,128)} %down_partials.1), calls=%async_computation.3 | async-start | bytes 131072 | tf_op jit(solution)/shard_map/all_to_all | solution.py:453
  71.6 0.8 %copy-start.4 = (bf16[2,8192]{1,0:T(2,128)(2,1)S(1)}, bf16[2,8192]{1,0:T(2,128)(2,1)}, u32[]{:S(2)}) copy-start(bf16[2,8192]{1,0:T(2,128)(2,1)} %hidden_ref.3) | copy-start | bytes 98308

commit v12 on v10

--- a/solution.py
+++ b/solution.py
@@ -145,7 +145,6 @@
 
 MIB = 1 << 20
 LANES = 128
-BATCH = 4
 LONG = 10**10
 STREAM = 53 * MIB
 VMEM = pl.BlockSpec(memory_space=pltpu.VMEM)
@@ -299,90 +298,86 @@
     return part
 
 
-def project_out(gathered, weight, adapter, store, parts=16):
+def project_out(gathered, weight, parts=16):
     groups, rows, depth = gathered.shape
     count, step = groups * rows, depth // parts
-    rank, width = store.shape[1:]
-
-    def kernel(
-        adapter_ref, gathered_ref, weight_ref, store_ref, out_ref, up_ref, rows_ref, held_ref, sems,
-        up_sems,
-    ):
+
+    def kernel(gathered_ref, weight_ref, out_ref, near_ref, rows_ref, held_ref, sems, near_sem):
+        near = pltpu.make_async_copy(gathered_ref, near_ref, near_sem)
+        near.start()
         part = stream(weight_ref, held_ref, sems, parts)
-        picks = []
-        for r in range(count):
-            chosen = adapter_ref[r // rows, r % rows]
-            target = up_ref.at[pl.ds(r * rank, rank)]
-            picks.append(pltpu.make_async_copy(store_ref.at[chosen], target, up_sems.at[r]))
-            picks[-1].start()
+        near.wait()
         for j in range(groups):
-            rows_ref[pl.ds(j * rows, rows)] = gathered_ref[j]
+            rows_ref[pl.ds(j * rows, rows)] = near_ref[j]
         total = jnp.zeros(out_ref.shape, jnp.float32)
         for k in range(parts):
             total = total + jnp.dot(
                 rows_ref[:, pl.ds(k * step, step)], part(k), preferred_element_type=jnp.float32
             )
         out_ref[...] = total
-        for pick in picks:
-            pick.wait()
 
     return call(
         kernel,
         "project_out",
-        (
-            jax.ShapeDtypeStruct((count, weight.shape[1]), jnp.float32),
-            pltpu.VMEM((count * rank, width), store.dtype),
-        ),
-        [SMEM, VMEM, ANY, ANY],
-        weight.size * 2 + count * rank * width * 2,
+        pltpu.VMEM((count, weight.shape[1]), jnp.float32),
+        [ANY] * 2,
+        weight.size * 2,
         limit=STREAM,
         flops=2 * count * weight.size,
         scratch_shapes=[
+            pltpu.VMEM(gathered.shape, gathered.dtype),
             pltpu.VMEM((count, depth), gathered.dtype),
             pltpu.VMEM(weight.shape, weight.dtype),
             pltpu.SemaphoreType.DMA((parts,)),
-            pltpu.SemaphoreType.DMA((count,)),
+            pltpu.SemaphoreType.DMA,
         ],
-    )(adapter, gathered, weight, store)
-
-
-def down_partials(gathered, adapter, store):
+    )(gathered, weight)
+
+
+def down_partials(gathered, adapter, down_store, up_store):
     groups, rows, _ = gathered.shape
     count = groups * rows
-    rank, depth = store.shape[1:]
-
-    def kernel(adapter_ref, gathered_ref, store_ref, out_ref, rows_ref):
+    rank, depth = down_store.shape[1:]
+    width = up_store.shape[2]
+
+    def kernel(adapter_ref, gathered_ref, down_ref, up_ref, out_ref, picked_ref, held_ref, rows_ref):
         start = pl.multiple_of(lax.axis_index("mp") * depth, depth)
         for j in range(groups):
             rows_ref[pl.ds(j * rows, rows)] = gathered_ref[j, :, pl.ds(start, depth)]
+        for r in range(count):
+            chosen = adapter_ref[r // rows, r % rows]
+            held_ref[pl.ds(r * rank, rank)] = down_ref[chosen]
+            picked_ref[pl.ds(r * rank, rank)] = up_ref[chosen]
+        every = lax.dot_general(
+            rows_ref[...],
+            held_ref[...],
+            (((1,), (1,)), ((), ())),
+            preferred_element_type=jnp.float32,
+        )
         row = lax.broadcasted_iota(jnp.int32, (count, LANES), 0)
         lane = lax.broadcasted_iota(jnp.int32, (count, LANES), 1)
         total = jnp.zeros((count, LANES), jnp.float32)
-        for k in range(count // BATCH):
-            chosen = [adapter_ref[r // rows, r % rows] for r in range(k * BATCH, (k + 1) * BATCH)]
-            every = lax.dot_general(
-                rows_ref[...],
-                jnp.concatenate([store_ref[c] for c in chosen]),
-                (((1,), (1,)), ((), ())),
-                preferred_element_type=jnp.float32,
-            )
-            for s in range(BATCH * rank // LANES):
-                first = k * BATCH * rank + s * LANES
-                mine = row == (lane + first) // rank
-                total = total + jnp.where(mine, every[:, s * LANES : (s + 1) * LANES], 0.0)
+        for s in range(0, count * rank, LANES):
+            total = total + jnp.where(row == (lane + s) // rank, every[:, s : s + LANES], 0.0)
         for c in range(groups):
             out_ref[c] = total
 
     return call(
         kernel,
         "down_partials",
-        jax.ShapeDtypeStruct((groups, count, LANES), jnp.float32),
-        [SMEM, VMEM, VMEM],
-        2 * count * rank * depth,
-        limit=4 * MIB,
+        (
+            jax.ShapeDtypeStruct((groups, count, LANES), jnp.float32),
+            pltpu.VMEM((count * rank, width), up_store.dtype),
+        ),
+        [SMEM] + [VMEM] * 3,
+        2 * count * rank * (depth + width),
+        limit=5 * MIB,
         flops=2 * count * count * rank * depth,
-        scratch_shapes=[pltpu.VMEM((count, depth), gathered.dtype)],
-    )(adapter, gathered, store)
+        scratch_shapes=[
+            pltpu.VMEM((count * rank, depth), down_store.dtype),
+            pltpu.VMEM((count, depth), gathered.dtype),
+        ],
+    )(adapter, gathered, down_store, up_store)
 
 
 def add_up(base, partials, up):
@@ -518,11 +513,11 @@
     context, adapter = lax.optimization_barrier((context, adapter))
     gathered = exchange(jnp.broadcast_to(context[None], (mp_size, *context.shape)))
 
-    partials = exchange(
-        down_partials(gathered, adapter, adapter_down_matrices.swapaxes(1, 2))
-    )
-    base, up = project_out(gathered, output_weight, adapter, adapter_up_matrices)
-    projected = add_up(base, partials, up)
+    partials, up = down_partials(
+        gathered, adapter, adapter_down_matrices.swapaxes(1, 2), adapter_up_matrices
+    )
+    partials = exchange(partials)
+    projected = add_up(project_out(gathered, output_weight), partials, up)
     return add_rows(hidden, exchange(projected))
 
 

time: 73.4 us -> 71 us (0.967)
  Pallas kernels: 14.3 us -> 12 us
    pallas_call x2, Pallas kernels: 10.4 us -> 8.12 us  [the longest x1 6.21 us: project_out(): call(kernel, 'project_out', pltpu.VMEM((count, weight.shape[1]), jnp.floa...]
  transfers between devices with their start and end apart: 2 -> 2, of which waited for: 1 -> 2; matrix products, arithmetic and copies ran while one was open for 0% -> 0% of each run, Pallas kernels for 13% -> 10%
where the time goes in v12:
time: 71 us; the launch traced here: 70.7 us
  blocking collectives  49.9 us (70%)
  Pallas kernels  12 us (17%)
  starting transfers between devices  3.57 us (5%)
  local copies, waits for them, and re-layouts  1.86 us (3%)
  waiting for transfers between devices  1.48 us (2%)
  matrix products  0.9 us (1%)
    all_to_all x4, blocking collectives, exchange(): return lax.all_to_all(blocks, axes, split_axis=0, concat_axis=0, tiled=True)  49.9 us
    pallas_call x1, Pallas kernels, project_out(): call(kernel, 'project_out', pltpu.VMEM((count, weight.shape[1]), jnp.floa...  6.21 us
    all_to_all x1, starting transfers between devices, exchange(): return lax.all_to_all(blocks, axes, split_axis=0, concat_axis=0, tiled=True)  3.57 us
    pallas_call x1, Pallas kernels, project_qkv(): call(kernel, 'project_qkv', jax.ShapeDtypeStruct((2 * groups, rows, width...  1.93 us
    pallas_call x1, Pallas kernels, down_partials(): call(kernel, 'down_partials', (jax.ShapeDtypeStruct((groups, count, LANES...  1.92 us
    unnamed x32, local copies, waits for them, and re-layouts  1.67 us
  transfers between devices with their start and end apart: 2, of which 2 were waited for; matrix products, arithmetic and copies ran while one was open for 0% of the time, Pallas kernels for 10%

profile of v12, /device:TPU:0, one launch (start us, length us, event | category | flops | bytes accessed | tf_op | source)
XLA Modules:
  0.0 70.7 jit_solution(2874477937400122418)
XLA Ops:
  0.0 0.0 slice-start.4
  0.0 0.8 %copy-done.6 = bf16[8192]{0:T(1024)(128)(2,1)S(1)} copy-done((bf16[8192]{0:T(1024)(128)(2,1)S(1)}, bf16[8192]{0:T(1024)(128)(2,1)}, u32[]{:S(2)}) %copy-start.6) | copy-done | bytes 16408
  0.8 0.0 copy-done.1
  0.9 0.0 slice-start.5
  0.9 0.0 slice-start.6
  0.9 0.2 norm_rows.1
  1.1 16.2 %all_to_all.25.near_ref = bf16[8,2,8192]{2,1,0:T(2,128)(2,1)S(1)} all-to-all(bf16[8,2,8192]{2,1,0:T(2,128)(2,1)S(1)} %norm_rows.1), channel_id=1, replica_groups=mesh['groups'=2,'mp'=8,'batch'=2] {'mp'}, dimensions={0} | all-to-all | bytes 524288 | tf_op jit(solution)/shard_map/all_to_all | solution.py:438
  17.3 0.0 collective-permute-start
  17.4 0.7 %turns.1 = (bf16[16,8192]{1,0:T(8,128)(2,1)S(1)}, f32[2,128]{1,0:T(2,128)S(1)}, f32[2,128]{1,0:T(2,128)S(1)}, f32[2,256]{1,0:T(2,128)S(1)}, bf16[2,128]{1,0:T(2,128)(2,1)S(1)}) custom-call(s32[2]{0:T(128)S(1)} %copy-done.3, s32[2]{0:T(128)S(1)} %copy-done.4, s32[1,2]{1,0:T(1,128)S(1)} %copy-done.5, bf16[8,2,8192]{2,1,0:T(2,128)(2,1)S(1)} %all_to_all.25.near_ref, ...), custom_call_target="tpu_custom_call" | custom-call | bytes 524288 | tf_op jit(solution)/shard_map/turns/pallas_call | solution.py:229
  18.1 0.8 %collective-permute-done.far_ref = bf16[8,2,8192]{2,1,0:T(2,128)(2,1)S(1)} collective-permute-done((bf16[8,2,8192]{2,1,0:T(2,128)(2,1)S(1)}, bf16[8,2,8192]{2,1,0:T(2,128)(2,1)S(1)}, u32[]{:S(2)}, u32[]{:S(2)}) %collective-permute-start) | collective-permute-done | bytes 262176 | tf_op jit(solution)/shard_map/ppermute | solution.py:434
  18.9 0.0 copy-start.7
  18.9 1.9 %project_qkv.1 = bf16[16,2,768]{2,1,0:T(2,128)(2,1)S(1)} custom-call(bf16[16,8192]{1,0:T(8,128)(2,1)S(1)} %get-tuple-element.14.lined_ref, bf16[8,2,8192]{2,1,0:T(2,128)(2,1)S(1)} %collective-permute-done.far_ref, bf16[8192,640]{1,0:T(8,128)(2,1)S(1)} %bitcast.66, bf16[2,128]{1,0:T(2,128)(2,1)S(1)} %get-tuple-element.15.adapter_ref), custom_call_target="tpu_custom_call" | custom-call | flops 10000000000 | bytes 10485760 | tf_op jit(solution)/shard_map/project_qkv/pallas_call | solution.py:273
  20.9 10.5 %all_to_all.26 = bf16[16,2,768]{2,1,0:T(2,128)(2,1)S(1)} all-to-all(bf16[16,2,768]{2,1,0:T(2,128)(2,1)S(1)} %project_qkv.1), channel_id=1, replica_groups=mesh['groups'=2,'mp'=8,'batch'=2] {'mp','batch'}, dimensions={0} | all-to-all | bytes 98304 | tf_op jit(solution)/shard_map/all_to_all | solution.py:438
  31.5 0.1 convert_reduce_fusion
  31.6 0.1 slice_negate_fusion.1
  31.7 0.1 fusion.10
  31.8 0.1 fusion.18
  31.8 0.1 fusion.9
  31.9 0.1 fusion.15
  32.1 0.5 fusion.20
  32.5 0.2 fusion.7
  32.8 0.3 fusion.2
  33.1 0.1 broadcast_in_dim.5
  33.3 11.4 %all_to_all.27.gathered_ref = bf16[8,2,8192]{2,1,0:T(2,128)(2,1)S(1)} all-to-all(bf16[8,2,8192]{2,1,0:T(2,128)(2,1)S(1)} %broadcast_in_dim.5), channel_id=1, replica_groups=mesh['groups'=2,'mp'=8,'batch'=2] {'mp'}, dimensions={0} | all-to-all | bytes 524288 | tf_op jit(solution)/shard_map/all_to_all | solution.py:438
  44.7 1.9 %down_partials.1 = (f32[8,16,128]{2,1,0:T(8,128)}, bf16[1024,1024]{1,0:T(8,128)(2,1)S(1)}) custom-call(s32[8,2]{1,0:T(8,128)S(1)} %convert_element_type.43.adapter_ref, bf16[8,2,8192]{2,1,0:T(2,128)(2,1)S(1)} %all_to_all.27.gathered_ref, bf16[64,64,1024]{2,1,0:T(8,128)(2,1)S(1)} %bitcast.62, bf16[64,64,1024]{2,1,0:T(8,128)(2,1)S(1)} %bitcast.64), custom_call_target="tpu_custom_call" | custom-call | flops 33554432 | bytes 4194304 | tf_op jit(solution)/shard_map/down_partials/pallas_call | solution.py:365
  46.6 3.6 %all-to-all-start.3 = ((f32[8,16,128]{2,1,0:T(8,128)}), f32[8,16,128]{2,1,0:T(8,128)S(1)}, u32[]{:S(2)}, u32[]{:S(2)}) async-start(f32[8,16,128]{2,1,0:T(8,128)} %get-tuple-element.21), calls=%async_computation.3 | async-start | bytes 131072 | tf_op jit(solution)/shard_map/all_to_all | solution.py:438
  50.2 6.2 %project_out.1.base_ref = f32[16,1024]{1,0:T(8,128)S(1)} custom-call(bf16[8,2,8192]{2,1,0:T(2,128)(2,1)S(1)} %all_to_all.27.gathered_ref, bf16[8192,1024]{1,0:T(8,128)(2,1)} %weight_ref.3), custom_call_target="tpu_custom_call" | custom-call | flops 268435456 | bytes 16777216 | tf_op jit(solution)/shard_map/project_out/pallas_call | solution.py:319
  56.4 0.7 all-to-all-done.3.partials_ref
  57.1 0.4 add_up.1
  57.5 11.8 %all_to_all.28.parts_ref = bf16[8,2,1024]{2,1,0:T(2,128)(2,1)S(1)} all-to-all(bf16[8,2,1024]{2,1,0:T(2,128)(2,1)S(1)} %add_up.1), channel_id=1, replica_groups=mesh['groups'=2,'mp'=8,'batch'=2] {'mp'}, dimensions={0} | all-to-all | bytes 65536 | tf_op jit(solution)/shard_map/all_to_all | solution.py:438
  69.3 0.8 %copy-done.2 = bf16[2,8192]{1,0:T(2,128)(2,1)S(1)} copy-done((bf16[2,8192]{1,0:T(2,128)(2,1)S(1)}, bf16[2,8192]{1,0:T(2,128)(2,1)}, u32[]{:S(2)}) %copy-start.2) | copy-done | bytes 32792
  70.1 0.7 add_rows.1
  (38 shorter events, 0.2 us)
Async XLA Ops:
  0.0 32.1 %copy-start = (bf16[2,256,1024]{2,1,0:T(8,128)(2,1)S(1)}, bf16[2,256,1024]{2,1,0:T(8,128)(2,1)}, u32[]{:S(2)}) copy-start(bf16[2,256,1024]{2,1,0:T(8,128)(2,1)} %param.15) | copy-start | bytes 3145732
  0.0 0.8 %copy-start.6 = (bf16[8192]{0:T(1024)(128)(2,1)S(1)}, bf16[8192]{0:T(1024)(128)(2,1)}, u32[]{:S(2)}) copy-start(bf16[8192]{0:T(1024)(128)(2,1)} %param.12) | copy-start | bytes 49156
  0.0 0.9 %copy-start.1 = (bf16[2,8192]{1,0:T(2,128)(2,1)S(1)}, bf16[2,8192]{1,0:T(2,128)(2,1)}, u32[]{:S(2)}) copy-start(bf16[2,8192]{1,0:T(2,128)(2,1)} %hidden_ref.3) | copy-start | bytes 98308
  0.0 18.9 %slice-start.4 = ((s8[10485760]{0:T(1024)(128)(4,1)}), s8[4194304]{0:T(1024)(128)(4,1)S(1)}, s32[]{:S(2)}) async-start(s8[10485760]{0:T(1024)(128)(4,1)} %bitcast.65), calls=%async_computation.9 | async-start | bytes 8388608
  0.9 16.5 %copy-start.3 = (s32[2]{0:T(128)S(1)}, s32[2]{0:T(128)}, u32[]{:S(2)}) copy-start(s32[2]{0:T(128)} %lengths_ref.1) | copy-start | bytes 28
  0.9 16.5 %copy-start.4 = (s32[2]{0:T(128)S(1)}, s32[2]{0:T(128)}, u32[]{:S(2)}) copy-start(s32[2]{0:T(128)} %slots_ref.1) | copy-start | bytes 28
  0.9 16.5 %copy-start.5 = (s32[1,2]{1,0:T(1,128)S(1)}, s32[1,2]{1,0:T(1,128)}, u32[]{:S(2)}) copy-start(s32[1,2]{1,0:T(1,128)} %requests_ref.1) | copy-start | bytes 28
  0.9 18.0 %slice-start.5 = ((s8[10485760]{0:T(1024)(128)(4,1)}), s8[4194304]{0:T(1024)(128)(4,1)S(1)}, s32[]{:S(2)}) async-start(s8[10485760]{0:T(1024)(128)(4,1)} %bitcast.65), calls=%async_computation.10 | async-start | bytes 8388608
  0.9 18.0 %slice-start.6 = ((s8[10485760]{0:T(1024)(128)(4,1)}), s8[2097152]{0:T(1024)(128)(4,1)S(1)}, s32[]{:S(2)}) async-start(s8[10485760]{0:T(1024)(128)(4,1)} %bitcast.65), calls=%async_computation.11 | async-start | bytes 4194304
  17.3 1.5 %collective-permute-start = (bf16[8,2,8192]{2,1,0:T(2,128)(2,1)S(1)}, bf16[8,2,8192]{2,1,0:T(2,128)(2,1)S(1)}, u32[]{:S(2)}, u32[]{:S(2)}) collective-permute-start(bf16[8,2,8192]{2,1,0:T(2,128)(2,1)S(1)} %all_to_all.25.near_ref), channel_id=1, source_target_pairs={{0,1},{1,0},{2,3},{3,2},{4,5},{5,4},{6,7},{7,6},{8,9},{9,8},{10,11... | collective-permute-start | bytes 786440 | tf_op jit(solution)/shard_map/ppermute | solution.py:434
  18.9 25.8 %slice-start = ((s8[8388608]{0:T(1024)(128)(4,1)}), s8[4194304]{0:T(1024)(128)(4,1)S(1)}, s32[]{:S(2)}) async-start(s8[8388608]{0:T(1024)(128)(4,1)} %bitcast.60), calls=%async_computation.5 | async-start | bytes 8388608
  18.9 25.8 %slice-start.2 = ((s8[8388608]{0:T(1024)(128)(4,1)}), s8[4194304]{0:T(1024)(128)(4,1)S(1)}, s32[]{:S(2)}) async-start(s8[8388608]{0:T(1024)(128)(4,1)} %bitcast.63), calls=%async_computation.7 | async-start | bytes 8388608
  18.9 13.9 %copy-start.7 = (bf16[2,256,1024]{2,1,0:T(8,128)(2,1)S(1)}, bf16[2,256,1024]{2,1,0:T(8,128)(2,1)}, u32[]{:S(2)}) copy-start(bf16[2,256,1024]{2,1,0:T(8,128)(2,1)} %param.16) | copy-start | bytes 3145732
  18.9 25.8 %slice-start.1 = ((s8[8388608]{0:T(1024)(128)(4,1)}), s8[4194304]{0:T(1024)(128)(4,1)S(1)}, s32[]{:S(2)}) async-start(s8[8388608]{0:T(1024)(128)(4,1)} %bitcast.60), calls=%async_computation.6 | async-start | bytes 8388608
  18.9 25.8 %slice-start.3 = ((s8[8388608]{0:T(1024)(128)(4,1)}), s8[4194304]{0:T(1024)(128)(4,1)S(1)}, s32[]{:S(2)}) async-start(s8[8388608]{0:T(1024)(128)(4,1)} %bitcast.63), calls=%async_computation.8 | async-start | bytes 8388608
  46.6 10.5 %all-to-all-start.3 = ((f32[8,16,128]{2,1,0:T(8,128)}), f32[8,16,128]{2,1,0:T(8,128)S(1)}, u32[]{:S(2)}, u32[]{:S(2)}) async-start(f32[8,16,128]{2,1,0:T(8,128)} %get-tuple-element.21), calls=%async_computation.3 | async-start | bytes 131072 | tf_op jit(solution)/shard_map/all_to_all | solution.py:438
  69.3 0.8 %copy-start.2 = (bf16[2,8192]{1,0:T(2,128)(2,1)S(1)}, bf16[2,8192]{1,0:T(2,128)(2,1)}, u32[]{:S(2)}) copy-start(bf16[2,8192]{1,0:T(2,128)(2,1)} %hidden_ref.3) | copy-start | bytes 98308

commit v13 on v12

--- a/solution.py
+++ b/solution.py
@@ -408,7 +408,7 @@
         [VMEM] * 3,
         up.size * 2,
         limit=4 * MIB,
-        flops=2 * count * up.size,
+        flops=LONG,
     )(base, partials, up)
 
 
@@ -416,8 +416,8 @@
     width = parts.shape[2]
 
     def kernel(hidden_ref, parts_ref, out_ref):
-        for k in range(parts.shape[0]):
-            part = pl.ds(k * width, width)
+        for k, place in enumerate(order(parts.shape[0])):
+            part = pl.ds(place * width, width)
             total = hidden_ref[:, part].astype(jnp.float32) + parts_ref[k].astype(jnp.float32)
             out_ref[:, part] = total.astype(jnp.bfloat16)
 
@@ -434,8 +434,27 @@
     return lax.ppermute(block, "batch", [(0, 1), (1, 0)])
 
 
-def exchange(blocks, axes="mp"):
-    return lax.all_to_all(blocks, axes, split_axis=0, concat_axis=0, tiled=True)
+def order(size):
+    return [(k + size // 2) % size for k in range(size)]
+
+
+def exchange(blocks):
+    group = order(lax.axis_size("mp"))
+    return lax.all_to_all(
+        blocks, "mp", split_axis=0, concat_axis=0, tiled=True, axis_index_groups=[group]
+    )
+
+
+def exchange_all(blocks):
+    group = [2 * j + core for j in order(lax.axis_size("mp")) for core in range(2)]
+    return lax.all_to_all(
+        blocks,
+        ("mp", "batch"),
+        split_axis=0,
+        concat_axis=0,
+        tiled=True,
+        axis_index_groups=[group],
+    )
 
 
 def attend(qkv, cosine, sine, key_cache, value_cache, mask):
@@ -504,10 +523,10 @@
         near, frequency, lengths, slots, requests, key_cache.shape[1]
     )
     columns = project_qkv(lined, swap_cores(near), query_key_value_weight, adapter)
-    mixed = exchange(columns, ("mp", "batch"))
+    mixed = exchange_all(columns)
     adapter = mixed.reshape(mp_size, -1, rows, width + LANES)[:, :, :, width]
     adapter = jnp.sum(adapter.astype(jnp.float32), 1).astype(jnp.int32)
-    qkv = mixed[:, :, :width].transpose(1, 0, 2).reshape(rows, -1)
+    qkv = jnp.roll(mixed[:, :, :width], mp_size, 0).transpose(1, 0, 2).reshape(rows, -1)
 
     context = attend(qkv, cosine, sine, key_cache, value_cache, mask)
     context, adapter = lax.optimization_barrier((context, adapter))

time: 71 us -> 68.3 us (0.962)
  blocking collectives: 49.9 us -> 43.9 us
  local copies, waits for them, and re-layouts: 1.86 us -> 4.02 us
  starting transfers between devices: 3.57 us -> 5.25 us
    all_to_all x4, blocking collectives: 49.9 us -> 43.9 us  [the longest x3 34.3 us: exchange(): lax.all_to_all(blocks, 'mp', split_axis=0, concat_axis=0, tiled=True, axi...]
    unnamed x32 -> x34, local copies, waits for them, and re-layouts: 1.67 us -> 3.83 us
    all_to_all x1, starting transfers between devices: 3.57 us -> 5.25 us  [exchange(): lax.all_to_all(blocks, 'mp', split_axis=0, concat_axis=0, tiled=True, axi...]
  transfers between devices with their start and end apart: 2 -> 2, of which waited for: 2 -> 1; matrix products, arithmetic and copies ran while one was open for 0% -> 0% of each run, Pallas kernels for 10% -> 10%
where the time goes in v13:
time: 68.3 us; the launch traced here: 67.9 us
  blocking collectives  43.9 us (64%)
  Pallas kernels  12 us (18%)
  starting transfers between devices  5.25 us (8%)
  local copies, waits for them, and re-layouts  4.02 us (6%)
  matrix products  0.9 us (1%)
  waiting for transfers between devices  0.8 us (1%)
  other arithmetic  0.73 us (1%)
    all_to_all x3, blocking collectives, exchange(): lax.all_to_all(blocks, 'mp', split_axis=0, concat_axis=0, tiled=True, axi...  34.3 us
    all_to_all x1, blocking collectives, exchange_all(): lax.all_to_all(blocks, ('mp', 'batch'), split_axis=0, concat_axis=0, tile...  9.62 us
    pallas_call x1, Pallas kernels, project_out(): call(kernel, 'project_out', pltpu.VMEM((count, weight.shape[1]), jnp.floa...  6.21 us
    all_to_all x1, starting transfers between devices, exchange(): lax.all_to_all(blocks, 'mp', split_axis=0, concat_axis=0, tiled=True, axi...  5.25 us
    unnamed x34, local copies, waits for them, and re-layouts  3.83 us
    pallas_call x1, Pallas kernels, down_partials(): call(kernel, 'down_partials', (jax.ShapeDtypeStruct((groups, count, LANES...  1.93 us
    pallas_call x1, Pallas kernels, project_qkv(): call(kernel, 'project_qkv', jax.ShapeDtypeStruct((2 * groups, rows, width...  1.92 us
  transfers between devices with their start and end apart: 2, of which 1 were waited for; matrix products, arithmetic and copies ran while one was open for 0% of the time, Pallas kernels for 10%

profile of v13, /device:TPU:0, one launch (start us, length us, event | category | flops | bytes accessed | tf_op | source)
XLA Modules:
  0.0 67.9 jit_solution(3728601911374774650)
XLA Ops:
  0.0 0.0 slice-start.4
  0.0 0.8 %copy-done.7 = bf16[8192]{0:T(1024)(128)(2,1)S(1)} copy-done((bf16[8192]{0:T(1024)(128)(2,1)S(1)}, bf16[8192]{0:T(1024)(128)(2,1)}, u32[]{:S(2)}) %copy-start.7) | copy-done | bytes 16408
  0.8 0.0 copy-done.1
  0.9 0.0 slice-start.5
  0.9 0.0 slice-start.6
  0.9 0.2 norm_rows.1
  1.1 14.4 %all_to_all.25.near_ref = bf16[8,2,8192]{2,1,0:T(2,128)(2,1)S(1)} all-to-all(bf16[8,2,8192]{2,1,0:T(2,128)(2,1)S(1)} %norm_rows.1), channel_id=1, replica_groups={{8,10,12,14,0,2,4,6},{9,11,13,15,1,3,5,7},{24,26,28,30,16,18,20,22},{25..., dimensions={0} | all-to-all | bytes 524288 | tf_op jit(solution)/shard_map/all_to_all | solution.py:443
  15.6 0.7 %turns.1 = (bf16[16,8192]{1,0:T(8,128)(2,1)S(1)}, f32[2,128]{1,0:T(2,128)S(1)}, f32[2,128]{1,0:T(2,128)S(1)}, f32[2,256]{1,0:T(2,128)S(1)}, bf16[2,128]{1,0:T(2,128)(2,1)S(1)}) custom-call(s32[2]{0:T(128)S(1)} %copy-done.2, s32[2]{0:T(128)S(1)} %copy-done.3, s32[1,2]{1,0:T(1,128)S(1)} %copy-done.4, bf16[8,2,8192]{2,1,0:T(2,128)(2,1)S(1)} %all_to_all.25.near_ref, ...), custom_call_target="tpu_custom_call" | custom-call | bytes 524288 | tf_op jit(solution)/shard_map/turns/pallas_call | solution.py:229
  16.3 0.8 %collective-permute-done.far_ref = bf16[8,2,8192]{2,1,0:T(2,128)(2,1)S(1)} collective-permute-done((bf16[8,2,8192]{2,1,0:T(2,128)(2,1)S(1)}, bf16[8,2,8192]{2,1,0:T(2,128)(2,1)S(1)}, u32[]{:S(2)}, u32[]{:S(2)}) %collective-permute-start) | collective-permute-done | bytes 262176 | tf_op jit(solution)/shard_map/ppermute | solution.py:434
  17.1 0.0 copy-start.8
  17.1 1.9 %project_qkv.1 = bf16[16,2,768]{2,1,0:T(2,128)(2,1)S(1)} custom-call(bf16[16,8192]{1,0:T(8,128)(2,1)S(1)} %get-tuple-element.14.lined_ref, bf16[8,2,8192]{2,1,0:T(2,128)(2,1)S(1)} %collective-permute-done.far_ref, bf16[8192,640]{1,0:T(8,128)(2,1)S(1)} %bitcast.66, bf16[2,128]{1,0:T(2,128)(2,1)S(1)} %get-tuple-element.15.adapter_ref), custom_call_target="tpu_custom_call" | custom-call | flops 10000000000 | bytes 10485760 | tf_op jit(solution)/shard_map/project_qkv/pallas_call | solution.py:273
  19.1 9.6 %all_to_all.26 = bf16[16,2,768]{2,1,0:T(2,128)(2,1)S(1)} all-to-all(bf16[16,2,768]{2,1,0:T(2,128)(2,1)S(1)} %project_qkv.1), channel_id=1, replica_groups={{8,9,10,11,12,13,14,15,0,1,2,3,4,5,6,7},{24,25,26,27,28,29,30,31,16,17,..., dimensions={0} | all-to-all | bytes 98304 | tf_op jit(solution)/shard_map/all_to_all | solution.py:450
  28.7 0.1 pad_maximum_fusion
  28.8 0.1 convert_reduce_fusion
  28.9 0.1 slice_negate_fusion.1
  29.0 0.1 fusion.10
  29.1 0.1 fusion.18
  29.2 0.1 fusion.9
  29.3 0.1 fusion.15
  29.4 0.5 fusion.21
  29.9 0.2 fusion.7
  30.1 0.3 fusion.2
  30.5 0.1 broadcast_in_dim.5
  30.6 10.6 %all_to_all.27.gathered_ref = bf16[8,2,8192]{2,1,0:T(2,128)(2,1)S(1)} all-to-all(bf16[8,2,8192]{2,1,0:T(2,128)(2,1)S(1)} %broadcast_in_dim.5), channel_id=1, replica_groups={{8,10,12,14,0,2,4,6},{9,11,13,15,1,3,5,7},{24,26,28,30,16,18,20,22},{25..., dimensions={0} | all-to-all | bytes 524288 | tf_op jit(solution)/shard_map/all_to_all | solution.py:443
  41.3 1.9 %down_partials.1 = (f32[8,16,128]{2,1,0:T(8,128)}, bf16[1024,1024]{1,0:T(8,128)(2,1)S(1)}) custom-call(s32[8,2]{1,0:T(8,128)S(1)} %convert_element_type.43.adapter_ref, bf16[8,2,8192]{2,1,0:T(2,128)(2,1)S(1)} %all_to_all.27.gathered_ref, bf16[64,64,1024]{2,1,0:T(8,128)(2,1)S(1)} %bitcast.62, bf16[64,64,1024]{2,1,0:T(8,128)(2,1)S(1)} %bitcast.64), custom_call_target="tpu_custom_call" | custom-call | flops 33554432 | bytes 4194304 | tf_op jit(solution)/shard_map/down_partials/pallas_call | solution.py:365
  43.3 1.3 %copy-done.5 = bf16[1024,1024]{1,0:T(8,128)(2,1)} copy-done((bf16[1024,1024]{1,0:T(8,128)(2,1)}, bf16[1024,1024]{1,0:T(8,128)(2,1)S(1)}, u32[]{:S(2)}) %copy-start.5) | copy-done | bytes 2097176
  44.6 5.3 %all-to-all-start.3 = ((f32[8,16,128]{2,1,0:T(8,128)}), f32[8,16,128]{2,1,0:T(8,128)S(1)}, u32[]{:S(2)}, u32[]{:S(2)}) async-start(f32[8,16,128]{2,1,0:T(8,128)} %get-tuple-element.21), calls=%async_computation.3 | async-start | bytes 131072 | tf_op jit(solution)/shard_map/all_to_all | solution.py:443
  49.8 6.2 %project_out.1.base_ref = f32[16,1024]{1,0:T(8,128)S(1)} custom-call(bf16[8,2,8192]{2,1,0:T(2,128)(2,1)S(1)} %all_to_all.27.gathered_ref, bf16[8192,1024]{1,0:T(8,128)(2,1)} %weight_ref.3), custom_call_target="tpu_custom_call" | custom-call | flops 268435456 | bytes 16777216 | tf_op jit(solution)/shard_map/project_out/pallas_call | solution.py:319
  56.1 1.6 %copy-done.6 = bf16[1024,1024]{1,0:T(8,128)(2,1)S(1)} copy-done((bf16[1024,1024]{1,0:T(8,128)(2,1)S(1)}, bf16[1024,1024]{1,0:T(8,128)(2,1)}, u32[]{:S(2)}) %copy-start.6) | copy-done | bytes 2097176
  57.7 0.4 add_up.1
  58.1 9.2 %all_to_all.28.parts_ref = bf16[8,2,1024]{2,1,0:T(2,128)(2,1)S(1)} all-to-all(bf16[8,2,1024]{2,1,0:T(2,128)(2,1)S(1)} %add_up.1), channel_id=1, replica_groups={{8,10,12,14,0,2,4,6},{9,11,13,15,1,3,5,7},{24,26,28,30,16,18,20,22},{25..., dimensions={0} | all-to-all | bytes 65536 | tf_op jit(solution)/shard_map/all_to_all | solution.py:443
  67.3 0.7 add_rows.1
  (41 shorter events, 0.2 us)
Async XLA Ops:
  0.0 29.4 %copy-start = (bf16[2,256,1024]{2,1,0:T(8,128)(2,1)S(1)}, bf16[2,256,1024]{2,1,0:T(8,128)(2,1)}, u32[]{:S(2)}) copy-start(bf16[2,256,1024]{2,1,0:T(8,128)(2,1)} %param.15) | copy-start | bytes 3145732
  0.0 0.8 %copy-start.7 = (bf16[8192]{0:T(1024)(128)(2,1)S(1)}, bf16[8192]{0:T(1024)(128)(2,1)}, u32[]{:S(2)}) copy-start(bf16[8192]{0:T(1024)(128)(2,1)} %param.12) | copy-start | bytes 49156
  0.0 0.9 %copy-start.1 = (bf16[2,8192]{1,0:T(2,128)(2,1)S(1)}, bf16[2,8192]{1,0:T(2,128)(2,1)}, u32[]{:S(2)}) copy-start(bf16[2,8192]{1,0:T(2,128)(2,1)} %hidden_ref.3) | copy-start | bytes 98308
  0.0 17.1 %slice-start.4 = ((s8[10485760]{0:T(1024)(128)(4,1)}), s8[4194304]{0:T(1024)(128)(4,1)S(1)}, s32[]{:S(2)}) async-start(s8[10485760]{0:T(1024)(128)(4,1)} %bitcast.65), calls=%async_computation.9 | async-start | bytes 8388608
  0.9 14.7 %copy-start.2 = (s32[2]{0:T(128)S(1)}, s32[2]{0:T(128)}, u32[]{:S(2)}) copy-start(s32[2]{0:T(128)} %lengths_ref.1) | copy-start | bytes 28
  0.9 14.7 %copy-start.3 = (s32[2]{0:T(128)S(1)}, s32[2]{0:T(128)}, u32[]{:S(2)}) copy-start(s32[2]{0:T(128)} %slots_ref.1) | copy-start | bytes 28
  0.9 14.7 %copy-start.4 = (s32[1,2]{1,0:T(1,128)S(1)}, s32[1,2]{1,0:T(1,128)}, u32[]{:S(2)}) copy-start(s32[1,2]{1,0:T(1,128)} %requests_ref.1) | copy-start | bytes 28
  0.9 16.2 %slice-start.5 = ((s8[10485760]{0:T(1024)(128)(4,1)}), s8[4194304]{0:T(1024)(128)(4,1)S(1)}, s32[]{:S(2)}) async-start(s8[10485760]{0:T(1024)(128)(4,1)} %bitcast.65), calls=%async_computation.10 | async-start | bytes 8388608
  0.9 16.2 %slice-start.6 = ((s8[10485760]{0:T(1024)(128)(4,1)}), s8[2097152]{0:T(1024)(128)(4,1)S(1)}, s32[]{:S(2)}) async-start(s8[10485760]{0:T(1024)(128)(4,1)} %bitcast.65), calls=%async_computation.11 | async-start | bytes 4194304
  15.5 1.5 %collective-permute-start = (bf16[8,2,8192]{2,1,0:T(2,128)(2,1)S(1)}, bf16[8,2,8192]{2,1,0:T(2,128)(2,1)S(1)}, u32[]{:S(2)}, u32[]{:S(2)}) collective-permute-start(bf16[8,2,8192]{2,1,0:T(2,128)(2,1)S(1)} %all_to_all.25.near_ref), channel_id=1, source_target_pairs={{0,1},{1,0},{2,3},{3,2},{4,5},{5,4},{6,7},{7,6},{8,9},{9,8},{10,11... | collective-permute-start | bytes 786440 | tf_op jit(solution)/shard_map/ppermute | solution.py:434
  17.1 24.2 %slice-start = ((s8[8388608]{0:T(1024)(128)(4,1)}), s8[4194304]{0:T(1024)(128)(4,1)S(1)}, s32[]{:S(2)}) async-start(s8[8388608]{0:T(1024)(128)(4,1)} %bitcast.60), calls=%async_computation.5 | async-start | bytes 8388608
  17.1 24.2 %slice-start.2 = ((s8[8388608]{0:T(1024)(128)(4,1)}), s8[4194304]{0:T(1024)(128)(4,1)S(1)}, s32[]{:S(2)}) async-start(s8[8388608]{0:T(1024)(128)(4,1)} %bitcast.63), calls=%async_computation.7 | async-start | bytes 8388608
  17.1 13.0 %copy-start.8 = (bf16[2,256,1024]{2,1,0:T(8,128)(2,1)S(1)}, bf16[2,256,1024]{2,1,0:T(8,128)(2,1)}, u32[]{:S(2)}) copy-start(bf16[2,256,1024]{2,1,0:T(8,128)(2,1)} %param.16) | copy-start | bytes 3145732
  17.1 24.2 %slice-start.1 = ((s8[8388608]{0:T(1024)(128)(4,1)}), s8[4194304]{0:T(1024)(128)(4,1)S(1)}, s32[]{:S(2)}) async-start(s8[8388608]{0:T(1024)(128)(4,1)} %bitcast.60), calls=%async_computation.6 | async-start | bytes 8388608
  17.1 24.2 %slice-start.3 = ((s8[8388608]{0:T(1024)(128)(4,1)}), s8[4194304]{0:T(1024)(128)(4,1)S(1)}, s32[]{:S(2)}) async-start(s8[8388608]{0:T(1024)(128)(4,1)} %bitcast.63), calls=%async_computation.8 | async-start | bytes 8388608
  43.3 1.3 %copy-start.5 = (bf16[1024,1024]{1,0:T(8,128)(2,1)}, bf16[1024,1024]{1,0:T(8,128)(2,1)S(1)}, u32[]{:S(2)}) copy-start(bf16[1024,1024]{1,0:T(8,128)(2,1)S(1)} %get-tuple-element.22.up_ref) | copy-start | bytes 6291460
  44.6 11.5 %all-to-all-start.3 = ((f32[8,16,128]{2,1,0:T(8,128)}), f32[8,16,128]{2,1,0:T(8,128)S(1)}, u32[]{:S(2)}, u32[]{:S(2)}) async-start(f32[8,16,128]{2,1,0:T(8,128)} %get-tuple-element.21), calls=%async_computation.3 | async-start | bytes 131072 | tf_op jit(solution)/shard_map/all_to_all | solution.py:443
  56.1 1.6 %copy-start.6 = (bf16[1024,1024]{1,0:T(8,128)(2,1)S(1)}, bf16[1024,1024]{1,0:T(8,128)(2,1)}, u32[]{:S(2)}) copy-start(bf16[1024,1024]{1,0:T(8,128)(2,1)} %copy-done.5) | copy-start | bytes 6291460

commit v14 on v13

--- a/solution.py
+++ b/solution.py
@@ -262,7 +262,7 @@
         for e in range(2):
             for j in range(groups):
                 place = e * half + j * rows
-                device = 2 * j + (core ^ e)
+                device = 2 * j + (core ^ e ^ 1)
                 out_ref[device, :, pl.ds(0, width)] = total[place : place + rows].astype(
                     jnp.bfloat16
                 )
@@ -298,14 +298,19 @@
     return part
 
 
-def project_out(gathered, weight, parts=16):
+def project_out(gathered, weight, hidden, parts=16):
     groups, rows, depth = gathered.shape
     count, step = groups * rows, depth // parts
 
-    def kernel(gathered_ref, weight_ref, out_ref, near_ref, rows_ref, held_ref, sems, near_sem):
+    def kernel(
+        gathered_ref, weight_ref, hidden_ref, out_ref, kept_ref, near_ref, rows_ref, held_ref,
+        sems, near_sem, kept_sem,
+    ):
         near = pltpu.make_async_copy(gathered_ref, near_ref, near_sem)
         near.start()
         part = stream(weight_ref, held_ref, sems, parts)
+        kept = pltpu.make_async_copy(hidden_ref, kept_ref, kept_sem)
+        kept.start()
         near.wait()
         for j in range(groups):
             rows_ref[pl.ds(j * rows, rows)] = near_ref[j]
@@ -315,12 +320,16 @@
                 rows_ref[:, pl.ds(k * step, step)], part(k), preferred_element_type=jnp.float32
             )
         out_ref[...] = total
+        kept.wait()
 
     return call(
         kernel,
         "project_out",
-        pltpu.VMEM((count, weight.shape[1]), jnp.float32),
-        [ANY] * 2,
+        (
+            pltpu.VMEM((count, weight.shape[1]), jnp.float32),
+            pltpu.VMEM(hidden.shape, hidden.dtype),
+        ),
+        [ANY] * 3,
         weight.size * 2,
         limit=STREAM,
         flops=2 * count * weight.size,
@@ -330,8 +339,9 @@
             pltpu.VMEM(weight.shape, weight.dtype),
             pltpu.SemaphoreType.DMA((parts,)),
             pltpu.SemaphoreType.DMA,
+            pltpu.SemaphoreType.DMA,
         ],
-    )(gathered, weight)
+    )(gathered, weight, hidden)
 
 
 def down_partials(gathered, adapter, down_store, up_store):
@@ -408,7 +418,7 @@
         [VMEM] * 3,
         up.size * 2,
         limit=4 * MIB,
-        flops=LONG,
+        flops=2 * count * up.size,
     )(base, partials, up)
 
 
@@ -446,7 +456,7 @@
 
 
 def exchange_all(blocks):
-    group = [2 * j + core for j in order(lax.axis_size("mp")) for core in range(2)]
+    group = [2 * j + core for j in order(lax.axis_size("mp")) for core in (1, 0)]
     return lax.all_to_all(
         blocks,
         ("mp", "batch"),
@@ -526,7 +536,8 @@
     mixed = exchange_all(columns)
     adapter = mixed.reshape(mp_size, -1, rows, width + LANES)[:, :, :, width]
     adapter = jnp.sum(adapter.astype(jnp.float32), 1).astype(jnp.int32)
-    qkv = jnp.roll(mixed[:, :, :width], mp_size, 0).transpose(1, 0, 2).reshape(rows, -1)
+    qkv = mixed[:, :, :width].reshape(mp_size, 2, rows, width)
+    qkv = jnp.roll(qkv[:, ::-1], mp_size // 2, 0).transpose(2, 0, 1, 3).reshape(rows, -1)
 
     context = attend(qkv, cosine, sine, key_cache, value_cache, mask)
     context, adapter = lax.optimization_barrier((context, adapter))
@@ -536,8 +547,8 @@
         gathered, adapter, adapter_down_matrices.swapaxes(1, 2), adapter_up_matrices
     )
     partials = exchange(partials)
-    projected = add_up(project_out(gathered, output_weight), partials, up)
-    return add_rows(hidden, exchange(projected))
+    base, kept = project_out(gathered, output_weight, hidden)
+    return add_rows(kept, exchange(add_up(base, partials, up)))
 
 
 def body(*arguments):

time: 68.3 us -> 73.9 us (1.082)
  local copies, waits for them, and re-layouts: 4.02 us -> 10 us
    unnamed x34 -> x32, local copies, waits for them, and re-layouts: 3.83 us -> 9.78 us
  transfers between devices with their start and end apart: 2 -> 2, of which waited for: 1 -> 1; matrix products, arithmetic and copies ran while one was open for 0% -> 0% of each run, Pallas kernels for 10% -> 9%
where the time goes in v14:
time: 73.9 us; the launch traced here: 73.4 us
  blocking collectives  43.4 us (59%)
  Pallas kernels  12 us (16%)
  local copies, waits for them, and re-layouts  10 us (14%)
  starting transfers between devices  5.25 us (7%)
  matrix products  0.9 us (1%)
  waiting for transfers between devices  0.8 us (1%)
    all_to_all x3, blocking collectives, exchange(): lax.all_to_all(blocks, 'mp', split_axis=0, concat_axis=0, tiled=True, axi...  34.3 us
    unnamed x32, local copies, waits for them, and re-layouts  9.78 us
    all_to_all x1, blocking collectives, exchange_all(): lax.all_to_all(blocks, ('mp', 'batch'), split_axis=0, concat_axis=0, tile...  9.11 us
    pallas_call x1, Pallas kernels, project_out(): call(kernel, 'project_out', (pltpu.VMEM((count, weight.shape[1]), jnp.flo...  6.22 us
    all_to_all x1, starting transfers between devices, exchange(): lax.all_to_all(blocks, 'mp', split_axis=0, concat_axis=0, tiled=True, axi...  5.25 us
    pallas_call x1, Pallas kernels, project_qkv(): call(kernel, 'project_qkv', jax.ShapeDtypeStruct((2 * groups, rows, width...  1.92 us
    pallas_call x1, Pallas kernels, down_partials(): call(kernel, 'down_partials', (jax.ShapeDtypeStruct((groups, count, LANES...  1.92 us
  transfers between devices with their start and end apart: 2, of which 1 were waited for; matrix products, arithmetic and copies ran while one was open for 0% of the time, Pallas kernels for 9%

profile of v14, /device:TPU:0, one launch (start us, length us, event | category | flops | bytes accessed | tf_op | source)
XLA Modules:
  0.0 73.4 jit_solution(4664680012560749162)
XLA Ops:
  0.0 0.8 %copy-done.10 = bf16[8192]{0:T(1024)(128)(2,1)S(1)} copy-done((bf16[8192]{0:T(1024)(128)(2,1)S(1)}, bf16[8192]{0:T(1024)(128)(2,1)}, u32[]{:S(2)}) %copy-start.10) | copy-done | bytes 16408
  0.8 0.0 copy-done.3
  0.9 0.0 slice-start.1
  0.9 0.2 norm_rows.1
  1.1 14.4 %all_to_all.25.near_ref = bf16[8,2,8192]{2,1,0:T(2,128)(2,1)S(1)} all-to-all(bf16[8,2,8192]{2,1,0:T(2,128)(2,1)S(1)} %norm_rows.1), channel_id=1, replica_groups={{8,10,12,14,0,2,4,6},{9,11,13,15,1,3,5,7},{24,26,28,30,16,18,20,22},{25..., dimensions={0} | all-to-all | bytes 524288 | tf_op jit(solution)/shard_map/all_to_all | solution.py:453
  15.6 0.7 turns.1
  16.3 0.8 %collective-permute-done.far_ref = bf16[8,2,8192]{2,1,0:T(2,128)(2,1)S(1)} collective-permute-done((bf16[8,2,8192]{2,1,0:T(2,128)(2,1)S(1)}, bf16[8,2,8192]{2,1,0:T(2,128)(2,1)S(1)}, u32[]{:S(2)}, u32[]{:S(2)}) %collective-permute-start) | collective-permute-done | bytes 262176 | tf_op jit(solution)/shard_map/ppermute | solution.py:444
  17.1 1.9 %project_qkv.1 = bf16[16,2,768]{2,1,0:T(2,128)(2,1)S(1)} custom-call(bf16[16,8192]{1,0:T(8,128)(2,1)S(1)} %get-tuple-element.16.lined_ref, bf16[8,2,8192]{2,1,0:T(2,128)(2,1)S(1)} %collective-permute-done.far_ref, bf16[8192,640]{1,0:T(8,128)(2,1)S(1)} %bitcast.64, bf16[2,128]{1,0:T(2,128)(2,1)S(1)} %get-tuple-element.17.adapter_ref), custom_call_target="tpu_custom_call" | custom-call | flops 10000000000 | bytes 10485760 | tf_op jit(solution)/shard_map/project_qkv/pallas_call | solution.py:273
  19.0 9.1 %all_to_all.26 = bf16[16,2,768]{2,1,0:T(2,128)(2,1)S(1)} all-to-all(bf16[16,2,768]{2,1,0:T(2,128)(2,1)S(1)} %project_qkv.1), channel_id=1, replica_groups={{9,8,11,10,13,12,15,14,1,0,3,2,5,4,7,6},{25,24,27,26,29,28,31,30,17,16,..., dimensions={0} | all-to-all | bytes 98304 | tf_op jit(solution)/shard_map/all_to_all | solution.py:460
  28.2 0.1 pad_maximum_fusion
  28.4 0.1 slice_negate_fusion.1
  28.4 0.1 fusion.10
  28.5 0.1 fusion.18
  28.6 0.1 fusion.9
  28.7 0.1 fusion.15
  28.8 0.5 fusion.21
  29.3 0.2 fusion.7
  29.5 0.3 fusion.2
  29.9 0.1 convert_reduce_fusion
  30.0 0.1 broadcast_in_dim.5
  30.1 10.6 %all_to_all.27.gathered_ref = bf16[8,2,8192]{2,1,0:T(2,128)(2,1)S(1)} all-to-all(bf16[8,2,8192]{2,1,0:T(2,128)(2,1)S(1)} %broadcast_in_dim.5), channel_id=1, replica_groups={{8,10,12,14,0,2,4,6},{9,11,13,15,1,3,5,7},{24,26,28,30,16,18,20,22},{25..., dimensions={0} | all-to-all | bytes 524288 | tf_op jit(solution)/shard_map/all_to_all | solution.py:453
  40.8 3.4 %copy-done.1 = bf16[64,1024,64]{1,2,0:T(8,128)(2,1)S(1)} copy-done((bf16[64,1024,64]{1,2,0:T(8,128)(2,1)S(1)}, bf16[64,1024,64]{1,2,0:T(8,128)(2,1)}, u32[]{:S(2)}) %copy-start.1) | copy-done | bytes 8388632
  44.2 3.4 %copy-done.2 = bf16[64,64,1024]{2,1,0:T(8,128)(2,1)S(1)} copy-done((bf16[64,64,1024]{2,1,0:T(8,128)(2,1)S(1)}, bf16[64,64,1024]{2,1,0:T(8,128)(2,1)}, u32[]{:S(2)}) %copy-start.2) | copy-done | bytes 8388632
  47.6 1.9 %down_partials.1 = (f32[8,16,128]{2,1,0:T(8,128)}, bf16[1024,1024]{1,0:T(8,128)(2,1)S(1)}) custom-call(s32[8,2]{1,0:T(8,128)S(1)} %convert_element_type.43.adapter_ref, bf16[8,2,8192]{2,1,0:T(2,128)(2,1)S(1)} %all_to_all.27.gathered_ref, bf16[64,64,1024]{2,1,0:T(8,128)(2,1)S(1)} %bitcast.62, bf16[64,64,1024]{2,1,0:T(8,128)(2,1)S(1)} %copy-done.2), custom_call_target="tpu_custom_call" | custom-call | flops 33554432 | bytes 4194304 | tf_op jit(solution)/shard_map/down_partials/pallas_call | solution.py:375
  49.5 5.3 %all-to-all-start.3 = ((f32[8,16,128]{2,1,0:T(8,128)}), f32[8,16,128]{2,1,0:T(8,128)S(1)}, u32[]{:S(2)}, u32[]{:S(2)}) async-start(f32[8,16,128]{2,1,0:T(8,128)} %get-tuple-element.25), calls=%async_computation.3 | async-start | bytes 131072 | tf_op jit(solution)/shard_map/all_to_all | solution.py:453
  54.7 0.8 %copy-done.4 = bf16[2,8192]{1,0:T(2,128)(2,1)S(1)} copy-done((bf16[2,8192]{1,0:T(2,128)(2,1)S(1)}, bf16[2,8192]{1,0:T(2,128)(2,1)}, u32[]{:S(2)}) %copy-start.4) | copy-done | bytes 32792
  55.5 6.2 %project_out.1 = (f32[16,1024]{1,0:T(8,128)S(1)}, bf16[2,8192]{1,0:T(2,128)(2,1)S(1)}) custom-call(bf16[8,2,8192]{2,1,0:T(2,128)(2,1)S(1)} %all_to_all.27.gathered_ref, bf16[8192,1024]{1,0:T(8,128)(2,1)} %weight_ref.3, bf16[2,8192]{1,0:T(2,128)(2,1)S(1)} %copy-done.4), custom_call_target="tpu_custom_call" | custom-call | flops 268435456 | bytes 16777216 | tf_op jit(solution)/shard_map/project_out/pallas_call | solution.py:325
  61.7 0.6 copy-done.5
  62.3 0.4 add_up.1
  62.7 9.2 %all_to_all.28.parts_ref = bf16[8,2,1024]{2,1,0:T(2,128)(2,1)S(1)} all-to-all(bf16[8,2,1024]{2,1,0:T(2,128)(2,1)S(1)} %add_up.1), channel_id=1, replica_groups={{8,10,12,14,0,2,4,6},{9,11,13,15,1,3,5,7},{24,26,28,30,16,18,20,22},{25..., dimensions={0} | all-to-all | bytes 65536 | tf_op jit(solution)/shard_map/all_to_all | solution.py:453
  72.0 0.8 %copy-done.6 = bf16[2,8192]{1,0:T(2,128)(2,1)S(1)} copy-done((bf16[2,8192]{1,0:T(2,128)(2,1)S(1)}, bf16[2,8192]{1,0:T(2,128)(2,1)}, u32[]{:S(2)}) %copy-start.6) | copy-done | bytes 32792
  72.7 0.7 add_rows.1
  (39 shorter events, 0.3 us)
Async XLA Ops:
  0.0 28.8 %copy-start = (bf16[2,256,1024]{2,1,0:T(8,128)(2,1)S(1)}, bf16[2,256,1024]{2,1,0:T(8,128)(2,1)}, u32[]{:S(2)}) copy-start(bf16[2,256,1024]{2,1,0:T(8,128)(2,1)} %param.15) | copy-start | bytes 3145732
  0.0 0.8 %copy-start.10 = (bf16[8192]{0:T(1024)(128)(2,1)S(1)}, bf16[8192]{0:T(1024)(128)(2,1)}, u32[]{:S(2)}) copy-start(bf16[8192]{0:T(1024)(128)(2,1)} %param.12) | copy-start | bytes 49156
  0.0 0.9 %copy-start.3 = (bf16[2,8192]{1,0:T(2,128)(2,1)S(1)}, bf16[2,8192]{1,0:T(2,128)(2,1)}, u32[]{:S(2)}) copy-start(bf16[2,8192]{1,0:T(2,128)(2,1)} %hidden_ref.3) | copy-start | bytes 98308
  0.0 17.1 %slice-start = ((s8[10485760]{0:T(1024)(128)(4,1)}), s8[4194304]{0:T(1024)(128)(4,1)S(1)}, s32[]{:S(2)}) async-start(s8[10485760]{0:T(1024)(128)(4,1)} %bitcast.63), calls=%async_computation.5 | async-start | bytes 8388608
  0.9 14.7 %copy-start.7 = (s32[2]{0:T(128)S(1)}, s32[2]{0:T(128)}, u32[]{:S(2)}) copy-start(s32[2]{0:T(128)} %lengths_ref.1) | copy-start | bytes 28
  0.9 14.7 %copy-start.8 = (s32[2]{0:T(128)S(1)}, s32[2]{0:T(128)}, u32[]{:S(2)}) copy-start(s32[2]{0:T(128)} %slots_ref.1) | copy-start | bytes 28
  0.9 14.7 %copy-start.9 = (s32[1,2]{1,0:T(1,128)S(1)}, s32[1,2]{1,0:T(1,128)}, u32[]{:S(2)}) copy-start(s32[1,2]{1,0:T(1,128)} %requests_ref.1) | copy-start | bytes 28
  0.9 16.2 %slice-start.1 = ((s8[10485760]{0:T(1024)(128)(4,1)}), s8[4194304]{0:T(1024)(128)(4,1)S(1)}, s32[]{:S(2)}) async-start(s8[10485760]{0:T(1024)(128)(4,1)} %bitcast.63), calls=%async_computation.6 | async-start | bytes 8388608
  0.9 16.2 %slice-start.2 = ((s8[10485760]{0:T(1024)(128)(4,1)}), s8[2097152]{0:T(1024)(128)(4,1)S(1)}, s32[]{:S(2)}) async-start(s8[10485760]{0:T(1024)(128)(4,1)} %bitcast.63), calls=%async_computation.7 | async-start | bytes 4194304
  15.5 1.5 %collective-permute-start = (bf16[8,2,8192]{2,1,0:T(2,128)(2,1)S(1)}, bf16[8,2,8192]{2,1,0:T(2,128)(2,1)S(1)}, u32[]{:S(2)}, u32[]{:S(2)}) collective-permute-start(bf16[8,2,8192]{2,1,0:T(2,128)(2,1)S(1)} %all_to_all.25.near_ref), channel_id=1, source_target_pairs={{0,1},{1,0},{2,3},{3,2},{4,5},{5,4},{6,7},{7,6},{8,9},{9,8},{10,11... | collective-permute-start | bytes 786440 | tf_op jit(solution)/shard_map/ppermute | solution.py:444
  17.1 12.4 %copy-start.11 = (bf16[2,256,1024]{2,1,0:T(8,128)(2,1)S(1)}, bf16[2,256,1024]{2,1,0:T(8,128)(2,1)}, u32[]{:S(2)}) copy-start(bf16[2,256,1024]{2,1,0:T(8,128)(2,1)} %param.16) | copy-start | bytes 3145732
  40.8 3.4 %copy-start.1 = (bf16[64,1024,64]{1,2,0:T(8,128)(2,1)S(1)}, bf16[64,1024,64]{1,2,0:T(8,128)(2,1)}, u32[]{:S(2)}) copy-start(bf16[64,1024,64]{1,2,0:T(8,128)(2,1)} %param.20) | copy-start | bytes 25165828
  44.2 3.4 %copy-start.2 = (bf16[64,64,1024]{2,1,0:T(8,128)(2,1)S(1)}, bf16[64,64,1024]{2,1,0:T(8,128)(2,1)}, u32[]{:S(2)}) copy-start(bf16[64,64,1024]{2,1,0:T(8,128)(2,1)} %up_ref.1) | copy-start | bytes 25165828
  49.5 12.9 %all-to-all-start.3 = ((f32[8,16,128]{2,1,0:T(8,128)}), f32[8,16,128]{2,1,0:T(8,128)S(1)}, u32[]{:S(2)}, u32[]{:S(2)}) async-start(f32[8,16,128]{2,1,0:T(8,128)} %get-tuple-element.25), calls=%async_computation.3 | async-start | bytes 131072 | tf_op jit(solution)/shard_map/all_to_all | solution.py:453
  54.7 0.8 %copy-start.4 = (bf16[2,8192]{1,0:T(2,128)(2,1)S(1)}, bf16[2,8192]{1,0:T(2,128)(2,1)}, u32[]{:S(2)}) copy-start(bf16[2,8192]{1,0:T(2,128)(2,1)} %hidden_ref.3) | copy-start | bytes 98308
  61.7 0.6 copy-start.5
  72.0 0.8 %copy-start.6 = (bf16[2,8192]{1,0:T(2,128)(2,1)S(1)}, bf16[2,8192]{1,0:T(2,128)(2,1)}, u32[]{:S(2)}) copy-start(bf16[2,8192]{1,0:T(2,128)(2,1)} %copy-done.5) | copy-start | bytes 98308

commit v15 on v13

--- a/solution.py
+++ b/solution.py
@@ -262,7 +262,7 @@
         for e in range(2):
             for j in range(groups):
                 place = e * half + j * rows
-                device = 2 * j + (core ^ e)
+                device = 2 * j + (core ^ e ^ 1)
                 out_ref[device, :, pl.ds(0, width)] = total[place : place + rows].astype(
                     jnp.bfloat16
                 )
@@ -345,7 +345,7 @@
         for j in range(groups):
             rows_ref[pl.ds(j * rows, rows)] = gathered_ref[j, :, pl.ds(start, depth)]
         for r in range(count):
-            chosen = adapter_ref[r // rows, r % rows]
+            chosen = adapter_ref[r, 0]
             held_ref[pl.ds(r * rank, rank)] = down_ref[chosen]
             picked_ref[pl.ds(r * rank, rank)] = up_ref[chosen]
         every = lax.dot_general(
@@ -408,7 +408,7 @@
         [VMEM] * 3,
         up.size * 2,
         limit=4 * MIB,
-        flops=LONG,
+        flops=2 * count * up.size,
     )(base, partials, up)
 
 
@@ -446,7 +446,7 @@
 
 
 def exchange_all(blocks):
-    group = [2 * j + core for j in order(lax.axis_size("mp")) for core in range(2)]
+    group = [2 * j + core for j in order(lax.axis_size("mp")) for core in (1, 0)]
     return lax.all_to_all(
         blocks,
         ("mp", "batch"),
@@ -457,47 +457,108 @@
     )
 
 
-def attend(qkv, cosine, sine, key_cache, value_cache, mask):
-    rows = qkv.shape[0]
-    query_width = HEADS * HEAD_DIM
-    kv_width = KV_HEADS * HEAD_DIM
+def attend(mixed, cosine, sine, mask, key_cache, value_cache, copies):
+    rows, context = key_cache.shape[:2]
     group = HEADS // KV_HEADS
-    scale = HEAD_DIM ** (-0.5)
-
-    def turn(part):
-        vec = part.astype(jnp.float32).reshape(rows, -1, HEAD_DIM)
-        half = HEAD_DIM // 2
-        turned = jnp.concatenate([-vec[..., half:], vec[..., :half]], -1)
-        return (vec * cosine[:, None] + turned * sine[:, None]).astype(jnp.bfloat16)
-
-    query = turn(qkv[:, :query_width])
-    fresh_key = turn(qkv[:, query_width : query_width + kv_width])
-    fresh_value = (
-        qkv[:, query_width + kv_width :].astype(jnp.float32).reshape(rows, KV_HEADS, HEAD_DIM)
-    )
-    grouped = query.reshape(rows, KV_HEADS, group, HEAD_DIM)
-    cached = key_cache.reshape(rows, -1, KV_HEADS, HEAD_DIM)
-    stored = value_cache.reshape(rows, -1, KV_HEADS, HEAD_DIM)
-    scores = (
-        jnp.einsum("rgqd,rtgd->rgqt", grouped, cached, preferred_element_type=jnp.float32) * scale
-    )
-    scores = scores + mask[:, None, None, :]
-    own = (
-        jnp.einsum("rgqd,rgd->rgq", grouped, fresh_key, preferred_element_type=jnp.float32) * scale
-    )
-    top = jnp.maximum(jnp.max(scores, -1), own)
-    expo = jnp.exp(scores - top[..., None])
-    own_exp = jnp.exp(own - top)
-    total = jnp.sum(expo, -1) + own_exp
-    probs = (expo / total[..., None]).astype(jnp.bfloat16)
-    own_prob = (own_exp / total).astype(jnp.bfloat16)
-    context_vector = jnp.einsum(
-        "rgqt,rtgd->rgqd", probs, stored, preferred_element_type=jnp.float32
-    )
-    context_vector = (
-        context_vector + own_prob.astype(jnp.float32)[..., None] * fresh_value[:, :, None, :]
-    )
-    return context_vector.reshape(rows, query_width).astype(jnp.bfloat16)
+    heads = HEADS + 2 * KV_HEADS
+    width = mixed.shape[2] - LANES
+    per_device = width // HEAD_DIM
+    devices = order(mixed.shape[0] // 2)
+
+    def kernel(
+        mixed_ref, cosine_ref, sine_ref, mask_ref, key_ref, value_ref, out_ref, adapter_ref,
+        vec_ref, context_ref,
+    ):
+        for k, j in enumerate(devices):
+            for core in range(2):
+                block = mixed_ref[2 * k + 1 - core].astype(jnp.float32)
+                for c in range(per_device):
+                    head = (2 * j + core) * per_device + c
+                    vec_ref[pl.ds(head * rows, rows)] = block[:, c * HEAD_DIM : (c + 1) * HEAD_DIM]
+            both = mixed_ref[2 * k, :, pl.ds(width, LANES)].astype(jnp.float32)
+            both = both + mixed_ref[2 * k + 1, :, pl.ds(width, LANES)].astype(jnp.float32)
+            adapter_ref[pl.ds(k * rows, rows)] = both.astype(jnp.int32)
+
+        def tiled(pair, count):
+            return jnp.concatenate([pair] * count)
+
+        keyed = (HEADS + KV_HEADS) * rows
+        vec = vec_ref[pl.ds(0, keyed)]
+        turned = pltpu.roll(vec, HEAD_DIM // 2, 1)
+        lane = lax.broadcasted_iota(jnp.int32, (rows, HEAD_DIM), 1)
+        signed = jnp.where(lane < HEAD_DIM // 2, -sine_ref[...], sine_ref[...])
+        pairs = keyed // rows
+        vec = vec * tiled(cosine_ref[...], pairs) + turned * tiled(signed, pairs)
+        vec = vec.astype(jnp.bfloat16)
+        query = vec[: HEADS * rows]
+        fresh_key = vec[HEADS * rows :].astype(jnp.float32)
+        fresh_value = vec_ref[pl.ds(keyed, KV_HEADS * rows)]
+        size = group * rows
+        owner = lax.broadcasted_iota(jnp.int32, (size, 1), 0) % rows
+
+        def of_owner(products):
+            result = products[0]
+            for r in range(1, rows):
+                result = jnp.where(owner == r, products[r], result)
+            return result
+
+        scores, own_key, own_value = [], [], []
+        for g in range(KV_HEADS):
+            lanes = pl.ds(g * HEAD_DIM, HEAD_DIM)
+            part = query[g * size : (g + 1) * size]
+            products = [
+                lax.dot_general(
+                    part,
+                    key_ref[r, :, lanes],
+                    (((1,), (1,)), ((), ())),
+                    preferred_element_type=jnp.float32,
+                )
+                for r in range(rows)
+            ]
+            scores.append(of_owner(products))
+            own_key.append(tiled(fresh_key[g * rows : (g + 1) * rows], group))
+            own_value.append(tiled(fresh_value[g * rows : (g + 1) * rows], group))
+        scale = HEAD_DIM ** (-0.5)
+        scores = jnp.concatenate(scores) * scale + tiled(mask_ref[...], HEADS)
+        own = jnp.sum(query.astype(jnp.float32) * jnp.concatenate(own_key), 1, keepdims=True)
+        own = own * scale
+        top = jnp.maximum(jnp.max(scores, 1, keepdims=True), own)
+        expo = jnp.exp(scores - top)
+        own_exp = jnp.exp(own - top)
+        total = jnp.sum(expo, 1, keepdims=True) + own_exp
+        probs = (expo / total).astype(jnp.bfloat16)
+        own_prob = (own_exp / total).astype(jnp.bfloat16).astype(jnp.float32)
+        for g in range(KV_HEADS):
+            lanes = pl.ds(g * HEAD_DIM, HEAD_DIM)
+            part = probs[g * size : (g + 1) * size]
+            products = [
+                jnp.dot(part, value_ref[r, :, lanes], preferred_element_type=jnp.float32)
+                for r in range(rows)
+            ]
+            result = of_owner(products) + own_prob[g * size : (g + 1) * size] * own_value[g]
+            for h in range(group):
+                place = pl.ds((g * group + h) * HEAD_DIM, HEAD_DIM)
+                context_ref[:, place] = result[h * rows : (h + 1) * rows]
+        rounded = context_ref[...].astype(jnp.bfloat16)
+        for c in range(copies):
+            out_ref[c] = rounded
+
+    return call(
+        kernel,
+        "attend",
+        (
+            jax.ShapeDtypeStruct((copies, rows, HEADS * HEAD_DIM), jnp.bfloat16),
+            jax.ShapeDtypeStruct((copies * rows, LANES), jnp.int32),
+        ),
+        [VMEM] * 6,
+        key_cache.size * 4,
+        limit=4 * MIB,
+        flops=LONG,
+        scratch_shapes=[
+            pltpu.VMEM((heads * rows, HEAD_DIM), jnp.float32),
+            pltpu.VMEM((rows, HEADS * HEAD_DIM), jnp.float32),
+        ],
+    )(mixed, cosine, sine, mask, key_cache, value_cache)
 
 
 def fast_body(
@@ -513,10 +574,7 @@
     adapter_down_matrices,
     adapter_up_matrices,
 ):
-    rows = hidden.shape[0]
     mp_size = lax.axis_size("mp")
-    width = query_key_value_weight.shape[1]
-
     frequency = frequencies(exponents())
     near = exchange(norm_rows(hidden, attention_norm_gain, frequency, mp_size))
     lined, cosine, sine, mask, adapter = turns(
@@ -524,13 +582,8 @@
     )
     columns = project_qkv(lined, swap_cores(near), query_key_value_weight, adapter)
     mixed = exchange_all(columns)
-    adapter = mixed.reshape(mp_size, -1, rows, width + LANES)[:, :, :, width]
-    adapter = jnp.sum(adapter.astype(jnp.float32), 1).astype(jnp.int32)
-    qkv = jnp.roll(mixed[:, :, :width], mp_size, 0).transpose(1, 0, 2).reshape(rows, -1)
-
-    context = attend(qkv, cosine, sine, key_cache, value_cache, mask)
-    context, adapter = lax.optimization_barrier((context, adapter))
-    gathered = exchange(jnp.broadcast_to(context[None], (mp_size, *context.shape)))
+    context, adapter = attend(mixed, cosine, sine, mask, key_cache, value_cache, mp_size)
+    gathered = exchange(context)
 
     partials, up = down_partials(
         gathered, adapter, adapter_down_matrices.swapaxes(1, 2), adapter_up_matrices

time: 68.3 us -> 64.5 us (0.944)
  local copies, waits for them, and re-layouts: 4.02 us -> 0.81 us
  Pallas kernels: 12 us -> 12.9 us
  matrix products: 0.9 us -> 0 us
  other arithmetic: 0.73 us -> 0.01 us
    unnamed x34 -> x28, local copies, waits for them, and re-layouts: 3.83 us -> 0.79 us
    dot_general x3 -> x0, matrix products: 0.9 us -> none  [the longest x1 0.46 us: attend(): jnp.einsum('rgqd,rtgd->rgqt', grouped, cached, preferred_element_type=jnp...]
    pallas_call x0 -> x1, Pallas kernels: none -> 0.77 us  [attend(): call(kernel, 'attend', (jax.ShapeDtypeStruct((copies, rows, HEADS * HEAD_...]
  transfers between devices with their start and end apart: 2 -> 2, of which waited for: 1 -> 1; matrix products, arithmetic and copies ran while one was open for 0% -> 0% of each run, Pallas kernels for 10% -> 11%
where the time goes in v15:
time: 64.5 us; the launch traced here: 64 us
  blocking collectives  44.1 us (68%)
  Pallas kernels  12.9 us (20%)
  starting transfers between devices  5.25 us (8%)
  local copies, waits for them, and re-layouts  0.81 us (1%)
  waiting for transfers between devices  0.8 us (1%)
    all_to_all x3, blocking collectives, exchange(): lax.all_to_all(blocks, 'mp', split_axis=0, concat_axis=0, tiled=True, axi...  34.7 us
    all_to_all x1, blocking collectives, exchange_all(): lax.all_to_all(blocks, ('mp', 'batch'), split_axis=0, concat_axis=0, tile...  9.38 us
    pallas_call x1, Pallas kernels, project_out(): call(kernel, 'project_out', pltpu.VMEM((count, weight.shape[1]), jnp.floa...  6.21 us
    all_to_all x1, starting transfers between devices, exchange(): lax.all_to_all(blocks, 'mp', split_axis=0, concat_axis=0, tiled=True, axi...  5.25 us
    pallas_call x1, Pallas kernels, down_partials(): call(kernel, 'down_partials', (jax.ShapeDtypeStruct((groups, count, LANES...  2.01 us
    pallas_call x1, Pallas kernels, project_qkv(): call(kernel, 'project_qkv', jax.ShapeDtypeStruct((2 * groups, rows, width...  1.92 us
  transfers between devices with their start and end apart: 2, of which 1 were waited for; matrix products, arithmetic and copies ran while one was open for 0% of the time, Pallas kernels for 11%

profile of v15, /device:TPU:0, one launch (start us, length us, event | category | flops | bytes accessed | tf_op | source)
XLA Modules:
  0.0 64.0 jit_solution(4034273926414890897)
XLA Ops:
  0.0 0.7 %copy-done.6 = bf16[8192]{0:T(1024)(128)(2,1)S(1)} copy-done((bf16[8192]{0:T(1024)(128)(2,1)S(1)}, bf16[8192]{0:T(1024)(128)(2,1)}, u32[]{:S(2)}) %copy-start.6) | copy-done | bytes 16408
  0.7 0.0 copy-done
  0.8 0.0 slice-start.5
  0.8 0.0 slice-start.6
  0.8 0.2 norm_rows.1
  1.0 14.4 %all_to_all.25.near_ref = bf16[8,2,8192]{2,1,0:T(2,128)(2,1)S(1)} all-to-all(bf16[8,2,8192]{2,1,0:T(2,128)(2,1)S(1)} %norm_rows.1), channel_id=1, replica_groups={{8,10,12,14,0,2,4,6},{9,11,13,15,1,3,5,7},{24,26,28,30,16,18,20,22},{25..., dimensions={0} | all-to-all | bytes 524288 | tf_op jit(solution)/shard_map/all_to_all | solution.py:443
  15.4 0.0 collective-permute-start
  15.4 0.0 copy-done.1
  15.4 0.0 copy-done.2
  15.5 0.0 copy-done.3
  15.5 0.7 %turns.1 = (bf16[16,8192]{1,0:T(8,128)(2,1)S(1)}, f32[2,128]{1,0:T(2,128)S(1)}, f32[2,128]{1,0:T(2,128)S(1)}, f32[2,256]{1,0:T(2,128)S(1)}, bf16[2,128]{1,0:T(2,128)(2,1)S(1)}) custom-call(s32[2]{0:T(128)S(1)} %copy-done.1, s32[2]{0:T(128)S(1)} %copy-done.2, s32[1,2]{1,0:T(1,128)S(1)} %copy-done.3, bf16[8,2,8192]{2,1,0:T(2,128)(2,1)S(1)} %all_to_all.25.near_ref, ...), custom_call_target="tpu_custom_call" | custom-call | bytes 524288 | tf_op jit(solution)/shard_map/turns/pallas_call | solution.py:229
  16.2 0.8 %collective-permute-done.far_ref = bf16[8,2,8192]{2,1,0:T(2,128)(2,1)S(1)} collective-permute-done((bf16[8,2,8192]{2,1,0:T(2,128)(2,1)S(1)}, bf16[8,2,8192]{2,1,0:T(2,128)(2,1)S(1)}, u32[]{:S(2)}, u32[]{:S(2)}) %collective-permute-start) | collective-permute-done | bytes 262176 | tf_op jit(solution)/shard_map/ppermute | solution.py:434
  17.0 0.0 slice-done.4
  17.0 0.0 slice-done.5
  17.0 0.0 slice-done.6
  17.0 0.0 copy-start.4
  17.0 0.0 copy-start.5
  17.0 0.0 slice-start
  17.0 0.0 slice-start.2
  17.0 1.9 %project_qkv.1 = bf16[16,2,768]{2,1,0:T(2,128)(2,1)S(1)} custom-call(bf16[16,8192]{1,0:T(8,128)(2,1)S(1)} %get-tuple-element.14.lined_ref, bf16[8,2,8192]{2,1,0:T(2,128)(2,1)S(1)} %collective-permute-done.far_ref, bf16[8192,640]{1,0:T(8,128)(2,1)S(1)} %bitcast.7, bf16[2,128]{1,0:T(2,128)(2,1)S(1)} %get-tuple-element.15.adapter_ref), custom_call_target="tpu_custom_call" | custom-call | flops 10000000000 | bytes 10485760 | tf_op jit(solution)/shard_map/project_qkv/pallas_call | solution.py:273
  19.0 9.4 %all_to_all.26.mixed_ref = bf16[16,2,768]{2,1,0:T(2,128)(2,1)S(1)} all-to-all(bf16[16,2,768]{2,1,0:T(2,128)(2,1)S(1)} %project_qkv.1), channel_id=1, replica_groups={{9,8,11,10,13,12,15,14,1,0,3,2,5,4,7,6},{25,24,27,26,29,28,31,30,17,16,..., dimensions={0} | all-to-all | bytes 98304 | tf_op jit(solution)/shard_map/all_to_all | solution.py:450
  28.4 0.0 copy-done.4
  28.4 0.8 %attend.1 = (bf16[8,2,8192]{2,1,0:T(2,128)(2,1)S(1)}, s32[16,128]{1,0:T(8,128)S(1)}) custom-call(bf16[16,2,768]{2,1,0:T(2,128)(2,1)S(1)} %all_to_all.26.mixed_ref, f32[2,128]{1,0:T(2,128)S(1)} %get-tuple-element.16.cosine_ref, f32[2,128]{1,0:T(2,128)S(1)} %get-tuple-element.17.sine_ref, f32[2,256]{1,0:T(2,128)S(1)} %get-tuple-element.18.mask_ref, ...), custom_call_target="tpu_custom_call" | custom-call | flops 10000000000 | bytes 2097152 | tf_op jit(solution)/shard_map/attend/pallas_call | solution.py:546
  29.2 11.0 %all_to_all.27.gathered_ref = bf16[8,2,8192]{2,1,0:T(2,128)(2,1)S(1)} all-to-all(bf16[8,2,8192]{2,1,0:T(2,128)(2,1)S(1)} %get-tuple-element.19), channel_id=1, replica_groups={{8,10,12,14,0,2,4,6},{9,11,13,15,1,3,5,7},{24,26,28,30,16,18,20,22},{25..., dimensions={0} | all-to-all | bytes 524288 | tf_op jit(solution)/shard_map/all_to_all | solution.py:443
  40.2 0.0 slice-done.2
  40.2 2.0 %down_partials.1 = (f32[8,16,128]{2,1,0:T(8,128)}, bf16[1024,1024]{1,0:T(8,128)(2,1)S(1)}) custom-call(s32[16,128]{1,0:T(8,128)S(1)} %get-tuple-element.20.adapter_ref, bf16[8,2,8192]{2,1,0:T(2,128)(2,1)S(1)} %all_to_all.27.gathered_ref, bf16[64,64,1024]{2,1,0:T(8,128)(2,1)S(1)} %bitcast.3, bf16[64,64,1024]{2,1,0:T(8,128)(2,1)S(1)} %bitcast.5), custom_call_target="tpu_custom_call" | custom-call | flops 33554432 | bytes 4194304 | tf_op jit(solution)/shard_map/down_partials/pallas_call | solution.py:365
  42.2 5.3 %all-to-all-start.3 = ((f32[8,16,128]{2,1,0:T(8,128)}), f32[8,16,128]{2,1,0:T(8,128)S(1)}, u32[]{:S(2)}, u32[]{:S(2)}) async-start(f32[8,16,128]{2,1,0:T(8,128)} %get-tuple-element.21), calls=%async_computation.3 | async-start | bytes 131072 | tf_op jit(solution)/shard_map/all_to_all | solution.py:443
  47.5 6.2 %project_out.1.base_ref = f32[16,1024]{1,0:T(8,128)S(1)} custom-call(bf16[8,2,8192]{2,1,0:T(2,128)(2,1)S(1)} %all_to_all.27.gathered_ref, bf16[8192,1024]{1,0:T(8,128)(2,1)} %weight_ref.3), custom_call_target="tpu_custom_call" | custom-call | flops 268435456 | bytes 16777216 | tf_op jit(solution)/shard_map/project_out/pallas_call | solution.py:319
  53.7 0.0 all-to-all-done.3.partials_ref
  53.7 0.4 add_up.1
  54.1 9.2 %all_to_all.28.parts_ref = bf16[8,2,1024]{2,1,0:T(2,128)(2,1)S(1)} all-to-all(bf16[8,2,1024]{2,1,0:T(2,128)(2,1)S(1)} %add_up.1), channel_id=1, replica_groups={{8,10,12,14,0,2,4,6},{9,11,13,15,1,3,5,7},{24,26,28,30,16,18,20,22},{25..., dimensions={0} | all-to-all | bytes 65536 | tf_op jit(solution)/shard_map/all_to_all | solution.py:443
  63.4 0.7 %add_rows.1 = bf16[2,8192]{1,0:T(2,128)(2,1)} custom-call(bf16[2,8192]{1,0:T(2,128)(2,1)S(1)} %copy-done, bf16[8,2,1024]{2,1,0:T(2,128)(2,1)S(1)} %all_to_all.28.parts_ref), custom_call_target="tpu_custom_call" | custom-call | bytes 98304 | tf_op jit(solution)/shard_map/add_rows/pallas_call | solution.py:424
  (18 shorter events, 0.1 us)
Async XLA Ops:
  0.0 0.7 %copy-start.6 = (bf16[8192]{0:T(1024)(128)(2,1)S(1)}, bf16[8192]{0:T(1024)(128)(2,1)}, u32[]{:S(2)}) copy-start(bf16[8192]{0:T(1024)(128)(2,1)} %param.12) | copy-start | bytes 49156
  0.0 0.8 %copy-start = (bf16[2,8192]{1,0:T(2,128)(2,1)S(1)}, bf16[2,8192]{1,0:T(2,128)(2,1)}, u32[]{:S(2)}) copy-start(bf16[2,8192]{1,0:T(2,128)(2,1)} %hidden_ref.3) | copy-start | bytes 98308
  0.0 17.0 %slice-start.4 = ((s8[10485760]{0:T(1024)(128)(4,1)}), s8[4194304]{0:T(1024)(128)(4,1)S(1)}, s32[]{:S(2)}) async-start(s8[10485760]{0:T(1024)(128)(4,1)} %bitcast.6), calls=%async_computation.9 | async-start | bytes 8388608
  0.8 14.7 %copy-start.1 = (s32[2]{0:T(128)S(1)}, s32[2]{0:T(128)}, u32[]{:S(2)}) copy-start(s32[2]{0:T(128)} %lengths_ref.1) | copy-start | bytes 28
  0.8 14.7 %copy-start.2 = (s32[2]{0:T(128)S(1)}, s32[2]{0:T(128)}, u32[]{:S(2)}) copy-start(s32[2]{0:T(128)} %slots_ref.1) | copy-start | bytes 28
  0.8 14.7 %copy-start.3 = (s32[1,2]{1,0:T(1,128)S(1)}, s32[1,2]{1,0:T(1,128)}, u32[]{:S(2)}) copy-start(s32[1,2]{1,0:T(1,128)} %requests_ref.1) | copy-start | bytes 28
  0.8 16.2 %slice-start.5 = ((s8[10485760]{0:T(1024)(128)(4,1)}), s8[4194304]{0:T(1024)(128)(4,1)S(1)}, s32[]{:S(2)}) async-start(s8[10485760]{0:T(1024)(128)(4,1)} %bitcast.6), calls=%async_computation.10 | async-start | bytes 8388608
  0.8 16.2 %slice-start.6 = ((s8[10485760]{0:T(1024)(128)(4,1)}), s8[2097152]{0:T(1024)(128)(4,1)S(1)}, s32[]{:S(2)}) async-start(s8[10485760]{0:T(1024)(128)(4,1)} %bitcast.6), calls=%async_computation.11 | async-start | bytes 4194304
  15.4 1.5 %collective-permute-start = (bf16[8,2,8192]{2,1,0:T(2,128)(2,1)S(1)}, bf16[8,2,8192]{2,1,0:T(2,128)(2,1)S(1)}, u32[]{:S(2)}, u32[]{:S(2)}) collective-permute-start(bf16[8,2,8192]{2,1,0:T(2,128)(2,1)S(1)} %all_to_all.25.near_ref), channel_id=1, source_target_pairs={{0,1},{1,0},{2,3},{3,2},{4,5},{5,4},{6,7},{7,6},{8,9},{9,8},{10,11... | collective-permute-start | bytes 786440 | tf_op jit(solution)/shard_map/ppermute | solution.py:434
  17.0 11.4 %copy-start.4 = (bf16[2,256,1024]{2,1,0:T(8,128)(2,1)S(1)}, bf16[2,256,1024]{2,1,0:T(8,128)(2,1)}, u32[]{:S(2)}) copy-start(bf16[2,256,1024]{2,1,0:T(8,128)(2,1)} %key_ref.1) | copy-start | bytes 3145732
  17.0 11.4 %copy-start.5 = (bf16[2,256,1024]{2,1,0:T(8,128)(2,1)S(1)}, bf16[2,256,1024]{2,1,0:T(8,128)(2,1)}, u32[]{:S(2)}) copy-start(bf16[2,256,1024]{2,1,0:T(8,128)(2,1)} %value_ref.1) | copy-start | bytes 3145732
  17.0 23.2 %slice-start = ((s8[8388608]{0:T(1024)(128)(4,1)}), s8[4194304]{0:T(1024)(128)(4,1)S(1)}, s32[]{:S(2)}) async-start(s8[8388608]{0:T(1024)(128)(4,1)} %bitcast.1), calls=%async_computation.5 | async-start | bytes 8388608
  17.0 23.2 %slice-start.2 = ((s8[8388608]{0:T(1024)(128)(4,1)}), s8[4194304]{0:T(1024)(128)(4,1)S(1)}, s32[]{:S(2)}) async-start(s8[8388608]{0:T(1024)(128)(4,1)} %bitcast.4), calls=%async_computation.7 | async-start | bytes 8388608
  28.4 11.8 %slice-start.1 = ((s8[8388608]{0:T(1024)(128)(4,1)}), s8[4194304]{0:T(1024)(128)(4,1)S(1)}, s32[]{:S(2)}) async-start(s8[8388608]{0:T(1024)(128)(4,1)} %bitcast.1), calls=%async_computation.6 | async-start | bytes 8388608
  28.4 11.8 %slice-start.3 = ((s8[8388608]{0:T(1024)(128)(4,1)}), s8[4194304]{0:T(1024)(128)(4,1)S(1)}, s32[]{:S(2)}) async-start(s8[8388608]{0:T(1024)(128)(4,1)} %bitcast.4), calls=%async_computation.8 | async-start | bytes 8388608
  42.2 11.5 %all-to-all-start.3 = ((f32[8,16,128]{2,1,0:T(8,128)}), f32[8,16,128]{2,1,0:T(8,128)S(1)}, u32[]{:S(2)}, u32[]{:S(2)}) async-start(f32[8,16,128]{2,1,0:T(8,128)} %get-tuple-element.21), calls=%async_computation.3 | async-start | bytes 131072 | tf_op jit(solution)/shard_map/all_to_all | solution.py:443

commit v16 on v15

--- a/solution.py
+++ b/solution.py
@@ -435,7 +435,7 @@
 
 
 def order(size):
-    return [(k + size // 2) % size for k in range(size)]
+    return [(k + size // 2 + 1) % size for k in range(size)]
 
 
 def exchange(blocks):

time: 64.5 us -> 63.6 us (0.986)
  blocking collectives: 44.1 us -> 43.4 us
    all_to_all x1, blocking collectives: 9.38 us -> 8.52 us  [exchange_all(): lax.all_to_all(blocks, ('mp', 'batch'), split_axis=0, concat_axis=0, tile...]
where the time goes in v16:
time: 63.6 us; the launch traced here: 63.1 us
  blocking collectives  43.4 us (68%)
  Pallas kernels  12.9 us (20%)
  starting transfers between devices  5.1 us (8%)
  local copies, waits for them, and re-layouts  0.81 us (1%)
  waiting for transfers between devices  0.8 us (1%)
    all_to_all x3, blocking collectives, exchange(): lax.all_to_all(blocks, 'mp', split_axis=0, concat_axis=0, tiled=True, axi...  34.9 us
    all_to_all x1, blocking collectives, exchange_all(): lax.all_to_all(blocks, ('mp', 'batch'), split_axis=0, concat_axis=0, tile...  8.52 us
    pallas_call x1, Pallas kernels, project_out(): call(kernel, 'project_out', pltpu.VMEM((count, weight.shape[1]), jnp.floa...  6.21 us
    all_to_all x1, starting transfers between devices, exchange(): lax.all_to_all(blocks, 'mp', split_axis=0, concat_axis=0, tiled=True, axi...  5.1 us
    pallas_call x1, Pallas kernels, down_partials(): call(kernel, 'down_partials', (jax.ShapeDtypeStruct((groups, count, LANES...  2.01 us
    pallas_call x1, Pallas kernels, project_qkv(): call(kernel, 'project_qkv', jax.ShapeDtypeStruct((2 * groups, rows, width...  1.92 us
  transfers between devices with their start and end apart: 2, of which 1 were waited for; matrix products, arithmetic and copies ran while one was open for 0% of the time, Pallas kernels for 11%

profile of v16, /device:TPU:0, one launch (start us, length us, event | category | flops | bytes accessed | tf_op | source)
XLA Modules:
  0.0 63.1 jit_solution(12834021410268824043)
XLA Ops:
  0.0 0.7 %copy-done.6 = bf16[8192]{0:T(1024)(128)(2,1)S(1)} copy-done((bf16[8192]{0:T(1024)(128)(2,1)S(1)}, bf16[8192]{0:T(1024)(128)(2,1)}, u32[]{:S(2)}) %copy-start.6) | copy-done | bytes 16408
  0.7 0.0 copy-done
  0.8 0.0 slice-start.5
  0.8 0.0 slice-start.6
  0.8 0.2 norm_rows.1
  1.0 14.6 %all_to_all.25.near_ref = bf16[8,2,8192]{2,1,0:T(2,128)(2,1)S(1)} all-to-all(bf16[8,2,8192]{2,1,0:T(2,128)(2,1)S(1)} %norm_rows.1), channel_id=1, replica_groups={{10,12,14,0,2,4,6,8},{11,13,15,1,3,5,7,9},{26,28,30,16,18,20,22,24},{27..., dimensions={0} | all-to-all | bytes 524288 | tf_op jit(solution)/shard_map/all_to_all | solution.py:443
  15.6 0.0 collective-permute-start
  15.6 0.0 copy-done.1
  15.6 0.0 copy-done.2
  15.6 0.0 copy-done.3
  15.6 0.7 %turns.1 = (bf16[16,8192]{1,0:T(8,128)(2,1)S(1)}, f32[2,128]{1,0:T(2,128)S(1)}, f32[2,128]{1,0:T(2,128)S(1)}, f32[2,256]{1,0:T(2,128)S(1)}, bf16[2,128]{1,0:T(2,128)(2,1)S(1)}) custom-call(s32[2]{0:T(128)S(1)} %copy-done.1, s32[2]{0:T(128)S(1)} %copy-done.2, s32[1,2]{1,0:T(1,128)S(1)} %copy-done.3, bf16[8,2,8192]{2,1,0:T(2,128)(2,1)S(1)} %all_to_all.25.near_ref, ...), custom_call_target="tpu_custom_call" | custom-call | bytes 524288 | tf_op jit(solution)/shard_map/turns/pallas_call | solution.py:229
  16.3 0.8 %collective-permute-done.far_ref = bf16[8,2,8192]{2,1,0:T(2,128)(2,1)S(1)} collective-permute-done((bf16[8,2,8192]{2,1,0:T(2,128)(2,1)S(1)}, bf16[8,2,8192]{2,1,0:T(2,128)(2,1)S(1)}, u32[]{:S(2)}, u32[]{:S(2)}) %collective-permute-start) | collective-permute-done | bytes 262176 | tf_op jit(solution)/shard_map/ppermute | solution.py:434
  17.1 0.0 slice-done.4
  17.1 0.0 slice-done.5
  17.1 0.0 slice-done.6
  17.1 0.0 copy-start.4
  17.1 0.0 copy-start.5
  17.2 0.0 slice-start
  17.2 0.0 slice-start.2
  17.2 1.9 %project_qkv.1 = bf16[16,2,768]{2,1,0:T(2,128)(2,1)S(1)} custom-call(bf16[16,8192]{1,0:T(8,128)(2,1)S(1)} %get-tuple-element.14.lined_ref, bf16[8,2,8192]{2,1,0:T(2,128)(2,1)S(1)} %collective-permute-done.far_ref, bf16[8192,640]{1,0:T(8,128)(2,1)S(1)} %bitcast.7, bf16[2,128]{1,0:T(2,128)(2,1)S(1)} %get-tuple-element.15.adapter_ref), custom_call_target="tpu_custom_call" | custom-call | flops 10000000000 | bytes 10485760 | tf_op jit(solution)/shard_map/project_qkv/pallas_call | solution.py:273
  19.1 8.5 %all_to_all.26.mixed_ref = bf16[16,2,768]{2,1,0:T(2,128)(2,1)S(1)} all-to-all(bf16[16,2,768]{2,1,0:T(2,128)(2,1)S(1)} %project_qkv.1), channel_id=1, replica_groups={{11,10,13,12,15,14,1,0,3,2,5,4,7,6,9,8},{27,26,29,28,31,30,17,16,19,18,..., dimensions={0} | all-to-all | bytes 98304 | tf_op jit(solution)/shard_map/all_to_all | solution.py:450
  27.6 0.0 copy-done.4
  27.6 0.0 copy-done.5
  27.6 0.8 %attend.1 = (bf16[8,2,8192]{2,1,0:T(2,128)(2,1)S(1)}, s32[16,128]{1,0:T(8,128)S(1)}) custom-call(bf16[16,2,768]{2,1,0:T(2,128)(2,1)S(1)} %all_to_all.26.mixed_ref, f32[2,128]{1,0:T(2,128)S(1)} %get-tuple-element.16.cosine_ref, f32[2,128]{1,0:T(2,128)S(1)} %get-tuple-element.17.sine_ref, f32[2,256]{1,0:T(2,128)S(1)} %get-tuple-element.18.mask_ref, ...), custom_call_target="tpu_custom_call" | custom-call | flops 10000000000 | bytes 2097152 | tf_op jit(solution)/shard_map/attend/pallas_call | solution.py:546
  28.4 12.0 %all_to_all.27.gathered_ref = bf16[8,2,8192]{2,1,0:T(2,128)(2,1)S(1)} all-to-all(bf16[8,2,8192]{2,1,0:T(2,128)(2,1)S(1)} %get-tuple-element.19), channel_id=1, replica_groups={{10,12,14,0,2,4,6,8},{11,13,15,1,3,5,7,9},{26,28,30,16,18,20,22,24},{27..., dimensions={0} | all-to-all | bytes 524288 | tf_op jit(solution)/shard_map/all_to_all | solution.py:443
  40.4 2.0 %down_partials.1 = (f32[8,16,128]{2,1,0:T(8,128)}, bf16[1024,1024]{1,0:T(8,128)(2,1)S(1)}) custom-call(s32[16,128]{1,0:T(8,128)S(1)} %get-tuple-element.20.adapter_ref, bf16[8,2,8192]{2,1,0:T(2,128)(2,1)S(1)} %all_to_all.27.gathered_ref, bf16[64,64,1024]{2,1,0:T(8,128)(2,1)S(1)} %bitcast.3, bf16[64,64,1024]{2,1,0:T(8,128)(2,1)S(1)} %bitcast.5), custom_call_target="tpu_custom_call" | custom-call | flops 33554432 | bytes 4194304 | tf_op jit(solution)/shard_map/down_partials/pallas_call | solution.py:365
  42.5 5.1 %all-to-all-start.3 = ((f32[8,16,128]{2,1,0:T(8,128)}), f32[8,16,128]{2,1,0:T(8,128)S(1)}, u32[]{:S(2)}, u32[]{:S(2)}) async-start(f32[8,16,128]{2,1,0:T(8,128)} %get-tuple-element.21), calls=%async_computation.3 | async-start | bytes 131072 | tf_op jit(solution)/shard_map/all_to_all | solution.py:443
  47.5 6.2 %project_out.1.base_ref = f32[16,1024]{1,0:T(8,128)S(1)} custom-call(bf16[8,2,8192]{2,1,0:T(2,128)(2,1)S(1)} %all_to_all.27.gathered_ref, bf16[8192,1024]{1,0:T(8,128)(2,1)} %weight_ref.3), custom_call_target="tpu_custom_call" | custom-call | flops 268435456 | bytes 16777216 | tf_op jit(solution)/shard_map/project_out/pallas_call | solution.py:319
  53.8 0.0 all-to-all-done.3.partials_ref
  53.8 0.4 add_up.1
  54.2 8.3 %all_to_all.28.parts_ref = bf16[8,2,1024]{2,1,0:T(2,128)(2,1)S(1)} all-to-all(bf16[8,2,1024]{2,1,0:T(2,128)(2,1)S(1)} %add_up.1), channel_id=1, replica_groups={{10,12,14,0,2,4,6,8},{11,13,15,1,3,5,7,9},{26,28,30,16,18,20,22,24},{27..., dimensions={0} | all-to-all | bytes 65536 | tf_op jit(solution)/shard_map/all_to_all | solution.py:443
  62.5 0.7 %add_rows.1 = bf16[2,8192]{1,0:T(2,128)(2,1)} custom-call(bf16[2,8192]{1,0:T(2,128)(2,1)S(1)} %copy-done, bf16[8,2,1024]{2,1,0:T(2,128)(2,1)S(1)} %all_to_all.28.parts_ref), custom_call_target="tpu_custom_call" | custom-call | bytes 98304 | tf_op jit(solution)/shard_map/add_rows/pallas_call | solution.py:424
  (18 shorter events, 0.1 us)
Async XLA Ops:
  0.0 0.7 %copy-start.6 = (bf16[8192]{0:T(1024)(128)(2,1)S(1)}, bf16[8192]{0:T(1024)(128)(2,1)}, u32[]{:S(2)}) copy-start(bf16[8192]{0:T(1024)(128)(2,1)} %param.12) | copy-start | bytes 49156
  0.0 0.8 %copy-start = (bf16[2,8192]{1,0:T(2,128)(2,1)S(1)}, bf16[2,8192]{1,0:T(2,128)(2,1)}, u32[]{:S(2)}) copy-start(bf16[2,8192]{1,0:T(2,128)(2,1)} %hidden_ref.3) | copy-start | bytes 98308
  0.0 17.1 %slice-start.4 = ((s8[10485760]{0:T(1024)(128)(4,1)}), s8[4194304]{0:T(1024)(128)(4,1)S(1)}, s32[]{:S(2)}) async-start(s8[10485760]{0:T(1024)(128)(4,1)} %bitcast.6), calls=%async_computation.9 | async-start | bytes 8388608
  0.8 14.8 %copy-start.1 = (s32[2]{0:T(128)S(1)}, s32[2]{0:T(128)}, u32[]{:S(2)}) copy-start(s32[2]{0:T(128)} %lengths_ref.1) | copy-start | bytes 28
  0.8 14.8 %copy-start.2 = (s32[2]{0:T(128)S(1)}, s32[2]{0:T(128)}, u32[]{:S(2)}) copy-start(s32[2]{0:T(128)} %slots_ref.1) | copy-start | bytes 28
  0.8 14.8 %copy-start.3 = (s32[1,2]{1,0:T(1,128)S(1)}, s32[1,2]{1,0:T(1,128)}, u32[]{:S(2)}) copy-start(s32[1,2]{1,0:T(1,128)} %requests_ref.1) | copy-start | bytes 28
  0.8 16.3 %slice-start.5 = ((s8[10485760]{0:T(1024)(128)(4,1)}), s8[4194304]{0:T(1024)(128)(4,1)S(1)}, s32[]{:S(2)}) async-start(s8[10485760]{0:T(1024)(128)(4,1)} %bitcast.6), calls=%async_computation.10 | async-start | bytes 8388608
  0.8 16.3 %slice-start.6 = ((s8[10485760]{0:T(1024)(128)(4,1)}), s8[2097152]{0:T(1024)(128)(4,1)S(1)}, s32[]{:S(2)}) async-start(s8[10485760]{0:T(1024)(128)(4,1)} %bitcast.6), calls=%async_computation.11 | async-start | bytes 4194304
  15.6 1.5 %collective-permute-start = (bf16[8,2,8192]{2,1,0:T(2,128)(2,1)S(1)}, bf16[8,2,8192]{2,1,0:T(2,128)(2,1)S(1)}, u32[]{:S(2)}, u32[]{:S(2)}) collective-permute-start(bf16[8,2,8192]{2,1,0:T(2,128)(2,1)S(1)} %all_to_all.25.near_ref), channel_id=1, source_target_pairs={{0,1},{1,0},{2,3},{3,2},{4,5},{5,4},{6,7},{7,6},{8,9},{9,8},{10,11... | collective-permute-start | bytes 786440 | tf_op jit(solution)/shard_map/ppermute | solution.py:434
  17.1 10.5 %copy-start.4 = (bf16[2,256,1024]{2,1,0:T(8,128)(2,1)S(1)}, bf16[2,256,1024]{2,1,0:T(8,128)(2,1)}, u32[]{:S(2)}) copy-start(bf16[2,256,1024]{2,1,0:T(8,128)(2,1)} %key_ref.1) | copy-start | bytes 3145732
  17.1 10.5 %copy-start.5 = (bf16[2,256,1024]{2,1,0:T(8,128)(2,1)S(1)}, bf16[2,256,1024]{2,1,0:T(8,128)(2,1)}, u32[]{:S(2)}) copy-start(bf16[2,256,1024]{2,1,0:T(8,128)(2,1)} %value_ref.1) | copy-start | bytes 3145732
  17.2 23.2 %slice-start = ((s8[8388608]{0:T(1024)(128)(4,1)}), s8[4194304]{0:T(1024)(128)(4,1)S(1)}, s32[]{:S(2)}) async-start(s8[8388608]{0:T(1024)(128)(4,1)} %bitcast.1), calls=%async_computation.5 | async-start | bytes 8388608
  17.2 23.2 %slice-start.2 = ((s8[8388608]{0:T(1024)(128)(4,1)}), s8[4194304]{0:T(1024)(128)(4,1)S(1)}, s32[]{:S(2)}) async-start(s8[8388608]{0:T(1024)(128)(4,1)} %bitcast.4), calls=%async_computation.7 | async-start | bytes 8388608
  27.6 12.8 %slice-start.1 = ((s8[8388608]{0:T(1024)(128)(4,1)}), s8[4194304]{0:T(1024)(128)(4,1)S(1)}, s32[]{:S(2)}) async-start(s8[8388608]{0:T(1024)(128)(4,1)} %bitcast.1), calls=%async_computation.6 | async-start | bytes 8388608
  27.6 12.8 %slice-start.3 = ((s8[8388608]{0:T(1024)(128)(4,1)}), s8[4194304]{0:T(1024)(128)(4,1)S(1)}, s32[]{:S(2)}) async-start(s8[8388608]{0:T(1024)(128)(4,1)} %bitcast.4), calls=%async_computation.8 | async-start | bytes 8388608
  42.5 11.3 %all-to-all-start.3 = ((f32[8,16,128]{2,1,0:T(8,128)}), f32[8,16,128]{2,1,0:T(8,128)S(1)}, u32[]{:S(2)}, u32[]{:S(2)}) async-start(f32[8,16,128]{2,1,0:T(8,128)} %get-tuple-element.21), calls=%async_computation.3 | async-start | bytes 131072 | tf_op jit(solution)/shard_map/all_to_all | solution.py:443

commit v17 on v16

--- a/solution.py
+++ b/solution.py
@@ -146,7 +146,6 @@
 MIB = 1 << 20
 LANES = 128
 LONG = 10**10
-STREAM = 53 * MIB
 VMEM = pl.BlockSpec(memory_space=pltpu.VMEM)
 SMEM = pl.BlockSpec(memory_space=pltpu.SMEM)
 ANY = pl.BlockSpec(memory_space=pl.ANY)
@@ -281,75 +280,25 @@
     )(lined, far, weight, adapter)
 
 
-def stream(weight_ref, held_ref, sems, parts):
-    depth = held_ref.shape[0] // parts
-    copies = []
-    for k in range(parts):
-        rows = pl.ds(k * depth, depth)
-        copies.append(
-            pltpu.make_async_copy(weight_ref.at[rows], held_ref.at[rows], sems.at[k])
-        )
-        copies[-1].start()
-
-    def part(k):
-        copies[k].wait()
-        return held_ref[pl.ds(k * depth, depth)]
-
-    return part
-
-
-def project_out(gathered, weight, parts=16):
-    groups, rows, depth = gathered.shape
-    count, step = groups * rows, depth // parts
-
-    def kernel(gathered_ref, weight_ref, out_ref, near_ref, rows_ref, held_ref, sems, near_sem):
-        near = pltpu.make_async_copy(gathered_ref, near_ref, near_sem)
-        near.start()
-        part = stream(weight_ref, held_ref, sems, parts)
-        near.wait()
-        for j in range(groups):
-            rows_ref[pl.ds(j * rows, rows)] = near_ref[j]
-        total = jnp.zeros(out_ref.shape, jnp.float32)
-        for k in range(parts):
-            total = total + jnp.dot(
-                rows_ref[:, pl.ds(k * step, step)], part(k), preferred_element_type=jnp.float32
-            )
-        out_ref[...] = total
-
-    return call(
-        kernel,
-        "project_out",
-        pltpu.VMEM((count, weight.shape[1]), jnp.float32),
-        [ANY] * 2,
-        weight.size * 2,
-        limit=STREAM,
-        flops=2 * count * weight.size,
-        scratch_shapes=[
-            pltpu.VMEM(gathered.shape, gathered.dtype),
-            pltpu.VMEM((count, depth), gathered.dtype),
-            pltpu.VMEM(weight.shape, weight.dtype),
-            pltpu.SemaphoreType.DMA((parts,)),
-            pltpu.SemaphoreType.DMA,
-        ],
-    )(gathered, weight)
-
-
-def down_partials(gathered, adapter, down_store, up_store):
-    groups, rows, _ = gathered.shape
+def project_out(gathered, adapter, weight, down_store, up_store, chunk=1024):
+    groups, rows, features = gathered.shape
     count = groups * rows
     rank, depth = down_store.shape[1:]
-    width = up_store.shape[2]
-
-    def kernel(adapter_ref, gathered_ref, down_ref, up_ref, out_ref, picked_ref, held_ref, rows_ref):
-        start = pl.multiple_of(lax.axis_index("mp") * depth, depth)
+    columns = weight.shape[1]
+
+    def kernel(
+        adapter_ref, gathered_ref, weight_ref, down_ref, up_ref, partial_ref, base_ref, picked_ref,
+        rows_ref, held_ref,
+    ):
         for j in range(groups):
-            rows_ref[pl.ds(j * rows, rows)] = gathered_ref[j, :, pl.ds(start, depth)]
+            rows_ref[pl.ds(j * rows, rows)] = gathered_ref[j]
         for r in range(count):
             chosen = adapter_ref[r, 0]
             held_ref[pl.ds(r * rank, rank)] = down_ref[chosen]
             picked_ref[pl.ds(r * rank, rank)] = up_ref[chosen]
+        start = pl.multiple_of(lax.axis_index("mp") * depth, depth)
         every = lax.dot_general(
-            rows_ref[...],
+            rows_ref[:, pl.ds(start, depth)],
             held_ref[...],
             (((1,), (1,)), ((), ())),
             preferred_element_type=jnp.float32,
@@ -360,24 +309,32 @@
         for s in range(0, count * rank, LANES):
             total = total + jnp.where(row == (lane + s) // rank, every[:, s : s + LANES], 0.0)
         for c in range(groups):
-            out_ref[c] = total
-
-    return call(
-        kernel,
-        "down_partials",
+            partial_ref[c] = total
+        total = jnp.zeros((count, columns), jnp.float32)
+        for k in range(features // chunk):
+            part = pl.ds(k * chunk, chunk)
+            total = total + jnp.dot(
+                rows_ref[:, part], weight_ref[part, :], preferred_element_type=jnp.float32
+            )
+        base_ref[...] = total
+
+    return call(
+        kernel,
+        "project_out",
         (
             jax.ShapeDtypeStruct((groups, count, LANES), jnp.float32),
-            pltpu.VMEM((count * rank, width), up_store.dtype),
+            jax.ShapeDtypeStruct((count, columns), jnp.float32),
+            pltpu.VMEM((count * rank, columns), up_store.dtype),
         ),
-        [SMEM] + [VMEM] * 3,
-        2 * count * rank * (depth + width),
+        [SMEM] + [VMEM] * 4,
+        weight.size * 2,
         limit=5 * MIB,
-        flops=2 * count * count * rank * depth,
+        flops=LONG,
         scratch_shapes=[
+            pltpu.VMEM((count, features), gathered.dtype),
             pltpu.VMEM((count * rank, depth), down_store.dtype),
-            pltpu.VMEM((count, depth), gathered.dtype),
         ],
-    )(adapter, gathered, down_store, up_store)
+    )(adapter, gathered, weight, down_store, up_store)
 
 
 def add_up(base, partials, up):
@@ -435,7 +392,7 @@
 
 
 def order(size):
-    return [(k + size // 2 + 1) % size for k in range(size)]
+    return [(k + size - 1) % size for k in range(size)]
 
 
 def exchange(blocks):
@@ -585,11 +542,14 @@
     context, adapter = attend(mixed, cosine, sine, mask, key_cache, value_cache, mp_size)
     gathered = exchange(context)
 
-    partials, up = down_partials(
-        gathered, adapter, adapter_down_matrices.swapaxes(1, 2), adapter_up_matrices
-    )
-    partials = exchange(partials)
-    projected = add_up(project_out(gathered, output_weight), partials, up)
+    partials, base, up = project_out(
+        gathered,
+        adapter,
+        output_weight,
+        adapter_down_matrices.swapaxes(1, 2),
+        adapter_up_matrices,
+    )
+    projected = add_up(base, exchange(partials), up)
     return add_rows(hidden, exchange(projected))
 
 

time: 63.6 us -> 66 us (1.038)
  blocking collectives: 43.4 us -> 55.4 us
  starting transfers between devices: 5.1 us -> 0.01 us
  Pallas kernels: 12.9 us -> 8.29 us
    all_to_all x3 -> x4, blocking collectives: 34.9 us -> 47.1 us  [exchange(): lax.all_to_all(blocks, 'mp', split_axis=0, concat_axis=0, tiled=True, axi...]
    all_to_all x1 -> x0, starting transfers between devices: 5.1 us -> none  [exchange(): lax.all_to_all(blocks, 'mp', split_axis=0, concat_axis=0, tiled=True, axi...]
    pallas_call x2 -> x1, Pallas kernels: 8.22 us -> 3.63 us  [project_out(): call(kernel, 'project_out', (jax.ShapeDtypeStruct((groups, count, LANES),...]
  transfers between devices with their start and end apart: 2 -> 1, of which waited for: 1 -> 1; matrix products, arithmetic and copies ran while one was open for 0% -> 0% of each run, Pallas kernels for 11% -> 1%
where the time goes in v17:
time: 66 us; the launch traced here: 65.6 us
  blocking collectives  55.4 us (84%)
  Pallas kernels  8.29 us (13%)
  local copies, waits for them, and re-layouts  0.84 us (1%)
  waiting for transfers between devices  0.79 us (1%)
    all_to_all x4, blocking collectives, exchange(): lax.all_to_all(blocks, 'mp', split_axis=0, concat_axis=0, tiled=True, axi...  47.1 us
    all_to_all x1, blocking collectives, exchange_all(): lax.all_to_all(blocks, ('mp', 'batch'), split_axis=0, concat_axis=0, tile...  8.32 us
    pallas_call x1, Pallas kernels, project_out(): call(kernel, 'project_out', (jax.ShapeDtypeStruct((groups, count, LANES),...  3.63 us
    pallas_call x1, Pallas kernels, project_qkv(): call(kernel, 'project_qkv', jax.ShapeDtypeStruct((2 * groups, rows, width...  1.92 us
  transfers between devices with their start and end apart: 1, of which 1 were waited for; matrix products, arithmetic and copies ran while one was open for 0% of the time, Pallas kernels for 1%

profile of v17, /device:TPU:0, one launch (start us, length us, event | category | flops | bytes accessed | tf_op | source)
XLA Modules:
  0.0 65.6 jit_solution(13199443317500303195)
XLA Ops:
  0.0 0.7 %copy-done.6 = bf16[8192]{0:T(1024)(128)(2,1)S(1)} copy-done((bf16[8192]{0:T(1024)(128)(2,1)S(1)}, bf16[8192]{0:T(1024)(128)(2,1)}, u32[]{:S(2)}) %copy-start.6) | copy-done | bytes 16408
  0.7 0.0 copy-done
  0.8 0.0 slice-start.5
  0.8 0.0 slice-start.6
  0.8 0.2 norm_rows.1
  1.0 15.6 %all_to_all.25.near_ref = bf16[8,2,8192]{2,1,0:T(2,128)(2,1)S(1)} all-to-all(bf16[8,2,8192]{2,1,0:T(2,128)(2,1)S(1)} %norm_rows.1), channel_id=1, replica_groups={{14,0,2,4,6,8,10,12},{15,1,3,5,7,9,11,13},{30,16,18,20,22,24,26,28},{31..., dimensions={0} | all-to-all | bytes 524288 | tf_op jit(solution)/shard_map/all_to_all | solution.py:400
  16.6 0.0 collective-permute-start
  16.6 0.0 copy-done.1
  16.6 0.0 copy-done.2
  16.6 0.0 copy-done.3
  16.6 0.7 %turns.1 = (bf16[16,8192]{1,0:T(8,128)(2,1)S(1)}, f32[2,128]{1,0:T(2,128)S(1)}, f32[2,128]{1,0:T(2,128)S(1)}, f32[2,256]{1,0:T(2,128)S(1)}, bf16[2,128]{1,0:T(2,128)(2,1)S(1)}) custom-call(s32[2]{0:T(128)S(1)} %copy-done.1, s32[2]{0:T(128)S(1)} %copy-done.2, s32[1,2]{1,0:T(1,128)S(1)} %copy-done.3, bf16[8,2,8192]{2,1,0:T(2,128)(2,1)S(1)} %all_to_all.25.near_ref, ...), custom_call_target="tpu_custom_call" | custom-call | bytes 524288 | tf_op jit(solution)/shard_map/turns/pallas_call | solution.py:228
  17.3 0.8 %collective-permute-done.far_ref = bf16[8,2,8192]{2,1,0:T(2,128)(2,1)S(1)} collective-permute-done((bf16[8,2,8192]{2,1,0:T(2,128)(2,1)S(1)}, bf16[8,2,8192]{2,1,0:T(2,128)(2,1)S(1)}, u32[]{:S(2)}, u32[]{:S(2)}) %collective-permute-start) | collective-permute-done | bytes 262176 | tf_op jit(solution)/shard_map/ppermute | solution.py:391
  18.1 0.0 slice-done.4
  18.1 0.0 slice-done.5
  18.1 0.0 copy-start.4
  18.1 0.0 copy-start.5
  18.2 0.0 slice-start
  18.2 0.0 slice-start.1
  18.2 0.0 slice-start.7
  18.2 0.0 slice-start.9
  18.2 1.9 %project_qkv.1 = bf16[16,2,768]{2,1,0:T(2,128)(2,1)S(1)} custom-call(bf16[16,8192]{1,0:T(8,128)(2,1)S(1)} %get-tuple-element.15.lined_ref, bf16[8,2,8192]{2,1,0:T(2,128)(2,1)S(1)} %collective-permute-done.far_ref, bf16[8192,640]{1,0:T(8,128)(2,1)S(1)} %bitcast.4, bf16[2,128]{1,0:T(2,128)(2,1)S(1)} %get-tuple-element.16.adapter_ref), custom_call_target="tpu_custom_call" | custom-call | flops 10000000000 | bytes 10485760 | tf_op jit(solution)/shard_map/project_qkv/pallas_call | solution.py:272
  20.1 8.3 %all_to_all.26.mixed_ref = bf16[16,2,768]{2,1,0:T(2,128)(2,1)S(1)} all-to-all(bf16[16,2,768]{2,1,0:T(2,128)(2,1)S(1)} %project_qkv.1), channel_id=1, replica_groups={{15,14,1,0,3,2,5,4,7,6,9,8,11,10,13,12},{31,30,17,16,19,18,21,20,23,22,..., dimensions={0} | all-to-all | bytes 98304 | tf_op jit(solution)/shard_map/all_to_all | solution.py:407
  28.5 0.0 slice-start.8
  28.5 0.0 slice-start.10
  28.5 0.8 %attend.1 = (bf16[8,2,8192]{2,1,0:T(2,128)(2,1)S(1)}, s32[16,128]{1,0:T(8,128)S(1)}) custom-call(bf16[16,2,768]{2,1,0:T(2,128)(2,1)S(1)} %all_to_all.26.mixed_ref, f32[2,128]{1,0:T(2,128)S(1)} %get-tuple-element.17.cosine_ref, f32[2,128]{1,0:T(2,128)S(1)} %get-tuple-element.18.sine_ref, f32[2,256]{1,0:T(2,128)S(1)} %get-tuple-element.19.mask_ref, ...), custom_call_target="tpu_custom_call" | custom-call | flops 10000000000 | bytes 2097152 | tf_op jit(solution)/shard_map/attend/pallas_call | solution.py:503
  29.3 14.2 %all_to_all.27.gathered_ref = bf16[8,2,8192]{2,1,0:T(2,128)(2,1)S(1)} all-to-all(bf16[8,2,8192]{2,1,0:T(2,128)(2,1)S(1)} %get-tuple-element.21), channel_id=1, replica_groups={{14,0,2,4,6,8,10,12},{15,1,3,5,7,9,11,13},{30,16,18,20,22,24,26,28},{31..., dimensions={0} | all-to-all | bytes 524288 | tf_op jit(solution)/shard_map/all_to_all | solution.py:400
  43.4 0.0 slice-done.1
  43.5 3.6 %project_out.1 = (f32[8,16,128]{2,1,0:T(8,128)S(1)}, f32[16,1024]{1,0:T(8,128)S(1)}, bf16[1024,1024]{1,0:T(8,128)(2,1)S(1)}) custom-call(s32[16,128]{1,0:T(8,128)S(1)} %get-tuple-element.20.adapter_ref, bf16[8,2,8192]{2,1,0:T(2,128)(2,1)S(1)} %all_to_all.27.gathered_ref, bf16[8192,1024]{1,0:T(8,128)(2,1)S(1)} %bitcast.2, bf16[64,64,1024]{2,1,0:T(8,128)(2,1)S(1)} %bitcast.7, ...), custom_call_target="tpu_custom_call" | custom-call | flops 10000000000 | bytes 16777216 | tf_op jit(solution)/shard_map/project_out/pallas_call | solution.py:321
  47.2 8.8 %all_to_all.28.partials_ref = f32[8,16,128]{2,1,0:T(8,128)S(1)} all-to-all(f32[8,16,128]{2,1,0:T(8,128)S(1)} %get-tuple-element.23), channel_id=1, replica_groups={{14,0,2,4,6,8,10,12},{15,1,3,5,7,9,11,13},{30,16,18,20,22,24,26,28},{31..., dimensions={0} | all-to-all | bytes 131072 | tf_op jit(solution)/shard_map/all_to_all | solution.py:400
  56.0 0.4 add_up.1
  56.4 8.6 %all_to_all.29.parts_ref = bf16[8,2,1024]{2,1,0:T(2,128)(2,1)S(1)} all-to-all(bf16[8,2,1024]{2,1,0:T(2,128)(2,1)S(1)} %add_up.1), channel_id=1, replica_groups={{14,0,2,4,6,8,10,12},{15,1,3,5,7,9,11,13},{30,16,18,20,22,24,26,28},{31..., dimensions={0} | all-to-all | bytes 65536 | tf_op jit(solution)/shard_map/all_to_all | solution.py:400
  64.9 0.7 add_rows.1
  (25 shorter events, 0.1 us)
Async XLA Ops:
  0.0 0.7 %copy-start.6 = (bf16[8192]{0:T(1024)(128)(2,1)S(1)}, bf16[8192]{0:T(1024)(128)(2,1)}, u32[]{:S(2)}) copy-start(bf16[8192]{0:T(1024)(128)(2,1)} %param.12) | copy-start | bytes 49156
  0.0 0.8 %copy-start = (bf16[2,8192]{1,0:T(2,128)(2,1)S(1)}, bf16[2,8192]{1,0:T(2,128)(2,1)}, u32[]{:S(2)}) copy-start(bf16[2,8192]{1,0:T(2,128)(2,1)} %hidden_ref.3) | copy-start | bytes 98308
  0.0 18.1 %slice-start.4 = ((s8[10485760]{0:T(1024)(128)(4,1)}), s8[4194304]{0:T(1024)(128)(4,1)S(1)}, s32[]{:S(2)}) async-start(s8[10485760]{0:T(1024)(128)(4,1)} %bitcast.3), calls=%async_computation.9 | async-start | bytes 8388608
  0.8 15.8 %copy-start.1 = (s32[2]{0:T(128)S(1)}, s32[2]{0:T(128)}, u32[]{:S(2)}) copy-start(s32[2]{0:T(128)} %lengths_ref.1) | copy-start | bytes 28
  0.8 15.8 %copy-start.2 = (s32[2]{0:T(128)S(1)}, s32[2]{0:T(128)}, u32[]{:S(2)}) copy-start(s32[2]{0:T(128)} %slots_ref.1) | copy-start | bytes 28
  0.8 15.8 %copy-start.3 = (s32[1,2]{1,0:T(1,128)S(1)}, s32[1,2]{1,0:T(1,128)}, u32[]{:S(2)}) copy-start(s32[1,2]{1,0:T(1,128)} %requests_ref.1) | copy-start | bytes 28
  0.8 17.3 %slice-start.5 = ((s8[10485760]{0:T(1024)(128)(4,1)}), s8[4194304]{0:T(1024)(128)(4,1)S(1)}, s32[]{:S(2)}) async-start(s8[10485760]{0:T(1024)(128)(4,1)} %bitcast.3), calls=%async_computation.10 | async-start | bytes 8388608
  0.8 17.3 %slice-start.6 = ((s8[10485760]{0:T(1024)(128)(4,1)}), s8[2097152]{0:T(1024)(128)(4,1)S(1)}, s32[]{:S(2)}) async-start(s8[10485760]{0:T(1024)(128)(4,1)} %bitcast.3), calls=%async_computation.11 | async-start | bytes 4194304
  16.6 1.5 %collective-permute-start = (bf16[8,2,8192]{2,1,0:T(2,128)(2,1)S(1)}, bf16[8,2,8192]{2,1,0:T(2,128)(2,1)S(1)}, u32[]{:S(2)}, u32[]{:S(2)}) collective-permute-start(bf16[8,2,8192]{2,1,0:T(2,128)(2,1)S(1)} %all_to_all.25.near_ref), channel_id=1, source_target_pairs={{0,1},{1,0},{2,3},{3,2},{4,5},{5,4},{6,7},{7,6},{8,9},{9,8},{10,11... | collective-permute-start | bytes 786440 | tf_op jit(solution)/shard_map/ppermute | solution.py:391
  18.1 10.3 %copy-start.4 = (bf16[2,256,1024]{2,1,0:T(8,128)(2,1)S(1)}, bf16[2,256,1024]{2,1,0:T(8,128)(2,1)}, u32[]{:S(2)}) copy-start(bf16[2,256,1024]{2,1,0:T(8,128)(2,1)} %key_ref.1) | copy-start | bytes 3145732
  18.1 10.3 %copy-start.5 = (bf16[2,256,1024]{2,1,0:T(8,128)(2,1)S(1)}, bf16[2,256,1024]{2,1,0:T(8,128)(2,1)}, u32[]{:S(2)}) copy-start(bf16[2,256,1024]{2,1,0:T(8,128)(2,1)} %value_ref.1) | copy-start | bytes 3145732
  18.2 25.3 %slice-start = ((s8[16777216]{0:T(1024)(128)(4,1)}), s8[4194304]{0:T(1024)(128)(4,1)S(1)}, s32[]{:S(2)}) async-start(s8[16777216]{0:T(1024)(128)(4,1)} %bitcast.1), calls=%async_computation.5 | async-start | bytes 8388608
  18.2 25.3 %slice-start.1 = ((s8[16777216]{0:T(1024)(128)(4,1)}), s8[4194304]{0:T(1024)(128)(4,1)S(1)}, s32[]{:S(2)}) async-start(s8[16777216]{0:T(1024)(128)(4,1)} %bitcast.1), calls=%async_computation.6 | async-start | bytes 8388608
  18.2 25.3 %slice-start.7 = ((s8[8388608]{0:T(1024)(128)(4,1)}), s8[4194304]{0:T(1024)(128)(4,1)S(1)}, s32[]{:S(2)}) async-start(s8[8388608]{0:T(1024)(128)(4,1)} %bitcast.5), calls=%async_computation.12 | async-start | bytes 8388608
  18.2 25.3 %slice-start.9 = ((s8[8388608]{0:T(1024)(128)(4,1)}), s8[4194304]{0:T(1024)(128)(4,1)S(1)}, s32[]{:S(2)}) async-start(s8[8388608]{0:T(1024)(128)(4,1)} %bitcast.8), calls=%async_computation.14 | async-start | bytes 8388608
  28.5 15.0 %slice-start.2 = ((s8[16777216]{0:T(1024)(128)(4,1)}), s8[4194304]{0:T(1024)(128)(4,1)S(1)}, s32[]{:S(2)}) async-start(s8[16777216]{0:T(1024)(128)(4,1)} %bitcast.1), calls=%async_computation.7 | async-start | bytes 8388608
  28.5 15.0 %slice-start.3 = ((s8[16777216]{0:T(1024)(128)(4,1)}), s8[4194304]{0:T(1024)(128)(4,1)S(1)}, s32[]{:S(2)}) async-start(s8[16777216]{0:T(1024)(128)(4,1)} %bitcast.1), calls=%async_computation.8 | async-start | bytes 8388608
  28.5 15.0 %slice-start.8 = ((s8[8388608]{0:T(1024)(128)(4,1)}), s8[4194304]{0:T(1024)(128)(4,1)S(1)}, s32[]{:S(2)}) async-start(s8[8388608]{0:T(1024)(128)(4,1)} %bitcast.5), calls=%async_computation.13 | async-start | bytes 8388608
  28.5 15.0 %slice-start.10 = ((s8[8388608]{0:T(1024)(128)(4,1)}), s8[4194304]{0:T(1024)(128)(4,1)S(1)}, s32[]{:S(2)}) async-start(s8[8388608]{0:T(1024)(128)(4,1)} %bitcast.8), calls=%async_computation.15 | async-start | bytes 8388608

commit v18 on v17

--- a/solution.py
+++ b/solution.py
@@ -392,7 +392,7 @@
 
 
 def order(size):
-    return [(k + size - 1) % size for k in range(size)]
+    return [(k + size // 2 + 1) % size for k in range(size)]
 
 
 def exchange(blocks):

time: 66 us -> 62.6 us (0.948)
  blocking collectives: 55.4 us -> 52.1 us
    all_to_all x4, blocking collectives: 47.1 us -> 43.5 us  [exchange(): lax.all_to_all(blocks, 'mp', split_axis=0, concat_axis=0, tiled=True, axi...]
where the time goes in v18:
time: 62.6 us; the launch traced here: 62.2 us
  blocking collectives  52.1 us (83%)
  Pallas kernels  8.3 us (13%)
  local copies, waits for them, and re-layouts  0.84 us (1%)
  waiting for transfers between devices  0.79 us (1%)
    all_to_all x4, blocking collectives, exchange(): lax.all_to_all(blocks, 'mp', split_axis=0, concat_axis=0, tiled=True, axi...  43.5 us
    all_to_all x1, blocking collectives, exchange_all(): lax.all_to_all(blocks, ('mp', 'batch'), split_axis=0, concat_axis=0, tile...  8.52 us
    pallas_call x1, Pallas kernels, project_out(): call(kernel, 'project_out', (jax.ShapeDtypeStruct((groups, count, LANES),...  3.63 us
    pallas_call x1, Pallas kernels, project_qkv(): call(kernel, 'project_qkv', jax.ShapeDtypeStruct((2 * groups, rows, width...  1.92 us
  transfers between devices with their start and end apart: 1, of which 1 were waited for; matrix products, arithmetic and copies ran while one was open for 0% of the time, Pallas kernels for 1%

profile of v18, /device:TPU:0, one launch (start us, length us, event | category | flops | bytes accessed | tf_op | source)
XLA Modules:
  0.0 62.2 jit_solution(9043068958071164683)
XLA Ops:
  0.0 0.7 %copy-done.6 = bf16[8192]{0:T(1024)(128)(2,1)S(1)} copy-done((bf16[8192]{0:T(1024)(128)(2,1)S(1)}, bf16[8192]{0:T(1024)(128)(2,1)}, u32[]{:S(2)}) %copy-start.6) | copy-done | bytes 16408
  0.7 0.0 copy-done
  0.8 0.0 slice-start.5
  0.8 0.0 slice-start.6
  0.8 0.2 norm_rows.1
  1.0 14.6 %all_to_all.25.near_ref = bf16[8,2,8192]{2,1,0:T(2,128)(2,1)S(1)} all-to-all(bf16[8,2,8192]{2,1,0:T(2,128)(2,1)S(1)} %norm_rows.1), channel_id=1, replica_groups={{10,12,14,0,2,4,6,8},{11,13,15,1,3,5,7,9},{26,28,30,16,18,20,22,24},{27..., dimensions={0} | all-to-all | bytes 524288 | tf_op jit(solution)/shard_map/all_to_all | solution.py:400
  15.6 0.0 collective-permute-start
  15.6 0.0 copy-done.1
  15.6 0.0 copy-done.2
  15.6 0.0 copy-done.3
  15.6 0.7 %turns.1 = (bf16[16,8192]{1,0:T(8,128)(2,1)S(1)}, f32[2,128]{1,0:T(2,128)S(1)}, f32[2,128]{1,0:T(2,128)S(1)}, f32[2,256]{1,0:T(2,128)S(1)}, bf16[2,128]{1,0:T(2,128)(2,1)S(1)}) custom-call(s32[2]{0:T(128)S(1)} %copy-done.1, s32[2]{0:T(128)S(1)} %copy-done.2, s32[1,2]{1,0:T(1,128)S(1)} %copy-done.3, bf16[8,2,8192]{2,1,0:T(2,128)(2,1)S(1)} %all_to_all.25.near_ref, ...), custom_call_target="tpu_custom_call" | custom-call | bytes 524288 | tf_op jit(solution)/shard_map/turns/pallas_call | solution.py:228
  16.3 0.8 %collective-permute-done.far_ref = bf16[8,2,8192]{2,1,0:T(2,128)(2,1)S(1)} collective-permute-done((bf16[8,2,8192]{2,1,0:T(2,128)(2,1)S(1)}, bf16[8,2,8192]{2,1,0:T(2,128)(2,1)S(1)}, u32[]{:S(2)}, u32[]{:S(2)}) %collective-permute-start) | collective-permute-done | bytes 262176 | tf_op jit(solution)/shard_map/ppermute | solution.py:391
  17.1 0.0 slice-done.4
  17.1 0.0 copy-start.4
  17.1 0.0 copy-start.5
  17.2 0.0 slice-start
  17.2 0.0 slice-start.1
  17.2 0.0 slice-start.7
  17.2 0.0 slice-start.9
  17.2 1.9 %project_qkv.1 = bf16[16,2,768]{2,1,0:T(2,128)(2,1)S(1)} custom-call(bf16[16,8192]{1,0:T(8,128)(2,1)S(1)} %get-tuple-element.15.lined_ref, bf16[8,2,8192]{2,1,0:T(2,128)(2,1)S(1)} %collective-permute-done.far_ref, bf16[8192,640]{1,0:T(8,128)(2,1)S(1)} %bitcast.4, bf16[2,128]{1,0:T(2,128)(2,1)S(1)} %get-tuple-element.16.adapter_ref), custom_call_target="tpu_custom_call" | custom-call | flops 10000000000 | bytes 10485760 | tf_op jit(solution)/shard_map/project_qkv/pallas_call | solution.py:272
  19.1 8.5 %all_to_all.26.mixed_ref = bf16[16,2,768]{2,1,0:T(2,128)(2,1)S(1)} all-to-all(bf16[16,2,768]{2,1,0:T(2,128)(2,1)S(1)} %project_qkv.1), channel_id=1, replica_groups={{11,10,13,12,15,14,1,0,3,2,5,4,7,6,9,8},{27,26,29,28,31,30,17,16,19,18,..., dimensions={0} | all-to-all | bytes 98304 | tf_op jit(solution)/shard_map/all_to_all | solution.py:407
  27.7 0.0 copy-done.4
  27.7 0.0 slice-start.8
  27.7 0.0 slice-start.10
  27.7 0.8 %attend.1 = (bf16[8,2,8192]{2,1,0:T(2,128)(2,1)S(1)}, s32[16,128]{1,0:T(8,128)S(1)}) custom-call(bf16[16,2,768]{2,1,0:T(2,128)(2,1)S(1)} %all_to_all.26.mixed_ref, f32[2,128]{1,0:T(2,128)S(1)} %get-tuple-element.17.cosine_ref, f32[2,128]{1,0:T(2,128)S(1)} %get-tuple-element.18.sine_ref, f32[2,256]{1,0:T(2,128)S(1)} %get-tuple-element.19.mask_ref, ...), custom_call_target="tpu_custom_call" | custom-call | flops 10000000000 | bytes 2097152 | tf_op jit(solution)/shard_map/attend/pallas_call | solution.py:503
  28.5 12.1 %all_to_all.27.gathered_ref = bf16[8,2,8192]{2,1,0:T(2,128)(2,1)S(1)} all-to-all(bf16[8,2,8192]{2,1,0:T(2,128)(2,1)S(1)} %get-tuple-element.21), channel_id=1, replica_groups={{10,12,14,0,2,4,6,8},{11,13,15,1,3,5,7,9},{26,28,30,16,18,20,22,24},{27..., dimensions={0} | all-to-all | bytes 524288 | tf_op jit(solution)/shard_map/all_to_all | solution.py:400
  40.6 0.0 slice-done
  40.7 3.6 %project_out.1 = (f32[8,16,128]{2,1,0:T(8,128)S(1)}, f32[16,1024]{1,0:T(8,128)S(1)}, bf16[1024,1024]{1,0:T(8,128)(2,1)S(1)}) custom-call(s32[16,128]{1,0:T(8,128)S(1)} %get-tuple-element.20.adapter_ref, bf16[8,2,8192]{2,1,0:T(2,128)(2,1)S(1)} %all_to_all.27.gathered_ref, bf16[8192,1024]{1,0:T(8,128)(2,1)S(1)} %bitcast.2, bf16[64,64,1024]{2,1,0:T(8,128)(2,1)S(1)} %bitcast.7, ...), custom_call_target="tpu_custom_call" | custom-call | flops 10000000000 | bytes 16777216 | tf_op jit(solution)/shard_map/project_out/pallas_call | solution.py:321
  44.3 8.5 %all_to_all.28.partials_ref = f32[8,16,128]{2,1,0:T(8,128)S(1)} all-to-all(f32[8,16,128]{2,1,0:T(8,128)S(1)} %get-tuple-element.23), channel_id=1, replica_groups={{10,12,14,0,2,4,6,8},{11,13,15,1,3,5,7,9},{26,28,30,16,18,20,22,24},{27..., dimensions={0} | all-to-all | bytes 131072 | tf_op jit(solution)/shard_map/all_to_all | solution.py:400
  52.8 0.4 add_up.1
  53.2 8.3 %all_to_all.29.parts_ref = bf16[8,2,1024]{2,1,0:T(2,128)(2,1)S(1)} all-to-all(bf16[8,2,1024]{2,1,0:T(2,128)(2,1)S(1)} %add_up.1), channel_id=1, replica_groups={{10,12,14,0,2,4,6,8},{11,13,15,1,3,5,7,9},{26,28,30,16,18,20,22,24},{27..., dimensions={0} | all-to-all | bytes 65536 | tf_op jit(solution)/shard_map/all_to_all | solution.py:400
  61.6 0.7 %add_rows.1 = bf16[2,8192]{1,0:T(2,128)(2,1)} custom-call(bf16[2,8192]{1,0:T(2,128)(2,1)S(1)} %copy-done, bf16[8,2,1024]{2,1,0:T(2,128)(2,1)S(1)} %all_to_all.29.parts_ref), custom_call_target="tpu_custom_call" | custom-call | bytes 98304 | tf_op jit(solution)/shard_map/add_rows/pallas_call | solution.py:381
  (25 shorter events, 0.1 us)
Async XLA Ops:
  0.0 0.7 %copy-start.6 = (bf16[8192]{0:T(1024)(128)(2,1)S(1)}, bf16[8192]{0:T(1024)(128)(2,1)}, u32[]{:S(2)}) copy-start(bf16[8192]{0:T(1024)(128)(2,1)} %param.12) | copy-start | bytes 49156
  0.0 0.8 %copy-start = (bf16[2,8192]{1,0:T(2,128)(2,1)S(1)}, bf16[2,8192]{1,0:T(2,128)(2,1)}, u32[]{:S(2)}) copy-start(bf16[2,8192]{1,0:T(2,128)(2,1)} %hidden_ref.3) | copy-start | bytes 98308
  0.0 17.1 %slice-start.4 = ((s8[10485760]{0:T(1024)(128)(4,1)}), s8[4194304]{0:T(1024)(128)(4,1)S(1)}, s32[]{:S(2)}) async-start(s8[10485760]{0:T(1024)(128)(4,1)} %bitcast.3), calls=%async_computation.9 | async-start | bytes 8388608
  0.8 14.8 %copy-start.1 = (s32[2]{0:T(128)S(1)}, s32[2]{0:T(128)}, u32[]{:S(2)}) copy-start(s32[2]{0:T(128)} %lengths_ref.1) | copy-start | bytes 28
  0.8 14.8 %copy-start.2 = (s32[2]{0:T(128)S(1)}, s32[2]{0:T(128)}, u32[]{:S(2)}) copy-start(s32[2]{0:T(128)} %slots_ref.1) | copy-start | bytes 28
  0.8 14.8 %copy-start.3 = (s32[1,2]{1,0:T(1,128)S(1)}, s32[1,2]{1,0:T(1,128)}, u32[]{:S(2)}) copy-start(s32[1,2]{1,0:T(1,128)} %requests_ref.1) | copy-start | bytes 28
  0.8 16.3 %slice-start.5 = ((s8[10485760]{0:T(1024)(128)(4,1)}), s8[4194304]{0:T(1024)(128)(4,1)S(1)}, s32[]{:S(2)}) async-start(s8[10485760]{0:T(1024)(128)(4,1)} %bitcast.3), calls=%async_computation.10 | async-start | bytes 8388608
  0.8 16.3 %slice-start.6 = ((s8[10485760]{0:T(1024)(128)(4,1)}), s8[2097152]{0:T(1024)(128)(4,1)S(1)}, s32[]{:S(2)}) async-start(s8[10485760]{0:T(1024)(128)(4,1)} %bitcast.3), calls=%async_computation.11 | async-start | bytes 4194304
  15.6 1.5 %collective-permute-start = (bf16[8,2,8192]{2,1,0:T(2,128)(2,1)S(1)}, bf16[8,2,8192]{2,1,0:T(2,128)(2,1)S(1)}, u32[]{:S(2)}, u32[]{:S(2)}) collective-permute-start(bf16[8,2,8192]{2,1,0:T(2,128)(2,1)S(1)} %all_to_all.25.near_ref), channel_id=1, source_target_pairs={{0,1},{1,0},{2,3},{3,2},{4,5},{5,4},{6,7},{7,6},{8,9},{9,8},{10,11... | collective-permute-start | bytes 786440 | tf_op jit(solution)/shard_map/ppermute | solution.py:391
  17.1 10.5 %copy-start.4 = (bf16[2,256,1024]{2,1,0:T(8,128)(2,1)S(1)}, bf16[2,256,1024]{2,1,0:T(8,128)(2,1)}, u32[]{:S(2)}) copy-start(bf16[2,256,1024]{2,1,0:T(8,128)(2,1)} %key_ref.1) | copy-start | bytes 3145732
  17.1 10.5 %copy-start.5 = (bf16[2,256,1024]{2,1,0:T(8,128)(2,1)S(1)}, bf16[2,256,1024]{2,1,0:T(8,128)(2,1)}, u32[]{:S(2)}) copy-start(bf16[2,256,1024]{2,1,0:T(8,128)(2,1)} %value_ref.1) | copy-start | bytes 3145732
  17.2 23.4 %slice-start = ((s8[16777216]{0:T(1024)(128)(4,1)}), s8[4194304]{0:T(1024)(128)(4,1)S(1)}, s32[]{:S(2)}) async-start(s8[16777216]{0:T(1024)(128)(4,1)} %bitcast.1), calls=%async_computation.5 | async-start | bytes 8388608
  17.2 23.4 %slice-start.1 = ((s8[16777216]{0:T(1024)(128)(4,1)}), s8[4194304]{0:T(1024)(128)(4,1)S(1)}, s32[]{:S(2)}) async-start(s8[16777216]{0:T(1024)(128)(4,1)} %bitcast.1), calls=%async_computation.6 | async-start | bytes 8388608
  17.2 23.4 %slice-start.7 = ((s8[8388608]{0:T(1024)(128)(4,1)}), s8[4194304]{0:T(1024)(128)(4,1)S(1)}, s32[]{:S(2)}) async-start(s8[8388608]{0:T(1024)(128)(4,1)} %bitcast.5), calls=%async_computation.12 | async-start | bytes 8388608
  17.2 23.4 %slice-start.9 = ((s8[8388608]{0:T(1024)(128)(4,1)}), s8[4194304]{0:T(1024)(128)(4,1)S(1)}, s32[]{:S(2)}) async-start(s8[8388608]{0:T(1024)(128)(4,1)} %bitcast.8), calls=%async_computation.14 | async-start | bytes 8388608
  27.7 12.9 %slice-start.2 = ((s8[16777216]{0:T(1024)(128)(4,1)}), s8[4194304]{0:T(1024)(128)(4,1)S(1)}, s32[]{:S(2)}) async-start(s8[16777216]{0:T(1024)(128)(4,1)} %bitcast.1), calls=%async_computation.7 | async-start | bytes 8388608
  27.7 13.0 %slice-start.3 = ((s8[16777216]{0:T(1024)(128)(4,1)}), s8[4194304]{0:T(1024)(128)(4,1)S(1)}, s32[]{:S(2)}) async-start(s8[16777216]{0:T(1024)(128)(4,1)} %bitcast.1), calls=%async_computation.8 | async-start | bytes 8388608
  27.7 13.0 %slice-start.8 = ((s8[8388608]{0:T(1024)(128)(4,1)}), s8[4194304]{0:T(1024)(128)(4,1)S(1)}, s32[]{:S(2)}) async-start(s8[8388608]{0:T(1024)(128)(4,1)} %bitcast.5), calls=%async_computation.13 | async-start | bytes 8388608
  27.7 13.0 %slice-start.10 = ((s8[8388608]{0:T(1024)(128)(4,1)}), s8[4194304]{0:T(1024)(128)(4,1)S(1)}, s32[]{:S(2)}) async-start(s8[8388608]{0:T(1024)(128)(4,1)} %bitcast.8), calls=%async_computation.15 | async-start | bytes 8388608

commit v19 on v18

--- a/solution.py
+++ b/solution.py
@@ -392,7 +392,8 @@
 
 
 def order(size):
-    return [(k + size // 2 + 1) % size for k in range(size)]
+    half = size // 2
+    return [(k + 1) % half + start for k in range(half) for start in (half, 0)]
 
 
 def exchange(blocks):

time: 62.6 us -> 62.3 us (level)
  no operation moved by 1% of the time
where the time goes in v19:
time: 62.3 us; the launch traced here: 61.9 us
  blocking collectives  51.8 us (83%)
  Pallas kernels  8.29 us (13%)
  local copies, waits for them, and re-layouts  0.84 us (1%)
  waiting for transfers between devices  0.79 us (1%)
    all_to_all x4, blocking collectives, exchange(): lax.all_to_all(blocks, 'mp', split_axis=0, concat_axis=0, tiled=True, axi...  43.6 us
    all_to_all x1, blocking collectives, exchange_all(): lax.all_to_all(blocks, ('mp', 'batch'), split_axis=0, concat_axis=0, tile...  8.23 us
    pallas_call x1, Pallas kernels, project_out(): call(kernel, 'project_out', (jax.ShapeDtypeStruct((groups, count, LANES),...  3.63 us
    pallas_call x1, Pallas kernels, project_qkv(): call(kernel, 'project_qkv', jax.ShapeDtypeStruct((2 * groups, rows, width...  1.92 us
  transfers between devices with their start and end apart: 1, of which 1 were waited for; matrix products, arithmetic and copies ran while one was open for 0% of the time, Pallas kernels for 1%

profile of v19, /device:TPU:0, one launch (start us, length us, event | category | flops | bytes accessed | tf_op | source)
XLA Modules:
  0.0 61.9 jit_solution(10874949144104186490)
XLA Ops:
  0.0 0.7 %copy-done.6 = bf16[8192]{0:T(1024)(128)(2,1)S(1)} copy-done((bf16[8192]{0:T(1024)(128)(2,1)S(1)}, bf16[8192]{0:T(1024)(128)(2,1)}, u32[]{:S(2)}) %copy-start.6) | copy-done | bytes 16408
  0.7 0.0 copy-done
  0.8 0.0 slice-start.5
  0.8 0.0 slice-start.6
  0.8 0.2 norm_rows.1
  1.0 14.6 %all_to_all.25.near_ref = bf16[8,2,8192]{2,1,0:T(2,128)(2,1)S(1)} all-to-all(bf16[8,2,8192]{2,1,0:T(2,128)(2,1)S(1)} %norm_rows.1), channel_id=1, replica_groups={{10,2,12,4,14,6,8,0},{11,3,13,5,15,7,9,1},{26,18,28,20,30,22,24,16},{27..., dimensions={0} | all-to-all | bytes 524288 | tf_op jit(solution)/shard_map/all_to_all | solution.py:401
  15.6 0.0 collective-permute-start
  15.6 0.0 copy-done.1
  15.6 0.0 copy-done.2
  15.6 0.0 copy-done.3
  15.6 0.7 %turns.1 = (bf16[16,8192]{1,0:T(8,128)(2,1)S(1)}, f32[2,128]{1,0:T(2,128)S(1)}, f32[2,128]{1,0:T(2,128)S(1)}, f32[2,256]{1,0:T(2,128)S(1)}, bf16[2,128]{1,0:T(2,128)(2,1)S(1)}) custom-call(s32[2]{0:T(128)S(1)} %copy-done.1, s32[2]{0:T(128)S(1)} %copy-done.2, s32[1,2]{1,0:T(1,128)S(1)} %copy-done.3, bf16[8,2,8192]{2,1,0:T(2,128)(2,1)S(1)} %all_to_all.25.near_ref, ...), custom_call_target="tpu_custom_call" | custom-call | bytes 524288 | tf_op jit(solution)/shard_map/turns/pallas_call | solution.py:228
  16.3 0.8 %collective-permute-done.far_ref = bf16[8,2,8192]{2,1,0:T(2,128)(2,1)S(1)} collective-permute-done((bf16[8,2,8192]{2,1,0:T(2,128)(2,1)S(1)}, bf16[8,2,8192]{2,1,0:T(2,128)(2,1)S(1)}, u32[]{:S(2)}, u32[]{:S(2)}) %collective-permute-start) | collective-permute-done | bytes 262176 | tf_op jit(solution)/shard_map/ppermute | solution.py:391
  17.1 0.0 slice-done.5
  17.1 0.0 copy-start.4
  17.1 0.0 copy-start.5
  17.1 0.0 slice-start
  17.2 0.0 slice-start.1
  17.2 0.0 slice-start.7
  17.2 0.0 slice-start.9
  17.2 1.9 %project_qkv.1 = bf16[16,2,768]{2,1,0:T(2,128)(2,1)S(1)} custom-call(bf16[16,8192]{1,0:T(8,128)(2,1)S(1)} %get-tuple-element.15.lined_ref, bf16[8,2,8192]{2,1,0:T(2,128)(2,1)S(1)} %collective-permute-done.far_ref, bf16[8192,640]{1,0:T(8,128)(2,1)S(1)} %bitcast.4, bf16[2,128]{1,0:T(2,128)(2,1)S(1)} %get-tuple-element.16.adapter_ref), custom_call_target="tpu_custom_call" | custom-call | flops 10000000000 | bytes 10485760 | tf_op jit(solution)/shard_map/project_qkv/pallas_call | solution.py:272
  19.1 8.2 %all_to_all.26.mixed_ref = bf16[16,2,768]{2,1,0:T(2,128)(2,1)S(1)} all-to-all(bf16[16,2,768]{2,1,0:T(2,128)(2,1)S(1)} %project_qkv.1), channel_id=1, replica_groups={{11,10,3,2,13,12,5,4,15,14,7,6,9,8,1,0},{27,26,19,18,29,28,21,20,31,30,..., dimensions={0} | all-to-all | bytes 98304 | tf_op jit(solution)/shard_map/all_to_all | solution.py:408
  27.4 0.0 copy-done.5
  27.4 0.0 slice-start.8
  27.4 0.0 slice-start.10
  27.4 0.8 %attend.1 = (bf16[8,2,8192]{2,1,0:T(2,128)(2,1)S(1)}, s32[16,128]{1,0:T(8,128)S(1)}) custom-call(bf16[16,2,768]{2,1,0:T(2,128)(2,1)S(1)} %all_to_all.26.mixed_ref, f32[2,128]{1,0:T(2,128)S(1)} %get-tuple-element.17.cosine_ref, f32[2,128]{1,0:T(2,128)S(1)} %get-tuple-element.18.sine_ref, f32[2,256]{1,0:T(2,128)S(1)} %get-tuple-element.19.mask_ref, ...), custom_call_target="tpu_custom_call" | custom-call | flops 10000000000 | bytes 2097152 | tf_op jit(solution)/shard_map/attend/pallas_call | solution.py:504
  28.2 12.2 %all_to_all.27.gathered_ref = bf16[8,2,8192]{2,1,0:T(2,128)(2,1)S(1)} all-to-all(bf16[8,2,8192]{2,1,0:T(2,128)(2,1)S(1)} %get-tuple-element.21), channel_id=1, replica_groups={{10,2,12,4,14,6,8,0},{11,3,13,5,15,7,9,1},{26,18,28,20,30,22,24,16},{27..., dimensions={0} | all-to-all | bytes 524288 | tf_op jit(solution)/shard_map/all_to_all | solution.py:401
  40.4 0.0 slice-done.1
  40.4 3.6 %project_out.1 = (f32[8,16,128]{2,1,0:T(8,128)S(1)}, f32[16,1024]{1,0:T(8,128)S(1)}, bf16[1024,1024]{1,0:T(8,128)(2,1)S(1)}) custom-call(s32[16,128]{1,0:T(8,128)S(1)} %get-tuple-element.20.adapter_ref, bf16[8,2,8192]{2,1,0:T(2,128)(2,1)S(1)} %all_to_all.27.gathered_ref, bf16[8192,1024]{1,0:T(8,128)(2,1)S(1)} %bitcast.2, bf16[64,64,1024]{2,1,0:T(8,128)(2,1)S(1)} %bitcast.7, ...), custom_call_target="tpu_custom_call" | custom-call | flops 10000000000 | bytes 16777216 | tf_op jit(solution)/shard_map/project_out/pallas_call | solution.py:321
  44.1 8.5 %all_to_all.28.partials_ref = f32[8,16,128]{2,1,0:T(8,128)S(1)} all-to-all(f32[8,16,128]{2,1,0:T(8,128)S(1)} %get-tuple-element.23), channel_id=1, replica_groups={{10,2,12,4,14,6,8,0},{11,3,13,5,15,7,9,1},{26,18,28,20,30,22,24,16},{27..., dimensions={0} | all-to-all | bytes 131072 | tf_op jit(solution)/shard_map/all_to_all | solution.py:401
  52.5 0.4 add_up.1
  52.9 8.4 %all_to_all.29.parts_ref = bf16[8,2,1024]{2,1,0:T(2,128)(2,1)S(1)} all-to-all(bf16[8,2,1024]{2,1,0:T(2,128)(2,1)S(1)} %add_up.1), channel_id=1, replica_groups={{10,2,12,4,14,6,8,0},{11,3,13,5,15,7,9,1},{26,18,28,20,30,22,24,16},{27..., dimensions={0} | all-to-all | bytes 65536 | tf_op jit(solution)/shard_map/all_to_all | solution.py:401
  61.3 0.7 %add_rows.1 = bf16[2,8192]{1,0:T(2,128)(2,1)} custom-call(bf16[2,8192]{1,0:T(2,128)(2,1)S(1)} %copy-done, bf16[8,2,1024]{2,1,0:T(2,128)(2,1)S(1)} %all_to_all.29.parts_ref), custom_call_target="tpu_custom_call" | custom-call | bytes 98304 | tf_op jit(solution)/shard_map/add_rows/pallas_call | solution.py:381
  (25 shorter events, 0.1 us)
Async XLA Ops:
  0.0 0.7 %copy-start.6 = (bf16[8192]{0:T(1024)(128)(2,1)S(1)}, bf16[8192]{0:T(1024)(128)(2,1)}, u32[]{:S(2)}) copy-start(bf16[8192]{0:T(1024)(128)(2,1)} %param.12) | copy-start | bytes 49156
  0.0 0.8 %copy-start = (bf16[2,8192]{1,0:T(2,128)(2,1)S(1)}, bf16[2,8192]{1,0:T(2,128)(2,1)}, u32[]{:S(2)}) copy-start(bf16[2,8192]{1,0:T(2,128)(2,1)} %hidden_ref.3) | copy-start | bytes 98308
  0.0 17.1 %slice-start.4 = ((s8[10485760]{0:T(1024)(128)(4,1)}), s8[4194304]{0:T(1024)(128)(4,1)S(1)}, s32[]{:S(2)}) async-start(s8[10485760]{0:T(1024)(128)(4,1)} %bitcast.3), calls=%async_computation.9 | async-start | bytes 8388608
  0.8 14.8 %copy-start.1 = (s32[2]{0:T(128)S(1)}, s32[2]{0:T(128)}, u32[]{:S(2)}) copy-start(s32[2]{0:T(128)} %lengths_ref.1) | copy-start | bytes 28
  0.8 14.8 %copy-start.2 = (s32[2]{0:T(128)S(1)}, s32[2]{0:T(128)}, u32[]{:S(2)}) copy-start(s32[2]{0:T(128)} %slots_ref.1) | copy-start | bytes 28
  0.8 14.8 %copy-start.3 = (s32[1,2]{1,0:T(1,128)S(1)}, s32[1,2]{1,0:T(1,128)}, u32[]{:S(2)}) copy-start(s32[1,2]{1,0:T(1,128)} %requests_ref.1) | copy-start | bytes 28
  0.8 16.3 %slice-start.5 = ((s8[10485760]{0:T(1024)(128)(4,1)}), s8[4194304]{0:T(1024)(128)(4,1)S(1)}, s32[]{:S(2)}) async-start(s8[10485760]{0:T(1024)(128)(4,1)} %bitcast.3), calls=%async_computation.10 | async-start | bytes 8388608
  0.8 16.3 %slice-start.6 = ((s8[10485760]{0:T(1024)(128)(4,1)}), s8[2097152]{0:T(1024)(128)(4,1)S(1)}, s32[]{:S(2)}) async-start(s8[10485760]{0:T(1024)(128)(4,1)} %bitcast.3), calls=%async_computation.11 | async-start | bytes 4194304
  15.6 1.5 %collective-permute-start = (bf16[8,2,8192]{2,1,0:T(2,128)(2,1)S(1)}, bf16[8,2,8192]{2,1,0:T(2,128)(2,1)S(1)}, u32[]{:S(2)}, u32[]{:S(2)}) collective-permute-start(bf16[8,2,8192]{2,1,0:T(2,128)(2,1)S(1)} %all_to_all.25.near_ref), channel_id=1, source_target_pairs={{0,1},{1,0},{2,3},{3,2},{4,5},{5,4},{6,7},{7,6},{8,9},{9,8},{10,11... | collective-permute-start | bytes 786440 | tf_op jit(solution)/shard_map/ppermute | solution.py:391
  17.1 10.2 %copy-start.4 = (bf16[2,256,1024]{2,1,0:T(8,128)(2,1)S(1)}, bf16[2,256,1024]{2,1,0:T(8,128)(2,1)}, u32[]{:S(2)}) copy-start(bf16[2,256,1024]{2,1,0:T(8,128)(2,1)} %key_ref.1) | copy-start | bytes 3145732
  17.1 10.2 %copy-start.5 = (bf16[2,256,1024]{2,1,0:T(8,128)(2,1)S(1)}, bf16[2,256,1024]{2,1,0:T(8,128)(2,1)}, u32[]{:S(2)}) copy-start(bf16[2,256,1024]{2,1,0:T(8,128)(2,1)} %value_ref.1) | copy-start | bytes 3145732
  17.1 23.2 %slice-start = ((s8[16777216]{0:T(1024)(128)(4,1)}), s8[4194304]{0:T(1024)(128)(4,1)S(1)}, s32[]{:S(2)}) async-start(s8[16777216]{0:T(1024)(128)(4,1)} %bitcast.1), calls=%async_computation.5 | async-start | bytes 8388608
  17.2 23.2 %slice-start.1 = ((s8[16777216]{0:T(1024)(128)(4,1)}), s8[4194304]{0:T(1024)(128)(4,1)S(1)}, s32[]{:S(2)}) async-start(s8[16777216]{0:T(1024)(128)(4,1)} %bitcast.1), calls=%async_computation.6 | async-start | bytes 8388608
  17.2 23.2 %slice-start.7 = ((s8[8388608]{0:T(1024)(128)(4,1)}), s8[4194304]{0:T(1024)(128)(4,1)S(1)}, s32[]{:S(2)}) async-start(s8[8388608]{0:T(1024)(128)(4,1)} %bitcast.5), calls=%async_computation.12 | async-start | bytes 8388608
  17.2 23.2 %slice-start.9 = ((s8[8388608]{0:T(1024)(128)(4,1)}), s8[4194304]{0:T(1024)(128)(4,1)S(1)}, s32[]{:S(2)}) async-start(s8[8388608]{0:T(1024)(128)(4,1)} %bitcast.8), calls=%async_computation.14 | async-start | bytes 8388608
  27.4 13.0 %slice-start.2 = ((s8[16777216]{0:T(1024)(128)(4,1)}), s8[4194304]{0:T(1024)(128)(4,1)S(1)}, s32[]{:S(2)}) async-start(s8[16777216]{0:T(1024)(128)(4,1)} %bitcast.1), calls=%async_computation.7 | async-start | bytes 8388608
  27.4 13.0 %slice-start.3 = ((s8[16777216]{0:T(1024)(128)(4,1)}), s8[4194304]{0:T(1024)(128)(4,1)S(1)}, s32[]{:S(2)}) async-start(s8[16777216]{0:T(1024)(128)(4,1)} %bitcast.1), calls=%async_computation.8 | async-start | bytes 8388608
  27.4 13.0 %slice-start.8 = ((s8[8388608]{0:T(1024)(128)(4,1)}), s8[4194304]{0:T(1024)(128)(4,1)S(1)}, s32[]{:S(2)}) async-start(s8[8388608]{0:T(1024)(128)(4,1)} %bitcast.5), calls=%async_computation.13 | async-start | bytes 8388608
  27.4 13.0 %slice-start.10 = ((s8[8388608]{0:T(1024)(128)(4,1)}), s8[4194304]{0:T(1024)(128)(4,1)S(1)}, s32[]{:S(2)}) async-start(s8[8388608]{0:T(1024)(128)(4,1)} %bitcast.8), calls=%async_computation.15 | async-start | bytes 8388608

commit v20 on v19

--- a/solution.py
+++ b/solution.py
@@ -246,11 +246,11 @@
     half = groups * rows
 
     def kernel(lined_ref, far_ref, weight_ref, adapter_ref, out_ref, far_lined_ref):
-        for j in range(groups):
-            far_lined_ref[pl.ds(j * rows, rows)] = far_ref[j]
         total = jnp.zeros((2 * half, width), jnp.float32)
         for k in range(depth // chunk):
             part = pl.ds(k * chunk, chunk)
+            for j in range(groups):
+                far_lined_ref[pl.ds(j * rows, rows), part] = far_ref[j, :, part]
             total = total + jnp.dot(
                 jnp.concatenate([lined_ref[:, part], far_lined_ref[:, part]]),
                 weight_ref[part, :],
@@ -290,12 +290,20 @@
         adapter_ref, gathered_ref, weight_ref, down_ref, up_ref, partial_ref, base_ref, picked_ref,
         rows_ref, held_ref,
     ):
-        for j in range(groups):
-            rows_ref[pl.ds(j * rows, rows)] = gathered_ref[j]
-        for r in range(count):
-            chosen = adapter_ref[r, 0]
-            held_ref[pl.ds(r * rank, rank)] = down_ref[chosen]
-            picked_ref[pl.ds(r * rank, rank)] = up_ref[chosen]
+        base = jnp.zeros((count, columns), jnp.float32)
+        chunks = features // chunk
+        for k in range(chunks):
+            part = pl.ds(k * chunk, chunk)
+            for j in range(groups):
+                rows_ref[pl.ds(j * rows, rows), part] = gathered_ref[j, :, part]
+            base = base + jnp.dot(
+                rows_ref[:, part], weight_ref[part, :], preferred_element_type=jnp.float32
+            )
+            for r in range(k * count // chunks, (k + 1) * count // chunks):
+                chosen = adapter_ref[0, r]
+                held_ref[pl.ds(r * rank, rank)] = down_ref[chosen]
+                picked_ref[pl.ds(r * rank, rank)] = up_ref[chosen]
+        base_ref[...] = base
         start = pl.multiple_of(lax.axis_index("mp") * depth, depth)
         every = lax.dot_general(
             rows_ref[:, pl.ds(start, depth)],
@@ -310,13 +318,6 @@
             total = total + jnp.where(row == (lane + s) // rank, every[:, s : s + LANES], 0.0)
         for c in range(groups):
             partial_ref[c] = total
-        total = jnp.zeros((count, columns), jnp.float32)
-        for k in range(features // chunk):
-            part = pl.ds(k * chunk, chunk)
-            total = total + jnp.dot(
-                rows_ref[:, part], weight_ref[part, :], preferred_element_type=jnp.float32
-            )
-        base_ref[...] = total
 
     return call(
         kernel,
@@ -427,6 +428,8 @@
         mixed_ref, cosine_ref, sine_ref, mask_ref, key_ref, value_ref, out_ref, adapter_ref,
         vec_ref, context_ref,
     ):
+        place = lax.broadcasted_iota(jnp.int32, (1, LANES), 1)
+        adapter = jnp.zeros((1, LANES), jnp.float32)
         for k, j in enumerate(devices):
             for core in range(2):
                 block = mixed_ref[2 * k + 1 - core].astype(jnp.float32)
@@ -435,7 +438,9 @@
                     vec_ref[pl.ds(head * rows, rows)] = block[:, c * HEAD_DIM : (c + 1) * HEAD_DIM]
             both = mixed_ref[2 * k, :, pl.ds(width, LANES)].astype(jnp.float32)
             both = both + mixed_ref[2 * k + 1, :, pl.ds(width, LANES)].astype(jnp.float32)
-            adapter_ref[pl.ds(k * rows, rows)] = both.astype(jnp.int32)
+            for r in range(rows):
+                adapter = jnp.where(place == k * rows + r, both[r : r + 1], adapter)
+        adapter_ref[...] = adapter.astype(jnp.int32)
 
         def tiled(pair, count):
             return jnp.concatenate([pair] * count)
@@ -506,7 +511,7 @@
         "attend",
         (
             jax.ShapeDtypeStruct((copies, rows, HEADS * HEAD_DIM), jnp.bfloat16),
-            jax.ShapeDtypeStruct((copies * rows, LANES), jnp.int32),
+            jax.ShapeDtypeStruct((1, LANES), jnp.int32),
         ),
         [VMEM] * 6,
         key_cache.size * 4,

time: 62.3 us -> 62.1 us (level)
  no operation moved by 1% of the time
where the time goes in v20:
time: 62.1 us; the launch traced here: 61.7 us
  blocking collectives  51.9 us (84%)
  Pallas kernels  7.92 us (13%)
  local copies, waits for them, and re-layouts  0.84 us (1%)
  waiting for transfers between devices  0.79 us (1%)
    all_to_all x4, blocking collectives, exchange(): lax.all_to_all(blocks, 'mp', split_axis=0, concat_axis=0, tiled=True, axi...  43.7 us
    all_to_all x1, blocking collectives, exchange_all(): lax.all_to_all(blocks, ('mp', 'batch'), split_axis=0, concat_axis=0, tile...  8.23 us
    pallas_call x1, Pallas kernels, project_out(): call(kernel, 'project_out', (jax.ShapeDtypeStruct((groups, count, LANES),...  3.26 us
    pallas_call x1, Pallas kernels, project_qkv(): call(kernel, 'project_qkv', jax.ShapeDtypeStruct((2 * groups, rows, width...  1.92 us
  transfers between devices with their start and end apart: 1, of which 1 were waited for; matrix products, arithmetic and copies ran while one was open for 0% of the time, Pallas kernels for 1%

profile of v20, /device:TPU:0, one launch (start us, length us, event | category | flops | bytes accessed | tf_op | source)
XLA Modules:
  0.0 61.7 jit_solution(13829904597844886914)
XLA Ops:
  0.0 0.7 %copy-done.6 = bf16[8192]{0:T(1024)(128)(2,1)S(1)} copy-done((bf16[8192]{0:T(1024)(128)(2,1)S(1)}, bf16[8192]{0:T(1024)(128)(2,1)}, u32[]{:S(2)}) %copy-start.6) | copy-done | bytes 16408
  0.7 0.0 copy-done
  0.8 0.0 slice-start.5
  0.8 0.0 slice-start.6
  0.8 0.2 norm_rows.1
  1.0 14.6 %all_to_all.25.near_ref = bf16[8,2,8192]{2,1,0:T(2,128)(2,1)S(1)} all-to-all(bf16[8,2,8192]{2,1,0:T(2,128)(2,1)S(1)} %norm_rows.1), channel_id=1, replica_groups={{10,2,12,4,14,6,8,0},{11,3,13,5,15,7,9,1},{26,18,28,20,30,22,24,16},{27..., dimensions={0} | all-to-all | bytes 524288 | tf_op jit(solution)/shard_map/all_to_all | solution.py:402
  15.6 0.0 collective-permute-start
  15.6 0.0 copy-done.1
  15.6 0.0 copy-done.2
  15.6 0.0 copy-done.3
  15.6 0.7 %turns.1 = (bf16[16,8192]{1,0:T(8,128)(2,1)S(1)}, f32[2,128]{1,0:T(2,128)S(1)}, f32[2,128]{1,0:T(2,128)S(1)}, f32[2,256]{1,0:T(2,128)S(1)}, bf16[2,128]{1,0:T(2,128)(2,1)S(1)}) custom-call(s32[2]{0:T(128)S(1)} %copy-done.1, s32[2]{0:T(128)S(1)} %copy-done.2, s32[1,2]{1,0:T(1,128)S(1)} %copy-done.3, bf16[8,2,8192]{2,1,0:T(2,128)(2,1)S(1)} %all_to_all.25.near_ref, ...), custom_call_target="tpu_custom_call" | custom-call | bytes 524288 | tf_op jit(solution)/shard_map/turns/pallas_call | solution.py:228
  16.3 0.8 %collective-permute-done.far_ref = bf16[8,2,8192]{2,1,0:T(2,128)(2,1)S(1)} collective-permute-done((bf16[8,2,8192]{2,1,0:T(2,128)(2,1)S(1)}, bf16[8,2,8192]{2,1,0:T(2,128)(2,1)S(1)}, u32[]{:S(2)}, u32[]{:S(2)}) %collective-permute-start) | collective-permute-done | bytes 262176 | tf_op jit(solution)/shard_map/ppermute | solution.py:392
  17.1 0.0 slice-done.4
  17.1 0.0 slice-done.5
  17.1 0.0 copy-start.4
  17.1 0.0 copy-start.5
  17.1 0.0 slice-start
  17.2 0.0 slice-start.1
  17.2 0.0 slice-start.7
  17.2 0.0 slice-start.9
  17.2 1.9 %project_qkv.1 = bf16[16,2,768]{2,1,0:T(2,128)(2,1)S(1)} custom-call(bf16[16,8192]{1,0:T(8,128)(2,1)S(1)} %get-tuple-element.15.lined_ref, bf16[8,2,8192]{2,1,0:T(2,128)(2,1)S(1)} %collective-permute-done.far_ref, bf16[8192,640]{1,0:T(8,128)(2,1)S(1)} %bitcast.4, bf16[2,128]{1,0:T(2,128)(2,1)S(1)} %get-tuple-element.16.adapter_ref), custom_call_target="tpu_custom_call" | custom-call | flops 10000000000 | bytes 10485760 | tf_op jit(solution)/shard_map/project_qkv/pallas_call | solution.py:272
  19.1 8.2 %all_to_all.26.mixed_ref = bf16[16,2,768]{2,1,0:T(2,128)(2,1)S(1)} all-to-all(bf16[16,2,768]{2,1,0:T(2,128)(2,1)S(1)} %project_qkv.1), channel_id=1, replica_groups={{11,10,3,2,13,12,5,4,15,14,7,6,9,8,1,0},{27,26,19,18,29,28,21,20,31,30,..., dimensions={0} | all-to-all | bytes 98304 | tf_op jit(solution)/shard_map/all_to_all | solution.py:409
  27.4 0.0 copy-done.5
  27.4 0.0 slice-start.8
  27.4 0.0 slice-start.10
  27.4 0.8 %attend.1 = (bf16[8,2,8192]{2,1,0:T(2,128)(2,1)S(1)}, s32[1,128]{1,0:T(1,128)S(1)}) custom-call(bf16[16,2,768]{2,1,0:T(2,128)(2,1)S(1)} %all_to_all.26.mixed_ref, f32[2,128]{1,0:T(2,128)S(1)} %get-tuple-element.17.cosine_ref, f32[2,128]{1,0:T(2,128)S(1)} %get-tuple-element.18.sine_ref, f32[2,256]{1,0:T(2,128)S(1)} %get-tuple-element.19.mask_ref, ...), custom_call_target="tpu_custom_call" | custom-call | flops 10000000000 | bytes 2097152 | tf_op jit(solution)/shard_map/attend/pallas_call | solution.py:509
  28.2 12.2 %all_to_all.27.gathered_ref = bf16[8,2,8192]{2,1,0:T(2,128)(2,1)S(1)} all-to-all(bf16[8,2,8192]{2,1,0:T(2,128)(2,1)S(1)} %get-tuple-element.21), channel_id=1, replica_groups={{10,2,12,4,14,6,8,0},{11,3,13,5,15,7,9,1},{26,18,28,20,30,22,24,16},{27..., dimensions={0} | all-to-all | bytes 524288 | tf_op jit(solution)/shard_map/all_to_all | solution.py:402
  40.4 3.3 %project_out.1 = (f32[8,16,128]{2,1,0:T(8,128)S(1)}, f32[16,1024]{1,0:T(8,128)S(1)}, bf16[1024,1024]{1,0:T(8,128)(2,1)S(1)}) custom-call(s32[1,128]{1,0:T(1,128)S(1)} %get-tuple-element.20.adapter_ref, bf16[8,2,8192]{2,1,0:T(2,128)(2,1)S(1)} %all_to_all.27.gathered_ref, bf16[8192,1024]{1,0:T(8,128)(2,1)S(1)} %bitcast.2, bf16[64,64,1024]{2,1,0:T(8,128)(2,1)S(1)} %bitcast.7, ...), custom_call_target="tpu_custom_call" | custom-call | flops 10000000000 | bytes 16777216 | tf_op jit(solution)/shard_map/project_out/pallas_call | solution.py:322
  43.7 8.6 %all_to_all.28.partials_ref = f32[8,16,128]{2,1,0:T(8,128)S(1)} all-to-all(f32[8,16,128]{2,1,0:T(8,128)S(1)} %get-tuple-element.23), channel_id=1, replica_groups={{10,2,12,4,14,6,8,0},{11,3,13,5,15,7,9,1},{26,18,28,20,30,22,24,16},{27..., dimensions={0} | all-to-all | bytes 131072 | tf_op jit(solution)/shard_map/all_to_all | solution.py:402
  52.3 0.4 add_up.1
  52.7 8.4 %all_to_all.29.parts_ref = bf16[8,2,1024]{2,1,0:T(2,128)(2,1)S(1)} all-to-all(bf16[8,2,1024]{2,1,0:T(2,128)(2,1)S(1)} %add_up.1), channel_id=1, replica_groups={{10,2,12,4,14,6,8,0},{11,3,13,5,15,7,9,1},{26,18,28,20,30,22,24,16},{27..., dimensions={0} | all-to-all | bytes 65536 | tf_op jit(solution)/shard_map/all_to_all | solution.py:402
  61.0 0.7 %add_rows.1 = bf16[2,8192]{1,0:T(2,128)(2,1)} custom-call(bf16[2,8192]{1,0:T(2,128)(2,1)S(1)} %copy-done, bf16[8,2,1024]{2,1,0:T(2,128)(2,1)S(1)} %all_to_all.29.parts_ref), custom_call_target="tpu_custom_call" | custom-call | bytes 98304 | tf_op jit(solution)/shard_map/add_rows/pallas_call | solution.py:382
  (25 shorter events, 0.1 us)
Async XLA Ops:
  0.0 0.7 %copy-start.6 = (bf16[8192]{0:T(1024)(128)(2,1)S(1)}, bf16[8192]{0:T(1024)(128)(2,1)}, u32[]{:S(2)}) copy-start(bf16[8192]{0:T(1024)(128)(2,1)} %param.12) | copy-start | bytes 49156
  0.0 0.8 %copy-start = (bf16[2,8192]{1,0:T(2,128)(2,1)S(1)}, bf16[2,8192]{1,0:T(2,128)(2,1)}, u32[]{:S(2)}) copy-start(bf16[2,8192]{1,0:T(2,128)(2,1)} %hidden_ref.3) | copy-start | bytes 98308
  0.0 17.1 %slice-start.4 = ((s8[10485760]{0:T(1024)(128)(4,1)}), s8[4194304]{0:T(1024)(128)(4,1)S(1)}, s32[]{:S(2)}) async-start(s8[10485760]{0:T(1024)(128)(4,1)} %bitcast.3), calls=%async_computation.9 | async-start | bytes 8388608
  0.8 14.8 %copy-start.1 = (s32[2]{0:T(128)S(1)}, s32[2]{0:T(128)}, u32[]{:S(2)}) copy-start(s32[2]{0:T(128)} %lengths_ref.1) | copy-start | bytes 28
  0.8 14.8 %copy-start.2 = (s32[2]{0:T(128)S(1)}, s32[2]{0:T(128)}, u32[]{:S(2)}) copy-start(s32[2]{0:T(128)} %slots_ref.1) | copy-start | bytes 28
  0.8 14.8 %copy-start.3 = (s32[1,2]{1,0:T(1,128)S(1)}, s32[1,2]{1,0:T(1,128)}, u32[]{:S(2)}) copy-start(s32[1,2]{1,0:T(1,128)} %requests_ref.1) | copy-start | bytes 28
  0.8 16.3 %slice-start.5 = ((s8[10485760]{0:T(1024)(128)(4,1)}), s8[4194304]{0:T(1024)(128)(4,1)S(1)}, s32[]{:S(2)}) async-start(s8[10485760]{0:T(1024)(128)(4,1)} %bitcast.3), calls=%async_computation.10 | async-start | bytes 8388608
  0.8 16.3 %slice-start.6 = ((s8[10485760]{0:T(1024)(128)(4,1)}), s8[2097152]{0:T(1024)(128)(4,1)S(1)}, s32[]{:S(2)}) async-start(s8[10485760]{0:T(1024)(128)(4,1)} %bitcast.3), calls=%async_computation.11 | async-start | bytes 4194304
  15.6 1.5 %collective-permute-start = (bf16[8,2,8192]{2,1,0:T(2,128)(2,1)S(1)}, bf16[8,2,8192]{2,1,0:T(2,128)(2,1)S(1)}, u32[]{:S(2)}, u32[]{:S(2)}) collective-permute-start(bf16[8,2,8192]{2,1,0:T(2,128)(2,1)S(1)} %all_to_all.25.near_ref), channel_id=1, source_target_pairs={{0,1},{1,0},{2,3},{3,2},{4,5},{5,4},{6,7},{7,6},{8,9},{9,8},{10,11... | collective-permute-start | bytes 786440 | tf_op jit(solution)/shard_map/ppermute | solution.py:392
  17.1 10.2 %copy-start.4 = (bf16[2,256,1024]{2,1,0:T(8,128)(2,1)S(1)}, bf16[2,256,1024]{2,1,0:T(8,128)(2,1)}, u32[]{:S(2)}) copy-start(bf16[2,256,1024]{2,1,0:T(8,128)(2,1)} %key_ref.1) | copy-start | bytes 3145732
  17.1 10.2 %copy-start.5 = (bf16[2,256,1024]{2,1,0:T(8,128)(2,1)S(1)}, bf16[2,256,1024]{2,1,0:T(8,128)(2,1)}, u32[]{:S(2)}) copy-start(bf16[2,256,1024]{2,1,0:T(8,128)(2,1)} %value_ref.1) | copy-start | bytes 3145732
  17.1 23.2 %slice-start = ((s8[16777216]{0:T(1024)(128)(4,1)}), s8[4194304]{0:T(1024)(128)(4,1)S(1)}, s32[]{:S(2)}) async-start(s8[16777216]{0:T(1024)(128)(4,1)} %bitcast.1), calls=%async_computation.5 | async-start | bytes 8388608
  17.2 23.2 %slice-start.1 = ((s8[16777216]{0:T(1024)(128)(4,1)}), s8[4194304]{0:T(1024)(128)(4,1)S(1)}, s32[]{:S(2)}) async-start(s8[16777216]{0:T(1024)(128)(4,1)} %bitcast.1), calls=%async_computation.6 | async-start | bytes 8388608
  17.2 23.2 %slice-start.7 = ((s8[8388608]{0:T(1024)(128)(4,1)}), s8[4194304]{0:T(1024)(128)(4,1)S(1)}, s32[]{:S(2)}) async-start(s8[8388608]{0:T(1024)(128)(4,1)} %bitcast.5), calls=%async_computation.12 | async-start | bytes 8388608
  17.2 23.2 %slice-start.9 = ((s8[8388608]{0:T(1024)(128)(4,1)}), s8[4194304]{0:T(1024)(128)(4,1)S(1)}, s32[]{:S(2)}) async-start(s8[8388608]{0:T(1024)(128)(4,1)} %bitcast.8), calls=%async_computation.14 | async-start | bytes 8388608
  27.4 13.0 %slice-start.2 = ((s8[16777216]{0:T(1024)(128)(4,1)}), s8[4194304]{0:T(1024)(128)(4,1)S(1)}, s32[]{:S(2)}) async-start(s8[16777216]{0:T(1024)(128)(4,1)} %bitcast.1), calls=%async_computation.7 | async-start | bytes 8388608
  27.4 13.0 %slice-start.3 = ((s8[16777216]{0:T(1024)(128)(4,1)}), s8[4194304]{0:T(1024)(128)(4,1)S(1)}, s32[]{:S(2)}) async-start(s8[16777216]{0:T(1024)(128)(4,1)} %bitcast.1), calls=%async_computation.8 | async-start | bytes 8388608
  27.4 13.0 %slice-start.8 = ((s8[8388608]{0:T(1024)(128)(4,1)}), s8[4194304]{0:T(1024)(128)(4,1)S(1)}, s32[]{:S(2)}) async-start(s8[8388608]{0:T(1024)(128)(4,1)} %bitcast.5), calls=%async_computation.13 | async-start | bytes 8388608
  27.4 13.0 %slice-start.10 = ((s8[8388608]{0:T(1024)(128)(4,1)}), s8[4194304]{0:T(1024)(128)(4,1)S(1)}, s32[]{:S(2)}) async-start(s8[8388608]{0:T(1024)(128)(4,1)} %bitcast.8), calls=%async_computation.15 | async-start | bytes 8388608

commit v21 on v20

--- a/solution.py
+++ b/solution.py
@@ -265,9 +265,7 @@
                 out_ref[device, :, pl.ds(0, width)] = total[place : place + rows].astype(
                     jnp.bfloat16
                 )
-                out_ref[device, :, pl.ds(width, LANES)] = (
-                    adapter if e == 0 else jnp.zeros_like(adapter)
-                )
+                out_ref[device, :, pl.ds(width, LANES)] = adapter
 
     return call(
         kernel,
@@ -280,73 +278,83 @@
     )(lined, far, weight, adapter)
 
 
-def project_out(gathered, adapter, weight, down_store, up_store, chunk=1024):
-    groups, rows, features = gathered.shape
-    count = groups * rows
+def project_out(gathered, adapter, weight, down_store, up_store):
+    blocks, rows, features = gathered.shape
+    groups, count = blocks // 2, blocks * rows // 2
     rank, depth = down_store.shape[1:]
-    columns = weight.shape[1]
+    columns, half = weight.shape[1], depth // 2
 
     def kernel(
-        adapter_ref, gathered_ref, weight_ref, down_ref, up_ref, partial_ref, base_ref, picked_ref,
-        rows_ref, held_ref,
+        adapter_ref, gathered_ref, weight_ref, down_ref, up_ref, partial_ref, mine_ref, theirs_ref,
+        picked_ref, rows_ref, held_ref,
     ):
-        base = jnp.zeros((count, columns), jnp.float32)
-        chunks = features // chunk
-        for k in range(chunks):
-            part = pl.ds(k * chunk, chunk)
-            for j in range(groups):
-                rows_ref[pl.ds(j * rows, rows), part] = gathered_ref[j, :, part]
+        core = lax.axis_index("batch")
+        start = pl.multiple_of(core * half, half)
+        base = jnp.zeros((2 * count, columns), jnp.float32)
+        for k in range(groups):
+            part = pl.ds(k * half, half)
+            for p in range(blocks):
+                place = pl.ds((p % 2 * groups + p // 2) * rows, rows)
+                rows_ref[place, part] = gathered_ref[p, :, part]
             base = base + jnp.dot(
-                rows_ref[:, part], weight_ref[part, :], preferred_element_type=jnp.float32
+                rows_ref[:, part],
+                weight_ref[pl.ds(pl.multiple_of(start + k * depth, half), half), :],
+                preferred_element_type=jnp.float32,
             )
-            for r in range(k * count // chunks, (k + 1) * count // chunks):
+            for r in range(k * 2 * count // groups, (k + 1) * 2 * count // groups):
                 chosen = adapter_ref[0, r]
-                held_ref[pl.ds(r * rank, rank)] = down_ref[chosen]
+                held_ref[pl.ds(r * rank, rank)] = down_ref[chosen, :, pl.ds(start, half)]
+            for r in range(k * count // groups, (k + 1) * count // groups):
+                chosen = adapter_ref[0, (1 - core) * count + r]
                 picked_ref[pl.ds(r * rank, rank)] = up_ref[chosen]
-        base_ref[...] = base
-        start = pl.multiple_of(lax.axis_index("mp") * depth, depth)
+        first, second = base[count:], base[:count]
+        mine_ref[...] = jnp.where(core == 0, first, second)
+        theirs_ref[...] = jnp.where(core == 0, second, first)
         every = lax.dot_general(
-            rows_ref[:, pl.ds(start, depth)],
+            rows_ref[:, pl.ds(pl.multiple_of(lax.axis_index("mp") * half, half), half)],
             held_ref[...],
             (((1,), (1,)), ((), ())),
             preferred_element_type=jnp.float32,
         )
-        row = lax.broadcasted_iota(jnp.int32, (count, LANES), 0)
-        lane = lax.broadcasted_iota(jnp.int32, (count, LANES), 1)
-        total = jnp.zeros((count, LANES), jnp.float32)
-        for s in range(0, count * rank, LANES):
+        row = lax.broadcasted_iota(jnp.int32, (2 * count, LANES), 0)
+        lane = lax.broadcasted_iota(jnp.int32, (2 * count, LANES), 1)
+        total = jnp.zeros((2 * count, LANES), jnp.float32)
+        for s in range(0, 2 * count * rank, LANES):
             total = total + jnp.where(row == (lane + s) // rank, every[:, s : s + LANES], 0.0)
-        for c in range(groups):
-            partial_ref[c] = total
-
+        for p in range(blocks):
+            partial_ref[p] = total[p % 2 * count : (p % 2 + 1) * count]
+
+    sums = jax.ShapeDtypeStruct((count, columns), jnp.float32)
     return call(
         kernel,
         "project_out",
         (
-            jax.ShapeDtypeStruct((groups, count, LANES), jnp.float32),
-            jax.ShapeDtypeStruct((count, columns), jnp.float32),
+            jax.ShapeDtypeStruct((blocks, count, LANES), jnp.float32),
+            sums,
+            sums,
             pltpu.VMEM((count * rank, columns), up_store.dtype),
         ),
         [SMEM] + [VMEM] * 4,
         weight.size * 2,
-        limit=5 * MIB,
+        limit=6 * MIB,
         flops=LONG,
         scratch_shapes=[
-            pltpu.VMEM((count, features), gathered.dtype),
-            pltpu.VMEM((count * rank, depth), down_store.dtype),
+            pltpu.VMEM((2 * count, features), gathered.dtype),
+            pltpu.VMEM((2 * count * rank, half), down_store.dtype),
         ],
     )(adapter, gathered, weight, down_store, up_store)
 
 
-def add_up(base, partials, up):
-    groups, count, _ = partials.shape
+def add_up(mine, other, partials, up):
+    blocks, count, _ = partials.shape
+    groups = blocks // 2
     depth, width = up.shape
     rank = depth // count
 
-    def kernel(base_ref, partials_ref, up_ref, out_ref):
+    def kernel(mine_ref, other_ref, partials_ref, up_ref, out_ref):
         total = partials_ref[0]
-        for c in range(1, groups):
-            total = total + partials_ref[c]
+        for p in range(1, blocks):
+            total = total + partials_ref[p]
         down = total.astype(jnp.bfloat16).astype(jnp.float32)
         row = lax.broadcasted_iota(jnp.int32, (count, LANES), 0)
         lane = lax.broadcasted_iota(jnp.int32, (count, LANES), 1)
@@ -355,7 +363,8 @@
             spread.append(jnp.where(row == (lane + s) // rank, down, 0.0))
         spread = jnp.concatenate(spread, 1).astype(jnp.bfloat16)
         delta = jnp.dot(spread, up_ref[...], preferred_element_type=jnp.float32)
-        result = (base_ref[...] + ADAPTER_SCALE * delta).astype(jnp.bfloat16)
+        base = mine_ref[...] + other_ref[...]
+        result = (base + ADAPTER_SCALE * delta).astype(jnp.bfloat16)
         for j in range(groups):
             out_ref[j] = result[j * count // groups : (j + 1) * count // groups]
 
@@ -363,11 +372,11 @@
         kernel,
         "add_up",
         jax.ShapeDtypeStruct((groups, count // groups, width), jnp.bfloat16),
-        [VMEM] * 3,
+        [VMEM] * 4,
         up.size * 2,
         limit=4 * MIB,
         flops=2 * count * up.size,
-    )(base, partials, up)
+    )(mine, other, partials, up)
 
 
 def add_rows(hidden, parts):
@@ -423,6 +432,7 @@
     width = mixed.shape[2] - LANES
     per_device = width // HEAD_DIM
     devices = order(mixed.shape[0] // 2)
+    part_width = HEADS * HEAD_DIM // (2 * copies)
 
     def kernel(
         mixed_ref, cosine_ref, sine_ref, mask_ref, key_ref, value_ref, out_ref, adapter_ref,
@@ -436,10 +446,10 @@
                 for c in range(per_device):
                     head = (2 * j + core) * per_device + c
                     vec_ref[pl.ds(head * rows, rows)] = block[:, c * HEAD_DIM : (c + 1) * HEAD_DIM]
-            both = mixed_ref[2 * k, :, pl.ds(width, LANES)].astype(jnp.float32)
-            both = both + mixed_ref[2 * k + 1, :, pl.ds(width, LANES)].astype(jnp.float32)
-            for r in range(rows):
-                adapter = jnp.where(place == k * rows + r, both[r : r + 1], adapter)
+                ids = mixed_ref[2 * k + 1 - core, :, pl.ds(width, LANES)].astype(jnp.float32)
+                first = ((1 - core) * len(devices) + k) * rows
+                for r in range(rows):
+                    adapter = jnp.where(place == first + r, ids[r : r + 1], adapter)
         adapter_ref[...] = adapter.astype(jnp.int32)
 
         def tiled(pair, count):
@@ -500,17 +510,21 @@
             ]
             result = of_owner(products) + own_prob[g * size : (g + 1) * size] * own_value[g]
             for h in range(group):
-                place = pl.ds((g * group + h) * HEAD_DIM, HEAD_DIM)
-                context_ref[:, place] = result[h * rows : (h + 1) * rows]
-        rounded = context_ref[...].astype(jnp.bfloat16)
-        for c in range(copies):
-            out_ref[c] = rounded
+                first = (g * group + h) * HEAD_DIM
+                core, first = first // part_width % 2, first // part_width // 2 * part_width + (
+                    first % part_width
+                )
+                context_ref[core, :, pl.ds(first, HEAD_DIM)] = result[h * rows : (h + 1) * rows]
+        for core in range(2):
+            rounded = context_ref[core].astype(jnp.bfloat16)
+            for k in range(copies):
+                out_ref[2 * k + 1 - core] = rounded
 
     return call(
         kernel,
         "attend",
         (
-            jax.ShapeDtypeStruct((copies, rows, HEADS * HEAD_DIM), jnp.bfloat16),
+            jax.ShapeDtypeStruct((2 * copies, rows, HEADS * HEAD_DIM // 2), jnp.bfloat16),
             jax.ShapeDtypeStruct((1, LANES), jnp.int32),
         ),
         [VMEM] * 6,
@@ -519,7 +533,7 @@
         flops=LONG,
         scratch_shapes=[
             pltpu.VMEM((heads * rows, HEAD_DIM), jnp.float32),
-            pltpu.VMEM((rows, HEADS * HEAD_DIM), jnp.float32),
+            pltpu.VMEM((2, rows, HEADS * HEAD_DIM // 2), jnp.float32),
         ],
     )(mixed, cosine, sine, mask, key_cache, value_cache)
 
@@ -546,16 +560,16 @@
     columns = project_qkv(lined, swap_cores(near), query_key_value_weight, adapter)
     mixed = exchange_all(columns)
     context, adapter = attend(mixed, cosine, sine, mask, key_cache, value_cache, mp_size)
-    gathered = exchange(context)
-
-    partials, base, up = project_out(
+    gathered = exchange_all(context)
+
+    partials, mine, theirs, up = project_out(
         gathered,
         adapter,
         output_weight,
         adapter_down_matrices.swapaxes(1, 2),
         adapter_up_matrices,
     )
-    projected = add_up(base, exchange(partials), up)
+    projected = add_up(mine, swap_cores(theirs), exchange_all(partials), up)
     return add_rows(hidden, exchange(projected))
 
 

time: 62.1 us -> 63.7 us (1.026)
  blocking collectives: 51.9 us -> 44 us
  starting transfers between devices: 0.01 us -> 5.08 us
  waiting for transfers between devices: 0.79 us -> 4.94 us
    all_to_all x4 -> x2, blocking collectives: 43.7 us -> 23.2 us  [exchange(): lax.all_to_all(blocks, 'mp', split_axis=0, concat_axis=0, tiled=True, axi...]
    all_to_all x1 -> x2, blocking collectives: 8.23 us -> 20.8 us  [exchange_all(): lax.all_to_all(blocks, ('mp', 'batch'), split_axis=0, concat_axis=0, tile...]
    all_to_all x0 -> x1, starting transfers between devices: none -> 5 us  [exchange_all(): lax.all_to_all(blocks, ('mp', 'batch'), split_axis=0, concat_axis=0, tile...]
    all_to_all x0 -> x1, waiting for transfers between devices: none -> 2.97 us  [exchange_all(): lax.all_to_all(blocks, ('mp', 'batch'), split_axis=0, concat_axis=0, tile...]
    ppermute x1 -> x2, waiting for transfers between devices: 0.79 us -> 1.97 us  [swap_cores(): return lax.ppermute(block, 'batch', [(0, 1), (1, 0)])]
  transfers between devices with their start and end apart: 1 -> 3, of which waited for: 1 -> 3; matrix products, arithmetic and copies ran while one was open for 0% -> 0% of each run, Pallas kernels for 1% -> 1%
where the time goes in v21:
time: 63.7 us; the launch traced here: 63.3 us
  blocking collectives  44 us (69%)
  Pallas kernels  8.17 us (13%)
  starting transfers between devices  5.08 us (8%)
  waiting for transfers between devices  4.94 us (8%)
  local copies, waits for them, and re-layouts  0.84 us (1%)
    all_to_all x2, blocking collectives, exchange(): lax.all_to_all(blocks, 'mp', split_axis=0, concat_axis=0, tiled=True, axi...  23.2 us
    all_to_all x2, blocking collectives, exchange_all(): lax.all_to_all(blocks, ('mp', 'batch'), split_axis=0, concat_axis=0, tile...  20.8 us
    all_to_all x1, starting transfers between devices, exchange_all(): lax.all_to_all(blocks, ('mp', 'batch'), split_axis=0, concat_axis=0, tile...  5 us
    pallas_call x1, Pallas kernels, project_out(): call(kernel, 'project_out', (jax.ShapeDtypeStruct((blocks, count, LANES),...  3.5 us
    all_to_all x1, waiting for transfers between devices, exchange_all(): lax.all_to_all(blocks, ('mp', 'batch'), split_axis=0, concat_axis=0, tile...  2.97 us
    ppermute x2, waiting for transfers between devices, swap_cores(): return lax.ppermute(block, 'batch', [(0, 1), (1, 0)])  1.97 us
    pallas_call x1, Pallas kernels, project_qkv(): call(kernel, 'project_qkv', jax.ShapeDtypeStruct((2 * groups, rows, width...  1.93 us
  transfers between devices with their start and end apart: 3, of which 3 were waited for; matrix products, arithmetic and copies ran while one was open for 0% of the time, Pallas kernels for 1%

profile of v21, /device:TPU:0, one launch (start us, length us, event | category | flops | bytes accessed | tf_op | source)
XLA Modules:
  0.0 63.3 jit_solution(11945015396235444412)
XLA Ops:
  0.0 0.7 %copy-done.6 = bf16[8192]{0:T(1024)(128)(2,1)S(1)} copy-done((bf16[8192]{0:T(1024)(128)(2,1)S(1)}, bf16[8192]{0:T(1024)(128)(2,1)}, u32[]{:S(2)}) %copy-start.6) | copy-done | bytes 16408
  0.7 0.0 copy-done
  0.8 0.0 slice-start.5
  0.8 0.0 slice-start.6
  0.8 0.2 norm_rows.1
  1.0 14.6 %all_to_all.25.near_ref = bf16[8,2,8192]{2,1,0:T(2,128)(2,1)S(1)} all-to-all(bf16[8,2,8192]{2,1,0:T(2,128)(2,1)S(1)} %norm_rows.1), channel_id=1, replica_groups={{10,2,12,4,14,6,8,0},{11,3,13,5,15,7,9,1},{26,18,28,20,30,22,24,16},{27..., dimensions={0} | all-to-all | bytes 524288 | tf_op jit(solution)/shard_map/all_to_all | solution.py:411
  15.6 0.0 collective-permute-start
  15.6 0.7 %turns.1 = (bf16[16,8192]{1,0:T(8,128)(2,1)S(1)}, f32[2,128]{1,0:T(2,128)S(1)}, f32[2,128]{1,0:T(2,128)S(1)}, f32[2,256]{1,0:T(2,128)S(1)}, bf16[2,128]{1,0:T(2,128)(2,1)S(1)}) custom-call(s32[2]{0:T(128)S(1)} %copy-done.1, s32[2]{0:T(128)S(1)} %copy-done.2, s32[1,2]{1,0:T(1,128)S(1)} %copy-done.3, bf16[8,2,8192]{2,1,0:T(2,128)(2,1)S(1)} %all_to_all.25.near_ref, ...), custom_call_target="tpu_custom_call" | custom-call | bytes 524288 | tf_op jit(solution)/shard_map/turns/pallas_call | solution.py:228
  16.3 0.8 %collective-permute-done.far_ref = bf16[8,2,8192]{2,1,0:T(2,128)(2,1)S(1)} collective-permute-done((bf16[8,2,8192]{2,1,0:T(2,128)(2,1)S(1)}, bf16[8,2,8192]{2,1,0:T(2,128)(2,1)S(1)}, u32[]{:S(2)}, u32[]{:S(2)}) %collective-permute-start) | collective-permute-done | bytes 262176 | tf_op jit(solution)/shard_map/ppermute | solution.py:401
  17.1 0.0 slice-done.6
  17.1 0.0 copy-start.4
  17.1 0.0 copy-start.5
  17.1 0.0 slice-start
  17.2 0.0 slice-start.1
  17.2 0.0 slice-start.7
  17.2 0.0 slice-start.9
  17.2 1.9 %project_qkv.1 = bf16[16,2,768]{2,1,0:T(2,128)(2,1)S(1)} custom-call(bf16[16,8192]{1,0:T(8,128)(2,1)S(1)} %get-tuple-element.16.lined_ref, bf16[8,2,8192]{2,1,0:T(2,128)(2,1)S(1)} %collective-permute-done.far_ref, bf16[8192,640]{1,0:T(8,128)(2,1)S(1)} %bitcast.4, bf16[2,128]{1,0:T(2,128)(2,1)S(1)} %get-tuple-element.17.adapter_ref), custom_call_target="tpu_custom_call" | custom-call | flops 10000000000 | bytes 10485760 | tf_op jit(solution)/shard_map/project_qkv/pallas_call | solution.py:270
  19.1 8.2 %all_to_all.26.mixed_ref = bf16[16,2,768]{2,1,0:T(2,128)(2,1)S(1)} all-to-all(bf16[16,2,768]{2,1,0:T(2,128)(2,1)S(1)} %project_qkv.1), channel_id=1, replica_groups={{11,10,3,2,13,12,5,4,15,14,7,6,9,8,1,0},{27,26,19,18,29,28,21,20,31,30,..., dimensions={0} | all-to-all | bytes 98304 | tf_op jit(solution)/shard_map/all_to_all | solution.py:418
  27.4 0.0 slice-start.8
  27.4 0.0 slice-start.10
  27.4 0.8 %attend.1 = (bf16[16,2,4096]{2,1,0:T(2,128)(2,1)S(1)}, s32[1,128]{1,0:T(1,128)S(1)}) custom-call(bf16[16,2,768]{2,1,0:T(2,128)(2,1)S(1)} %all_to_all.26.mixed_ref, f32[2,128]{1,0:T(2,128)S(1)} %get-tuple-element.18.cosine_ref, f32[2,128]{1,0:T(2,128)S(1)} %get-tuple-element.19.sine_ref, f32[2,256]{1,0:T(2,128)S(1)} %get-tuple-element.20.mask_ref, ...), custom_call_target="tpu_custom_call" | custom-call | flops 10000000000 | bytes 2097152 | tf_op jit(solution)/shard_map/attend/pallas_call | solution.py:523
  28.2 12.5 %all_to_all.27.gathered_ref = bf16[16,2,4096]{2,1,0:T(2,128)(2,1)S(1)} all-to-all(bf16[16,2,4096]{2,1,0:T(2,128)(2,1)S(1)} %get-tuple-element.22), channel_id=1, replica_groups={{11,10,3,2,13,12,5,4,15,14,7,6,9,8,1,0},{27,26,19,18,29,28,21,20,31,30,..., dimensions={0} | all-to-all | bytes 524288 | tf_op jit(solution)/shard_map/all_to_all | solution.py:418
  40.7 0.0 slice-done.9
  40.7 0.0 slice-done.2
  40.8 3.5 %project_out.1 = (f32[16,16,128]{2,1,0:T(8,128)}, f32[16,1024]{1,0:T(8,128)S(1)}, f32[16,1024]{1,0:T(8,128)S(1)}, bf16[1024,1024]{1,0:T(8,128)(2,1)S(1)}) custom-call(s32[1,128]{1,0:T(1,128)S(1)} %get-tuple-element.21.adapter_ref, bf16[16,2,4096]{2,1,0:T(2,128)(2,1)S(1)} %all_to_all.27.gathered_ref, bf16[8192,1024]{1,0:T(8,128)(2,1)S(1)} %bitcast.2, ...), custom_call_target="tpu_custom_call" | custom-call | flops 10000000000 | bytes 16777216 | tf_op jit(solution)/shard_map/project_out/pallas_call | solution.py:328
  44.3 5.0 %all-to-all-start.3 = ((f32[16,16,128]{2,1,0:T(8,128)}), f32[16,16,128]{2,1,0:T(8,128)S(1)}, u32[]{:S(2)}, u32[]{:S(2)}) async-start(f32[16,16,128]{2,1,0:T(8,128)} %get-tuple-element.25), calls=%async_computation.3 | async-start | bytes 262144 | tf_op jit(solution)/shard_map/all_to_all | solution.py:418
  49.3 0.1 collective-permute-start.1
  49.4 1.2 %collective-permute-done.1.other_ref = f32[16,1024]{1,0:T(8,128)S(1)} collective-permute-done((f32[16,1024]{1,0:T(8,128)S(1)}, f32[16,1024]{1,0:T(8,128)S(1)}, u32[]{:S(2)}, u32[]{:S(2)}) %collective-permute-start.1) | collective-permute-done | bytes 65568 | tf_op jit(solution)/shard_map/ppermute | solution.py:401
  50.6 3.0 %all-to-all-done.3.partials_ref = f32[16,16,128]{2,1,0:T(8,128)S(1)} async-done(((f32[16,16,128]{2,1,0:T(8,128)}), f32[16,16,128]{2,1,0:T(8,128)S(1)}, u32[]{:S(2)}, u32[]{:S(2)}) %all-to-all-start.3) | async-done | bytes 131104 | tf_op jit(solution)/shard_map/all_to_all | solution.py:418
  53.5 0.4 add_up.1
  53.9 8.7 %all_to_all.28.parts_ref = bf16[8,2,1024]{2,1,0:T(2,128)(2,1)S(1)} all-to-all(bf16[8,2,1024]{2,1,0:T(2,128)(2,1)S(1)} %add_up.1), channel_id=1, replica_groups={{10,2,12,4,14,6,8,0},{11,3,13,5,15,7,9,1},{26,18,28,20,30,22,24,16},{27..., dimensions={0} | all-to-all | bytes 65536 | tf_op jit(solution)/shard_map/all_to_all | solution.py:411
  62.6 0.7 %add_rows.1 = bf16[2,8192]{1,0:T(2,128)(2,1)} custom-call(bf16[2,8192]{1,0:T(2,128)(2,1)S(1)} %copy-done, bf16[8,2,1024]{2,1,0:T(2,128)(2,1)S(1)} %all_to_all.28.parts_ref), custom_call_target="tpu_custom_call" | custom-call | bytes 98304 | tf_op jit(solution)/shard_map/add_rows/pallas_call | solution.py:391
  (28 shorter events, 0.1 us)
Async XLA Ops:
  0.0 0.7 %copy-start.6 = (bf16[8192]{0:T(1024)(128)(2,1)S(1)}, bf16[8192]{0:T(1024)(128)(2,1)}, u32[]{:S(2)}) copy-start(bf16[8192]{0:T(1024)(128)(2,1)} %param.12) | copy-start | bytes 49156
  0.0 0.8 %copy-start = (bf16[2,8192]{1,0:T(2,128)(2,1)S(1)}, bf16[2,8192]{1,0:T(2,128)(2,1)}, u32[]{:S(2)}) copy-start(bf16[2,8192]{1,0:T(2,128)(2,1)} %hidden_ref.3) | copy-start | bytes 98308
  0.0 17.1 %slice-start.4 = ((s8[10485760]{0:T(1024)(128)(4,1)}), s8[4194304]{0:T(1024)(128)(4,1)S(1)}, s32[]{:S(2)}) async-start(s8[10485760]{0:T(1024)(128)(4,1)} %bitcast.3), calls=%async_computation.9 | async-start | bytes 8388608
  0.8 14.8 %copy-start.1 = (s32[2]{0:T(128)S(1)}, s32[2]{0:T(128)}, u32[]{:S(2)}) copy-start(s32[2]{0:T(128)} %lengths_ref.1) | copy-start | bytes 28
  0.8 14.8 %copy-start.2 = (s32[2]{0:T(128)S(1)}, s32[2]{0:T(128)}, u32[]{:S(2)}) copy-start(s32[2]{0:T(128)} %slots_ref.1) | copy-start | bytes 28
  0.8 14.8 %copy-start.3 = (s32[1,2]{1,0:T(1,128)S(1)}, s32[1,2]{1,0:T(1,128)}, u32[]{:S(2)}) copy-start(s32[1,2]{1,0:T(1,128)} %requests_ref.1) | copy-start | bytes 28
  0.8 16.3 %slice-start.5 = ((s8[10485760]{0:T(1024)(128)(4,1)}), s8[4194304]{0:T(1024)(128)(4,1)S(1)}, s32[]{:S(2)}) async-start(s8[10485760]{0:T(1024)(128)(4,1)} %bitcast.3), calls=%async_computation.10 | async-start | bytes 8388608
  0.8 16.3 %slice-start.6 = ((s8[10485760]{0:T(1024)(128)(4,1)}), s8[2097152]{0:T(1024)(128)(4,1)S(1)}, s32[]{:S(2)}) async-start(s8[10485760]{0:T(1024)(128)(4,1)} %bitcast.3), calls=%async_computation.11 | async-start | bytes 4194304
  15.6 1.5 %collective-permute-start = (bf16[8,2,8192]{2,1,0:T(2,128)(2,1)S(1)}, bf16[8,2,8192]{2,1,0:T(2,128)(2,1)S(1)}, u32[]{:S(2)}, u32[]{:S(2)}) collective-permute-start(bf16[8,2,8192]{2,1,0:T(2,128)(2,1)S(1)} %all_to_all.25.near_ref), channel_id=1, source_target_pairs={{0,1},{1,0},{2,3},{3,2},{4,5},{5,4},{6,7},{7,6},{8,9},{9,8},{10,11... | collective-permute-start | bytes 786440 | tf_op jit(solution)/shard_map/ppermute | solution.py:401
  17.1 10.2 %copy-start.4 = (bf16[2,256,1024]{2,1,0:T(8,128)(2,1)S(1)}, bf16[2,256,1024]{2,1,0:T(8,128)(2,1)}, u32[]{:S(2)}) copy-start(bf16[2,256,1024]{2,1,0:T(8,128)(2,1)} %key_ref.1) | copy-start | bytes 3145732
  17.1 10.2 %copy-start.5 = (bf16[2,256,1024]{2,1,0:T(8,128)(2,1)S(1)}, bf16[2,256,1024]{2,1,0:T(8,128)(2,1)}, u32[]{:S(2)}) copy-start(bf16[2,256,1024]{2,1,0:T(8,128)(2,1)} %value_ref.1) | copy-start | bytes 3145732
  17.1 23.6 %slice-start = ((s8[16777216]{0:T(1024)(128)(4,1)}), s8[4194304]{0:T(1024)(128)(4,1)S(1)}, s32[]{:S(2)}) async-start(s8[16777216]{0:T(1024)(128)(4,1)} %bitcast.1), calls=%async_computation.5 | async-start | bytes 8388608
  17.2 23.6 %slice-start.1 = ((s8[16777216]{0:T(1024)(128)(4,1)}), s8[4194304]{0:T(1024)(128)(4,1)S(1)}, s32[]{:S(2)}) async-start(s8[16777216]{0:T(1024)(128)(4,1)} %bitcast.1), calls=%async_computation.6 | async-start | bytes 8388608
  17.2 23.6 %slice-start.7 = ((s8[8388608]{0:T(1024)(128)(4,1)}), s8[4194304]{0:T(1024)(128)(4,1)S(1)}, s32[]{:S(2)}) async-start(s8[8388608]{0:T(1024)(128)(4,1)} %bitcast.5), calls=%async_computation.12 | async-start | bytes 8388608
  17.2 23.5 %slice-start.9 = ((s8[8388608]{0:T(1024)(128)(4,1)}), s8[4194304]{0:T(1024)(128)(4,1)S(1)}, s32[]{:S(2)}) async-start(s8[8388608]{0:T(1024)(128)(4,1)} %bitcast.8), calls=%async_computation.14 | async-start | bytes 8388608
  27.4 13.4 %slice-start.2 = ((s8[16777216]{0:T(1024)(128)(4,1)}), s8[4194304]{0:T(1024)(128)(4,1)S(1)}, s32[]{:S(2)}) async-start(s8[16777216]{0:T(1024)(128)(4,1)} %bitcast.1), calls=%async_computation.7 | async-start | bytes 8388608
  27.4 13.4 %slice-start.3 = ((s8[16777216]{0:T(1024)(128)(4,1)}), s8[4194304]{0:T(1024)(128)(4,1)S(1)}, s32[]{:S(2)}) async-start(s8[16777216]{0:T(1024)(128)(4,1)} %bitcast.1), calls=%async_computation.8 | async-start | bytes 8388608
  27.4 13.4 %slice-start.8 = ((s8[8388608]{0:T(1024)(128)(4,1)}), s8[4194304]{0:T(1024)(128)(4,1)S(1)}, s32[]{:S(2)}) async-start(s8[8388608]{0:T(1024)(128)(4,1)} %bitcast.5), calls=%async_computation.13 | async-start | bytes 8388608
  27.4 13.4 %slice-start.10 = ((s8[8388608]{0:T(1024)(128)(4,1)}), s8[4194304]{0:T(1024)(128)(4,1)S(1)}, s32[]{:S(2)}) async-start(s8[8388608]{0:T(1024)(128)(4,1)} %bitcast.8), calls=%async_computation.15 | async-start | bytes 8388608
  44.3 9.2 %all-to-all-start.3 = ((f32[16,16,128]{2,1,0:T(8,128)}), f32[16,16,128]{2,1,0:T(8,128)S(1)}, u32[]{:S(2)}, u32[]{:S(2)}) async-start(f32[16,16,128]{2,1,0:T(8,128)} %get-tuple-element.25), calls=%async_computation.3 | async-start | bytes 262144 | tf_op jit(solution)/shard_map/all_to_all | solution.py:418
  49.3 1.3 %collective-permute-start.1 = (f32[16,1024]{1,0:T(8,128)S(1)}, f32[16,1024]{1,0:T(8,128)S(1)}, u32[]{:S(2)}, u32[]{:S(2)}) collective-permute-start(f32[16,1024]{1,0:T(8,128)S(1)} %get-tuple-element.24), channel_id=1, source_target_pairs={{0,1},{1,0},{2,3},{3,2},{4,5},{5,4},{6,7},{7,6},{8,9},{9,8},{10,11... | collective-permute-start | bytes 196616 | tf_op jit(solution)/shard_map/ppermute | solution.py:401

commit v22 on v20

--- a/solution.py
+++ b/solution.py
@@ -240,7 +240,7 @@
     )(lengths, slots, requests, near, frequency)
 
 
-def project_qkv(lined, far, weight, adapter, chunk=1024):
+def project_qkv(lined, far, weight, adapter, chunk=4096):
     groups, rows, _ = far.shape
     depth, width = weight.shape
     half = groups * rows
@@ -280,7 +280,7 @@
     )(lined, far, weight, adapter)
 
 
-def project_out(gathered, adapter, weight, down_store, up_store, chunk=1024):
+def project_out(gathered, adapter, weight, down_store, up_store, chunk=2048):
     groups, rows, features = gathered.shape
     count = groups * rows
     rank, depth = down_store.shape[1:]

time: 62.1 us -> 62 us (level)
  no operation moved by 1% of the time
where the time goes in v22:
time: 62 us; the launch traced here: 61.6 us
  blocking collectives  51.9 us (84%)
  Pallas kernels  7.87 us (13%)
  local copies, waits for them, and re-layouts  0.84 us (1%)
  waiting for transfers between devices  0.79 us (1%)
    all_to_all x4, blocking collectives, exchange(): lax.all_to_all(blocks, 'mp', split_axis=0, concat_axis=0, tiled=True, axi...  43.7 us
    all_to_all x1, blocking collectives, exchange_all(): lax.all_to_all(blocks, ('mp', 'batch'), split_axis=0, concat_axis=0, tile...  8.23 us
    pallas_call x1, Pallas kernels, project_out(): call(kernel, 'project_out', (jax.ShapeDtypeStruct((groups, count, LANES),...  3.26 us
    pallas_call x1, Pallas kernels, project_qkv(): call(kernel, 'project_qkv', jax.ShapeDtypeStruct((2 * groups, rows, width...  1.87 us
  transfers between devices with their start and end apart: 1, of which 1 were waited for; matrix products, arithmetic and copies ran while one was open for 0% of the time, Pallas kernels for 1%

profile of v22, /device:TPU:0, one launch (start us, length us, event | category | flops | bytes accessed | tf_op | source)
XLA Modules:
  0.0 61.6 jit_solution(4786862344763140891)
XLA Ops:
  0.0 0.7 %copy-done.6 = bf16[8192]{0:T(1024)(128)(2,1)S(1)} copy-done((bf16[8192]{0:T(1024)(128)(2,1)S(1)}, bf16[8192]{0:T(1024)(128)(2,1)}, u32[]{:S(2)}) %copy-start.6) | copy-done | bytes 16408
  0.7 0.0 copy-done
  0.8 0.0 slice-start.5
  0.8 0.0 slice-start.6
  0.8 0.2 norm_rows.1
  1.0 14.6 %all_to_all.25.near_ref = bf16[8,2,8192]{2,1,0:T(2,128)(2,1)S(1)} all-to-all(bf16[8,2,8192]{2,1,0:T(2,128)(2,1)S(1)} %norm_rows.1), channel_id=1, replica_groups={{10,2,12,4,14,6,8,0},{11,3,13,5,15,7,9,1},{26,18,28,20,30,22,24,16},{27..., dimensions={0} | all-to-all | bytes 524288 | tf_op jit(solution)/shard_map/all_to_all | solution.py:402
  15.6 0.0 collective-permute-start
  15.6 0.0 copy-done.1
  15.6 0.0 copy-done.2
  15.6 0.0 copy-done.3
  15.6 0.7 %turns.1 = (bf16[16,8192]{1,0:T(8,128)(2,1)S(1)}, f32[2,128]{1,0:T(2,128)S(1)}, f32[2,128]{1,0:T(2,128)S(1)}, f32[2,256]{1,0:T(2,128)S(1)}, bf16[2,128]{1,0:T(2,128)(2,1)S(1)}) custom-call(s32[2]{0:T(128)S(1)} %copy-done.1, s32[2]{0:T(128)S(1)} %copy-done.2, s32[1,2]{1,0:T(1,128)S(1)} %copy-done.3, bf16[8,2,8192]{2,1,0:T(2,128)(2,1)S(1)} %all_to_all.25.near_ref, ...), custom_call_target="tpu_custom_call" | custom-call | bytes 524288 | tf_op jit(solution)/shard_map/turns/pallas_call | solution.py:228
  16.3 0.8 %collective-permute-done.far_ref = bf16[8,2,8192]{2,1,0:T(2,128)(2,1)S(1)} collective-permute-done((bf16[8,2,8192]{2,1,0:T(2,128)(2,1)S(1)}, bf16[8,2,8192]{2,1,0:T(2,128)(2,1)S(1)}, u32[]{:S(2)}, u32[]{:S(2)}) %collective-permute-start) | collective-permute-done | bytes 262176 | tf_op jit(solution)/shard_map/ppermute | solution.py:392
  17.1 0.0 slice-done.4
  17.1 0.0 slice-done.5
  17.1 0.0 copy-start.4
  17.1 0.0 copy-start.5
  17.1 0.0 slice-start
  17.2 0.0 slice-start.1
  17.2 0.0 slice-start.7
  17.2 0.0 slice-start.9
  17.2 1.9 %project_qkv.1 = bf16[16,2,768]{2,1,0:T(2,128)(2,1)S(1)} custom-call(bf16[16,8192]{1,0:T(8,128)(2,1)S(1)} %get-tuple-element.15.lined_ref, bf16[8,2,8192]{2,1,0:T(2,128)(2,1)S(1)} %collective-permute-done.far_ref, bf16[8192,640]{1,0:T(8,128)(2,1)S(1)} %bitcast.4, bf16[2,128]{1,0:T(2,128)(2,1)S(1)} %get-tuple-element.16.adapter_ref), custom_call_target="tpu_custom_call" | custom-call | flops 10000000000 | bytes 10485760 | tf_op jit(solution)/shard_map/project_qkv/pallas_call | solution.py:272
  19.1 8.2 %all_to_all.26.mixed_ref = bf16[16,2,768]{2,1,0:T(2,128)(2,1)S(1)} all-to-all(bf16[16,2,768]{2,1,0:T(2,128)(2,1)S(1)} %project_qkv.1), channel_id=1, replica_groups={{11,10,3,2,13,12,5,4,15,14,7,6,9,8,1,0},{27,26,19,18,29,28,21,20,31,30,..., dimensions={0} | all-to-all | bytes 98304 | tf_op jit(solution)/shard_map/all_to_all | solution.py:409
  27.3 0.0 slice-start.8
  27.3 0.0 slice-start.10
  27.3 0.8 %attend.1 = (bf16[8,2,8192]{2,1,0:T(2,128)(2,1)S(1)}, s32[1,128]{1,0:T(1,128)S(1)}) custom-call(bf16[16,2,768]{2,1,0:T(2,128)(2,1)S(1)} %all_to_all.26.mixed_ref, f32[2,128]{1,0:T(2,128)S(1)} %get-tuple-element.17.cosine_ref, f32[2,128]{1,0:T(2,128)S(1)} %get-tuple-element.18.sine_ref, f32[2,256]{1,0:T(2,128)S(1)} %get-tuple-element.19.mask_ref, ...), custom_call_target="tpu_custom_call" | custom-call | flops 10000000000 | bytes 2097152 | tf_op jit(solution)/shard_map/attend/pallas_call | solution.py:509
  28.1 12.2 %all_to_all.27.gathered_ref = bf16[8,2,8192]{2,1,0:T(2,128)(2,1)S(1)} all-to-all(bf16[8,2,8192]{2,1,0:T(2,128)(2,1)S(1)} %get-tuple-element.21), channel_id=1, replica_groups={{10,2,12,4,14,6,8,0},{11,3,13,5,15,7,9,1},{26,18,28,20,30,22,24,16},{27..., dimensions={0} | all-to-all | bytes 524288 | tf_op jit(solution)/shard_map/all_to_all | solution.py:402
  40.3 0.0 slice-done.1
  40.4 3.3 %project_out.1 = (f32[8,16,128]{2,1,0:T(8,128)S(1)}, f32[16,1024]{1,0:T(8,128)S(1)}, bf16[1024,1024]{1,0:T(8,128)(2,1)S(1)}) custom-call(s32[1,128]{1,0:T(1,128)S(1)} %get-tuple-element.20.adapter_ref, bf16[8,2,8192]{2,1,0:T(2,128)(2,1)S(1)} %all_to_all.27.gathered_ref, bf16[8192,1024]{1,0:T(8,128)(2,1)S(1)} %bitcast.2, bf16[64,64,1024]{2,1,0:T(8,128)(2,1)S(1)} %bitcast.7, ...), custom_call_target="tpu_custom_call" | custom-call | flops 10000000000 | bytes 16777216 | tf_op jit(solution)/shard_map/project_out/pallas_call | solution.py:322
  43.6 8.6 %all_to_all.28.partials_ref = f32[8,16,128]{2,1,0:T(8,128)S(1)} all-to-all(f32[8,16,128]{2,1,0:T(8,128)S(1)} %get-tuple-element.23), channel_id=1, replica_groups={{10,2,12,4,14,6,8,0},{11,3,13,5,15,7,9,1},{26,18,28,20,30,22,24,16},{27..., dimensions={0} | all-to-all | bytes 131072 | tf_op jit(solution)/shard_map/all_to_all | solution.py:402
  52.2 0.4 add_up.1
  52.6 8.4 %all_to_all.29.parts_ref = bf16[8,2,1024]{2,1,0:T(2,128)(2,1)S(1)} all-to-all(bf16[8,2,1024]{2,1,0:T(2,128)(2,1)S(1)} %add_up.1), channel_id=1, replica_groups={{10,2,12,4,14,6,8,0},{11,3,13,5,15,7,9,1},{26,18,28,20,30,22,24,16},{27..., dimensions={0} | all-to-all | bytes 65536 | tf_op jit(solution)/shard_map/all_to_all | solution.py:402
  61.0 0.7 %add_rows.1 = bf16[2,8192]{1,0:T(2,128)(2,1)} custom-call(bf16[2,8192]{1,0:T(2,128)(2,1)S(1)} %copy-done, bf16[8,2,1024]{2,1,0:T(2,128)(2,1)S(1)} %all_to_all.29.parts_ref), custom_call_target="tpu_custom_call" | custom-call | bytes 98304 | tf_op jit(solution)/shard_map/add_rows/pallas_call | solution.py:382
  (25 shorter events, 0.1 us)
Async XLA Ops:
  0.0 0.7 %copy-start.6 = (bf16[8192]{0:T(1024)(128)(2,1)S(1)}, bf16[8192]{0:T(1024)(128)(2,1)}, u32[]{:S(2)}) copy-start(bf16[8192]{0:T(1024)(128)(2,1)} %param.12) | copy-start | bytes 49156
  0.0 0.8 %copy-start = (bf16[2,8192]{1,0:T(2,128)(2,1)S(1)}, bf16[2,8192]{1,0:T(2,128)(2,1)}, u32[]{:S(2)}) copy-start(bf16[2,8192]{1,0:T(2,128)(2,1)} %hidden_ref.3) | copy-start | bytes 98308
  0.0 17.1 %slice-start.4 = ((s8[10485760]{0:T(1024)(128)(4,1)}), s8[4194304]{0:T(1024)(128)(4,1)S(1)}, s32[]{:S(2)}) async-start(s8[10485760]{0:T(1024)(128)(4,1)} %bitcast.3), calls=%async_computation.9 | async-start | bytes 8388608
  0.8 14.8 %copy-start.1 = (s32[2]{0:T(128)S(1)}, s32[2]{0:T(128)}, u32[]{:S(2)}) copy-start(s32[2]{0:T(128)} %lengths_ref.1) | copy-start | bytes 28
  0.8 14.8 %copy-start.2 = (s32[2]{0:T(128)S(1)}, s32[2]{0:T(128)}, u32[]{:S(2)}) copy-start(s32[2]{0:T(128)} %slots_ref.1) | copy-start | bytes 28
  0.8 14.8 %copy-start.3 = (s32[1,2]{1,0:T(1,128)S(1)}, s32[1,2]{1,0:T(1,128)}, u32[]{:S(2)}) copy-start(s32[1,2]{1,0:T(1,128)} %requests_ref.1) | copy-start | bytes 28
  0.8 16.3 %slice-start.5 = ((s8[10485760]{0:T(1024)(128)(4,1)}), s8[4194304]{0:T(1024)(128)(4,1)S(1)}, s32[]{:S(2)}) async-start(s8[10485760]{0:T(1024)(128)(4,1)} %bitcast.3), calls=%async_computation.10 | async-start | bytes 8388608
  0.8 16.3 %slice-start.6 = ((s8[10485760]{0:T(1024)(128)(4,1)}), s8[2097152]{0:T(1024)(128)(4,1)S(1)}, s32[]{:S(2)}) async-start(s8[10485760]{0:T(1024)(128)(4,1)} %bitcast.3), calls=%async_computation.11 | async-start | bytes 4194304
  15.6 1.5 %collective-permute-start = (bf16[8,2,8192]{2,1,0:T(2,128)(2,1)S(1)}, bf16[8,2,8192]{2,1,0:T(2,128)(2,1)S(1)}, u32[]{:S(2)}, u32[]{:S(2)}) collective-permute-start(bf16[8,2,8192]{2,1,0:T(2,128)(2,1)S(1)} %all_to_all.25.near_ref), channel_id=1, source_target_pairs={{0,1},{1,0},{2,3},{3,2},{4,5},{5,4},{6,7},{7,6},{8,9},{9,8},{10,11... | collective-permute-start | bytes 786440 | tf_op jit(solution)/shard_map/ppermute | solution.py:392
  17.1 10.2 %copy-start.4 = (bf16[2,256,1024]{2,1,0:T(8,128)(2,1)S(1)}, bf16[2,256,1024]{2,1,0:T(8,128)(2,1)}, u32[]{:S(2)}) copy-start(bf16[2,256,1024]{2,1,0:T(8,128)(2,1)} %key_ref.1) | copy-start | bytes 3145732
  17.1 10.2 %copy-start.5 = (bf16[2,256,1024]{2,1,0:T(8,128)(2,1)S(1)}, bf16[2,256,1024]{2,1,0:T(8,128)(2,1)}, u32[]{:S(2)}) copy-start(bf16[2,256,1024]{2,1,0:T(8,128)(2,1)} %value_ref.1) | copy-start | bytes 3145732
  17.1 23.1 %slice-start = ((s8[16777216]{0:T(1024)(128)(4,1)}), s8[4194304]{0:T(1024)(128)(4,1)S(1)}, s32[]{:S(2)}) async-start(s8[16777216]{0:T(1024)(128)(4,1)} %bitcast.1), calls=%async_computation.5 | async-start | bytes 8388608
  17.2 23.1 %slice-start.1 = ((s8[16777216]{0:T(1024)(128)(4,1)}), s8[4194304]{0:T(1024)(128)(4,1)S(1)}, s32[]{:S(2)}) async-start(s8[16777216]{0:T(1024)(128)(4,1)} %bitcast.1), calls=%async_computation.6 | async-start | bytes 8388608
  17.2 23.1 %slice-start.7 = ((s8[8388608]{0:T(1024)(128)(4,1)}), s8[4194304]{0:T(1024)(128)(4,1)S(1)}, s32[]{:S(2)}) async-start(s8[8388608]{0:T(1024)(128)(4,1)} %bitcast.5), calls=%async_computation.12 | async-start | bytes 8388608
  17.2 23.1 %slice-start.9 = ((s8[8388608]{0:T(1024)(128)(4,1)}), s8[4194304]{0:T(1024)(128)(4,1)S(1)}, s32[]{:S(2)}) async-start(s8[8388608]{0:T(1024)(128)(4,1)} %bitcast.8), calls=%async_computation.14 | async-start | bytes 8388608
  27.3 13.0 %slice-start.2 = ((s8[16777216]{0:T(1024)(128)(4,1)}), s8[4194304]{0:T(1024)(128)(4,1)S(1)}, s32[]{:S(2)}) async-start(s8[16777216]{0:T(1024)(128)(4,1)} %bitcast.1), calls=%async_computation.7 | async-start | bytes 8388608
  27.3 13.0 %slice-start.3 = ((s8[16777216]{0:T(1024)(128)(4,1)}), s8[4194304]{0:T(1024)(128)(4,1)S(1)}, s32[]{:S(2)}) async-start(s8[16777216]{0:T(1024)(128)(4,1)} %bitcast.1), calls=%async_computation.8 | async-start | bytes 8388608
  27.3 13.0 %slice-start.8 = ((s8[8388608]{0:T(1024)(128)(4,1)}), s8[4194304]{0:T(1024)(128)(4,1)S(1)}, s32[]{:S(2)}) async-start(s8[8388608]{0:T(1024)(128)(4,1)} %bitcast.5), calls=%async_computation.13 | async-start | bytes 8388608
  27.3 13.0 %slice-start.10 = ((s8[8388608]{0:T(1024)(128)(4,1)}), s8[4194304]{0:T(1024)(128)(4,1)S(1)}, s32[]{:S(2)}) async-start(s8[8388608]{0:T(1024)(128)(4,1)} %bitcast.8), calls=%async_computation.15 | async-start | bytes 8388608

commit v23 on v22

--- a/solution.py
+++ b/solution.py
@@ -288,22 +288,27 @@
 
     def kernel(
         adapter_ref, gathered_ref, weight_ref, down_ref, up_ref, partial_ref, base_ref, picked_ref,
-        rows_ref, held_ref,
+        rows_ref, held_ref, ids_ref, sem,
     ):
-        base = jnp.zeros((count, columns), jnp.float32)
-        chunks = features // chunk
-        for k in range(chunks):
+        fetch = pltpu.make_async_copy(adapter_ref, ids_ref, sem)
+        fetch.start()
+
+        def times_weight(k):
             part = pl.ds(k * chunk, chunk)
-            for j in range(groups):
-                rows_ref[pl.ds(j * rows, rows), part] = gathered_ref[j, :, part]
-            base = base + jnp.dot(
+            return jnp.dot(
                 rows_ref[:, part], weight_ref[part, :], preferred_element_type=jnp.float32
             )
-            for r in range(k * count // chunks, (k + 1) * count // chunks):
-                chosen = adapter_ref[0, r]
-                held_ref[pl.ds(r * rank, rank)] = down_ref[chosen]
-                picked_ref[pl.ds(r * rank, rank)] = up_ref[chosen]
-        base_ref[...] = base
+
+        def pick(store_ref, target_ref, first, last):
+            for r in range(first, last):
+                target_ref[pl.ds(r * rank, rank)] = store_ref[ids_ref[0, r]]
+
+        for j in range(groups):
+            rows_ref[pl.ds(j * rows, rows)] = gathered_ref[j]
+        base = times_weight(0)
+        fetch.wait()
+        pick(down_ref, held_ref, 0, count)
+        base = base + times_weight(1)
         start = pl.multiple_of(lax.axis_index("mp") * depth, depth)
         every = lax.dot_general(
             rows_ref[:, pl.ds(start, depth)],
@@ -318,6 +323,11 @@
             total = total + jnp.where(row == (lane + s) // rank, every[:, s : s + LANES], 0.0)
         for c in range(groups):
             partial_ref[c] = total
+        left = features // chunk - 2
+        for k in range(left):
+            pick(up_ref, picked_ref, k * count // left, (k + 1) * count // left)
+            base = base + times_weight(k + 2)
+        base_ref[...] = base
 
     return call(
         kernel,
@@ -327,13 +337,15 @@
             jax.ShapeDtypeStruct((count, columns), jnp.float32),
             pltpu.VMEM((count * rank, columns), up_store.dtype),
         ),
-        [SMEM] + [VMEM] * 4,
+        [ANY] + [VMEM] * 4,
         weight.size * 2,
-        limit=5 * MIB,
+        limit=8 * MIB,
         flops=LONG,
         scratch_shapes=[
             pltpu.VMEM((count, features), gathered.dtype),
             pltpu.VMEM((count * rank, depth), down_store.dtype),
+            pltpu.SMEM(adapter.shape, adapter.dtype),
+            pltpu.SemaphoreType.DMA,
         ],
     )(adapter, gathered, weight, down_store, up_store)
 

time: 62 us -> 62 us (level)
  no operation moved by 1% of the time
where the time goes in v23:
time: 62 us; the launch traced here: 61.6 us
  blocking collectives  51.8 us (84%)
  Pallas kernels  7.99 us (13%)
  local copies, waits for them, and re-layouts  0.84 us (1%)
  waiting for transfers between devices  0.79 us (1%)
    all_to_all x4, blocking collectives, exchange(): lax.all_to_all(blocks, 'mp', split_axis=0, concat_axis=0, tiled=True, axi...  43.5 us
    all_to_all x1, blocking collectives, exchange_all(): lax.all_to_all(blocks, ('mp', 'batch'), split_axis=0, concat_axis=0, tile...  8.23 us
    pallas_call x1, Pallas kernels, project_out(): call(kernel, 'project_out', (jax.ShapeDtypeStruct((groups, count, LANES),...  3.38 us
    pallas_call x1, Pallas kernels, project_qkv(): call(kernel, 'project_qkv', jax.ShapeDtypeStruct((2 * groups, rows, width...  1.87 us
  transfers between devices with their start and end apart: 1, of which 1 were waited for; matrix products, arithmetic and copies ran while one was open for 0% of the time, Pallas kernels for 1%

profile of v23, /device:TPU:0, one launch (start us, length us, event | category | flops | bytes accessed | tf_op | source)
XLA Modules:
  0.0 61.6 jit_solution(5463767889241824863)
XLA Ops:
  0.0 0.7 %copy-done.6 = bf16[8192]{0:T(1024)(128)(2,1)S(1)} copy-done((bf16[8192]{0:T(1024)(128)(2,1)S(1)}, bf16[8192]{0:T(1024)(128)(2,1)}, u32[]{:S(2)}) %copy-start.6) | copy-done | bytes 16408
  0.7 0.0 copy-done
  0.8 0.0 slice-start.5
  0.8 0.0 slice-start.6
  0.8 0.2 norm_rows.1
  1.0 14.6 %all_to_all.25.near_ref = bf16[8,2,8192]{2,1,0:T(2,128)(2,1)S(1)} all-to-all(bf16[8,2,8192]{2,1,0:T(2,128)(2,1)S(1)} %norm_rows.1), channel_id=1, replica_groups={{10,2,12,4,14,6,8,0},{11,3,13,5,15,7,9,1},{26,18,28,20,30,22,24,16},{27..., dimensions={0} | all-to-all | bytes 524288 | tf_op jit(solution)/shard_map/all_to_all | solution.py:414
  15.6 0.0 collective-permute-start
  15.6 0.0 copy-done.1
  15.6 0.0 copy-done.2
  15.6 0.0 copy-done.3
  15.6 0.7 %turns.1 = (bf16[16,8192]{1,0:T(8,128)(2,1)S(1)}, f32[2,128]{1,0:T(2,128)S(1)}, f32[2,128]{1,0:T(2,128)S(1)}, f32[2,256]{1,0:T(2,128)S(1)}, bf16[2,128]{1,0:T(2,128)(2,1)S(1)}) custom-call(s32[2]{0:T(128)S(1)} %copy-done.1, s32[2]{0:T(128)S(1)} %copy-done.2, s32[1,2]{1,0:T(1,128)S(1)} %copy-done.3, bf16[8,2,8192]{2,1,0:T(2,128)(2,1)S(1)} %all_to_all.25.near_ref, ...), custom_call_target="tpu_custom_call" | custom-call | bytes 524288 | tf_op jit(solution)/shard_map/turns/pallas_call | solution.py:228
  16.3 0.8 %collective-permute-done.far_ref = bf16[8,2,8192]{2,1,0:T(2,128)(2,1)S(1)} collective-permute-done((bf16[8,2,8192]{2,1,0:T(2,128)(2,1)S(1)}, bf16[8,2,8192]{2,1,0:T(2,128)(2,1)S(1)}, u32[]{:S(2)}, u32[]{:S(2)}) %collective-permute-start) | collective-permute-done | bytes 262176 | tf_op jit(solution)/shard_map/ppermute | solution.py:404
  17.1 0.0 slice-done.4
  17.1 0.0 slice-done.5
  17.1 0.0 copy-start.4
  17.1 0.0 copy-start.5
  17.1 0.0 slice-start
  17.2 0.0 slice-start.1
  17.2 0.0 slice-start.7
  17.2 0.0 slice-start.9
  17.2 1.9 %project_qkv.1 = bf16[16,2,768]{2,1,0:T(2,128)(2,1)S(1)} custom-call(bf16[16,8192]{1,0:T(8,128)(2,1)S(1)} %get-tuple-element.15.lined_ref, bf16[8,2,8192]{2,1,0:T(2,128)(2,1)S(1)} %collective-permute-done.far_ref, bf16[8192,640]{1,0:T(8,128)(2,1)S(1)} %bitcast.4, bf16[2,128]{1,0:T(2,128)(2,1)S(1)} %get-tuple-element.16.adapter_ref), custom_call_target="tpu_custom_call" | custom-call | flops 10000000000 | bytes 10485760 | tf_op jit(solution)/shard_map/project_qkv/pallas_call | solution.py:272
  19.1 8.2 %all_to_all.26.mixed_ref = bf16[16,2,768]{2,1,0:T(2,128)(2,1)S(1)} all-to-all(bf16[16,2,768]{2,1,0:T(2,128)(2,1)S(1)} %project_qkv.1), channel_id=1, replica_groups={{11,10,3,2,13,12,5,4,15,14,7,6,9,8,1,0},{27,26,19,18,29,28,21,20,31,30,..., dimensions={0} | all-to-all | bytes 98304 | tf_op jit(solution)/shard_map/all_to_all | solution.py:421
  27.3 0.0 slice-start.8
  27.3 0.0 slice-start.10
  27.3 0.8 %attend.1 = (bf16[8,2,8192]{2,1,0:T(2,128)(2,1)S(1)}, s32[1,128]{1,0:T(1,128)S(1)}) custom-call(bf16[16,2,768]{2,1,0:T(2,128)(2,1)S(1)} %all_to_all.26.mixed_ref, f32[2,128]{1,0:T(2,128)S(1)} %get-tuple-element.17.cosine_ref, f32[2,128]{1,0:T(2,128)S(1)} %get-tuple-element.18.sine_ref, f32[2,256]{1,0:T(2,128)S(1)} %get-tuple-element.19.mask_ref, ...), custom_call_target="tpu_custom_call" | custom-call | flops 10000000000 | bytes 2097152 | tf_op jit(solution)/shard_map/attend/pallas_call | solution.py:521
  28.1 12.2 %all_to_all.27.gathered_ref = bf16[8,2,8192]{2,1,0:T(2,128)(2,1)S(1)} all-to-all(bf16[8,2,8192]{2,1,0:T(2,128)(2,1)S(1)} %get-tuple-element.21), channel_id=1, replica_groups={{10,2,12,4,14,6,8,0},{11,3,13,5,15,7,9,1},{26,18,28,20,30,22,24,16},{27..., dimensions={0} | all-to-all | bytes 524288 | tf_op jit(solution)/shard_map/all_to_all | solution.py:414
  40.3 0.0 slice-done
  40.4 3.4 %project_out.1 = (f32[8,16,128]{2,1,0:T(8,128)S(1)}, f32[16,1024]{1,0:T(8,128)S(1)}, bf16[1024,1024]{1,0:T(8,128)(2,1)S(1)}) custom-call(s32[1,128]{1,0:T(1,128)S(1)} %get-tuple-element.20.adapter_ref, bf16[8,2,8192]{2,1,0:T(2,128)(2,1)S(1)} %all_to_all.27.gathered_ref, bf16[8192,1024]{1,0:T(8,128)(2,1)S(1)} %bitcast.2, bf16[64,64,1024]{2,1,0:T(8,128)(2,1)S(1)} %bitcast.7, ...), custom_call_target="tpu_custom_call" | custom-call | flops 10000000000 | bytes 16777216 | tf_op jit(solution)/shard_map/project_out/pallas_call | solution.py:332
  43.8 8.5 %all_to_all.28.partials_ref = f32[8,16,128]{2,1,0:T(8,128)S(1)} all-to-all(f32[8,16,128]{2,1,0:T(8,128)S(1)} %get-tuple-element.23), channel_id=1, replica_groups={{10,2,12,4,14,6,8,0},{11,3,13,5,15,7,9,1},{26,18,28,20,30,22,24,16},{27..., dimensions={0} | all-to-all | bytes 131072 | tf_op jit(solution)/shard_map/all_to_all | solution.py:414
  52.2 0.4 add_up.1
  52.6 8.4 %all_to_all.29.parts_ref = bf16[8,2,1024]{2,1,0:T(2,128)(2,1)S(1)} all-to-all(bf16[8,2,1024]{2,1,0:T(2,128)(2,1)S(1)} %add_up.1), channel_id=1, replica_groups={{10,2,12,4,14,6,8,0},{11,3,13,5,15,7,9,1},{26,18,28,20,30,22,24,16},{27..., dimensions={0} | all-to-all | bytes 65536 | tf_op jit(solution)/shard_map/all_to_all | solution.py:414
  61.0 0.7 %add_rows.1 = bf16[2,8192]{1,0:T(2,128)(2,1)} custom-call(bf16[2,8192]{1,0:T(2,128)(2,1)S(1)} %copy-done, bf16[8,2,1024]{2,1,0:T(2,128)(2,1)S(1)} %all_to_all.29.parts_ref), custom_call_target="tpu_custom_call" | custom-call | bytes 98304 | tf_op jit(solution)/shard_map/add_rows/pallas_call | solution.py:394
  (25 shorter events, 0.1 us)
Async XLA Ops:
  0.0 0.7 %copy-start.6 = (bf16[8192]{0:T(1024)(128)(2,1)S(1)}, bf16[8192]{0:T(1024)(128)(2,1)}, u32[]{:S(2)}) copy-start(bf16[8192]{0:T(1024)(128)(2,1)} %param.12) | copy-start | bytes 49156
  0.0 0.8 %copy-start = (bf16[2,8192]{1,0:T(2,128)(2,1)S(1)}, bf16[2,8192]{1,0:T(2,128)(2,1)}, u32[]{:S(2)}) copy-start(bf16[2,8192]{1,0:T(2,128)(2,1)} %hidden_ref.3) | copy-start | bytes 98308
  0.0 17.1 %slice-start.4 = ((s8[10485760]{0:T(1024)(128)(4,1)}), s8[4194304]{0:T(1024)(128)(4,1)S(1)}, s32[]{:S(2)}) async-start(s8[10485760]{0:T(1024)(128)(4,1)} %bitcast.3), calls=%async_computation.9 | async-start | bytes 8388608
  0.8 14.8 %copy-start.1 = (s32[2]{0:T(128)S(1)}, s32[2]{0:T(128)}, u32[]{:S(2)}) copy-start(s32[2]{0:T(128)} %lengths_ref.1) | copy-start | bytes 28
  0.8 14.8 %copy-start.2 = (s32[2]{0:T(128)S(1)}, s32[2]{0:T(128)}, u32[]{:S(2)}) copy-start(s32[2]{0:T(128)} %slots_ref.1) | copy-start | bytes 28
  0.8 14.8 %copy-start.3 = (s32[1,2]{1,0:T(1,128)S(1)}, s32[1,2]{1,0:T(1,128)}, u32[]{:S(2)}) copy-start(s32[1,2]{1,0:T(1,128)} %requests_ref.1) | copy-start | bytes 28
  0.8 16.3 %slice-start.5 = ((s8[10485760]{0:T(1024)(128)(4,1)}), s8[4194304]{0:T(1024)(128)(4,1)S(1)}, s32[]{:S(2)}) async-start(s8[10485760]{0:T(1024)(128)(4,1)} %bitcast.3), calls=%async_computation.10 | async-start | bytes 8388608
  0.8 16.3 %slice-start.6 = ((s8[10485760]{0:T(1024)(128)(4,1)}), s8[2097152]{0:T(1024)(128)(4,1)S(1)}, s32[]{:S(2)}) async-start(s8[10485760]{0:T(1024)(128)(4,1)} %bitcast.3), calls=%async_computation.11 | async-start | bytes 4194304
  15.6 1.5 %collective-permute-start = (bf16[8,2,8192]{2,1,0:T(2,128)(2,1)S(1)}, bf16[8,2,8192]{2,1,0:T(2,128)(2,1)S(1)}, u32[]{:S(2)}, u32[]{:S(2)}) collective-permute-start(bf16[8,2,8192]{2,1,0:T(2,128)(2,1)S(1)} %all_to_all.25.near_ref), channel_id=1, source_target_pairs={{0,1},{1,0},{2,3},{3,2},{4,5},{5,4},{6,7},{7,6},{8,9},{9,8},{10,11... | collective-permute-start | bytes 786440 | tf_op jit(solution)/shard_map/ppermute | solution.py:404
  17.1 10.2 %copy-start.4 = (bf16[2,256,1024]{2,1,0:T(8,128)(2,1)S(1)}, bf16[2,256,1024]{2,1,0:T(8,128)(2,1)}, u32[]{:S(2)}) copy-start(bf16[2,256,1024]{2,1,0:T(8,128)(2,1)} %key_ref.1) | copy-start | bytes 3145732
  17.1 10.2 %copy-start.5 = (bf16[2,256,1024]{2,1,0:T(8,128)(2,1)S(1)}, bf16[2,256,1024]{2,1,0:T(8,128)(2,1)}, u32[]{:S(2)}) copy-start(bf16[2,256,1024]{2,1,0:T(8,128)(2,1)} %value_ref.1) | copy-start | bytes 3145732
  17.1 23.2 %slice-start = ((s8[16777216]{0:T(1024)(128)(4,1)}), s8[4194304]{0:T(1024)(128)(4,1)S(1)}, s32[]{:S(2)}) async-start(s8[16777216]{0:T(1024)(128)(4,1)} %bitcast.1), calls=%async_computation.5 | async-start | bytes 8388608
  17.2 23.1 %slice-start.1 = ((s8[16777216]{0:T(1024)(128)(4,1)}), s8[4194304]{0:T(1024)(128)(4,1)S(1)}, s32[]{:S(2)}) async-start(s8[16777216]{0:T(1024)(128)(4,1)} %bitcast.1), calls=%async_computation.6 | async-start | bytes 8388608
  17.2 23.1 %slice-start.7 = ((s8[8388608]{0:T(1024)(128)(4,1)}), s8[4194304]{0:T(1024)(128)(4,1)S(1)}, s32[]{:S(2)}) async-start(s8[8388608]{0:T(1024)(128)(4,1)} %bitcast.5), calls=%async_computation.12 | async-start | bytes 8388608
  17.2 23.1 %slice-start.9 = ((s8[8388608]{0:T(1024)(128)(4,1)}), s8[4194304]{0:T(1024)(128)(4,1)S(1)}, s32[]{:S(2)}) async-start(s8[8388608]{0:T(1024)(128)(4,1)} %bitcast.8), calls=%async_computation.14 | async-start | bytes 8388608
  27.3 13.0 %slice-start.2 = ((s8[16777216]{0:T(1024)(128)(4,1)}), s8[4194304]{0:T(1024)(128)(4,1)S(1)}, s32[]{:S(2)}) async-start(s8[16777216]{0:T(1024)(128)(4,1)} %bitcast.1), calls=%async_computation.7 | async-start | bytes 8388608
  27.3 13.0 %slice-start.3 = ((s8[16777216]{0:T(1024)(128)(4,1)}), s8[4194304]{0:T(1024)(128)(4,1)S(1)}, s32[]{:S(2)}) async-start(s8[16777216]{0:T(1024)(128)(4,1)} %bitcast.1), calls=%async_computation.8 | async-start | bytes 8388608
  27.3 13.0 %slice-start.8 = ((s8[8388608]{0:T(1024)(128)(4,1)}), s8[4194304]{0:T(1024)(128)(4,1)S(1)}, s32[]{:S(2)}) async-start(s8[8388608]{0:T(1024)(128)(4,1)} %bitcast.5), calls=%async_computation.13 | async-start | bytes 8388608
  27.3 13.0 %slice-start.10 = ((s8[8388608]{0:T(1024)(128)(4,1)}), s8[4194304]{0:T(1024)(128)(4,1)S(1)}, s32[]{:S(2)}) async-start(s8[8388608]{0:T(1024)(128)(4,1)} %bitcast.8), calls=%async_computation.15 | async-start | bytes 8388608

commit v24 on v22

--- a/solution.py
+++ b/solution.py
@@ -240,6 +240,16 @@
     )(lengths, slots, requests, near, frequency)
 
 
+def halves_product(rows, weight_ref, part, cut):
+    return jnp.concatenate(
+        [
+            jnp.dot(rows, weight_ref[part, :cut], preferred_element_type=jnp.float32),
+            jnp.dot(rows, weight_ref[part, cut:], preferred_element_type=jnp.float32),
+        ],
+        1,
+    )
+
+
 def project_qkv(lined, far, weight, adapter, chunk=4096):
     groups, rows, _ = far.shape
     depth, width = weight.shape
@@ -251,11 +261,8 @@
             part = pl.ds(k * chunk, chunk)
             for j in range(groups):
                 far_lined_ref[pl.ds(j * rows, rows), part] = far_ref[j, :, part]
-            total = total + jnp.dot(
-                jnp.concatenate([lined_ref[:, part], far_lined_ref[:, part]]),
-                weight_ref[part, :],
-                preferred_element_type=jnp.float32,
-            )
+            lined = jnp.concatenate([lined_ref[:, part], far_lined_ref[:, part]])
+            total = total + halves_product(lined, weight_ref, part, 3 * LANES)
         core = lax.axis_index("batch")
         adapter = adapter_ref[...]
         for e in range(2):
@@ -296,9 +303,7 @@
             part = pl.ds(k * chunk, chunk)
             for j in range(groups):
                 rows_ref[pl.ds(j * rows, rows), part] = gathered_ref[j, :, part]
-            base = base + jnp.dot(
-                rows_ref[:, part], weight_ref[part, :], preferred_element_type=jnp.float32
-            )
+            base = base + halves_product(rows_ref[:, part], weight_ref, part, columns // 2)
             for r in range(k * count // chunks, (k + 1) * count // chunks):
                 chosen = adapter_ref[0, r]
                 held_ref[pl.ds(r * rank, rank)] = down_ref[chosen]

time: 62 us -> 61.8 us (level)
  no operation moved by 1% of the time
where the time goes in v24:
time: 61.8 us; the launch traced here: 61.5 us
  blocking collectives  51.9 us (84%)
  Pallas kernels  7.7 us (12%)
  local copies, waits for them, and re-layouts  0.84 us (1%)
  waiting for transfers between devices  0.79 us (1%)
    all_to_all x4, blocking collectives, exchange(): lax.all_to_all(blocks, 'mp', split_axis=0, concat_axis=0, tiled=True, axi...  43.7 us
    all_to_all x1, blocking collectives, exchange_all(): lax.all_to_all(blocks, ('mp', 'batch'), split_axis=0, concat_axis=0, tile...  8.23 us
    pallas_call x1, Pallas kernels, project_out(): call(kernel, 'project_out', (jax.ShapeDtypeStruct((groups, count, LANES),...  3.26 us
    pallas_call x1, Pallas kernels, project_qkv(): call(kernel, 'project_qkv', jax.ShapeDtypeStruct((2 * groups, rows, width...  1.7 us
  transfers between devices with their start and end apart: 1, of which 1 were waited for; matrix products, arithmetic and copies ran while one was open for 0% of the time, Pallas kernels for 1%

profile of v24, /device:TPU:0, one launch (start us, length us, event | category | flops | bytes accessed | tf_op | source)
XLA Modules:
  0.0 61.5 jit_solution(13980021708725942891)
XLA Ops:
  0.0 0.7 %copy-done.6 = bf16[8192]{0:T(1024)(128)(2,1)S(1)} copy-done((bf16[8192]{0:T(1024)(128)(2,1)S(1)}, bf16[8192]{0:T(1024)(128)(2,1)}, u32[]{:S(2)}) %copy-start.6) | copy-done | bytes 16408
  0.7 0.0 copy-done
  0.8 0.0 slice-start.5
  0.8 0.0 slice-start.6
  0.8 0.2 norm_rows.1
  1.0 14.6 %all_to_all.25.near_ref = bf16[8,2,8192]{2,1,0:T(2,128)(2,1)S(1)} all-to-all(bf16[8,2,8192]{2,1,0:T(2,128)(2,1)S(1)} %norm_rows.1), channel_id=1, replica_groups={{10,2,12,4,14,6,8,0},{11,3,13,5,15,7,9,1},{26,18,28,20,30,22,24,16},{27..., dimensions={0} | all-to-all | bytes 524288 | tf_op jit(solution)/shard_map/all_to_all | solution.py:407
  15.6 0.0 collective-permute-start
  15.6 0.0 copy-done.1
  15.6 0.0 copy-done.2
  15.6 0.0 copy-done.3
  15.6 0.7 %turns.1 = (bf16[16,8192]{1,0:T(8,128)(2,1)S(1)}, f32[2,128]{1,0:T(2,128)S(1)}, f32[2,128]{1,0:T(2,128)S(1)}, f32[2,256]{1,0:T(2,128)S(1)}, bf16[2,128]{1,0:T(2,128)(2,1)S(1)}) custom-call(s32[2]{0:T(128)S(1)} %copy-done.1, s32[2]{0:T(128)S(1)} %copy-done.2, s32[1,2]{1,0:T(1,128)S(1)} %copy-done.3, bf16[8,2,8192]{2,1,0:T(2,128)(2,1)S(1)} %all_to_all.25.near_ref, ...), custom_call_target="tpu_custom_call" | custom-call | bytes 524288 | tf_op jit(solution)/shard_map/turns/pallas_call | solution.py:228
  16.3 0.8 %collective-permute-done.far_ref = bf16[8,2,8192]{2,1,0:T(2,128)(2,1)S(1)} collective-permute-done((bf16[8,2,8192]{2,1,0:T(2,128)(2,1)S(1)}, bf16[8,2,8192]{2,1,0:T(2,128)(2,1)S(1)}, u32[]{:S(2)}, u32[]{:S(2)}) %collective-permute-start) | collective-permute-done | bytes 262176 | tf_op jit(solution)/shard_map/ppermute | solution.py:397
  17.1 0.0 slice-done.6
  17.1 0.0 copy-start.4
  17.1 0.0 copy-start.5
  17.1 0.0 slice-start
  17.2 0.0 slice-start.1
  17.2 0.0 slice-start.7
  17.2 0.0 slice-start.9
  17.2 1.7 %project_qkv.1 = bf16[16,2,768]{2,1,0:T(2,128)(2,1)S(1)} custom-call(bf16[16,8192]{1,0:T(8,128)(2,1)S(1)} %get-tuple-element.15.lined_ref, bf16[8,2,8192]{2,1,0:T(2,128)(2,1)S(1)} %collective-permute-done.far_ref, bf16[8192,640]{1,0:T(8,128)(2,1)S(1)} %bitcast.4, bf16[2,128]{1,0:T(2,128)(2,1)S(1)} %get-tuple-element.16.adapter_ref), custom_call_target="tpu_custom_call" | custom-call | flops 10000000000 | bytes 10485760 | tf_op jit(solution)/shard_map/project_qkv/pallas_call | solution.py:279
  18.9 8.2 %all_to_all.26.mixed_ref = bf16[16,2,768]{2,1,0:T(2,128)(2,1)S(1)} all-to-all(bf16[16,2,768]{2,1,0:T(2,128)(2,1)S(1)} %project_qkv.1), channel_id=1, replica_groups={{11,10,3,2,13,12,5,4,15,14,7,6,9,8,1,0},{27,26,19,18,29,28,21,20,31,30,..., dimensions={0} | all-to-all | bytes 98304 | tf_op jit(solution)/shard_map/all_to_all | solution.py:414
  27.1 0.0 copy-done.5
  27.1 0.0 slice-start.8
  27.2 0.0 slice-start.10
  27.2 0.8 %attend.1 = (bf16[8,2,8192]{2,1,0:T(2,128)(2,1)S(1)}, s32[1,128]{1,0:T(1,128)S(1)}) custom-call(bf16[16,2,768]{2,1,0:T(2,128)(2,1)S(1)} %all_to_all.26.mixed_ref, f32[2,128]{1,0:T(2,128)S(1)} %get-tuple-element.17.cosine_ref, f32[2,128]{1,0:T(2,128)S(1)} %get-tuple-element.18.sine_ref, f32[2,256]{1,0:T(2,128)S(1)} %get-tuple-element.19.mask_ref, ...), custom_call_target="tpu_custom_call" | custom-call | flops 10000000000 | bytes 2097152 | tf_op jit(solution)/shard_map/attend/pallas_call | solution.py:514
  28.0 12.2 %all_to_all.27.gathered_ref = bf16[8,2,8192]{2,1,0:T(2,128)(2,1)S(1)} all-to-all(bf16[8,2,8192]{2,1,0:T(2,128)(2,1)S(1)} %get-tuple-element.21), channel_id=1, replica_groups={{10,2,12,4,14,6,8,0},{11,3,13,5,15,7,9,1},{26,18,28,20,30,22,24,16},{27..., dimensions={0} | all-to-all | bytes 524288 | tf_op jit(solution)/shard_map/all_to_all | solution.py:407
  40.1 0.0 slice-done.1
  40.2 3.3 %project_out.1 = (f32[8,16,128]{2,1,0:T(8,128)S(1)}, f32[16,1024]{1,0:T(8,128)S(1)}, bf16[1024,1024]{1,0:T(8,128)(2,1)S(1)}) custom-call(s32[1,128]{1,0:T(1,128)S(1)} %get-tuple-element.20.adapter_ref, bf16[8,2,8192]{2,1,0:T(2,128)(2,1)S(1)} %all_to_all.27.gathered_ref, bf16[8192,1024]{1,0:T(8,128)(2,1)S(1)} %bitcast.2, bf16[64,64,1024]{2,1,0:T(8,128)(2,1)S(1)} %bitcast.7, ...), custom_call_target="tpu_custom_call" | custom-call | flops 10000000000 | bytes 16777216 | tf_op jit(solution)/shard_map/project_out/pallas_call | solution.py:327
  43.5 8.6 %all_to_all.28.partials_ref = f32[8,16,128]{2,1,0:T(8,128)S(1)} all-to-all(f32[8,16,128]{2,1,0:T(8,128)S(1)} %get-tuple-element.23), channel_id=1, replica_groups={{10,2,12,4,14,6,8,0},{11,3,13,5,15,7,9,1},{26,18,28,20,30,22,24,16},{27..., dimensions={0} | all-to-all | bytes 131072 | tf_op jit(solution)/shard_map/all_to_all | solution.py:407
  52.0 0.4 add_up.1
  52.4 8.4 %all_to_all.29.parts_ref = bf16[8,2,1024]{2,1,0:T(2,128)(2,1)S(1)} all-to-all(bf16[8,2,1024]{2,1,0:T(2,128)(2,1)S(1)} %add_up.1), channel_id=1, replica_groups={{10,2,12,4,14,6,8,0},{11,3,13,5,15,7,9,1},{26,18,28,20,30,22,24,16},{27..., dimensions={0} | all-to-all | bytes 65536 | tf_op jit(solution)/shard_map/all_to_all | solution.py:407
  60.8 0.7 %add_rows.1 = bf16[2,8192]{1,0:T(2,128)(2,1)} custom-call(bf16[2,8192]{1,0:T(2,128)(2,1)S(1)} %copy-done, bf16[8,2,1024]{2,1,0:T(2,128)(2,1)S(1)} %all_to_all.29.parts_ref), custom_call_target="tpu_custom_call" | custom-call | bytes 98304 | tf_op jit(solution)/shard_map/add_rows/pallas_call | solution.py:387
  (25 shorter events, 0.1 us)
Async XLA Ops:
  0.0 0.7 %copy-start.6 = (bf16[8192]{0:T(1024)(128)(2,1)S(1)}, bf16[8192]{0:T(1024)(128)(2,1)}, u32[]{:S(2)}) copy-start(bf16[8192]{0:T(1024)(128)(2,1)} %param.12) | copy-start | bytes 49156
  0.0 0.8 %copy-start = (bf16[2,8192]{1,0:T(2,128)(2,1)S(1)}, bf16[2,8192]{1,0:T(2,128)(2,1)}, u32[]{:S(2)}) copy-start(bf16[2,8192]{1,0:T(2,128)(2,1)} %hidden_ref.3) | copy-start | bytes 98308
  0.0 17.1 %slice-start.4 = ((s8[10485760]{0:T(1024)(128)(4,1)}), s8[4194304]{0:T(1024)(128)(4,1)S(1)}, s32[]{:S(2)}) async-start(s8[10485760]{0:T(1024)(128)(4,1)} %bitcast.3), calls=%async_computation.9 | async-start | bytes 8388608
  0.8 14.8 %copy-start.1 = (s32[2]{0:T(128)S(1)}, s32[2]{0:T(128)}, u32[]{:S(2)}) copy-start(s32[2]{0:T(128)} %lengths_ref.1) | copy-start | bytes 28
  0.8 14.8 %copy-start.2 = (s32[2]{0:T(128)S(1)}, s32[2]{0:T(128)}, u32[]{:S(2)}) copy-start(s32[2]{0:T(128)} %slots_ref.1) | copy-start | bytes 28
  0.8 14.8 %copy-start.3 = (s32[1,2]{1,0:T(1,128)S(1)}, s32[1,2]{1,0:T(1,128)}, u32[]{:S(2)}) copy-start(s32[1,2]{1,0:T(1,128)} %requests_ref.1) | copy-start | bytes 28
  0.8 16.3 %slice-start.5 = ((s8[10485760]{0:T(1024)(128)(4,1)}), s8[4194304]{0:T(1024)(128)(4,1)S(1)}, s32[]{:S(2)}) async-start(s8[10485760]{0:T(1024)(128)(4,1)} %bitcast.3), calls=%async_computation.10 | async-start | bytes 8388608
  0.8 16.3 %slice-start.6 = ((s8[10485760]{0:T(1024)(128)(4,1)}), s8[2097152]{0:T(1024)(128)(4,1)S(1)}, s32[]{:S(2)}) async-start(s8[10485760]{0:T(1024)(128)(4,1)} %bitcast.3), calls=%async_computation.11 | async-start | bytes 4194304
  15.6 1.5 %collective-permute-start = (bf16[8,2,8192]{2,1,0:T(2,128)(2,1)S(1)}, bf16[8,2,8192]{2,1,0:T(2,128)(2,1)S(1)}, u32[]{:S(2)}, u32[]{:S(2)}) collective-permute-start(bf16[8,2,8192]{2,1,0:T(2,128)(2,1)S(1)} %all_to_all.25.near_ref), channel_id=1, source_target_pairs={{0,1},{1,0},{2,3},{3,2},{4,5},{5,4},{6,7},{7,6},{8,9},{9,8},{10,11... | collective-permute-start | bytes 786440 | tf_op jit(solution)/shard_map/ppermute | solution.py:397
  17.1 10.0 %copy-start.4 = (bf16[2,256,1024]{2,1,0:T(8,128)(2,1)S(1)}, bf16[2,256,1024]{2,1,0:T(8,128)(2,1)}, u32[]{:S(2)}) copy-start(bf16[2,256,1024]{2,1,0:T(8,128)(2,1)} %key_ref.1) | copy-start | bytes 3145732
  17.1 10.0 %copy-start.5 = (bf16[2,256,1024]{2,1,0:T(8,128)(2,1)S(1)}, bf16[2,256,1024]{2,1,0:T(8,128)(2,1)}, u32[]{:S(2)}) copy-start(bf16[2,256,1024]{2,1,0:T(8,128)(2,1)} %value_ref.1) | copy-start | bytes 3145732
  17.1 23.0 %slice-start = ((s8[16777216]{0:T(1024)(128)(4,1)}), s8[4194304]{0:T(1024)(128)(4,1)S(1)}, s32[]{:S(2)}) async-start(s8[16777216]{0:T(1024)(128)(4,1)} %bitcast.1), calls=%async_computation.5 | async-start | bytes 8388608
  17.2 23.0 %slice-start.1 = ((s8[16777216]{0:T(1024)(128)(4,1)}), s8[4194304]{0:T(1024)(128)(4,1)S(1)}, s32[]{:S(2)}) async-start(s8[16777216]{0:T(1024)(128)(4,1)} %bitcast.1), calls=%async_computation.6 | async-start | bytes 8388608
  17.2 23.0 %slice-start.7 = ((s8[8388608]{0:T(1024)(128)(4,1)}), s8[4194304]{0:T(1024)(128)(4,1)S(1)}, s32[]{:S(2)}) async-start(s8[8388608]{0:T(1024)(128)(4,1)} %bitcast.5), calls=%async_computation.12 | async-start | bytes 8388608
  17.2 23.0 %slice-start.9 = ((s8[8388608]{0:T(1024)(128)(4,1)}), s8[4194304]{0:T(1024)(128)(4,1)S(1)}, s32[]{:S(2)}) async-start(s8[8388608]{0:T(1024)(128)(4,1)} %bitcast.8), calls=%async_computation.14 | async-start | bytes 8388608
  27.1 13.0 %slice-start.2 = ((s8[16777216]{0:T(1024)(128)(4,1)}), s8[4194304]{0:T(1024)(128)(4,1)S(1)}, s32[]{:S(2)}) async-start(s8[16777216]{0:T(1024)(128)(4,1)} %bitcast.1), calls=%async_computation.7 | async-start | bytes 8388608
  27.1 13.0 %slice-start.3 = ((s8[16777216]{0:T(1024)(128)(4,1)}), s8[4194304]{0:T(1024)(128)(4,1)S(1)}, s32[]{:S(2)}) async-start(s8[16777216]{0:T(1024)(128)(4,1)} %bitcast.1), calls=%async_computation.8 | async-start | bytes 8388608
  27.1 13.0 %slice-start.8 = ((s8[8388608]{0:T(1024)(128)(4,1)}), s8[4194304]{0:T(1024)(128)(4,1)S(1)}, s32[]{:S(2)}) async-start(s8[8388608]{0:T(1024)(128)(4,1)} %bitcast.5), calls=%async_computation.13 | async-start | bytes 8388608
  27.2 13.0 %slice-start.10 = ((s8[8388608]{0:T(1024)(128)(4,1)}), s8[4194304]{0:T(1024)(128)(4,1)S(1)}, s32[]{:S(2)}) async-start(s8[8388608]{0:T(1024)(128)(4,1)} %bitcast.8), calls=%async_computation.15 | async-start | bytes 8388608

commit v25 on v22

--- a/solution.py
+++ b/solution.py
@@ -240,22 +240,26 @@
     )(lengths, slots, requests, near, frequency)
 
 
-def project_qkv(lined, far, weight, adapter, chunk=4096):
+def column_parts(columns):
+    return [slice(c, min(c + 2 * LANES, columns)) for c in range(0, columns, 2 * LANES)]
+
+
+def project_qkv(lined, far, weight, adapter):
     groups, rows, _ = far.shape
     depth, width = weight.shape
     half = groups * rows
 
     def kernel(lined_ref, far_ref, weight_ref, adapter_ref, out_ref, far_lined_ref):
-        total = jnp.zeros((2 * half, width), jnp.float32)
-        for k in range(depth // chunk):
-            part = pl.ds(k * chunk, chunk)
-            for j in range(groups):
-                far_lined_ref[pl.ds(j * rows, rows), part] = far_ref[j, :, part]
-            total = total + jnp.dot(
-                jnp.concatenate([lined_ref[:, part], far_lined_ref[:, part]]),
-                weight_ref[part, :],
-                preferred_element_type=jnp.float32,
-            )
+        for j in range(groups):
+            far_lined_ref[pl.ds(j * rows, rows)] = far_ref[j]
+        lined = jnp.concatenate([lined_ref[...], far_lined_ref[...]])
+        total = jnp.concatenate(
+            [
+                jnp.dot(lined, weight_ref[:, part], preferred_element_type=jnp.float32)
+                for part in column_parts(width)
+            ],
+            1,
+        )
         core = lax.axis_index("batch")
         adapter = adapter_ref[...]
         for e in range(2):
@@ -280,7 +284,7 @@
     )(lined, far, weight, adapter)
 
 
-def project_out(gathered, adapter, weight, down_store, up_store, chunk=2048):
+def project_out(gathered, adapter, weight, down_store, up_store):
     groups, rows, features = gathered.shape
     count = groups * rows
     rank, depth = down_store.shape[1:]
@@ -290,20 +294,17 @@
         adapter_ref, gathered_ref, weight_ref, down_ref, up_ref, partial_ref, base_ref, picked_ref,
         rows_ref, held_ref,
     ):
-        base = jnp.zeros((count, columns), jnp.float32)
-        chunks = features // chunk
-        for k in range(chunks):
-            part = pl.ds(k * chunk, chunk)
-            for j in range(groups):
-                rows_ref[pl.ds(j * rows, rows), part] = gathered_ref[j, :, part]
-            base = base + jnp.dot(
-                rows_ref[:, part], weight_ref[part, :], preferred_element_type=jnp.float32
+        for j in range(groups):
+            rows_ref[pl.ds(j * rows, rows)] = gathered_ref[j]
+        parts = column_parts(columns)
+        for k, part in enumerate(parts):
+            base_ref[:, part] = jnp.dot(
+                rows_ref[...], weight_ref[:, part], preferred_element_type=jnp.float32
             )
-            for r in range(k * count // chunks, (k + 1) * count // chunks):
+            for r in range(k * count // len(parts), (k + 1) * count // len(parts)):
                 chosen = adapter_ref[0, r]
                 held_ref[pl.ds(r * rank, rank)] = down_ref[chosen]
                 picked_ref[pl.ds(r * rank, rank)] = up_ref[chosen]
-        base_ref[...] = base
         start = pl.multiple_of(lax.axis_index("mp") * depth, depth)
         every = lax.dot_general(
             rows_ref[:, pl.ds(start, depth)],

time: 62 us -> 62 us (level)
  no operation moved by 1% of the time
where the time goes in v25:
time: 62 us; the launch traced here: 61.6 us
  blocking collectives  51.9 us (84%)
  Pallas kernels  7.87 us (13%)
  local copies, waits for them, and re-layouts  0.84 us (1%)
  waiting for transfers between devices  0.79 us (1%)
    all_to_all x4, blocking collectives, exchange(): lax.all_to_all(blocks, 'mp', split_axis=0, concat_axis=0, tiled=True, axi...  43.7 us
    all_to_all x1, blocking collectives, exchange_all(): lax.all_to_all(blocks, ('mp', 'batch'), split_axis=0, concat_axis=0, tile...  8.23 us
    pallas_call x1, Pallas kernels, project_out(): call(kernel, 'project_out', (jax.ShapeDtypeStruct((groups, count, LANES),...  3.27 us
    pallas_call x1, Pallas kernels, project_qkv(): call(kernel, 'project_qkv', jax.ShapeDtypeStruct((2 * groups, rows, width...  1.86 us
  transfers between devices with their start and end apart: 1, of which 1 were waited for; matrix products, arithmetic and copies ran while one was open for 0% of the time, Pallas kernels for 1%

profile of v25, /device:TPU:0, one launch (start us, length us, event | category | flops | bytes accessed | tf_op | source)
XLA Modules:
  0.0 61.6 jit_solution(11901656540414621702)
XLA Ops:
  0.0 0.7 %copy-done.6 = bf16[8192]{0:T(1024)(128)(2,1)S(1)} copy-done((bf16[8192]{0:T(1024)(128)(2,1)S(1)}, bf16[8192]{0:T(1024)(128)(2,1)}, u32[]{:S(2)}) %copy-start.6) | copy-done | bytes 16408
  0.7 0.0 copy-done
  0.8 0.0 slice-start.5
  0.8 0.0 slice-start.6
  0.8 0.2 norm_rows.1
  1.0 14.6 %all_to_all.25.near_ref = bf16[8,2,8192]{2,1,0:T(2,128)(2,1)S(1)} all-to-all(bf16[8,2,8192]{2,1,0:T(2,128)(2,1)S(1)} %norm_rows.1), channel_id=1, replica_groups={{10,2,12,4,14,6,8,0},{11,3,13,5,15,7,9,1},{26,18,28,20,30,22,24,16},{27..., dimensions={0} | all-to-all | bytes 524288 | tf_op jit(solution)/shard_map/all_to_all | solution.py:403
  15.6 0.0 collective-permute-start
  15.6 0.0 copy-done.1
  15.6 0.0 copy-done.2
  15.6 0.0 copy-done.3
  15.6 0.7 %turns.1 = (bf16[16,8192]{1,0:T(8,128)(2,1)S(1)}, f32[2,128]{1,0:T(2,128)S(1)}, f32[2,128]{1,0:T(2,128)S(1)}, f32[2,256]{1,0:T(2,128)S(1)}, bf16[2,128]{1,0:T(2,128)(2,1)S(1)}) custom-call(s32[2]{0:T(128)S(1)} %copy-done.1, s32[2]{0:T(128)S(1)} %copy-done.2, s32[1,2]{1,0:T(1,128)S(1)} %copy-done.3, bf16[8,2,8192]{2,1,0:T(2,128)(2,1)S(1)} %all_to_all.25.near_ref, ...), custom_call_target="tpu_custom_call" | custom-call | bytes 524288 | tf_op jit(solution)/shard_map/turns/pallas_call | solution.py:228
  16.3 0.8 %collective-permute-done.far_ref = bf16[8,2,8192]{2,1,0:T(2,128)(2,1)S(1)} collective-permute-done((bf16[8,2,8192]{2,1,0:T(2,128)(2,1)S(1)}, bf16[8,2,8192]{2,1,0:T(2,128)(2,1)S(1)}, u32[]{:S(2)}, u32[]{:S(2)}) %collective-permute-start) | collective-permute-done | bytes 262176 | tf_op jit(solution)/shard_map/ppermute | solution.py:393
  17.1 0.0 slice-done.4
  17.1 0.0 slice-done.5
  17.1 0.0 copy-start.4
  17.1 0.0 copy-start.5
  17.1 0.0 slice-start
  17.2 0.0 slice-start.1
  17.2 0.0 slice-start.7
  17.2 0.0 slice-start.9
  17.2 1.9 %project_qkv.1 = bf16[16,2,768]{2,1,0:T(2,128)(2,1)S(1)} custom-call(bf16[16,8192]{1,0:T(8,128)(2,1)S(1)} %get-tuple-element.15.lined_ref, bf16[8,2,8192]{2,1,0:T(2,128)(2,1)S(1)} %collective-permute-done.far_ref, bf16[8192,640]{1,0:T(8,128)(2,1)S(1)} %bitcast.4, bf16[2,128]{1,0:T(2,128)(2,1)S(1)} %get-tuple-element.16.adapter_ref), custom_call_target="tpu_custom_call" | custom-call | flops 10000000000 | bytes 10485760 | tf_op jit(solution)/shard_map/project_qkv/pallas_call | solution.py:276
  19.1 8.2 %all_to_all.26.mixed_ref = bf16[16,2,768]{2,1,0:T(2,128)(2,1)S(1)} all-to-all(bf16[16,2,768]{2,1,0:T(2,128)(2,1)S(1)} %project_qkv.1), channel_id=1, replica_groups={{11,10,3,2,13,12,5,4,15,14,7,6,9,8,1,0},{27,26,19,18,29,28,21,20,31,30,..., dimensions={0} | all-to-all | bytes 98304 | tf_op jit(solution)/shard_map/all_to_all | solution.py:410
  27.3 0.0 slice-start.8
  27.3 0.0 slice-start.10
  27.3 0.8 %attend.1 = (bf16[8,2,8192]{2,1,0:T(2,128)(2,1)S(1)}, s32[1,128]{1,0:T(1,128)S(1)}) custom-call(bf16[16,2,768]{2,1,0:T(2,128)(2,1)S(1)} %all_to_all.26.mixed_ref, f32[2,128]{1,0:T(2,128)S(1)} %get-tuple-element.17.cosine_ref, f32[2,128]{1,0:T(2,128)S(1)} %get-tuple-element.18.sine_ref, f32[2,256]{1,0:T(2,128)S(1)} %get-tuple-element.19.mask_ref, ...), custom_call_target="tpu_custom_call" | custom-call | flops 10000000000 | bytes 2097152 | tf_op jit(solution)/shard_map/attend/pallas_call | solution.py:510
  28.1 12.2 %all_to_all.27.gathered_ref = bf16[8,2,8192]{2,1,0:T(2,128)(2,1)S(1)} all-to-all(bf16[8,2,8192]{2,1,0:T(2,128)(2,1)S(1)} %get-tuple-element.21), channel_id=1, replica_groups={{10,2,12,4,14,6,8,0},{11,3,13,5,15,7,9,1},{26,18,28,20,30,22,24,16},{27..., dimensions={0} | all-to-all | bytes 524288 | tf_op jit(solution)/shard_map/all_to_all | solution.py:403
  40.3 0.0 slice-done.1
  40.4 3.3 %project_out.1 = (f32[8,16,128]{2,1,0:T(8,128)S(1)}, f32[16,1024]{1,0:T(8,128)S(1)}, bf16[1024,1024]{1,0:T(8,128)(2,1)S(1)}) custom-call(s32[1,128]{1,0:T(1,128)S(1)} %get-tuple-element.20.adapter_ref, bf16[8,2,8192]{2,1,0:T(2,128)(2,1)S(1)} %all_to_all.27.gathered_ref, bf16[8192,1024]{1,0:T(8,128)(2,1)S(1)} %bitcast.2, bf16[64,64,1024]{2,1,0:T(8,128)(2,1)S(1)} %bitcast.7, ...), custom_call_target="tpu_custom_call" | custom-call | flops 10000000000 | bytes 16777216 | tf_op jit(solution)/shard_map/project_out/pallas_call | solution.py:323
  43.7 8.6 %all_to_all.28.partials_ref = f32[8,16,128]{2,1,0:T(8,128)S(1)} all-to-all(f32[8,16,128]{2,1,0:T(8,128)S(1)} %get-tuple-element.23), channel_id=1, replica_groups={{10,2,12,4,14,6,8,0},{11,3,13,5,15,7,9,1},{26,18,28,20,30,22,24,16},{27..., dimensions={0} | all-to-all | bytes 131072 | tf_op jit(solution)/shard_map/all_to_all | solution.py:403
  52.2 0.4 add_up.1
  52.6 8.4 %all_to_all.29.parts_ref = bf16[8,2,1024]{2,1,0:T(2,128)(2,1)S(1)} all-to-all(bf16[8,2,1024]{2,1,0:T(2,128)(2,1)S(1)} %add_up.1), channel_id=1, replica_groups={{10,2,12,4,14,6,8,0},{11,3,13,5,15,7,9,1},{26,18,28,20,30,22,24,16},{27..., dimensions={0} | all-to-all | bytes 65536 | tf_op jit(solution)/shard_map/all_to_all | solution.py:403
  61.0 0.7 %add_rows.1 = bf16[2,8192]{1,0:T(2,128)(2,1)} custom-call(bf16[2,8192]{1,0:T(2,128)(2,1)S(1)} %copy-done, bf16[8,2,1024]{2,1,0:T(2,128)(2,1)S(1)} %all_to_all.29.parts_ref), custom_call_target="tpu_custom_call" | custom-call | bytes 98304 | tf_op jit(solution)/shard_map/add_rows/pallas_call | solution.py:383
  (25 shorter events, 0.1 us)
Async XLA Ops:
  0.0 0.7 %copy-start.6 = (bf16[8192]{0:T(1024)(128)(2,1)S(1)}, bf16[8192]{0:T(1024)(128)(2,1)}, u32[]{:S(2)}) copy-start(bf16[8192]{0:T(1024)(128)(2,1)} %param.12) | copy-start | bytes 49156
  0.0 0.8 %copy-start = (bf16[2,8192]{1,0:T(2,128)(2,1)S(1)}, bf16[2,8192]{1,0:T(2,128)(2,1)}, u32[]{:S(2)}) copy-start(bf16[2,8192]{1,0:T(2,128)(2,1)} %hidden_ref.3) | copy-start | bytes 98308
  0.0 17.1 %slice-start.4 = ((s8[10485760]{0:T(1024)(128)(4,1)}), s8[4194304]{0:T(1024)(128)(4,1)S(1)}, s32[]{:S(2)}) async-start(s8[10485760]{0:T(1024)(128)(4,1)} %bitcast.3), calls=%async_computation.9 | async-start | bytes 8388608
  0.8 14.8 %copy-start.1 = (s32[2]{0:T(128)S(1)}, s32[2]{0:T(128)}, u32[]{:S(2)}) copy-start(s32[2]{0:T(128)} %lengths_ref.1) | copy-start | bytes 28
  0.8 14.8 %copy-start.2 = (s32[2]{0:T(128)S(1)}, s32[2]{0:T(128)}, u32[]{:S(2)}) copy-start(s32[2]{0:T(128)} %slots_ref.1) | copy-start | bytes 28
  0.8 14.8 %copy-start.3 = (s32[1,2]{1,0:T(1,128)S(1)}, s32[1,2]{1,0:T(1,128)}, u32[]{:S(2)}) copy-start(s32[1,2]{1,0:T(1,128)} %requests_ref.1) | copy-start | bytes 28
  0.8 16.3 %slice-start.5 = ((s8[10485760]{0:T(1024)(128)(4,1)}), s8[4194304]{0:T(1024)(128)(4,1)S(1)}, s32[]{:S(2)}) async-start(s8[10485760]{0:T(1024)(128)(4,1)} %bitcast.3), calls=%async_computation.10 | async-start | bytes 8388608
  0.8 16.3 %slice-start.6 = ((s8[10485760]{0:T(1024)(128)(4,1)}), s8[2097152]{0:T(1024)(128)(4,1)S(1)}, s32[]{:S(2)}) async-start(s8[10485760]{0:T(1024)(128)(4,1)} %bitcast.3), calls=%async_computation.11 | async-start | bytes 4194304
  15.6 1.5 %collective-permute-start = (bf16[8,2,8192]{2,1,0:T(2,128)(2,1)S(1)}, bf16[8,2,8192]{2,1,0:T(2,128)(2,1)S(1)}, u32[]{:S(2)}, u32[]{:S(2)}) collective-permute-start(bf16[8,2,8192]{2,1,0:T(2,128)(2,1)S(1)} %all_to_all.25.near_ref), channel_id=1, source_target_pairs={{0,1},{1,0},{2,3},{3,2},{4,5},{5,4},{6,7},{7,6},{8,9},{9,8},{10,11... | collective-permute-start | bytes 786440 | tf_op jit(solution)/shard_map/ppermute | solution.py:393
  17.1 10.2 %copy-start.4 = (bf16[2,256,1024]{2,1,0:T(8,128)(2,1)S(1)}, bf16[2,256,1024]{2,1,0:T(8,128)(2,1)}, u32[]{:S(2)}) copy-start(bf16[2,256,1024]{2,1,0:T(8,128)(2,1)} %key_ref.1) | copy-start | bytes 3145732
  17.1 10.2 %copy-start.5 = (bf16[2,256,1024]{2,1,0:T(8,128)(2,1)S(1)}, bf16[2,256,1024]{2,1,0:T(8,128)(2,1)}, u32[]{:S(2)}) copy-start(bf16[2,256,1024]{2,1,0:T(8,128)(2,1)} %value_ref.1) | copy-start | bytes 3145732
  17.1 23.1 %slice-start = ((s8[16777216]{0:T(1024)(128)(4,1)}), s8[4194304]{0:T(1024)(128)(4,1)S(1)}, s32[]{:S(2)}) async-start(s8[16777216]{0:T(1024)(128)(4,1)} %bitcast.1), calls=%async_computation.5 | async-start | bytes 8388608
  17.2 23.1 %slice-start.1 = ((s8[16777216]{0:T(1024)(128)(4,1)}), s8[4194304]{0:T(1024)(128)(4,1)S(1)}, s32[]{:S(2)}) async-start(s8[16777216]{0:T(1024)(128)(4,1)} %bitcast.1), calls=%async_computation.6 | async-start | bytes 8388608
  17.2 23.1 %slice-start.7 = ((s8[8388608]{0:T(1024)(128)(4,1)}), s8[4194304]{0:T(1024)(128)(4,1)S(1)}, s32[]{:S(2)}) async-start(s8[8388608]{0:T(1024)(128)(4,1)} %bitcast.5), calls=%async_computation.12 | async-start | bytes 8388608
  17.2 23.1 %slice-start.9 = ((s8[8388608]{0:T(1024)(128)(4,1)}), s8[4194304]{0:T(1024)(128)(4,1)S(1)}, s32[]{:S(2)}) async-start(s8[8388608]{0:T(1024)(128)(4,1)} %bitcast.8), calls=%async_computation.14 | async-start | bytes 8388608
  27.3 13.0 %slice-start.2 = ((s8[16777216]{0:T(1024)(128)(4,1)}), s8[4194304]{0:T(1024)(128)(4,1)S(1)}, s32[]{:S(2)}) async-start(s8[16777216]{0:T(1024)(128)(4,1)} %bitcast.1), calls=%async_computation.7 | async-start | bytes 8388608
  27.3 13.0 %slice-start.3 = ((s8[16777216]{0:T(1024)(128)(4,1)}), s8[4194304]{0:T(1024)(128)(4,1)S(1)}, s32[]{:S(2)}) async-start(s8[16777216]{0:T(1024)(128)(4,1)} %bitcast.1), calls=%async_computation.8 | async-start | bytes 8388608
  27.3 13.0 %slice-start.8 = ((s8[8388608]{0:T(1024)(128)(4,1)}), s8[4194304]{0:T(1024)(128)(4,1)S(1)}, s32[]{:S(2)}) async-start(s8[8388608]{0:T(1024)(128)(4,1)} %bitcast.5), calls=%async_computation.13 | async-start | bytes 8388608
  27.3 13.0 %slice-start.10 = ((s8[8388608]{0:T(1024)(128)(4,1)}), s8[4194304]{0:T(1024)(128)(4,1)S(1)}, s32[]{:S(2)}) async-start(s8[8388608]{0:T(1024)(128)(4,1)} %bitcast.8), calls=%async_computation.15 | async-start | bytes 8388608

commit v26 on v24

--- a/solution.py
+++ b/solution.py
@@ -240,6 +240,10 @@
     )(lengths, slots, requests, near, frequency)
 
 
+def column_parts(columns):
+    return [slice(c, min(c + 2 * LANES, columns)) for c in range(0, columns, 2 * LANES)]
+
+
 def halves_product(rows, weight_ref, part, cut):
     return jnp.concatenate(
         [
@@ -287,7 +291,7 @@
     )(lined, far, weight, adapter)
 
 
-def project_out(gathered, adapter, weight, down_store, up_store, chunk=2048):
+def project_out(gathered, adapter, weight, down_store, up_store):
     groups, rows, features = gathered.shape
     count = groups * rows
     rank, depth = down_store.shape[1:]
@@ -297,30 +301,32 @@
         adapter_ref, gathered_ref, weight_ref, down_ref, up_ref, partial_ref, base_ref, picked_ref,
         rows_ref, held_ref,
     ):
-        base = jnp.zeros((count, columns), jnp.float32)
-        chunks = features // chunk
-        for k in range(chunks):
-            part = pl.ds(k * chunk, chunk)
-            for j in range(groups):
-                rows_ref[pl.ds(j * rows, rows), part] = gathered_ref[j, :, part]
-            base = base + halves_product(rows_ref[:, part], weight_ref, part, columns // 2)
-            for r in range(k * count // chunks, (k + 1) * count // chunks):
+        for j in range(groups):
+            rows_ref[pl.ds(j * rows, rows)] = gathered_ref[j]
+        start = pl.multiple_of(lax.axis_index("mp") * depth, depth)
+        slices = rows_ref[:, pl.ds(start, depth)]
+        row = lax.broadcasted_iota(jnp.int32, (count, LANES), 0)
+        lane = lax.broadcasted_iota(jnp.int32, (count, LANES), 1)
+        total = jnp.zeros((count, LANES), jnp.float32)
+        parts = column_parts(columns)
+        few = count // len(parts)
+        for k, part in enumerate(parts):
+            for r in range(k * few, (k + 1) * few):
                 chosen = adapter_ref[0, r]
                 held_ref[pl.ds(r * rank, rank)] = down_ref[chosen]
                 picked_ref[pl.ds(r * rank, rank)] = up_ref[chosen]
-        base_ref[...] = base
-        start = pl.multiple_of(lax.axis_index("mp") * depth, depth)
-        every = lax.dot_general(
-            rows_ref[:, pl.ds(start, depth)],
-            held_ref[...],
-            (((1,), (1,)), ((), ())),
-            preferred_element_type=jnp.float32,
-        )
-        row = lax.broadcasted_iota(jnp.int32, (count, LANES), 0)
-        lane = lax.broadcasted_iota(jnp.int32, (count, LANES), 1)
-        total = jnp.zeros((count, LANES), jnp.float32)
-        for s in range(0, count * rank, LANES):
-            total = total + jnp.where(row == (lane + s) // rank, every[:, s : s + LANES], 0.0)
+            every = lax.dot_general(
+                slices,
+                held_ref[pl.ds(k * few * rank, few * rank)],
+                (((1,), (1,)), ((), ())),
+                preferred_element_type=jnp.float32,
+            )
+            for s in range(0, few * rank, LANES):
+                mine = row == (lane + k * few * rank + s) // rank
+                total = total + jnp.where(mine, every[:, s : s + LANES], 0.0)
+            base_ref[:, part] = jnp.dot(
+                rows_ref[...], weight_ref[:, part], preferred_element_type=jnp.float32
+            )
         for c in range(groups):
             partial_ref[c] = total
 

time: 61.8 us -> 62 us (level)
  no operation moved by 1% of the time
where the time goes in v26:
time: 62 us; the launch traced here: 61.6 us
  blocking collectives  51.8 us (84%)
  Pallas kernels  7.96 us (13%)
  local copies, waits for them, and re-layouts  0.84 us (1%)
  waiting for transfers between devices  0.79 us (1%)
    all_to_all x4, blocking collectives, exchange(): lax.all_to_all(blocks, 'mp', split_axis=0, concat_axis=0, tiled=True, axi...  43.6 us
    all_to_all x1, blocking collectives, exchange_all(): lax.all_to_all(blocks, ('mp', 'batch'), split_axis=0, concat_axis=0, tile...  8.23 us
    pallas_call x1, Pallas kernels, project_out(): call(kernel, 'project_out', (jax.ShapeDtypeStruct((groups, count, LANES),...  3.52 us
    pallas_call x1, Pallas kernels, project_qkv(): call(kernel, 'project_qkv', jax.ShapeDtypeStruct((2 * groups, rows, width...  1.7 us
  transfers between devices with their start and end apart: 1, of which 1 were waited for; matrix products, arithmetic and copies ran while one was open for 0% of the time, Pallas kernels for 1%

profile of v26, /device:TPU:0, one launch (start us, length us, event | category | flops | bytes accessed | tf_op | source)
XLA Modules:
  0.0 61.6 jit_solution(3502183834455907110)
XLA Ops:
  0.0 0.7 %copy-done.6 = bf16[8192]{0:T(1024)(128)(2,1)S(1)} copy-done((bf16[8192]{0:T(1024)(128)(2,1)S(1)}, bf16[8192]{0:T(1024)(128)(2,1)}, u32[]{:S(2)}) %copy-start.6) | copy-done | bytes 16408
  0.7 0.0 copy-done
  0.8 0.0 slice-start.5
  0.8 0.0 slice-start.6
  0.8 0.2 norm_rows.1
  1.0 14.6 %all_to_all.25.near_ref = bf16[8,2,8192]{2,1,0:T(2,128)(2,1)S(1)} all-to-all(bf16[8,2,8192]{2,1,0:T(2,128)(2,1)S(1)} %norm_rows.1), channel_id=1, replica_groups={{10,2,12,4,14,6,8,0},{11,3,13,5,15,7,9,1},{26,18,28,20,30,22,24,16},{27..., dimensions={0} | all-to-all | bytes 524288 | tf_op jit(solution)/shard_map/all_to_all | solution.py:413
  15.6 0.0 collective-permute-start
  15.6 0.0 copy-done.1
  15.6 0.0 copy-done.2
  15.6 0.0 copy-done.3
  15.6 0.7 %turns.1 = (bf16[16,8192]{1,0:T(8,128)(2,1)S(1)}, f32[2,128]{1,0:T(2,128)S(1)}, f32[2,128]{1,0:T(2,128)S(1)}, f32[2,256]{1,0:T(2,128)S(1)}, bf16[2,128]{1,0:T(2,128)(2,1)S(1)}) custom-call(s32[2]{0:T(128)S(1)} %copy-done.1, s32[2]{0:T(128)S(1)} %copy-done.2, s32[1,2]{1,0:T(1,128)S(1)} %copy-done.3, bf16[8,2,8192]{2,1,0:T(2,128)(2,1)S(1)} %all_to_all.25.near_ref, ...), custom_call_target="tpu_custom_call" | custom-call | bytes 524288 | tf_op jit(solution)/shard_map/turns/pallas_call | solution.py:228
  16.3 0.8 %collective-permute-done.far_ref = bf16[8,2,8192]{2,1,0:T(2,128)(2,1)S(1)} collective-permute-done((bf16[8,2,8192]{2,1,0:T(2,128)(2,1)S(1)}, bf16[8,2,8192]{2,1,0:T(2,128)(2,1)S(1)}, u32[]{:S(2)}, u32[]{:S(2)}) %collective-permute-start) | collective-permute-done | bytes 262176 | tf_op jit(solution)/shard_map/ppermute | solution.py:403
  17.1 0.0 slice-done.6
  17.1 0.0 copy-start.4
  17.1 0.0 copy-start.5
  17.1 0.0 slice-start
  17.2 0.0 slice-start.1
  17.2 0.0 slice-start.7
  17.2 0.0 slice-start.9
  17.2 1.7 %project_qkv.1 = bf16[16,2,768]{2,1,0:T(2,128)(2,1)S(1)} custom-call(bf16[16,8192]{1,0:T(8,128)(2,1)S(1)} %get-tuple-element.15.lined_ref, bf16[8,2,8192]{2,1,0:T(2,128)(2,1)S(1)} %collective-permute-done.far_ref, bf16[8192,640]{1,0:T(8,128)(2,1)S(1)} %bitcast.4, bf16[2,128]{1,0:T(2,128)(2,1)S(1)} %get-tuple-element.16.adapter_ref), custom_call_target="tpu_custom_call" | custom-call | flops 10000000000 | bytes 10485760 | tf_op jit(solution)/shard_map/project_qkv/pallas_call | solution.py:283
  18.9 8.2 %all_to_all.26.mixed_ref = bf16[16,2,768]{2,1,0:T(2,128)(2,1)S(1)} all-to-all(bf16[16,2,768]{2,1,0:T(2,128)(2,1)S(1)} %project_qkv.1), channel_id=1, replica_groups={{11,10,3,2,13,12,5,4,15,14,7,6,9,8,1,0},{27,26,19,18,29,28,21,20,31,30,..., dimensions={0} | all-to-all | bytes 98304 | tf_op jit(solution)/shard_map/all_to_all | solution.py:420
  27.1 0.0 copy-done.5
  27.1 0.0 slice-start.8
  27.2 0.0 slice-start.10
  27.2 0.8 %attend.1 = (bf16[8,2,8192]{2,1,0:T(2,128)(2,1)S(1)}, s32[1,128]{1,0:T(1,128)S(1)}) custom-call(bf16[16,2,768]{2,1,0:T(2,128)(2,1)S(1)} %all_to_all.26.mixed_ref, f32[2,128]{1,0:T(2,128)S(1)} %get-tuple-element.17.cosine_ref, f32[2,128]{1,0:T(2,128)S(1)} %get-tuple-element.18.sine_ref, f32[2,256]{1,0:T(2,128)S(1)} %get-tuple-element.19.mask_ref, ...), custom_call_target="tpu_custom_call" | custom-call | flops 10000000000 | bytes 2097152 | tf_op jit(solution)/shard_map/attend/pallas_call | solution.py:520
  28.0 12.2 %all_to_all.27.gathered_ref = bf16[8,2,8192]{2,1,0:T(2,128)(2,1)S(1)} all-to-all(bf16[8,2,8192]{2,1,0:T(2,128)(2,1)S(1)} %get-tuple-element.21), channel_id=1, replica_groups={{10,2,12,4,14,6,8,0},{11,3,13,5,15,7,9,1},{26,18,28,20,30,22,24,16},{27..., dimensions={0} | all-to-all | bytes 524288 | tf_op jit(solution)/shard_map/all_to_all | solution.py:413
  40.1 0.0 slice-done.1
  40.2 3.5 %project_out.1 = (f32[8,16,128]{2,1,0:T(8,128)S(1)}, f32[16,1024]{1,0:T(8,128)S(1)}, bf16[1024,1024]{1,0:T(8,128)(2,1)S(1)}) custom-call(s32[1,128]{1,0:T(1,128)S(1)} %get-tuple-element.20.adapter_ref, bf16[8,2,8192]{2,1,0:T(2,128)(2,1)S(1)} %all_to_all.27.gathered_ref, bf16[8192,1024]{1,0:T(8,128)(2,1)S(1)} %bitcast.2, bf16[64,64,1024]{2,1,0:T(8,128)(2,1)S(1)} %bitcast.7, ...), custom_call_target="tpu_custom_call" | custom-call | flops 10000000000 | bytes 16777216 | tf_op jit(solution)/shard_map/project_out/pallas_call | solution.py:333
  43.7 8.5 %all_to_all.28.partials_ref = f32[8,16,128]{2,1,0:T(8,128)S(1)} all-to-all(f32[8,16,128]{2,1,0:T(8,128)S(1)} %get-tuple-element.23), channel_id=1, replica_groups={{10,2,12,4,14,6,8,0},{11,3,13,5,15,7,9,1},{26,18,28,20,30,22,24,16},{27..., dimensions={0} | all-to-all | bytes 131072 | tf_op jit(solution)/shard_map/all_to_all | solution.py:413
  52.2 0.4 add_up.1
  52.6 8.4 %all_to_all.29.parts_ref = bf16[8,2,1024]{2,1,0:T(2,128)(2,1)S(1)} all-to-all(bf16[8,2,1024]{2,1,0:T(2,128)(2,1)S(1)} %add_up.1), channel_id=1, replica_groups={{10,2,12,4,14,6,8,0},{11,3,13,5,15,7,9,1},{26,18,28,20,30,22,24,16},{27..., dimensions={0} | all-to-all | bytes 65536 | tf_op jit(solution)/shard_map/all_to_all | solution.py:413
  61.0 0.7 %add_rows.1 = bf16[2,8192]{1,0:T(2,128)(2,1)} custom-call(bf16[2,8192]{1,0:T(2,128)(2,1)S(1)} %copy-done, bf16[8,2,1024]{2,1,0:T(2,128)(2,1)S(1)} %all_to_all.29.parts_ref), custom_call_target="tpu_custom_call" | custom-call | bytes 98304 | tf_op jit(solution)/shard_map/add_rows/pallas_call | solution.py:393
  (25 shorter events, 0.1 us)
Async XLA Ops:
  0.0 0.7 %copy-start.6 = (bf16[8192]{0:T(1024)(128)(2,1)S(1)}, bf16[8192]{0:T(1024)(128)(2,1)}, u32[]{:S(2)}) copy-start(bf16[8192]{0:T(1024)(128)(2,1)} %param.12) | copy-start | bytes 49156
  0.0 0.8 %copy-start = (bf16[2,8192]{1,0:T(2,128)(2,1)S(1)}, bf16[2,8192]{1,0:T(2,128)(2,1)}, u32[]{:S(2)}) copy-start(bf16[2,8192]{1,0:T(2,128)(2,1)} %hidden_ref.3) | copy-start | bytes 98308
  0.0 17.1 %slice-start.4 = ((s8[10485760]{0:T(1024)(128)(4,1)}), s8[4194304]{0:T(1024)(128)(4,1)S(1)}, s32[]{:S(2)}) async-start(s8[10485760]{0:T(1024)(128)(4,1)} %bitcast.3), calls=%async_computation.9 | async-start | bytes 8388608
  0.8 14.8 %copy-start.1 = (s32[2]{0:T(128)S(1)}, s32[2]{0:T(128)}, u32[]{:S(2)}) copy-start(s32[2]{0:T(128)} %lengths_ref.1) | copy-start | bytes 28
  0.8 14.8 %copy-start.2 = (s32[2]{0:T(128)S(1)}, s32[2]{0:T(128)}, u32[]{:S(2)}) copy-start(s32[2]{0:T(128)} %slots_ref.1) | copy-start | bytes 28
  0.8 14.8 %copy-start.3 = (s32[1,2]{1,0:T(1,128)S(1)}, s32[1,2]{1,0:T(1,128)}, u32[]{:S(2)}) copy-start(s32[1,2]{1,0:T(1,128)} %requests_ref.1) | copy-start | bytes 28
  0.8 16.3 %slice-start.5 = ((s8[10485760]{0:T(1024)(128)(4,1)}), s8[4194304]{0:T(1024)(128)(4,1)S(1)}, s32[]{:S(2)}) async-start(s8[10485760]{0:T(1024)(128)(4,1)} %bitcast.3), calls=%async_computation.10 | async-start | bytes 8388608
  0.8 16.3 %slice-start.6 = ((s8[10485760]{0:T(1024)(128)(4,1)}), s8[2097152]{0:T(1024)(128)(4,1)S(1)}, s32[]{:S(2)}) async-start(s8[10485760]{0:T(1024)(128)(4,1)} %bitcast.3), calls=%async_computation.11 | async-start | bytes 4194304
  15.6 1.5 %collective-permute-start = (bf16[8,2,8192]{2,1,0:T(2,128)(2,1)S(1)}, bf16[8,2,8192]{2,1,0:T(2,128)(2,1)S(1)}, u32[]{:S(2)}, u32[]{:S(2)}) collective-permute-start(bf16[8,2,8192]{2,1,0:T(2,128)(2,1)S(1)} %all_to_all.25.near_ref), channel_id=1, source_target_pairs={{0,1},{1,0},{2,3},{3,2},{4,5},{5,4},{6,7},{7,6},{8,9},{9,8},{10,11... | collective-permute-start | bytes 786440 | tf_op jit(solution)/shard_map/ppermute | solution.py:403
  17.1 10.0 %copy-start.4 = (bf16[2,256,1024]{2,1,0:T(8,128)(2,1)S(1)}, bf16[2,256,1024]{2,1,0:T(8,128)(2,1)}, u32[]{:S(2)}) copy-start(bf16[2,256,1024]{2,1,0:T(8,128)(2,1)} %key_ref.1) | copy-start | bytes 3145732
  17.1 10.0 %copy-start.5 = (bf16[2,256,1024]{2,1,0:T(8,128)(2,1)S(1)}, bf16[2,256,1024]{2,1,0:T(8,128)(2,1)}, u32[]{:S(2)}) copy-start(bf16[2,256,1024]{2,1,0:T(8,128)(2,1)} %value_ref.1) | copy-start | bytes 3145732
  17.1 23.0 %slice-start = ((s8[16777216]{0:T(1024)(128)(4,1)}), s8[4194304]{0:T(1024)(128)(4,1)S(1)}, s32[]{:S(2)}) async-start(s8[16777216]{0:T(1024)(128)(4,1)} %bitcast.1), calls=%async_computation.5 | async-start | bytes 8388608
  17.2 23.0 %slice-start.1 = ((s8[16777216]{0:T(1024)(128)(4,1)}), s8[4194304]{0:T(1024)(128)(4,1)S(1)}, s32[]{:S(2)}) async-start(s8[16777216]{0:T(1024)(128)(4,1)} %bitcast.1), calls=%async_computation.6 | async-start | bytes 8388608
  17.2 23.0 %slice-start.7 = ((s8[8388608]{0:T(1024)(128)(4,1)}), s8[4194304]{0:T(1024)(128)(4,1)S(1)}, s32[]{:S(2)}) async-start(s8[8388608]{0:T(1024)(128)(4,1)} %bitcast.5), calls=%async_computation.12 | async-start | bytes 8388608
  17.2 23.0 %slice-start.9 = ((s8[8388608]{0:T(1024)(128)(4,1)}), s8[4194304]{0:T(1024)(128)(4,1)S(1)}, s32[]{:S(2)}) async-start(s8[8388608]{0:T(1024)(128)(4,1)} %bitcast.8), calls=%async_computation.14 | async-start | bytes 8388608
  27.1 13.0 %slice-start.2 = ((s8[16777216]{0:T(1024)(128)(4,1)}), s8[4194304]{0:T(1024)(128)(4,1)S(1)}, s32[]{:S(2)}) async-start(s8[16777216]{0:T(1024)(128)(4,1)} %bitcast.1), calls=%async_computation.7 | async-start | bytes 8388608
  27.1 13.0 %slice-start.3 = ((s8[16777216]{0:T(1024)(128)(4,1)}), s8[4194304]{0:T(1024)(128)(4,1)S(1)}, s32[]{:S(2)}) async-start(s8[16777216]{0:T(1024)(128)(4,1)} %bitcast.1), calls=%async_computation.8 | async-start | bytes 8388608
  27.1 13.0 %slice-start.8 = ((s8[8388608]{0:T(1024)(128)(4,1)}), s8[4194304]{0:T(1024)(128)(4,1)S(1)}, s32[]{:S(2)}) async-start(s8[8388608]{0:T(1024)(128)(4,1)} %bitcast.5), calls=%async_computation.13 | async-start | bytes 8388608
  27.2 13.0 %slice-start.10 = ((s8[8388608]{0:T(1024)(128)(4,1)}), s8[4194304]{0:T(1024)(128)(4,1)S(1)}, s32[]{:S(2)}) async-start(s8[8388608]{0:T(1024)(128)(4,1)} %bitcast.8), calls=%async_computation.15 | async-start | bytes 8388608

commit v27 on v24

--- a/solution.py
+++ b/solution.py
@@ -240,6 +240,10 @@
     )(lengths, slots, requests, near, frequency)
 
 
+def column_parts(columns):
+    return [slice(c, min(c + 2 * LANES, columns)) for c in range(0, columns, 2 * LANES)]
+
+
 def halves_product(rows, weight_ref, part, cut):
     return jnp.concatenate(
         [
@@ -287,7 +291,7 @@
     )(lined, far, weight, adapter)
 
 
-def project_out(gathered, adapter, weight, down_store, up_store, chunk=2048):
+def project_out(gathered, adapter, weight, down_store, up_store):
     groups, rows, features = gathered.shape
     count = groups * rows
     rank, depth = down_store.shape[1:]
@@ -297,18 +301,17 @@
         adapter_ref, gathered_ref, weight_ref, down_ref, up_ref, partial_ref, base_ref, picked_ref,
         rows_ref, held_ref,
     ):
-        base = jnp.zeros((count, columns), jnp.float32)
-        chunks = features // chunk
-        for k in range(chunks):
-            part = pl.ds(k * chunk, chunk)
-            for j in range(groups):
-                rows_ref[pl.ds(j * rows, rows), part] = gathered_ref[j, :, part]
-            base = base + halves_product(rows_ref[:, part], weight_ref, part, columns // 2)
-            for r in range(k * count // chunks, (k + 1) * count // chunks):
+        for j in range(groups):
+            rows_ref[pl.ds(j * rows, rows)] = gathered_ref[j]
+        parts = column_parts(columns)
+        for k, part in enumerate(parts):
+            base_ref[:, part] = jnp.dot(
+                rows_ref[...], weight_ref[:, part], preferred_element_type=jnp.float32
+            )
+            for r in range(k * count // len(parts), (k + 1) * count // len(parts)):
                 chosen = adapter_ref[0, r]
                 held_ref[pl.ds(r * rank, rank)] = down_ref[chosen]
                 picked_ref[pl.ds(r * rank, rank)] = up_ref[chosen]
-        base_ref[...] = base
         start = pl.multiple_of(lax.axis_index("mp") * depth, depth)
         every = lax.dot_general(
             rows_ref[:, pl.ds(start, depth)],

time: 61.8 us -> 61.8 us (level)
  no operation moved by 1% of the time
where the time goes in v27:
time: 61.8 us; the launch traced here: 61.5 us
  blocking collectives  51.9 us (84%)
  Pallas kernels  7.71 us (12%)
  local copies, waits for them, and re-layouts  0.84 us (1%)
  waiting for transfers between devices  0.79 us (1%)
    all_to_all x4, blocking collectives, exchange(): lax.all_to_all(blocks, 'mp', split_axis=0, concat_axis=0, tiled=True, axi...  43.7 us
    all_to_all x1, blocking collectives, exchange_all(): lax.all_to_all(blocks, ('mp', 'batch'), split_axis=0, concat_axis=0, tile...  8.23 us
    pallas_call x1, Pallas kernels, project_out(): call(kernel, 'project_out', (jax.ShapeDtypeStruct((groups, count, LANES),...  3.27 us
    pallas_call x1, Pallas kernels, project_qkv(): call(kernel, 'project_qkv', jax.ShapeDtypeStruct((2 * groups, rows, width...  1.7 us
  transfers between devices with their start and end apart: 1, of which 1 were waited for; matrix products, arithmetic and copies ran while one was open for 0% of the time, Pallas kernels for 1%

profile of v27, /device:TPU:0, one launch (start us, length us, event | category | flops | bytes accessed | tf_op | source)
XLA Modules:
  0.0 61.5 jit_solution(4307542860453014128)
XLA Ops:
  0.0 0.7 %copy-done.6 = bf16[8192]{0:T(1024)(128)(2,1)S(1)} copy-done((bf16[8192]{0:T(1024)(128)(2,1)S(1)}, bf16[8192]{0:T(1024)(128)(2,1)}, u32[]{:S(2)}) %copy-start.6) | copy-done | bytes 16408
  0.7 0.0 copy-done
  0.8 0.0 slice-start.5
  0.8 0.0 slice-start.6
  0.8 0.2 norm_rows.1
  1.0 14.6 %all_to_all.25.near_ref = bf16[8,2,8192]{2,1,0:T(2,128)(2,1)S(1)} all-to-all(bf16[8,2,8192]{2,1,0:T(2,128)(2,1)S(1)} %norm_rows.1), channel_id=1, replica_groups={{10,2,12,4,14,6,8,0},{11,3,13,5,15,7,9,1},{26,18,28,20,30,22,24,16},{27..., dimensions={0} | all-to-all | bytes 524288 | tf_op jit(solution)/shard_map/all_to_all | solution.py:410
  15.6 0.0 collective-permute-start
  15.6 0.0 copy-done.1
  15.6 0.0 copy-done.2
  15.6 0.0 copy-done.3
  15.6 0.7 %turns.1 = (bf16[16,8192]{1,0:T(8,128)(2,1)S(1)}, f32[2,128]{1,0:T(2,128)S(1)}, f32[2,128]{1,0:T(2,128)S(1)}, f32[2,256]{1,0:T(2,128)S(1)}, bf16[2,128]{1,0:T(2,128)(2,1)S(1)}) custom-call(s32[2]{0:T(128)S(1)} %copy-done.1, s32[2]{0:T(128)S(1)} %copy-done.2, s32[1,2]{1,0:T(1,128)S(1)} %copy-done.3, bf16[8,2,8192]{2,1,0:T(2,128)(2,1)S(1)} %all_to_all.25.near_ref, ...), custom_call_target="tpu_custom_call" | custom-call | bytes 524288 | tf_op jit(solution)/shard_map/turns/pallas_call | solution.py:228
  16.3 0.8 %collective-permute-done.far_ref = bf16[8,2,8192]{2,1,0:T(2,128)(2,1)S(1)} collective-permute-done((bf16[8,2,8192]{2,1,0:T(2,128)(2,1)S(1)}, bf16[8,2,8192]{2,1,0:T(2,128)(2,1)S(1)}, u32[]{:S(2)}, u32[]{:S(2)}) %collective-permute-start) | collective-permute-done | bytes 262176 | tf_op jit(solution)/shard_map/ppermute | solution.py:400
  17.1 0.0 slice-done.6
  17.1 0.0 copy-start.4
  17.1 0.0 copy-start.5
  17.1 0.0 slice-start
  17.2 0.0 slice-start.1
  17.2 0.0 slice-start.7
  17.2 0.0 slice-start.9
  17.2 1.7 %project_qkv.1 = bf16[16,2,768]{2,1,0:T(2,128)(2,1)S(1)} custom-call(bf16[16,8192]{1,0:T(8,128)(2,1)S(1)} %get-tuple-element.15.lined_ref, bf16[8,2,8192]{2,1,0:T(2,128)(2,1)S(1)} %collective-permute-done.far_ref, bf16[8192,640]{1,0:T(8,128)(2,1)S(1)} %bitcast.4, bf16[2,128]{1,0:T(2,128)(2,1)S(1)} %get-tuple-element.16.adapter_ref), custom_call_target="tpu_custom_call" | custom-call | flops 10000000000 | bytes 10485760 | tf_op jit(solution)/shard_map/project_qkv/pallas_call | solution.py:283
  18.9 8.2 %all_to_all.26.mixed_ref = bf16[16,2,768]{2,1,0:T(2,128)(2,1)S(1)} all-to-all(bf16[16,2,768]{2,1,0:T(2,128)(2,1)S(1)} %project_qkv.1), channel_id=1, replica_groups={{11,10,3,2,13,12,5,4,15,14,7,6,9,8,1,0},{27,26,19,18,29,28,21,20,31,30,..., dimensions={0} | all-to-all | bytes 98304 | tf_op jit(solution)/shard_map/all_to_all | solution.py:417
  27.1 0.0 copy-done.5
  27.1 0.0 slice-start.8
  27.2 0.0 slice-start.10
  27.2 0.8 %attend.1 = (bf16[8,2,8192]{2,1,0:T(2,128)(2,1)S(1)}, s32[1,128]{1,0:T(1,128)S(1)}) custom-call(bf16[16,2,768]{2,1,0:T(2,128)(2,1)S(1)} %all_to_all.26.mixed_ref, f32[2,128]{1,0:T(2,128)S(1)} %get-tuple-element.17.cosine_ref, f32[2,128]{1,0:T(2,128)S(1)} %get-tuple-element.18.sine_ref, f32[2,256]{1,0:T(2,128)S(1)} %get-tuple-element.19.mask_ref, ...), custom_call_target="tpu_custom_call" | custom-call | flops 10000000000 | bytes 2097152 | tf_op jit(solution)/shard_map/attend/pallas_call | solution.py:517
  28.0 12.2 %all_to_all.27.gathered_ref = bf16[8,2,8192]{2,1,0:T(2,128)(2,1)S(1)} all-to-all(bf16[8,2,8192]{2,1,0:T(2,128)(2,1)S(1)} %get-tuple-element.21), channel_id=1, replica_groups={{10,2,12,4,14,6,8,0},{11,3,13,5,15,7,9,1},{26,18,28,20,30,22,24,16},{27..., dimensions={0} | all-to-all | bytes 524288 | tf_op jit(solution)/shard_map/all_to_all | solution.py:410
  40.1 0.0 slice-done.1
  40.2 3.3 %project_out.1 = (f32[8,16,128]{2,1,0:T(8,128)S(1)}, f32[16,1024]{1,0:T(8,128)S(1)}, bf16[1024,1024]{1,0:T(8,128)(2,1)S(1)}) custom-call(s32[1,128]{1,0:T(1,128)S(1)} %get-tuple-element.20.adapter_ref, bf16[8,2,8192]{2,1,0:T(2,128)(2,1)S(1)} %all_to_all.27.gathered_ref, bf16[8192,1024]{1,0:T(8,128)(2,1)S(1)} %bitcast.2, bf16[64,64,1024]{2,1,0:T(8,128)(2,1)S(1)} %bitcast.7, ...), custom_call_target="tpu_custom_call" | custom-call | flops 10000000000 | bytes 16777216 | tf_op jit(solution)/shard_map/project_out/pallas_call | solution.py:330
  43.5 8.6 %all_to_all.28.partials_ref = f32[8,16,128]{2,1,0:T(8,128)S(1)} all-to-all(f32[8,16,128]{2,1,0:T(8,128)S(1)} %get-tuple-element.23), channel_id=1, replica_groups={{10,2,12,4,14,6,8,0},{11,3,13,5,15,7,9,1},{26,18,28,20,30,22,24,16},{27..., dimensions={0} | all-to-all | bytes 131072 | tf_op jit(solution)/shard_map/all_to_all | solution.py:410
  52.0 0.4 add_up.1
  52.5 8.4 %all_to_all.29.parts_ref = bf16[8,2,1024]{2,1,0:T(2,128)(2,1)S(1)} all-to-all(bf16[8,2,1024]{2,1,0:T(2,128)(2,1)S(1)} %add_up.1), channel_id=1, replica_groups={{10,2,12,4,14,6,8,0},{11,3,13,5,15,7,9,1},{26,18,28,20,30,22,24,16},{27..., dimensions={0} | all-to-all | bytes 65536 | tf_op jit(solution)/shard_map/all_to_all | solution.py:410
  60.8 0.7 %add_rows.1 = bf16[2,8192]{1,0:T(2,128)(2,1)} custom-call(bf16[2,8192]{1,0:T(2,128)(2,1)S(1)} %copy-done, bf16[8,2,1024]{2,1,0:T(2,128)(2,1)S(1)} %all_to_all.29.parts_ref), custom_call_target="tpu_custom_call" | custom-call | bytes 98304 | tf_op jit(solution)/shard_map/add_rows/pallas_call | solution.py:390
  (25 shorter events, 0.1 us)
Async XLA Ops:
  0.0 0.7 %copy-start.6 = (bf16[8192]{0:T(1024)(128)(2,1)S(1)}, bf16[8192]{0:T(1024)(128)(2,1)}, u32[]{:S(2)}) copy-start(bf16[8192]{0:T(1024)(128)(2,1)} %param.12) | copy-start | bytes 49156
  0.0 0.8 %copy-start = (bf16[2,8192]{1,0:T(2,128)(2,1)S(1)}, bf16[2,8192]{1,0:T(2,128)(2,1)}, u32[]{:S(2)}) copy-start(bf16[2,8192]{1,0:T(2,128)(2,1)} %hidden_ref.3) | copy-start | bytes 98308
  0.0 17.1 %slice-start.4 = ((s8[10485760]{0:T(1024)(128)(4,1)}), s8[4194304]{0:T(1024)(128)(4,1)S(1)}, s32[]{:S(2)}) async-start(s8[10485760]{0:T(1024)(128)(4,1)} %bitcast.3), calls=%async_computation.9 | async-start | bytes 8388608
  0.8 14.8 %copy-start.1 = (s32[2]{0:T(128)S(1)}, s32[2]{0:T(128)}, u32[]{:S(2)}) copy-start(s32[2]{0:T(128)} %lengths_ref.1) | copy-start | bytes 28
  0.8 14.8 %copy-start.2 = (s32[2]{0:T(128)S(1)}, s32[2]{0:T(128)}, u32[]{:S(2)}) copy-start(s32[2]{0:T(128)} %slots_ref.1) | copy-start | bytes 28
  0.8 14.8 %copy-start.3 = (s32[1,2]{1,0:T(1,128)S(1)}, s32[1,2]{1,0:T(1,128)}, u32[]{:S(2)}) copy-start(s32[1,2]{1,0:T(1,128)} %requests_ref.1) | copy-start | bytes 28
  0.8 16.3 %slice-start.5 = ((s8[10485760]{0:T(1024)(128)(4,1)}), s8[4194304]{0:T(1024)(128)(4,1)S(1)}, s32[]{:S(2)}) async-start(s8[10485760]{0:T(1024)(128)(4,1)} %bitcast.3), calls=%async_computation.10 | async-start | bytes 8388608
  0.8 16.3 %slice-start.6 = ((s8[10485760]{0:T(1024)(128)(4,1)}), s8[2097152]{0:T(1024)(128)(4,1)S(1)}, s32[]{:S(2)}) async-start(s8[10485760]{0:T(1024)(128)(4,1)} %bitcast.3), calls=%async_computation.11 | async-start | bytes 4194304
  15.6 1.5 %collective-permute-start = (bf16[8,2,8192]{2,1,0:T(2,128)(2,1)S(1)}, bf16[8,2,8192]{2,1,0:T(2,128)(2,1)S(1)}, u32[]{:S(2)}, u32[]{:S(2)}) collective-permute-start(bf16[8,2,8192]{2,1,0:T(2,128)(2,1)S(1)} %all_to_all.25.near_ref), channel_id=1, source_target_pairs={{0,1},{1,0},{2,3},{3,2},{4,5},{5,4},{6,7},{7,6},{8,9},{9,8},{10,11... | collective-permute-start | bytes 786440 | tf_op jit(solution)/shard_map/ppermute | solution.py:400
  17.1 10.0 %copy-start.4 = (bf16[2,256,1024]{2,1,0:T(8,128)(2,1)S(1)}, bf16[2,256,1024]{2,1,0:T(8,128)(2,1)}, u32[]{:S(2)}) copy-start(bf16[2,256,1024]{2,1,0:T(8,128)(2,1)} %key_ref.1) | copy-start | bytes 3145732
  17.1 10.0 %copy-start.5 = (bf16[2,256,1024]{2,1,0:T(8,128)(2,1)S(1)}, bf16[2,256,1024]{2,1,0:T(8,128)(2,1)}, u32[]{:S(2)}) copy-start(bf16[2,256,1024]{2,1,0:T(8,128)(2,1)} %value_ref.1) | copy-start | bytes 3145732
  17.1 23.0 %slice-start = ((s8[16777216]{0:T(1024)(128)(4,1)}), s8[4194304]{0:T(1024)(128)(4,1)S(1)}, s32[]{:S(2)}) async-start(s8[16777216]{0:T(1024)(128)(4,1)} %bitcast.1), calls=%async_computation.5 | async-start | bytes 8388608
  17.2 23.0 %slice-start.1 = ((s8[16777216]{0:T(1024)(128)(4,1)}), s8[4194304]{0:T(1024)(128)(4,1)S(1)}, s32[]{:S(2)}) async-start(s8[16777216]{0:T(1024)(128)(4,1)} %bitcast.1), calls=%async_computation.6 | async-start | bytes 8388608
  17.2 23.0 %slice-start.7 = ((s8[8388608]{0:T(1024)(128)(4,1)}), s8[4194304]{0:T(1024)(128)(4,1)S(1)}, s32[]{:S(2)}) async-start(s8[8388608]{0:T(1024)(128)(4,1)} %bitcast.5), calls=%async_computation.12 | async-start | bytes 8388608
  17.2 23.0 %slice-start.9 = ((s8[8388608]{0:T(1024)(128)(4,1)}), s8[4194304]{0:T(1024)(128)(4,1)S(1)}, s32[]{:S(2)}) async-start(s8[8388608]{0:T(1024)(128)(4,1)} %bitcast.8), calls=%async_computation.14 | async-start | bytes 8388608
  27.1 13.0 %slice-start.2 = ((s8[16777216]{0:T(1024)(128)(4,1)}), s8[4194304]{0:T(1024)(128)(4,1)S(1)}, s32[]{:S(2)}) async-start(s8[16777216]{0:T(1024)(128)(4,1)} %bitcast.1), calls=%async_computation.7 | async-start | bytes 8388608
  27.1 13.0 %slice-start.3 = ((s8[16777216]{0:T(1024)(128)(4,1)}), s8[4194304]{0:T(1024)(128)(4,1)S(1)}, s32[]{:S(2)}) async-start(s8[16777216]{0:T(1024)(128)(4,1)} %bitcast.1), calls=%async_computation.8 | async-start | bytes 8388608
  27.1 13.0 %slice-start.8 = ((s8[8388608]{0:T(1024)(128)(4,1)}), s8[4194304]{0:T(1024)(128)(4,1)S(1)}, s32[]{:S(2)}) async-start(s8[8388608]{0:T(1024)(128)(4,1)} %bitcast.5), calls=%async_computation.13 | async-start | bytes 8388608
  27.2 13.0 %slice-start.10 = ((s8[8388608]{0:T(1024)(128)(4,1)}), s8[4194304]{0:T(1024)(128)(4,1)S(1)}, s32[]{:S(2)}) async-start(s8[8388608]{0:T(1024)(128)(4,1)} %bitcast.8), calls=%async_computation.15 | async-start | bytes 8388608

commit v28 on v25

--- a/solution.py
+++ b/solution.py
@@ -317,14 +317,14 @@
         total = jnp.zeros((count, LANES), jnp.float32)
         for s in range(0, count * rank, LANES):
             total = total + jnp.where(row == (lane + s) // rank, every[:, s : s + LANES], 0.0)
-        for c in range(groups):
+        for c in range(2 * groups):
             partial_ref[c] = total
 
     return call(
         kernel,
         "project_out",
         (
-            jax.ShapeDtypeStruct((groups, count, LANES), jnp.float32),
+            jax.ShapeDtypeStruct((2 * groups, count, LANES), jnp.float32),
             jax.ShapeDtypeStruct((count, columns), jnp.float32),
             pltpu.VMEM((count * rank, columns), up_store.dtype),
         ),
@@ -340,14 +340,16 @@
 
 
 def add_up(base, partials, up):
-    groups, count, _ = partials.shape
+    blocks, count, _ = partials.shape
+    groups = blocks // 2
     depth, width = up.shape
     rank = depth // count
 
     def kernel(base_ref, partials_ref, up_ref, out_ref):
-        total = partials_ref[0]
+        near = 1 - lax.axis_index("batch")
+        total = partials_ref[near]
         for c in range(1, groups):
-            total = total + partials_ref[c]
+            total = total + partials_ref[2 * c + near]
         down = total.astype(jnp.bfloat16).astype(jnp.float32)
         row = lax.broadcasted_iota(jnp.int32, (count, LANES), 0)
         lane = lax.broadcasted_iota(jnp.int32, (count, LANES), 1)
@@ -357,13 +359,14 @@
         spread = jnp.concatenate(spread, 1).astype(jnp.bfloat16)
         delta = jnp.dot(spread, up_ref[...], preferred_element_type=jnp.float32)
         result = (base_ref[...] + ADAPTER_SCALE * delta).astype(jnp.bfloat16)
-        for j in range(groups):
-            out_ref[j] = result[j * count // groups : (j + 1) * count // groups]
+        for p in range(blocks):
+            j = p // 2
+            out_ref[p] = result[j * count // groups : (j + 1) * count // groups]
 
     return call(
         kernel,
         "add_up",
-        jax.ShapeDtypeStruct((groups, count // groups, width), jnp.bfloat16),
+        jax.ShapeDtypeStruct((blocks, count // groups, width), jnp.bfloat16),
         [VMEM] * 3,
         up.size * 2,
         limit=4 * MIB,
@@ -375,9 +378,10 @@
     width = parts.shape[2]
 
     def kernel(hidden_ref, parts_ref, out_ref):
-        for k, place in enumerate(order(parts.shape[0])):
+        near = 1 - lax.axis_index("batch")
+        for k, place in enumerate(order(parts.shape[0] // 2)):
             part = pl.ds(place * width, width)
-            total = hidden_ref[:, part].astype(jnp.float32) + parts_ref[k].astype(jnp.float32)
+            total = hidden_ref[:, part].astype(jnp.float32) + parts_ref[2 * k + near].astype(jnp.float32)
             out_ref[:, part] = total.astype(jnp.bfloat16)
 
     return call(
@@ -556,8 +560,8 @@
         adapter_down_matrices.swapaxes(1, 2),
         adapter_up_matrices,
     )
-    projected = add_up(base, exchange(partials), up)
-    return add_rows(hidden, exchange(projected))
+    projected = add_up(base, exchange_all(partials), up)
+    return add_rows(hidden, exchange_all(projected))
 
 
 def body(*arguments):

time: 62 us -> 62.5 us (level)
    all_to_all x1 -> x3, blocking collectives: 8.23 us -> 25.7 us  [exchange_all(): lax.all_to_all(blocks, ('mp', 'batch'), split_axis=0, concat_axis=0, tile...]
    all_to_all x4 -> x2, blocking collectives: 43.7 us -> 26.7 us  [exchange(): lax.all_to_all(blocks, 'mp', split_axis=0, concat_axis=0, tiled=True, axi...]
where the time goes in v28:
time: 62.5 us; the launch traced here: 62.2 us
  blocking collectives  52.4 us (84%)
  Pallas kernels  7.88 us (13%)
  local copies, waits for them, and re-layouts  0.84 us (1%)
  waiting for transfers between devices  0.79 us (1%)
    all_to_all x2, blocking collectives, exchange(): lax.all_to_all(blocks, 'mp', split_axis=0, concat_axis=0, tiled=True, axi...  26.7 us
    all_to_all x3, blocking collectives, exchange_all(): lax.all_to_all(blocks, ('mp', 'batch'), split_axis=0, concat_axis=0, tile...  25.7 us
    pallas_call x1, Pallas kernels, project_out(): call(kernel, 'project_out', (jax.ShapeDtypeStruct((2 * groups, count, LAN...  3.28 us
    pallas_call x1, Pallas kernels, project_qkv(): call(kernel, 'project_qkv', jax.ShapeDtypeStruct((2 * groups, rows, width...  1.86 us
  transfers between devices with their start and end apart: 1, of which 1 were waited for; matrix products, arithmetic and copies ran while one was open for 0% of the time, Pallas kernels for 1%

profile of v28, /device:TPU:0, one launch (start us, length us, event | category | flops | bytes accessed | tf_op | source)
XLA Modules:
  0.0 62.2 jit_solution(2366319235872872383)
XLA Ops:
  0.0 0.7 %copy-done.6 = bf16[8192]{0:T(1024)(128)(2,1)S(1)} copy-done((bf16[8192]{0:T(1024)(128)(2,1)S(1)}, bf16[8192]{0:T(1024)(128)(2,1)}, u32[]{:S(2)}) %copy-start.6) | copy-done | bytes 16408
  0.7 0.0 copy-done
  0.8 0.0 slice-start.5
  0.8 0.0 slice-start.6
  0.8 0.2 norm_rows.1
  1.0 14.6 %all_to_all.25.near_ref = bf16[8,2,8192]{2,1,0:T(2,128)(2,1)S(1)} all-to-all(bf16[8,2,8192]{2,1,0:T(2,128)(2,1)S(1)} %norm_rows.1), channel_id=1, replica_groups={{10,2,12,4,14,6,8,0},{11,3,13,5,15,7,9,1},{26,18,28,20,30,22,24,16},{27..., dimensions={0} | all-to-all | bytes 524288 | tf_op jit(solution)/shard_map/all_to_all | solution.py:407
  15.6 0.0 collective-permute-start
  15.6 0.0 copy-done.1
  15.6 0.0 copy-done.2
  15.6 0.0 copy-done.3
  15.6 0.7 %turns.1 = (bf16[16,8192]{1,0:T(8,128)(2,1)S(1)}, f32[2,128]{1,0:T(2,128)S(1)}, f32[2,128]{1,0:T(2,128)S(1)}, f32[2,256]{1,0:T(2,128)S(1)}, bf16[2,128]{1,0:T(2,128)(2,1)S(1)}) custom-call(s32[2]{0:T(128)S(1)} %copy-done.1, s32[2]{0:T(128)S(1)} %copy-done.2, s32[1,2]{1,0:T(1,128)S(1)} %copy-done.3, bf16[8,2,8192]{2,1,0:T(2,128)(2,1)S(1)} %all_to_all.25.near_ref, ...), custom_call_target="tpu_custom_call" | custom-call | bytes 524288 | tf_op jit(solution)/shard_map/turns/pallas_call | solution.py:228
  16.3 0.8 %collective-permute-done.far_ref = bf16[8,2,8192]{2,1,0:T(2,128)(2,1)S(1)} collective-permute-done((bf16[8,2,8192]{2,1,0:T(2,128)(2,1)S(1)}, bf16[8,2,8192]{2,1,0:T(2,128)(2,1)S(1)}, u32[]{:S(2)}, u32[]{:S(2)}) %collective-permute-start) | collective-permute-done | bytes 262176 | tf_op jit(solution)/shard_map/ppermute | solution.py:397
  17.1 0.0 slice-done.4
  17.1 0.0 slice-done.5
  17.1 0.0 copy-start.4
  17.1 0.0 copy-start.5
  17.1 0.0 slice-start
  17.2 0.0 slice-start.1
  17.2 0.0 slice-start.7
  17.2 0.0 slice-start.9
  17.2 1.9 %project_qkv.1 = bf16[16,2,768]{2,1,0:T(2,128)(2,1)S(1)} custom-call(bf16[16,8192]{1,0:T(8,128)(2,1)S(1)} %get-tuple-element.15.lined_ref, bf16[8,2,8192]{2,1,0:T(2,128)(2,1)S(1)} %collective-permute-done.far_ref, bf16[8192,640]{1,0:T(8,128)(2,1)S(1)} %bitcast.4, bf16[2,128]{1,0:T(2,128)(2,1)S(1)} %get-tuple-element.16.adapter_ref), custom_call_target="tpu_custom_call" | custom-call | flops 10000000000 | bytes 10485760 | tf_op jit(solution)/shard_map/project_qkv/pallas_call | solution.py:276
  19.1 8.2 %all_to_all.26.mixed_ref = bf16[16,2,768]{2,1,0:T(2,128)(2,1)S(1)} all-to-all(bf16[16,2,768]{2,1,0:T(2,128)(2,1)S(1)} %project_qkv.1), channel_id=1, replica_groups={{11,10,3,2,13,12,5,4,15,14,7,6,9,8,1,0},{27,26,19,18,29,28,21,20,31,30,..., dimensions={0} | all-to-all | bytes 98304 | tf_op jit(solution)/shard_map/all_to_all | solution.py:414
  27.3 0.0 slice-start.8
  27.3 0.0 slice-start.10
  27.3 0.8 %attend.1 = (bf16[8,2,8192]{2,1,0:T(2,128)(2,1)S(1)}, s32[1,128]{1,0:T(1,128)S(1)}) custom-call(bf16[16,2,768]{2,1,0:T(2,128)(2,1)S(1)} %all_to_all.26.mixed_ref, f32[2,128]{1,0:T(2,128)S(1)} %get-tuple-element.17.cosine_ref, f32[2,128]{1,0:T(2,128)S(1)} %get-tuple-element.18.sine_ref, f32[2,256]{1,0:T(2,128)S(1)} %get-tuple-element.19.mask_ref, ...), custom_call_target="tpu_custom_call" | custom-call | flops 10000000000 | bytes 2097152 | tf_op jit(solution)/shard_map/attend/pallas_call | solution.py:514
  28.1 12.2 %all_to_all.27.gathered_ref = bf16[8,2,8192]{2,1,0:T(2,128)(2,1)S(1)} all-to-all(bf16[8,2,8192]{2,1,0:T(2,128)(2,1)S(1)} %get-tuple-element.21), channel_id=1, replica_groups={{10,2,12,4,14,6,8,0},{11,3,13,5,15,7,9,1},{26,18,28,20,30,22,24,16},{27..., dimensions={0} | all-to-all | bytes 524288 | tf_op jit(solution)/shard_map/all_to_all | solution.py:407
  40.3 0.0 slice-done
  40.4 3.3 %project_out.1 = (f32[16,16,128]{2,1,0:T(8,128)S(1)}, f32[16,1024]{1,0:T(8,128)S(1)}, bf16[1024,1024]{1,0:T(8,128)(2,1)S(1)}) custom-call(s32[1,128]{1,0:T(1,128)S(1)} %get-tuple-element.20.adapter_ref, bf16[8,2,8192]{2,1,0:T(2,128)(2,1)S(1)} %all_to_all.27.gathered_ref, bf16[8192,1024]{1,0:T(8,128)(2,1)S(1)} %bitcast.2, bf16[64,64,1024]{2,1,0:T(8,128)(2,1)S(1)} %bitcast.7, ...), custom_call_target="tpu_custom_call" | custom-call | flops 10000000000 | bytes 16777216 | tf_op jit(solution)/shard_map/project_out/pallas_call | solution.py:323
  43.7 8.6 %all_to_all.28.partials_ref = f32[16,16,128]{2,1,0:T(8,128)S(1)} all-to-all(f32[16,16,128]{2,1,0:T(8,128)S(1)} %get-tuple-element.23), channel_id=1, replica_groups={{11,10,3,2,13,12,5,4,15,14,7,6,9,8,1,0},{27,26,19,18,29,28,21,20,31,30,..., dimensions={0} | all-to-all | bytes 262144 | tf_op jit(solution)/shard_map/all_to_all | solution.py:414
  52.2 0.4 add_up.1
  52.6 8.9 %all_to_all.29.parts_ref = bf16[16,2,1024]{2,1,0:T(2,128)(2,1)S(1)} all-to-all(bf16[16,2,1024]{2,1,0:T(2,128)(2,1)S(1)} %add_up.1), channel_id=1, replica_groups={{11,10,3,2,13,12,5,4,15,14,7,6,9,8,1,0},{27,26,19,18,29,28,21,20,31,30,..., dimensions={0} | all-to-all | bytes 131072 | tf_op jit(solution)/shard_map/all_to_all | solution.py:414
  61.5 0.7 %add_rows.1 = bf16[2,8192]{1,0:T(2,128)(2,1)} custom-call(bf16[2,8192]{1,0:T(2,128)(2,1)S(1)} %copy-done, bf16[16,2,1024]{2,1,0:T(2,128)(2,1)S(1)} %all_to_all.29.parts_ref), custom_call_target="tpu_custom_call" | custom-call | bytes 98304 | tf_op jit(solution)/shard_map/add_rows/pallas_call | solution.py:387
  (25 shorter events, 0.1 us)
Async XLA Ops:
  0.0 0.7 %copy-start.6 = (bf16[8192]{0:T(1024)(128)(2,1)S(1)}, bf16[8192]{0:T(1024)(128)(2,1)}, u32[]{:S(2)}) copy-start(bf16[8192]{0:T(1024)(128)(2,1)} %param.12) | copy-start | bytes 49156
  0.0 0.8 %copy-start = (bf16[2,8192]{1,0:T(2,128)(2,1)S(1)}, bf16[2,8192]{1,0:T(2,128)(2,1)}, u32[]{:S(2)}) copy-start(bf16[2,8192]{1,0:T(2,128)(2,1)} %hidden_ref.3) | copy-start | bytes 98308
  0.0 17.1 %slice-start.4 = ((s8[10485760]{0:T(1024)(128)(4,1)}), s8[4194304]{0:T(1024)(128)(4,1)S(1)}, s32[]{:S(2)}) async-start(s8[10485760]{0:T(1024)(128)(4,1)} %bitcast.3), calls=%async_computation.9 | async-start | bytes 8388608
  0.8 14.8 %copy-start.1 = (s32[2]{0:T(128)S(1)}, s32[2]{0:T(128)}, u32[]{:S(2)}) copy-start(s32[2]{0:T(128)} %lengths_ref.1) | copy-start | bytes 28
  0.8 14.8 %copy-start.2 = (s32[2]{0:T(128)S(1)}, s32[2]{0:T(128)}, u32[]{:S(2)}) copy-start(s32[2]{0:T(128)} %slots_ref.1) | copy-start | bytes 28
  0.8 14.8 %copy-start.3 = (s32[1,2]{1,0:T(1,128)S(1)}, s32[1,2]{1,0:T(1,128)}, u32[]{:S(2)}) copy-start(s32[1,2]{1,0:T(1,128)} %requests_ref.1) | copy-start | bytes 28
  0.8 16.3 %slice-start.5 = ((s8[10485760]{0:T(1024)(128)(4,1)}), s8[4194304]{0:T(1024)(128)(4,1)S(1)}, s32[]{:S(2)}) async-start(s8[10485760]{0:T(1024)(128)(4,1)} %bitcast.3), calls=%async_computation.10 | async-start | bytes 8388608
  0.8 16.3 %slice-start.6 = ((s8[10485760]{0:T(1024)(128)(4,1)}), s8[2097152]{0:T(1024)(128)(4,1)S(1)}, s32[]{:S(2)}) async-start(s8[10485760]{0:T(1024)(128)(4,1)} %bitcast.3), calls=%async_computation.11 | async-start | bytes 4194304
  15.6 1.5 %collective-permute-start = (bf16[8,2,8192]{2,1,0:T(2,128)(2,1)S(1)}, bf16[8,2,8192]{2,1,0:T(2,128)(2,1)S(1)}, u32[]{:S(2)}, u32[]{:S(2)}) collective-permute-start(bf16[8,2,8192]{2,1,0:T(2,128)(2,1)S(1)} %all_to_all.25.near_ref), channel_id=1, source_target_pairs={{0,1},{1,0},{2,3},{3,2},{4,5},{5,4},{6,7},{7,6},{8,9},{9,8},{10,11... | collective-permute-start | bytes 786440 | tf_op jit(solution)/shard_map/ppermute | solution.py:397
  17.1 10.2 %copy-start.4 = (bf16[2,256,1024]{2,1,0:T(8,128)(2,1)S(1)}, bf16[2,256,1024]{2,1,0:T(8,128)(2,1)}, u32[]{:S(2)}) copy-start(bf16[2,256,1024]{2,1,0:T(8,128)(2,1)} %key_ref.1) | copy-start | bytes 3145732
  17.1 10.2 %copy-start.5 = (bf16[2,256,1024]{2,1,0:T(8,128)(2,1)S(1)}, bf16[2,256,1024]{2,1,0:T(8,128)(2,1)}, u32[]{:S(2)}) copy-start(bf16[2,256,1024]{2,1,0:T(8,128)(2,1)} %value_ref.1) | copy-start | bytes 3145732
  17.1 23.1 %slice-start = ((s8[16777216]{0:T(1024)(128)(4,1)}), s8[4194304]{0:T(1024)(128)(4,1)S(1)}, s32[]{:S(2)}) async-start(s8[16777216]{0:T(1024)(128)(4,1)} %bitcast.1), calls=%async_computation.5 | async-start | bytes 8388608
  17.2 23.1 %slice-start.1 = ((s8[16777216]{0:T(1024)(128)(4,1)}), s8[4194304]{0:T(1024)(128)(4,1)S(1)}, s32[]{:S(2)}) async-start(s8[16777216]{0:T(1024)(128)(4,1)} %bitcast.1), calls=%async_computation.6 | async-start | bytes 8388608
  17.2 23.1 %slice-start.7 = ((s8[8388608]{0:T(1024)(128)(4,1)}), s8[4194304]{0:T(1024)(128)(4,1)S(1)}, s32[]{:S(2)}) async-start(s8[8388608]{0:T(1024)(128)(4,1)} %bitcast.5), calls=%async_computation.12 | async-start | bytes 8388608
  17.2 23.1 %slice-start.9 = ((s8[8388608]{0:T(1024)(128)(4,1)}), s8[4194304]{0:T(1024)(128)(4,1)S(1)}, s32[]{:S(2)}) async-start(s8[8388608]{0:T(1024)(128)(4,1)} %bitcast.8), calls=%async_computation.14 | async-start | bytes 8388608
  27.3 13.0 %slice-start.2 = ((s8[16777216]{0:T(1024)(128)(4,1)}), s8[4194304]{0:T(1024)(128)(4,1)S(1)}, s32[]{:S(2)}) async-start(s8[16777216]{0:T(1024)(128)(4,1)} %bitcast.1), calls=%async_computation.7 | async-start | bytes 8388608
  27.3 13.0 %slice-start.3 = ((s8[16777216]{0:T(1024)(128)(4,1)}), s8[4194304]{0:T(1024)(128)(4,1)S(1)}, s32[]{:S(2)}) async-start(s8[16777216]{0:T(1024)(128)(4,1)} %bitcast.1), calls=%async_computation.8 | async-start | bytes 8388608
  27.3 13.0 %slice-start.8 = ((s8[8388608]{0:T(1024)(128)(4,1)}), s8[4194304]{0:T(1024)(128)(4,1)S(1)}, s32[]{:S(2)}) async-start(s8[8388608]{0:T(1024)(128)(4,1)} %bitcast.5), calls=%async_computation.13 | async-start | bytes 8388608
  27.3 13.0 %slice-start.10 = ((s8[8388608]{0:T(1024)(128)(4,1)}), s8[4194304]{0:T(1024)(128)(4,1)S(1)}, s32[]{:S(2)}) async-start(s8[8388608]{0:T(1024)(128)(4,1)} %bitcast.8), calls=%async_computation.15 | async-start | bytes 8388608

commit v29 on v27

--- a/solution.py
+++ b/solution.py
@@ -254,7 +254,7 @@
     )
 
 
-def project_qkv(lined, far, weight, adapter, chunk=4096):
+def project_qkv(lined, far, weight, adapter, chunk=2048):
     groups, rows, _ = far.shape
     depth, width = weight.shape
     half = groups * rows
@@ -305,8 +305,11 @@
             rows_ref[pl.ds(j * rows, rows)] = gathered_ref[j]
         parts = column_parts(columns)
         for k, part in enumerate(parts):
+            cut = features // 2
             base_ref[:, part] = jnp.dot(
-                rows_ref[...], weight_ref[:, part], preferred_element_type=jnp.float32
+                rows_ref[:, :cut], weight_ref[:cut, part], preferred_element_type=jnp.float32
+            ) + jnp.dot(
+                rows_ref[:, cut:], weight_ref[cut:, part], preferred_element_type=jnp.float32
             )
             for r in range(k * count // len(parts), (k + 1) * count // len(parts)):
                 chosen = adapter_ref[0, r]

time: 61.8 us -> 61.9 us (level)
  no operation moved by 1% of the time
where the time goes in v29:
time: 61.9 us; the launch traced here: 61.5 us
  blocking collectives  51.9 us (84%)
  Pallas kernels  7.75 us (13%)
  local copies, waits for them, and re-layouts  0.84 us (1%)
  waiting for transfers between devices  0.79 us (1%)
    all_to_all x4, blocking collectives, exchange(): lax.all_to_all(blocks, 'mp', split_axis=0, concat_axis=0, tiled=True, axi...  43.7 us
    all_to_all x1, blocking collectives, exchange_all(): lax.all_to_all(blocks, ('mp', 'batch'), split_axis=0, concat_axis=0, tile...  8.23 us
    pallas_call x1, Pallas kernels, project_out(): call(kernel, 'project_out', (jax.ShapeDtypeStruct((groups, count, LANES),...  3.27 us
    pallas_call x1, Pallas kernels, project_qkv(): call(kernel, 'project_qkv', jax.ShapeDtypeStruct((2 * groups, rows, width...  1.74 us
  transfers between devices with their start and end apart: 1, of which 1 were waited for; matrix products, arithmetic and copies ran while one was open for 0% of the time, Pallas kernels for 1%

profile of v29, /device:TPU:0, one launch (start us, length us, event | category | flops | bytes accessed | tf_op | source)
XLA Modules:
  0.0 61.5 jit_solution(2861691903115640275)
XLA Ops:
  0.0 0.7 %copy-done.6 = bf16[8192]{0:T(1024)(128)(2,1)S(1)} copy-done((bf16[8192]{0:T(1024)(128)(2,1)S(1)}, bf16[8192]{0:T(1024)(128)(2,1)}, u32[]{:S(2)}) %copy-start.6) | copy-done | bytes 16408
  0.7 0.0 copy-done
  0.8 0.0 slice-start.5
  0.8 0.0 slice-start.6
  0.8 0.2 norm_rows.1
  1.0 14.6 %all_to_all.25.near_ref = bf16[8,2,8192]{2,1,0:T(2,128)(2,1)S(1)} all-to-all(bf16[8,2,8192]{2,1,0:T(2,128)(2,1)S(1)} %norm_rows.1), channel_id=1, replica_groups={{10,2,12,4,14,6,8,0},{11,3,13,5,15,7,9,1},{26,18,28,20,30,22,24,16},{27..., dimensions={0} | all-to-all | bytes 524288 | tf_op jit(solution)/shard_map/all_to_all | solution.py:413
  15.6 0.0 collective-permute-start
  15.6 0.0 copy-done.1
  15.6 0.0 copy-done.2
  15.6 0.7 %turns.1 = (bf16[16,8192]{1,0:T(8,128)(2,1)S(1)}, f32[2,128]{1,0:T(2,128)S(1)}, f32[2,128]{1,0:T(2,128)S(1)}, f32[2,256]{1,0:T(2,128)S(1)}, bf16[2,128]{1,0:T(2,128)(2,1)S(1)}) custom-call(s32[2]{0:T(128)S(1)} %copy-done.1, s32[2]{0:T(128)S(1)} %copy-done.2, s32[1,2]{1,0:T(1,128)S(1)} %copy-done.3, bf16[8,2,8192]{2,1,0:T(2,128)(2,1)S(1)} %all_to_all.25.near_ref, ...), custom_call_target="tpu_custom_call" | custom-call | bytes 524288 | tf_op jit(solution)/shard_map/turns/pallas_call | solution.py:228
  16.3 0.8 %collective-permute-done.far_ref = bf16[8,2,8192]{2,1,0:T(2,128)(2,1)S(1)} collective-permute-done((bf16[8,2,8192]{2,1,0:T(2,128)(2,1)S(1)}, bf16[8,2,8192]{2,1,0:T(2,128)(2,1)S(1)}, u32[]{:S(2)}, u32[]{:S(2)}) %collective-permute-start) | collective-permute-done | bytes 262176 | tf_op jit(solution)/shard_map/ppermute | solution.py:403
  17.1 0.0 slice-done.6
  17.1 0.0 copy-start.4
  17.1 0.0 copy-start.5
  17.1 0.0 slice-start
  17.2 0.0 slice-start.1
  17.2 0.0 slice-start.7
  17.2 0.0 slice-start.9
  17.2 1.7 %project_qkv.1 = bf16[16,2,768]{2,1,0:T(2,128)(2,1)S(1)} custom-call(bf16[16,8192]{1,0:T(8,128)(2,1)S(1)} %get-tuple-element.15.lined_ref, bf16[8,2,8192]{2,1,0:T(2,128)(2,1)S(1)} %collective-permute-done.far_ref, bf16[8192,640]{1,0:T(8,128)(2,1)S(1)} %bitcast.4, bf16[2,128]{1,0:T(2,128)(2,1)S(1)} %get-tuple-element.16.adapter_ref), custom_call_target="tpu_custom_call" | custom-call | flops 10000000000 | bytes 10485760 | tf_op jit(solution)/shard_map/project_qkv/pallas_call | solution.py:283
  19.0 8.2 %all_to_all.26.mixed_ref = bf16[16,2,768]{2,1,0:T(2,128)(2,1)S(1)} all-to-all(bf16[16,2,768]{2,1,0:T(2,128)(2,1)S(1)} %project_qkv.1), channel_id=1, replica_groups={{11,10,3,2,13,12,5,4,15,14,7,6,9,8,1,0},{27,26,19,18,29,28,21,20,31,30,..., dimensions={0} | all-to-all | bytes 98304 | tf_op jit(solution)/shard_map/all_to_all | solution.py:420
  27.2 0.0 copy-done.4
  27.2 0.0 slice-start.8
  27.2 0.0 slice-start.10
  27.2 0.8 %attend.1 = (bf16[8,2,8192]{2,1,0:T(2,128)(2,1)S(1)}, s32[1,128]{1,0:T(1,128)S(1)}) custom-call(bf16[16,2,768]{2,1,0:T(2,128)(2,1)S(1)} %all_to_all.26.mixed_ref, f32[2,128]{1,0:T(2,128)S(1)} %get-tuple-element.17.cosine_ref, f32[2,128]{1,0:T(2,128)S(1)} %get-tuple-element.18.sine_ref, f32[2,256]{1,0:T(2,128)S(1)} %get-tuple-element.19.mask_ref, ...), custom_call_target="tpu_custom_call" | custom-call | flops 10000000000 | bytes 2097152 | tf_op jit(solution)/shard_map/attend/pallas_call | solution.py:520
  28.0 12.2 %all_to_all.27.gathered_ref = bf16[8,2,8192]{2,1,0:T(2,128)(2,1)S(1)} all-to-all(bf16[8,2,8192]{2,1,0:T(2,128)(2,1)S(1)} %get-tuple-element.21), channel_id=1, replica_groups={{10,2,12,4,14,6,8,0},{11,3,13,5,15,7,9,1},{26,18,28,20,30,22,24,16},{27..., dimensions={0} | all-to-all | bytes 524288 | tf_op jit(solution)/shard_map/all_to_all | solution.py:413
  40.2 0.0 slice-done
  40.2 0.0 slice-done.7
  40.3 3.3 %project_out.1 = (f32[8,16,128]{2,1,0:T(8,128)S(1)}, f32[16,1024]{1,0:T(8,128)S(1)}, bf16[1024,1024]{1,0:T(8,128)(2,1)S(1)}) custom-call(s32[1,128]{1,0:T(1,128)S(1)} %get-tuple-element.20.adapter_ref, bf16[8,2,8192]{2,1,0:T(2,128)(2,1)S(1)} %all_to_all.27.gathered_ref, bf16[8192,1024]{1,0:T(8,128)(2,1)S(1)} %bitcast.2, bf16[64,64,1024]{2,1,0:T(8,128)(2,1)S(1)} %bitcast.7, ...), custom_call_target="tpu_custom_call" | custom-call | flops 10000000000 | bytes 16777216 | tf_op jit(solution)/shard_map/project_out/pallas_call | solution.py:333
  43.5 8.6 %all_to_all.28.partials_ref = f32[8,16,128]{2,1,0:T(8,128)S(1)} all-to-all(f32[8,16,128]{2,1,0:T(8,128)S(1)} %get-tuple-element.23), channel_id=1, replica_groups={{10,2,12,4,14,6,8,0},{11,3,13,5,15,7,9,1},{26,18,28,20,30,22,24,16},{27..., dimensions={0} | all-to-all | bytes 131072 | tf_op jit(solution)/shard_map/all_to_all | solution.py:413
  52.1 0.4 add_up.1
  52.5 8.4 %all_to_all.29.parts_ref = bf16[8,2,1024]{2,1,0:T(2,128)(2,1)S(1)} all-to-all(bf16[8,2,1024]{2,1,0:T(2,128)(2,1)S(1)} %add_up.1), channel_id=1, replica_groups={{10,2,12,4,14,6,8,0},{11,3,13,5,15,7,9,1},{26,18,28,20,30,22,24,16},{27..., dimensions={0} | all-to-all | bytes 65536 | tf_op jit(solution)/shard_map/all_to_all | solution.py:413
  60.9 0.7 %add_rows.1 = bf16[2,8192]{1,0:T(2,128)(2,1)} custom-call(bf16[2,8192]{1,0:T(2,128)(2,1)S(1)} %copy-done, bf16[8,2,1024]{2,1,0:T(2,128)(2,1)S(1)} %all_to_all.29.parts_ref), custom_call_target="tpu_custom_call" | custom-call | bytes 98304 | tf_op jit(solution)/shard_map/add_rows/pallas_call | solution.py:393
  (25 shorter events, 0.1 us)
Async XLA Ops:
  0.0 0.7 %copy-start.6 = (bf16[8192]{0:T(1024)(128)(2,1)S(1)}, bf16[8192]{0:T(1024)(128)(2,1)}, u32[]{:S(2)}) copy-start(bf16[8192]{0:T(1024)(128)(2,1)} %param.12) | copy-start | bytes 49156
  0.0 0.8 %copy-start = (bf16[2,8192]{1,0:T(2,128)(2,1)S(1)}, bf16[2,8192]{1,0:T(2,128)(2,1)}, u32[]{:S(2)}) copy-start(bf16[2,8192]{1,0:T(2,128)(2,1)} %hidden_ref.3) | copy-start | bytes 98308
  0.0 17.1 %slice-start.4 = ((s8[10485760]{0:T(1024)(128)(4,1)}), s8[4194304]{0:T(1024)(128)(4,1)S(1)}, s32[]{:S(2)}) async-start(s8[10485760]{0:T(1024)(128)(4,1)} %bitcast.3), calls=%async_computation.9 | async-start | bytes 8388608
  0.8 14.8 %copy-start.1 = (s32[2]{0:T(128)S(1)}, s32[2]{0:T(128)}, u32[]{:S(2)}) copy-start(s32[2]{0:T(128)} %lengths_ref.1) | copy-start | bytes 28
  0.8 14.8 %copy-start.2 = (s32[2]{0:T(128)S(1)}, s32[2]{0:T(128)}, u32[]{:S(2)}) copy-start(s32[2]{0:T(128)} %slots_ref.1) | copy-start | bytes 28
  0.8 14.8 %copy-start.3 = (s32[1,2]{1,0:T(1,128)S(1)}, s32[1,2]{1,0:T(1,128)}, u32[]{:S(2)}) copy-start(s32[1,2]{1,0:T(1,128)} %requests_ref.1) | copy-start | bytes 28
  0.8 16.3 %slice-start.5 = ((s8[10485760]{0:T(1024)(128)(4,1)}), s8[4194304]{0:T(1024)(128)(4,1)S(1)}, s32[]{:S(2)}) async-start(s8[10485760]{0:T(1024)(128)(4,1)} %bitcast.3), calls=%async_computation.10 | async-start | bytes 8388608
  0.8 16.3 %slice-start.6 = ((s8[10485760]{0:T(1024)(128)(4,1)}), s8[2097152]{0:T(1024)(128)(4,1)S(1)}, s32[]{:S(2)}) async-start(s8[10485760]{0:T(1024)(128)(4,1)} %bitcast.3), calls=%async_computation.11 | async-start | bytes 4194304
  15.6 1.5 %collective-permute-start = (bf16[8,2,8192]{2,1,0:T(2,128)(2,1)S(1)}, bf16[8,2,8192]{2,1,0:T(2,128)(2,1)S(1)}, u32[]{:S(2)}, u32[]{:S(2)}) collective-permute-start(bf16[8,2,8192]{2,1,0:T(2,128)(2,1)S(1)} %all_to_all.25.near_ref), channel_id=1, source_target_pairs={{0,1},{1,0},{2,3},{3,2},{4,5},{5,4},{6,7},{7,6},{8,9},{9,8},{10,11... | collective-permute-start | bytes 786440 | tf_op jit(solution)/shard_map/ppermute | solution.py:403
  17.1 10.1 %copy-start.4 = (bf16[2,256,1024]{2,1,0:T(8,128)(2,1)S(1)}, bf16[2,256,1024]{2,1,0:T(8,128)(2,1)}, u32[]{:S(2)}) copy-start(bf16[2,256,1024]{2,1,0:T(8,128)(2,1)} %key_ref.1) | copy-start | bytes 3145732
  17.1 10.0 %copy-start.5 = (bf16[2,256,1024]{2,1,0:T(8,128)(2,1)S(1)}, bf16[2,256,1024]{2,1,0:T(8,128)(2,1)}, u32[]{:S(2)}) copy-start(bf16[2,256,1024]{2,1,0:T(8,128)(2,1)} %value_ref.1) | copy-start | bytes 3145732
  17.1 23.0 %slice-start = ((s8[16777216]{0:T(1024)(128)(4,1)}), s8[4194304]{0:T(1024)(128)(4,1)S(1)}, s32[]{:S(2)}) async-start(s8[16777216]{0:T(1024)(128)(4,1)} %bitcast.1), calls=%async_computation.5 | async-start | bytes 8388608
  17.2 23.0 %slice-start.1 = ((s8[16777216]{0:T(1024)(128)(4,1)}), s8[4194304]{0:T(1024)(128)(4,1)S(1)}, s32[]{:S(2)}) async-start(s8[16777216]{0:T(1024)(128)(4,1)} %bitcast.1), calls=%async_computation.6 | async-start | bytes 8388608
  17.2 23.0 %slice-start.7 = ((s8[8388608]{0:T(1024)(128)(4,1)}), s8[4194304]{0:T(1024)(128)(4,1)S(1)}, s32[]{:S(2)}) async-start(s8[8388608]{0:T(1024)(128)(4,1)} %bitcast.5), calls=%async_computation.12 | async-start | bytes 8388608
  17.2 23.0 %slice-start.9 = ((s8[8388608]{0:T(1024)(128)(4,1)}), s8[4194304]{0:T(1024)(128)(4,1)S(1)}, s32[]{:S(2)}) async-start(s8[8388608]{0:T(1024)(128)(4,1)} %bitcast.8), calls=%async_computation.14 | async-start | bytes 8388608
  27.2 13.0 %slice-start.2 = ((s8[16777216]{0:T(1024)(128)(4,1)}), s8[4194304]{0:T(1024)(128)(4,1)S(1)}, s32[]{:S(2)}) async-start(s8[16777216]{0:T(1024)(128)(4,1)} %bitcast.1), calls=%async_computation.7 | async-start | bytes 8388608
  27.2 13.0 %slice-start.3 = ((s8[16777216]{0:T(1024)(128)(4,1)}), s8[4194304]{0:T(1024)(128)(4,1)S(1)}, s32[]{:S(2)}) async-start(s8[16777216]{0:T(1024)(128)(4,1)} %bitcast.1), calls=%async_computation.8 | async-start | bytes 8388608
  27.2 13.0 %slice-start.8 = ((s8[8388608]{0:T(1024)(128)(4,1)}), s8[4194304]{0:T(1024)(128)(4,1)S(1)}, s32[]{:S(2)}) async-start(s8[8388608]{0:T(1024)(128)(4,1)} %bitcast.5), calls=%async_computation.13 | async-start | bytes 8388608
  27.2 13.0 %slice-start.10 = ((s8[8388608]{0:T(1024)(128)(4,1)}), s8[4194304]{0:T(1024)(128)(4,1)S(1)}, s32[]{:S(2)}) async-start(s8[8388608]{0:T(1024)(128)(4,1)} %bitcast.8), calls=%async_computation.15 | async-start | bytes 8388608

commit v30 on v25

--- a/solution.py
+++ b/solution.py
@@ -395,7 +395,7 @@
 
 def order(size):
     half = size // 2
-    return [(k + 1) % half + start for k in range(half) for start in (half, 0)]
+    return [(k - 1) % half + start for k in range(half) for start in (0, half)]
 
 
 def exchange(blocks):

time: 62 us -> 62.8 us (1.013)
  blocking collectives: 51.9 us -> 52.6 us
    all_to_all x1, blocking collectives: 8.23 us -> 8.87 us  [exchange_all(): lax.all_to_all(blocks, ('mp', 'batch'), split_axis=0, concat_axis=0, tile...]
where the time goes in v30:
time: 62.8 us; the launch traced here: 62.4 us
  blocking collectives  52.6 us (84%)
  Pallas kernels  7.88 us (13%)
  local copies, waits for them, and re-layouts  0.84 us (1%)
  waiting for transfers between devices  0.79 us (1%)
    all_to_all x4, blocking collectives, exchange(): lax.all_to_all(blocks, 'mp', split_axis=0, concat_axis=0, tiled=True, axi...  43.8 us
    all_to_all x1, blocking collectives, exchange_all(): lax.all_to_all(blocks, ('mp', 'batch'), split_axis=0, concat_axis=0, tile...  8.87 us
    pallas_call x1, Pallas kernels, project_out(): call(kernel, 'project_out', (jax.ShapeDtypeStruct((groups, count, LANES),...  3.27 us
    pallas_call x1, Pallas kernels, project_qkv(): call(kernel, 'project_qkv', jax.ShapeDtypeStruct((2 * groups, rows, width...  1.87 us
  transfers between devices with their start and end apart: 1, of which 1 were waited for; matrix products, arithmetic and copies ran while one was open for 0% of the time, Pallas kernels for 1%

profile of v30, /device:TPU:0, one launch (start us, length us, event | category | flops | bytes accessed | tf_op | source)
XLA Modules:
  0.0 62.4 jit_solution(17034321922770329300)
XLA Ops:
  0.0 0.7 %copy-done.6 = bf16[8192]{0:T(1024)(128)(2,1)S(1)} copy-done((bf16[8192]{0:T(1024)(128)(2,1)S(1)}, bf16[8192]{0:T(1024)(128)(2,1)}, u32[]{:S(2)}) %copy-start.6) | copy-done | bytes 16408
  0.7 0.0 copy-done
  0.8 0.0 slice-start.5
  0.8 0.0 slice-start.6
  0.8 0.2 norm_rows.1
  1.0 14.9 %all_to_all.25.near_ref = bf16[8,2,8192]{2,1,0:T(2,128)(2,1)S(1)} all-to-all(bf16[8,2,8192]{2,1,0:T(2,128)(2,1)S(1)} %norm_rows.1), channel_id=1, replica_groups={{6,14,0,8,2,10,4,12},{7,15,1,9,3,11,5,13},{22,30,16,24,18,26,20,28},{23..., dimensions={0} | all-to-all | bytes 524288 | tf_op jit(solution)/shard_map/all_to_all | solution.py:403
  15.9 0.0 collective-permute-start
  15.9 0.0 copy-done.1
  15.9 0.0 copy-done.2
  16.0 0.0 copy-done.3
  16.0 0.7 %turns.1 = (bf16[16,8192]{1,0:T(8,128)(2,1)S(1)}, f32[2,128]{1,0:T(2,128)S(1)}, f32[2,128]{1,0:T(2,128)S(1)}, f32[2,256]{1,0:T(2,128)S(1)}, bf16[2,128]{1,0:T(2,128)(2,1)S(1)}) custom-call(s32[2]{0:T(128)S(1)} %copy-done.1, s32[2]{0:T(128)S(1)} %copy-done.2, s32[1,2]{1,0:T(1,128)S(1)} %copy-done.3, bf16[8,2,8192]{2,1,0:T(2,128)(2,1)S(1)} %all_to_all.25.near_ref, ...), custom_call_target="tpu_custom_call" | custom-call | bytes 524288 | tf_op jit(solution)/shard_map/turns/pallas_call | solution.py:228
  16.7 0.8 %collective-permute-done.far_ref = bf16[8,2,8192]{2,1,0:T(2,128)(2,1)S(1)} collective-permute-done((bf16[8,2,8192]{2,1,0:T(2,128)(2,1)S(1)}, bf16[8,2,8192]{2,1,0:T(2,128)(2,1)S(1)}, u32[]{:S(2)}, u32[]{:S(2)}) %collective-permute-start) | collective-permute-done | bytes 262176 | tf_op jit(solution)/shard_map/ppermute | solution.py:393
  17.5 0.0 slice-done.4
  17.5 0.0 slice-done.5
  17.5 0.0 copy-start.4
  17.5 0.0 copy-start.5
  17.5 0.0 slice-start
  17.5 0.0 slice-start.1
  17.5 0.0 slice-start.7
  17.6 0.0 slice-start.9
  17.6 1.9 %project_qkv.1 = bf16[16,2,768]{2,1,0:T(2,128)(2,1)S(1)} custom-call(bf16[16,8192]{1,0:T(8,128)(2,1)S(1)} %get-tuple-element.15.lined_ref, bf16[8,2,8192]{2,1,0:T(2,128)(2,1)S(1)} %collective-permute-done.far_ref, bf16[8192,640]{1,0:T(8,128)(2,1)S(1)} %bitcast.4, bf16[2,128]{1,0:T(2,128)(2,1)S(1)} %get-tuple-element.16.adapter_ref), custom_call_target="tpu_custom_call" | custom-call | flops 10000000000 | bytes 10485760 | tf_op jit(solution)/shard_map/project_qkv/pallas_call | solution.py:276
  19.4 8.9 %all_to_all.26.mixed_ref = bf16[16,2,768]{2,1,0:T(2,128)(2,1)S(1)} all-to-all(bf16[16,2,768]{2,1,0:T(2,128)(2,1)S(1)} %project_qkv.1), channel_id=1, replica_groups={{7,6,15,14,1,0,9,8,3,2,11,10,5,4,13,12},{23,22,31,30,17,16,25,24,19,18,..., dimensions={0} | all-to-all | bytes 98304 | tf_op jit(solution)/shard_map/all_to_all | solution.py:410
  28.3 0.0 slice-start.8
  28.3 0.0 slice-start.10
  28.4 0.8 %attend.1 = (bf16[8,2,8192]{2,1,0:T(2,128)(2,1)S(1)}, s32[1,128]{1,0:T(1,128)S(1)}) custom-call(bf16[16,2,768]{2,1,0:T(2,128)(2,1)S(1)} %all_to_all.26.mixed_ref, f32[2,128]{1,0:T(2,128)S(1)} %get-tuple-element.17.cosine_ref, f32[2,128]{1,0:T(2,128)S(1)} %get-tuple-element.18.sine_ref, f32[2,256]{1,0:T(2,128)S(1)} %get-tuple-element.19.mask_ref, ...), custom_call_target="tpu_custom_call" | custom-call | flops 10000000000 | bytes 2097152 | tf_op jit(solution)/shard_map/attend/pallas_call | solution.py:510
  29.1 11.5 %all_to_all.27.gathered_ref = bf16[8,2,8192]{2,1,0:T(2,128)(2,1)S(1)} all-to-all(bf16[8,2,8192]{2,1,0:T(2,128)(2,1)S(1)} %get-tuple-element.21), channel_id=1, replica_groups={{6,14,0,8,2,10,4,12},{7,15,1,9,3,11,5,13},{22,30,16,24,18,26,20,28},{23..., dimensions={0} | all-to-all | bytes 524288 | tf_op jit(solution)/shard_map/all_to_all | solution.py:403
  40.7 0.0 slice-done
  40.8 3.3 %project_out.1 = (f32[8,16,128]{2,1,0:T(8,128)S(1)}, f32[16,1024]{1,0:T(8,128)S(1)}, bf16[1024,1024]{1,0:T(8,128)(2,1)S(1)}) custom-call(s32[1,128]{1,0:T(1,128)S(1)} %get-tuple-element.20.adapter_ref, bf16[8,2,8192]{2,1,0:T(2,128)(2,1)S(1)} %all_to_all.27.gathered_ref, bf16[8192,1024]{1,0:T(8,128)(2,1)S(1)} %bitcast.2, bf16[64,64,1024]{2,1,0:T(8,128)(2,1)S(1)} %bitcast.7, ...), custom_call_target="tpu_custom_call" | custom-call | flops 10000000000 | bytes 16777216 | tf_op jit(solution)/shard_map/project_out/pallas_call | solution.py:323
  44.0 9.0 %all_to_all.28.partials_ref = f32[8,16,128]{2,1,0:T(8,128)S(1)} all-to-all(f32[8,16,128]{2,1,0:T(8,128)S(1)} %get-tuple-element.23), channel_id=1, replica_groups={{6,14,0,8,2,10,4,12},{7,15,1,9,3,11,5,13},{22,30,16,24,18,26,20,28},{23..., dimensions={0} | all-to-all | bytes 131072 | tf_op jit(solution)/shard_map/all_to_all | solution.py:403
  53.0 0.4 add_up.1
  53.4 8.3 %all_to_all.29.parts_ref = bf16[8,2,1024]{2,1,0:T(2,128)(2,1)S(1)} all-to-all(bf16[8,2,1024]{2,1,0:T(2,128)(2,1)S(1)} %add_up.1), channel_id=1, replica_groups={{6,14,0,8,2,10,4,12},{7,15,1,9,3,11,5,13},{22,30,16,24,18,26,20,28},{23..., dimensions={0} | all-to-all | bytes 65536 | tf_op jit(solution)/shard_map/all_to_all | solution.py:403
  61.8 0.7 %add_rows.1 = bf16[2,8192]{1,0:T(2,128)(2,1)} custom-call(bf16[2,8192]{1,0:T(2,128)(2,1)S(1)} %copy-done, bf16[8,2,1024]{2,1,0:T(2,128)(2,1)S(1)} %all_to_all.29.parts_ref), custom_call_target="tpu_custom_call" | custom-call | bytes 98304 | tf_op jit(solution)/shard_map/add_rows/pallas_call | solution.py:383
  (25 shorter events, 0.1 us)
Async XLA Ops:
  0.0 0.7 %copy-start.6 = (bf16[8192]{0:T(1024)(128)(2,1)S(1)}, bf16[8192]{0:T(1024)(128)(2,1)}, u32[]{:S(2)}) copy-start(bf16[8192]{0:T(1024)(128)(2,1)} %param.12) | copy-start | bytes 49156
  0.0 0.8 %copy-start = (bf16[2,8192]{1,0:T(2,128)(2,1)S(1)}, bf16[2,8192]{1,0:T(2,128)(2,1)}, u32[]{:S(2)}) copy-start(bf16[2,8192]{1,0:T(2,128)(2,1)} %hidden_ref.3) | copy-start | bytes 98308
  0.0 17.5 %slice-start.4 = ((s8[10485760]{0:T(1024)(128)(4,1)}), s8[4194304]{0:T(1024)(128)(4,1)S(1)}, s32[]{:S(2)}) async-start(s8[10485760]{0:T(1024)(128)(4,1)} %bitcast.3), calls=%async_computation.9 | async-start | bytes 8388608
  0.8 15.2 %copy-start.1 = (s32[2]{0:T(128)S(1)}, s32[2]{0:T(128)}, u32[]{:S(2)}) copy-start(s32[2]{0:T(128)} %lengths_ref.1) | copy-start | bytes 28
  0.8 15.2 %copy-start.2 = (s32[2]{0:T(128)S(1)}, s32[2]{0:T(128)}, u32[]{:S(2)}) copy-start(s32[2]{0:T(128)} %slots_ref.1) | copy-start | bytes 28
  0.8 15.2 %copy-start.3 = (s32[1,2]{1,0:T(1,128)S(1)}, s32[1,2]{1,0:T(1,128)}, u32[]{:S(2)}) copy-start(s32[1,2]{1,0:T(1,128)} %requests_ref.1) | copy-start | bytes 28
  0.8 16.7 %slice-start.5 = ((s8[10485760]{0:T(1024)(128)(4,1)}), s8[4194304]{0:T(1024)(128)(4,1)S(1)}, s32[]{:S(2)}) async-start(s8[10485760]{0:T(1024)(128)(4,1)} %bitcast.3), calls=%async_computation.10 | async-start | bytes 8388608
  0.8 16.7 %slice-start.6 = ((s8[10485760]{0:T(1024)(128)(4,1)}), s8[2097152]{0:T(1024)(128)(4,1)S(1)}, s32[]{:S(2)}) async-start(s8[10485760]{0:T(1024)(128)(4,1)} %bitcast.3), calls=%async_computation.11 | async-start | bytes 4194304
  15.9 1.5 %collective-permute-start = (bf16[8,2,8192]{2,1,0:T(2,128)(2,1)S(1)}, bf16[8,2,8192]{2,1,0:T(2,128)(2,1)S(1)}, u32[]{:S(2)}, u32[]{:S(2)}) collective-permute-start(bf16[8,2,8192]{2,1,0:T(2,128)(2,1)S(1)} %all_to_all.25.near_ref), channel_id=1, source_target_pairs={{0,1},{1,0},{2,3},{3,2},{4,5},{5,4},{6,7},{7,6},{8,9},{9,8},{10,11... | collective-permute-start | bytes 786440 | tf_op jit(solution)/shard_map/ppermute | solution.py:393
  17.5 10.8 %copy-start.4 = (bf16[2,256,1024]{2,1,0:T(8,128)(2,1)S(1)}, bf16[2,256,1024]{2,1,0:T(8,128)(2,1)}, u32[]{:S(2)}) copy-start(bf16[2,256,1024]{2,1,0:T(8,128)(2,1)} %key_ref.1) | copy-start | bytes 3145732
  17.5 10.8 %copy-start.5 = (bf16[2,256,1024]{2,1,0:T(8,128)(2,1)S(1)}, bf16[2,256,1024]{2,1,0:T(8,128)(2,1)}, u32[]{:S(2)}) copy-start(bf16[2,256,1024]{2,1,0:T(8,128)(2,1)} %value_ref.1) | copy-start | bytes 3145732
  17.5 23.1 %slice-start = ((s8[16777216]{0:T(1024)(128)(4,1)}), s8[4194304]{0:T(1024)(128)(4,1)S(1)}, s32[]{:S(2)}) async-start(s8[16777216]{0:T(1024)(128)(4,1)} %bitcast.1), calls=%async_computation.5 | async-start | bytes 8388608
  17.5 23.1 %slice-start.1 = ((s8[16777216]{0:T(1024)(128)(4,1)}), s8[4194304]{0:T(1024)(128)(4,1)S(1)}, s32[]{:S(2)}) async-start(s8[16777216]{0:T(1024)(128)(4,1)} %bitcast.1), calls=%async_computation.6 | async-start | bytes 8388608
  17.5 23.1 %slice-start.7 = ((s8[8388608]{0:T(1024)(128)(4,1)}), s8[4194304]{0:T(1024)(128)(4,1)S(1)}, s32[]{:S(2)}) async-start(s8[8388608]{0:T(1024)(128)(4,1)} %bitcast.5), calls=%async_computation.12 | async-start | bytes 8388608
  17.6 23.1 %slice-start.9 = ((s8[8388608]{0:T(1024)(128)(4,1)}), s8[4194304]{0:T(1024)(128)(4,1)S(1)}, s32[]{:S(2)}) async-start(s8[8388608]{0:T(1024)(128)(4,1)} %bitcast.8), calls=%async_computation.14 | async-start | bytes 8388608
  28.3 12.4 %slice-start.2 = ((s8[16777216]{0:T(1024)(128)(4,1)}), s8[4194304]{0:T(1024)(128)(4,1)S(1)}, s32[]{:S(2)}) async-start(s8[16777216]{0:T(1024)(128)(4,1)} %bitcast.1), calls=%async_computation.7 | async-start | bytes 8388608
  28.3 12.4 %slice-start.3 = ((s8[16777216]{0:T(1024)(128)(4,1)}), s8[4194304]{0:T(1024)(128)(4,1)S(1)}, s32[]{:S(2)}) async-start(s8[16777216]{0:T(1024)(128)(4,1)} %bitcast.1), calls=%async_computation.8 | async-start | bytes 8388608
  28.3 12.4 %slice-start.8 = ((s8[8388608]{0:T(1024)(128)(4,1)}), s8[4194304]{0:T(1024)(128)(4,1)S(1)}, s32[]{:S(2)}) async-start(s8[8388608]{0:T(1024)(128)(4,1)} %bitcast.5), calls=%async_computation.13 | async-start | bytes 8388608
  28.3 12.4 %slice-start.10 = ((s8[8388608]{0:T(1024)(128)(4,1)}), s8[4194304]{0:T(1024)(128)(4,1)S(1)}, s32[]{:S(2)}) async-start(s8[8388608]{0:T(1024)(128)(4,1)} %bitcast.8), calls=%async_computation.15 | async-start | bytes 8388608
